TPU v7x, 32 devices: a whole 2x2x4 slice. The times are simulated.
32 devices in a mesh: seq: 8 (over y, x, core), shard: 4 (over z).
Axes of the slice: x: 2, y: 2, z: 4, core: 2. Of those that a mesh axis runs over, the one named last changes fastest.
Arguments:
- tokens: bfloat16 [2, 1024, 2048], P(None, 'seq', 'shard')
- doc_starts: int32 [2, 16], replicated, may hold values from 0 to 1024, as said below
- norm_gain: float32 [2048], replicated, may hold values from 0.5 to 1.5
- query_weight: bfloat16 [2048, 2048], P('seq', 'shard'), may hold values from -0.125 to 0.125
- key_weight: bfloat16 [2048, 2048], P('seq', 'shard'), may hold values from -0.125 to 0.125
- value_weight: bfloat16 [2048, 4096], P('seq', 'shard'), may hold values from -0.125 to 0.125
- outgate_weight: bfloat16 [2048, 4096], P('seq', 'shard'), may hold values from -0.125 to 0.125
- beta_weight: bfloat16 [2048, 16], P('seq', 'shard')
- decay_weight: bfloat16 [2048, 16], P('seq', 'shard'), may hold values from -0.125 to 0.125
- query_conv: bfloat16 [2048, 4], P(('shard', 'seq')), may hold values from -3 to 3
- key_conv: bfloat16 [2048, 4], P(('shard', 'seq')), may hold values from -3 to 3
- value_conv: bfloat16 [4096, 4], P(('shard', 'seq')), may hold values from -3 to 3
- decay_log: float32 [16], replicated, may hold values from -12 to -2
- decay_bias: float32 [16], replicated, may hold values from -1 to 1
- head_gain: float32 [256], replicated, may hold values from 0.5 to 1.5
- output_weight: bfloat16 [4096, 2048], P('shard', 'seq'), may hold values from -0.1875 to 0.1875
- ffn_gain: float32 [2048], replicated, may hold values from 0.5 to 1.5
- gate_weight: bfloat16 [2048, 5632], P('seq', 'shard'), may hold values from -0.125 to 0.125
- up_weight: bfloat16 [2048, 5632], P('seq', 'shard'), may hold values from -0.125 to 0.125
- down_weight: bfloat16 [5632, 2048], P('shard', 'seq'), may hold values from -0.15625 to 0.15625
- cotangent: bfloat16 [2, 1024, 2048], P(None, 'seq', 'shard'), may hold values from -6 to 6
Outputs:
- output: float32 [2, 1024, 2048], P(None, 'seq', 'shard')
- grad_tokens: float32 [2, 1024, 2048], P(None, 'seq', 'shard')
- grad_norm_gain: float32 [2048], replicated
- grad_query_weight: float32 [2048, 2048], P('seq', 'shard')
- grad_key_weight: float32 [2048, 2048], P('seq', 'shard')
- grad_value_weight: float32 [2048, 4096], P('seq', 'shard')
- grad_outgate_weight: float32 [2048, 4096], P('seq', 'shard')
- grad_beta_weight: float32 [2048, 16], P('seq', 'shard')
- grad_decay_weight: float32 [2048, 16], P('seq', 'shard')
- grad_query_conv: float32 [2048, 4], P(('shard', 'seq'))
- grad_key_conv: float32 [2048, 4], P(('shard', 'seq'))
- grad_value_conv: float32 [4096, 4], P(('shard', 'seq'))
- grad_decay_log: float32 [16], replicated
- grad_decay_bias: float32 [16], replicated
- grad_head_gain: float32 [256], replicated
- grad_output_weight: float32 [4096, 2048], P('shard', 'seq')
- grad_ffn_gain: float32 [2048], replicated
- grad_gate_weight: float32 [2048, 5632], P('seq', 'shard')
- grad_up_weight: float32 [2048, 5632], P('seq', 'shard')
- grad_down_weight: float32 [5632, 2048], P('shard', 'seq')
Inputs may be any that keep to these rules, and one draw needn't show every extreme that they name: `doc_starts`: each row lists, never falling, the positions at which the documents of that sequence begin: its first entry is 0, and entries equal to 1024 begin nothing. In every draw one sequence, drawn from the seed, is a single document.
All inputs are finite; a program needn't handle non-finite values.
Results may differ from a plain program's by a relative error of at most 0.018.
Values may be sent and summed in bfloat16 or wider, within the bound.
A program may use at most 136 MiB of HBM per device.

v0:
```python
import jax
import jax.numpy as jnp
from jax import lax
from jax.sharding import PartitionSpec as P

SPAN = 64


EPSILON = 1e-06
EXACT_PRECISION = lax.Precision.HIGHEST


def shifted(value, axis, steps):
    count = lax.axis_size(axis)
    first, last = (max(0, -steps), min(count, count - steps))
    return lax.ppermute(value, axis, [(source, source + steps) for source in range(first, last)])


def entering(x, axis, combine, identity, reverse):
    devices, position = (lax.axis_size(axis), lax.axis_index(axis))
    everything = jax.tree.map(lambda part: lax.all_gather(part, axis), x)
    start = jax.tree.map(
        lambda part, zero: jnp.broadcast_to(jnp.asarray(zero, part.dtype), part.shape), x, identity
    )

    def turn(k, before):
        at = devices - 1 - k if reverse else k
        reached = at > position if reverse else at < position
        new = combine(before, jax.tree.map(lambda part: part[at], everything))
        return jax.tree.map(lambda a, b: jnp.where(reached, a, b), new, before)

    return lax.fori_loop(0, devices, turn, start)


def rounded(values):
    return lax.optimization_barrier(values.astype(jnp.bfloat16)).astype(jnp.float32)


def unit_rows(values):
    return values * lax.rsqrt(jnp.sum(values * values, axis=-1, keepdims=True) + EPSILON)


def block_terms(input_keys, write_rate, log_decay, keep_flag, doc_ids):
    span_length = input_keys.shape[0]
    cumulative = jnp.cumsum(log_decay, axis=0)
    positions = jnp.arange(span_length, dtype=jnp.int32)
    same_doc = doc_ids[:, None] == doc_ids[None, :]
    causal_mask = (positions[:, None] >= positions[None, :]) & same_doc
    strict_mask = (positions[:, None] > positions[None, :]) & same_doc
    inside = causal_mask.astype(jnp.float32)[:, :, None]
    decay_ratios = (
        jnp.exp(
            jnp.where(causal_mask[:, :, None], cumulative[:, None, :] - cumulative[None, :, :], 0.0)
        )
        * inside
    )
    incoming_decay = jnp.exp(cumulative) * jnp.cumprod(keep_flag)[:, None]
    key_intersection = jnp.einsum("thk,shk->tsh", input_keys, input_keys, precision=EXACT_PRECISION)
    coupling = (
        write_rate[:, None, :]
        * decay_ratios
        * key_intersection
        * strict_mask.astype(jnp.float32)[:, :, None]
    )
    system = jnp.eye(span_length, dtype=jnp.float32)[None] + jnp.transpose(coupling, (2, 0, 1))
    return (decay_ratios, incoming_decay, system)


def block_core(
    carried_state, input_query, input_keys, values_in, write_rate, log_decay, keep_flag, doc_ids
):
    span_length = input_keys.shape[0]
    decay_ratios, incoming_decay, system = block_terms(
        input_keys, write_rate, log_decay, keep_flag, doc_ids
    )
    state_readout = jnp.einsum("ijm,jmf->ijf", input_keys, carried_state, precision=EXACT_PRECISION)
    target = write_rate[:, :, None] * (values_in - incoming_decay[:, :, None] * state_readout)
    written_values = lax.linalg.triangular_solve(
        system, jnp.transpose(target, (1, 0, 2)), left_side=True, lower=True, unit_diagonal=True
    )
    scores = (
        jnp.einsum("thk,shk->tsh", input_query, input_keys, precision=EXACT_PRECISION)
        * decay_ratios
    )
    output_rows = incoming_decay[:, :, None] * jnp.einsum(
        "ijm,jmf->ijf", input_query, carried_state, precision=EXACT_PRECISION
    )
    output_rows = output_rows + jnp.einsum(
        "tsh,hsv->thv", scores, written_values, precision=EXACT_PRECISION
    )
    closing_state = incoming_decay[span_length - 1][:, None, None] * carried_state
    closing_state = closing_state + jnp.einsum(
        "tg,tgy,gtm->gym",
        decay_ratios[span_length - 1],
        input_keys,
        written_values,
        precision=EXACT_PRECISION,
    )
    return (closing_state, output_rows)


def block_transfer(product, input_keys, write_rate, log_decay, keep_flag, doc_ids):
    span_length = input_keys.shape[0]
    decay_ratios, incoming_decay, system = block_terms(
        input_keys, write_rate, log_decay, keep_flag, doc_ids
    )
    scaled_keys = (write_rate * incoming_decay)[:, :, None] * input_keys
    solved = lax.linalg.triangular_solve(
        system,
        jnp.transpose(scaled_keys, (1, 0, 2)),
        left_side=True,
        lower=True,
        unit_diagonal=True,
    )
    identity_k = jnp.eye(input_keys.shape[2], dtype=jnp.float32)
    stepper = incoming_decay[span_length - 1][:, None, None] * identity_k[None]
    stepper = stepper - jnp.einsum(
        "sh,shk,hsj->hkj",
        decay_ratios[span_length - 1],
        input_keys,
        solved,
        precision=EXACT_PRECISION,
    )
    return jnp.einsum("hkj,hjm->hkm", stepper, product, precision=EXACT_PRECISION)


def block_step(carried_state, pieces):
    return block_core(carried_state, *pieces)


def transfer_step(product, pieces):
    return (block_transfer(product, *pieces), None)


def split_blocks(arrays_in, block_count):
    return tuple((member.reshape((block_count, SPAN) + member.shape[1:]) for member in arrays_in))


def run_local(
    input_query, input_keys, values_in, write_rate, log_decay, keep_flag, doc_ids, start_state
):

    def run_one_sequence(
        query_seq, keys_seq, values_seq, rate_seq, decay_seq, keep_seq, ids_seq, state_seq
    ):
        block_count = query_seq.shape[0] // SPAN
        pieces = split_blocks(
            (query_seq, keys_seq, values_seq, rate_seq, decay_seq, keep_seq, ids_seq), block_count
        )
        closing_state, output_rows = lax.scan(block_step, state_seq, pieces)
        return (output_rows.reshape((query_seq.shape[0],) + output_rows.shape[2:]), closing_state)

    return jax.vmap(run_one_sequence)(
        input_query, input_keys, values_in, write_rate, log_decay, keep_flag, doc_ids, start_state
    )


def transfer_local(input_keys, write_rate, log_decay, keep_flag, doc_ids):

    def transfer_one_sequence(keys_seq, rate_seq, decay_seq, keep_seq, ids_seq):
        block_count = keys_seq.shape[0] // SPAN
        pieces = split_blocks((keys_seq, rate_seq, decay_seq, keep_seq, ids_seq), block_count)
        start_map = jnp.broadcast_to(
            jnp.eye(keys_seq.shape[2], dtype=jnp.float32),
            (keys_seq.shape[1], keys_seq.shape[2], keys_seq.shape[2]),
        )
        product, unused = lax.scan(transfer_step, start_map, pieces)
        return product

    return jax.vmap(transfer_one_sequence)(input_keys, write_rate, log_decay, keep_flag, doc_ids)


def compose(first_map, second_map):
    return (
        jnp.einsum("shkj,shjm->shkm", second_map[0], first_map[0], precision=EXACT_PRECISION),
        jnp.einsum("shkj,shjv->shkv", second_map[0], first_map[1], precision=EXACT_PRECISION)
        + second_map[1],
    )


def features(extended, weights, extended_ids, head_count, key_dim, value_dim):
    seq_count, total_len, channels = extended.shape
    tap_count = weights.shape[1]
    local_len = total_len - (tap_count - 1)
    current_ids = extended_ids[:, tap_count - 1 :]
    mixed_pre = jnp.zeros((seq_count, local_len, channels), jnp.float32)
    for tap_index in range(tap_count):
        same_doc = (extended_ids[:, tap_index : tap_index + local_len] == current_ids).astype(
            jnp.float32
        )[:, :, None]
        mixed_pre = (
            mixed_pre
            + extended[:, tap_index : tap_index + local_len] * same_doc * weights[:, tap_index]
        )
    acted = jax.nn.silu(mixed_pre)
    width_k = head_count * key_dim
    query_act = acted[:, :, :width_k].reshape(seq_count, local_len, head_count, key_dim)
    key_act = acted[:, :, width_k : 2 * width_k].reshape(seq_count, local_len, head_count, key_dim)
    value_act = acted[:, :, 2 * width_k :].reshape(seq_count, local_len, head_count, value_dim)
    return (unit_rows(query_act) * key_dim ** (-0.5), unit_rows(key_act), value_act)


def per_device(
    tokens,
    doc_starts,
    norm_gain,
    query_weight,
    key_weight,
    value_weight,
    outgate_weight,
    beta_weight,
    decay_weight,
    query_conv,
    key_conv,
    value_conv,
    decay_log,
    decay_bias,
    head_gain,
    output_weight,
    ffn_gain,
    gate_weight,
    up_weight,
    down_weight,
    cotangent,
):
    seq_count, local_len, feature_part = tokens.shape
    row_count = seq_count * local_len
    shard_count = lax.axis_size("shard")
    shard_pos = lax.axis_index("shard")
    model_dim = feature_part * shard_count
    head_count = beta_weight.shape[1]
    key_dim = query_weight.shape[1] // head_count
    value_dim = value_weight.shape[1] // head_count
    tap_count = query_conv.shape[1]
    width_k = head_count * key_dim
    feature_start = shard_pos * feature_part
    head_start = shard_pos * head_count

    def whole_rows(part_rows):
        return lax.all_gather(part_rows, "shard", axis=2, tiled=True)

    def summed_rows(term_rows):
        return lax.psum_scatter(term_rows, "shard", scatter_dimension=2, tiled=True)

    def row_total(partial_rows):
        return lax.psum(partial_rows, "shard")

    def project(matrix_one, matrix_two):
        return jnp.dot(matrix_one, matrix_two, preferred_element_type=jnp.float32)

    (
        full_query,
        full_key,
        full_value,
        full_outgate,
        full_beta,
        full_decay,
        full_qconv,
        full_kconv,
        full_vconv,
        full_output,
        full_gate,
        full_up,
        full_down,
    ) = (
        lax.all_gather(query_weight, "seq", axis=0, tiled=True),
        lax.all_gather(key_weight, "seq", axis=0, tiled=True),
        lax.all_gather(value_weight, "seq", axis=0, tiled=True),
        lax.all_gather(outgate_weight, "seq", axis=0, tiled=True),
        lax.all_gather(beta_weight, "seq", axis=0, tiled=True),
        lax.all_gather(decay_weight, "seq", axis=0, tiled=True),
        lax.all_gather(query_conv, "seq", axis=0, tiled=True),
        lax.all_gather(key_conv, "seq", axis=0, tiled=True),
        lax.all_gather(value_conv, "seq", axis=0, tiled=True),
        lax.all_gather(output_weight, "seq", axis=1, tiled=True),
        lax.all_gather(gate_weight, "seq", axis=0, tiled=True),
        lax.all_gather(up_weight, "seq", axis=0, tiled=True),
        lax.all_gather(down_weight, "seq", axis=1, tiled=True),
    )
    offset = lax.axis_index("seq") * local_len
    positions = offset + jnp.arange(local_len, dtype=jnp.int32)
    doc_ids = jnp.sum(
        (doc_starts[:, None, :] <= positions[None, :, None]).astype(jnp.int32), axis=2
    )
    keep_flag = 1.0 - jnp.max(
        (doc_starts[:, None, :] == positions[None, :, None]).astype(jnp.float32), axis=2
    )
    earlier_pos = offset - (tap_count - 1) + jnp.arange(tap_count - 1, dtype=jnp.int32)
    earlier_ids = jnp.sum(
        (doc_starts[:, None, :] <= earlier_pos[None, :, None]).astype(jnp.int32), axis=2
    )
    extended_ids = jnp.concatenate([earlier_ids, doc_ids], axis=1)
    whole_tokens = whole_rows(tokens).astype(jnp.float32)
    scale_one = lax.rsqrt(jnp.mean(whole_tokens * whole_tokens, axis=2, keepdims=True) + EPSILON)
    normed_one = (
        (whole_tokens * scale_one * norm_gain).astype(jnp.bfloat16).reshape(row_count, model_dim)
    )
    query_proj = project(normed_one, full_query).astype(jnp.bfloat16)
    key_proj = project(normed_one, full_key).astype(jnp.bfloat16)
    value_proj = project(normed_one, full_value).astype(jnp.bfloat16)
    gate_proj = project(normed_one, full_outgate).reshape(
        seq_count, local_len, head_count, value_dim
    )
    beta_proj = project(normed_one, full_beta).reshape(seq_count, local_len, head_count)
    decay_proj = project(normed_one, full_decay).reshape(seq_count, local_len, head_count)
    joined = jnp.concatenate([query_proj, key_proj, value_proj], axis=1).reshape(
        seq_count, local_len, -1
    )
    edge_rows = shifted(joined[:, local_len - (tap_count - 1) :], "seq", 1)
    extended = jnp.concatenate([edge_rows, joined], axis=1).astype(jnp.float32)
    conv_joined = jnp.concatenate([full_qconv, full_kconv, full_vconv], axis=0).astype(jnp.float32)

    def feature_piece(extended_arg, conv_arg):
        return features(extended_arg, conv_arg, extended_ids, head_count, key_dim, value_dim)

    (query_unit, keys_unit, values_act), feature_pull = jax.vjp(
        feature_piece, extended, conv_joined
    )
    input_query = rounded(query_unit)
    input_keys = rounded(keys_unit)
    values_in = rounded(values_act)
    local_log = lax.dynamic_slice_in_dim(decay_log, head_start, head_count)
    local_bias = lax.dynamic_slice_in_dim(decay_bias, head_start, head_count)
    write_rate = jax.nn.sigmoid(beta_proj)
    log_decay = -jnp.exp(local_log) * jax.nn.softplus(decay_proj + local_bias)
    zero_state = jnp.zeros((seq_count, head_count, key_dim, value_dim), jnp.float32)
    zero_outputs, carried_state = run_local(
        input_query, input_keys, values_in, write_rate, log_decay, keep_flag, doc_ids, zero_state
    )
    transfers = transfer_local(input_keys, write_rate, log_decay, keep_flag, doc_ids)
    identity_maps = (
        jnp.broadcast_to(jnp.eye(key_dim, dtype=jnp.float32), transfers.shape),
        zero_state,
    )
    start_state = entering((transfers, carried_state), "seq", compose, identity_maps, False)[1]

    def mixer_piece(
        query_arg,
        keys_arg,
        values_arg,
        beta_arg,
        decay_arg,
        gate_arg,
        log_arg,
        bias_arg,
        gain_arg,
        state_arg,
    ):
        rates = jax.nn.sigmoid(beta_arg)
        decays = -jnp.exp(log_arg) * jax.nn.softplus(decay_arg + bias_arg)
        output_rows, closing_state = run_local(
            query_arg, keys_arg, values_arg, rates, decays, keep_flag, doc_ids, state_arg
        )
        normed_heads = output_rows * lax.rsqrt(
            jnp.mean(output_rows * output_rows, axis=-1, keepdims=True) + EPSILON
        )
        return (normed_heads * gain_arg * jax.nn.silu(gate_arg), closing_state)

    (mixed_out, closing_state), mixer_pull = jax.vjp(
        mixer_piece,
        input_query,
        input_keys,
        values_in,
        beta_proj,
        decay_proj,
        gate_proj,
        local_log,
        local_bias,
        head_gain,
        start_state,
    )
    branch = mixed_out.astype(jnp.bfloat16).reshape(row_count, head_count * value_dim)
    attn_rows = summed_rows(project(branch, full_output).reshape(seq_count, local_len, model_dim))
    tokens_local = tokens.astype(jnp.float32)
    residual = tokens_local + attn_rows
    local_ffn_gain = lax.dynamic_slice_in_dim(ffn_gain, feature_start, feature_part)
    local_norm_gain = lax.dynamic_slice_in_dim(norm_gain, feature_start, feature_part)
    scale_two = lax.rsqrt(row_total(jnp.sum(residual * residual, axis=2)) / model_dim + EPSILON)[
        :, :, None
    ]
    normed_two = whole_rows((residual * scale_two * local_ffn_gain).astype(jnp.bfloat16)).reshape(
        row_count, model_dim
    )
    gate_vals = project(normed_two, full_gate)
    up_vals = project(normed_two, full_up)
    gate_act = jax.nn.silu(gate_vals)
    hidden = (gate_act * up_vals).astype(jnp.bfloat16)
    output = residual + summed_rows(
        project(hidden, full_down).reshape(seq_count, local_len, model_dim)
    )
    (
        full_query,
        full_key,
        full_value,
        full_outgate,
        full_beta,
        full_decay,
        full_qconv,
        full_kconv,
        full_vconv,
        full_output,
        full_gate,
        full_up,
        full_down,
    ) = (
        lax.all_gather(query_weight, "seq", axis=0, tiled=True),
        lax.all_gather(key_weight, "seq", axis=0, tiled=True),
        lax.all_gather(value_weight, "seq", axis=0, tiled=True),
        lax.all_gather(outgate_weight, "seq", axis=0, tiled=True),
        lax.all_gather(beta_weight, "seq", axis=0, tiled=True),
        lax.all_gather(decay_weight, "seq", axis=0, tiled=True),
        lax.all_gather(query_conv, "seq", axis=0, tiled=True),
        lax.all_gather(key_conv, "seq", axis=0, tiled=True),
        lax.all_gather(value_conv, "seq", axis=0, tiled=True),
        lax.all_gather(output_weight, "seq", axis=1, tiled=True),
        lax.all_gather(gate_weight, "seq", axis=0, tiled=True),
        lax.all_gather(up_weight, "seq", axis=0, tiled=True),
        lax.all_gather(down_weight, "seq", axis=1, tiled=True),
    )
    cot_rows = whole_rows(cotangent).reshape(row_count, model_dim)
    grad_hidden = jnp.einsum("rd,fd->rf", cot_rows, full_down, preferred_element_type=jnp.float32)
    grad_down = jnp.einsum("rf,rd->fd", hidden, cot_rows, preferred_element_type=jnp.float32)
    sigmoid_gate = jax.nn.sigmoid(gate_vals)
    grad_gate_vals = (
        grad_hidden * up_vals * sigmoid_gate * (1.0 + gate_vals * (1.0 - sigmoid_gate))
    ).astype(jnp.bfloat16)
    grad_up_vals = (grad_hidden * gate_act).astype(jnp.bfloat16)
    grad_gate = jnp.einsum(
        "rd,rf->df", normed_two, grad_gate_vals, preferred_element_type=jnp.float32
    )
    grad_up = jnp.einsum("rd,rf->df", normed_two, grad_up_vals, preferred_element_type=jnp.float32)
    grad_normed_two = jnp.einsum(
        "rf,df->rd", grad_gate_vals, full_gate, preferred_element_type=jnp.float32
    )
    grad_normed_two = grad_normed_two + jnp.einsum(
        "rf,df->rd", grad_up_vals, full_up, preferred_element_type=jnp.float32
    )
    grad_two = summed_rows(grad_normed_two.reshape(seq_count, local_len, model_dim))
    gained_two = local_ffn_gain * grad_two
    inner_two = row_total(jnp.sum(gained_two * residual, axis=2))[:, :, None] / model_dim
    grad_residual = cotangent.astype(jnp.float32) + scale_two * (
        gained_two - residual * scale_two * scale_two * inner_two
    )
    grad_ffn_part = jnp.sum(grad_two * residual * scale_two, axis=(0, 1))
    attn_cot = whole_rows(grad_residual.astype(jnp.bfloat16)).reshape(row_count, model_dim)
    grad_output = jnp.einsum("rv,rd->vd", branch, attn_cot, preferred_element_type=jnp.float32)
    grad_branch = jnp.einsum("rd,vd->rv", attn_cot, full_output, preferred_element_type=jnp.float32)
    grad_mixed = rounded(grad_branch).reshape(seq_count, local_len, head_count, value_dim)
    later_grad = mixer_pull((grad_mixed, zero_state))[9]
    flipped = jnp.swapaxes(transfers, 2, 3)
    end_grad = entering((flipped, later_grad), "seq", compose, identity_maps, True)[1]
    (
        grad_query,
        grad_keys,
        grad_values,
        grad_beta,
        grad_decay,
        grad_gate_heads,
        grad_log,
        grad_bias,
        grad_head_gain,
        grad_start,
    ) = mixer_pull((grad_mixed, end_grad))
    grad_extended, grad_conv = feature_pull(
        (rounded(grad_query), rounded(grad_keys), rounded(grad_values))
    )
    edge_grad = shifted(grad_extended[:, : tap_count - 1], "seq", -1)
    grad_joined = (
        grad_extended[:, tap_count - 1 :].at[:, local_len - (tap_count - 1) :].add(edge_grad)
    )
    grad_joined = grad_joined.astype(jnp.bfloat16).reshape(row_count, -1)
    grad_qproj = grad_joined[:, :width_k]
    grad_kproj = grad_joined[:, width_k : 2 * width_k]
    grad_vproj = grad_joined[:, 2 * width_k :]
    grad_gate_proj = grad_gate_heads.astype(jnp.bfloat16).reshape(row_count, head_count * value_dim)
    grad_beta_proj = grad_beta.astype(jnp.bfloat16).reshape(row_count, head_count)
    grad_decay_proj = grad_decay.astype(jnp.bfloat16).reshape(row_count, head_count)

    def weight_grad(grad_cols):
        return jnp.einsum("rd,rc->dc", normed_one, grad_cols, preferred_element_type=jnp.float32)

    def input_grad(grad_cols, weight_full):
        return jnp.einsum("rc,dc->rd", grad_cols, weight_full, preferred_element_type=jnp.float32)

    grad_normed_one = input_grad(grad_qproj, full_query) + input_grad(grad_kproj, full_key)
    grad_normed_one = (
        grad_normed_one
        + input_grad(grad_vproj, full_value)
        + input_grad(grad_gate_proj, full_outgate)
    )
    grad_normed_one = (
        grad_normed_one
        + input_grad(grad_beta_proj, full_beta)
        + input_grad(grad_decay_proj, full_decay)
    )
    grad_one = summed_rows(grad_normed_one.reshape(seq_count, local_len, model_dim))
    gained_one = local_norm_gain * grad_one
    inner_one = row_total(jnp.sum(gained_one * tokens_local, axis=2))[:, :, None] / model_dim
    grad_tokens = grad_residual + scale_one * (
        gained_one - tokens_local * scale_one * scale_one * inner_one
    )
    grad_norm_part = jnp.sum(grad_one * tokens_local * scale_one, axis=(0, 1))
    (
        out_query,
        out_key,
        out_value,
        out_outgate,
        out_beta,
        out_decay,
        out_qconv,
        out_kconv,
        out_vconv,
        out_output,
        out_gate,
        out_up,
        out_down,
    ) = (
        lax.psum_scatter(
            weight_grad(grad_qproj).astype(jnp.bfloat16), "seq", scatter_dimension=0, tiled=True
        ).astype(jnp.float32),
        lax.psum_scatter(
            weight_grad(grad_kproj).astype(jnp.bfloat16), "seq", scatter_dimension=0, tiled=True
        ).astype(jnp.float32),
        lax.psum_scatter(
            weight_grad(grad_vproj).astype(jnp.bfloat16), "seq", scatter_dimension=0, tiled=True
        ).astype(jnp.float32),
        lax.psum_scatter(
            weight_grad(grad_gate_proj).astype(jnp.bfloat16), "seq", scatter_dimension=0, tiled=True
        ).astype(jnp.float32),
        lax.psum_scatter(
            weight_grad(grad_beta_proj).astype(jnp.bfloat16), "seq", scatter_dimension=0, tiled=True
        ).astype(jnp.float32),
        lax.psum_scatter(
            weight_grad(grad_decay_proj).astype(jnp.bfloat16),
            "seq",
            scatter_dimension=0,
            tiled=True,
        ).astype(jnp.float32),
        lax.psum_scatter(
            grad_conv[:width_k].astype(jnp.bfloat16), "seq", scatter_dimension=0, tiled=True
        ).astype(jnp.float32),
        lax.psum_scatter(
            grad_conv[width_k : 2 * width_k].astype(jnp.bfloat16),
            "seq",
            scatter_dimension=0,
            tiled=True,
        ).astype(jnp.float32),
        lax.psum_scatter(
            grad_conv[2 * width_k :].astype(jnp.bfloat16), "seq", scatter_dimension=0, tiled=True
        ).astype(jnp.float32),
        lax.psum_scatter(
            grad_output.astype(jnp.bfloat16), "seq", scatter_dimension=1, tiled=True
        ).astype(jnp.float32),
        lax.psum_scatter(
            grad_gate.astype(jnp.bfloat16), "seq", scatter_dimension=0, tiled=True
        ).astype(jnp.float32),
        lax.psum_scatter(
            grad_up.astype(jnp.bfloat16), "seq", scatter_dimension=0, tiled=True
        ).astype(jnp.float32),
        lax.psum_scatter(
            grad_down.astype(jnp.bfloat16), "seq", scatter_dimension=1, tiled=True
        ).astype(jnp.float32),
    )

    def place_into(full_length, part_vals, start_at):
        return lax.dynamic_update_slice(
            jnp.zeros((full_length,), jnp.float32), part_vals, (start_at,)
        )

    total_heads = decay_log.shape[0]
    small_sums = lax.psum(
        (
            place_into(model_dim, grad_norm_part, feature_start),
            place_into(model_dim, grad_ffn_part, feature_start),
            grad_head_gain,
            place_into(total_heads, grad_log, head_start),
            place_into(total_heads, grad_bias, head_start),
        ),
        ("seq", "shard"),
    )
    return (
        output,
        grad_tokens,
        small_sums[0],
        out_query,
        out_key,
        out_value,
        out_outgate,
        out_beta,
        out_decay,
        out_qconv,
        out_kconv,
        out_vconv,
        small_sums[3],
        small_sums[4],
        small_sums[2],
        out_output,
        small_sums[1],
        out_gate,
        out_up,
        out_down,
    )


def solution(mesh):
    return jax.shard_map(
        per_device,
        mesh=mesh,
        in_specs=(
            P(None, "seq", "shard"),
            P(),
            P(),
            P("seq", "shard"),
            P("seq", "shard"),
            P("seq", "shard"),
            P("seq", "shard"),
            P("seq", "shard"),
            P("seq", "shard"),
            P(("shard", "seq"), None),
            P(("shard", "seq"), None),
            P(("shard", "seq"), None),
            P(),
            P(),
            P(),
            P("shard", "seq"),
            P(),
            P("seq", "shard"),
            P("seq", "shard"),
            P("shard", "seq"),
            P(None, "seq", "shard"),
        ),
        out_specs=(
            P(None, "seq", "shard"),
            P(None, "seq", "shard"),
            P(),
            P("seq", "shard"),
            P("seq", "shard"),
            P("seq", "shard"),
            P("seq", "shard"),
            P("seq", "shard"),
            P("seq", "shard"),
            P(("shard", "seq"), None),
            P(("shard", "seq"), None),
            P(("shard", "seq"), None),
            P(),
            P(),
            P(),
            P("shard", "seq"),
            P(),
            P("seq", "shard"),
            P("seq", "shard"),
            P("shard", "seq"),
        ),
        check_vma=False,
    )
```

profile of v0, /device:TPU:0, one launch (start us, length us, event | category | flops | bytes accessed | tf_op | source)
XLA Modules:
  0.0 1867.6 jit_solution(15734127620608428749)
XLA Ops:
  13.7 10.5 all_gather.86
  24.9 8.7 all_gather.92
  33.6 8.0 all-gather.5
  41.8 8.7 all-gather.4
  51.1 8.1 all_gather.93
  63.7 5.9 all-gather.27.cloned.1.call-done
  71.9 27.5 %all-gather.25.cloned.1.call-done = bf16[2048,512]{1,0:T(8,128)(2,1)} async-done(((bf16[256,512]{1,0:T(8,128)(2,1)}), bf16[2048,512]{1,0:T(8,128)(2,1)}) %all-gather.25.cloned.1.call-update) | async-done | bytes 2097168 | tf_op jit(solution)/shard_map/all_gather | solution.py:266
  101.7 36.2 %all-gather.29.cloned.1.call-done = bf16[2048,1024]{1,0:T(8,128)(2,1)} async-done(((bf16[256,1024]{1,0:T(8,128)(2,1)}), bf16[2048,1024]{1,0:T(8,128)(2,1)}) %all-gather.29.cloned.1.call-update) | async-done | bytes 4194320 | tf_op jit(solution)/shard_map/all_gather | solution.py:268
  149.5 4.4 fusion.274
  156.3 91.9 %while.157 = (s32[]{:T(128)}, f32[2,4,128,128]{3,2,1,0:T(8,128)S(1)}, f32[2,2,64,4]{3,2,1,0:T(8,128)}, f32[2,2,64]{2,1,0:T(2,128)}, s32[2,2,64]{2,1,0:T(2,128)S(...) while((s32[]{:T(128)}, ...), condition=%wide.region_8.9_spmd, body=%wide.region_5.8_spmd.sunk | while | flops 403486656 | bytes 5403633 | solution.py:167
  159.1 39.3 %custom-call.58 = f32[2,4,1,64,64]{3,4,2,1,0:T(8,128)S(1)} custom-call(f32[2,4,1,64,64]{4,3,2,1,0:T(8,128)S(1)} %fusion.511), custom_call_target="InvertDiagBlocksLowerTriangular" | custom-call | tf_op jit(solution)/shard_map/vmap()/while/body/eval_jaxpr/triangular_solve | solution.py:108
  205.1 39.3 %custom-call.58 = f32[2,4,1,64,64]{3,4,2,1,0:T(8,128)S(1)} custom-call(f32[2,4,1,64,64]{4,3,2,1,0:T(8,128)S(1)} %fusion.511), custom_call_target="InvertDiagBlocksLowerTriangular" | custom-call | tf_op jit(solution)/shard_map/vmap()/while/body/eval_jaxpr/triangular_solve | solution.py:108
  253.9 103.2 %while.160 = (s32[]{:T(128)}, f32[2,4,128,256]{3,2,1,0:T(8,128)S(1)}, f32[2,2,64,4]{3,2,1,0:T(8,128)}, f32[2,2,64]{2,1,0:T(2,128)}, s32[2,2,64]{2,1,0:T(2,128)S(...) while((s32[]{:T(128)}, ...), condition=%wide.region_12.14_spmd.clone, body=%wide.region_9.13_spmd.clone.sunk | while | flops 555562432 | bytes 7373403 | solution.py:150
  260.6 40.0 %custom-call.62 = f32[2,4,1,64,64]{3,4,2,1,0:T(8,128)S(1)} custom-call(f32[2,4,1,64,64]{4,3,2,1,0:T(8,128)} %fusion.583), custom_call_target="InvertDiagBlocksLowerTriangular" | custom-call | tf_op jit(solution)/shard_map/vmap()/while/body/eval_jaxpr/triangular_solve/custom-call.1 | solution.py:78
  312.2 40.0 %custom-call.62 = f32[2,4,1,64,64]{3,4,2,1,0:T(8,128)S(1)} custom-call(f32[2,4,1,64,64]{4,3,2,1,0:T(8,128)} %fusion.583), custom_call_target="InvertDiagBlocksLowerTriangular" | custom-call | tf_op jit(solution)/shard_map/vmap()/while/body/eval_jaxpr/triangular_solve/custom-call.1 | solution.py:78
  359.5 6.6 copy.661
  367.0 46.4 %all-gather.49.cloned.1.call-done = f32[16,4,128,256]{3,2,1,0:T(8,128)} async-done(((f32[2,4,128,256]{3,2,1,0:T(8,128)}), f32[16,4,128,256]{3,2,1,0:T(8,128)}) %all-gather.49.cloned.1.call-update) | async-done | bytes 8388624 | tf_op jit(solution)/shard_map/all_gather | solution.py:21
  413.4 34.8 %while.161 = (s32[]{:T(128)}, f32[2,4,128,256]{3,2,1,0:T(8,128)S(1)}, s32[]{:T(128)}, f32[8,2,4,128,128]{4,3,2,1,0:T(8,128)}, f32[8,2,4,128,256]{4,3,2,1,0:T(8,128)}, /*index=5*/s32[]{:T(128)}, s32[]{:T(128)}) while((s32[]{:T(128)}, f32[2,4,128,256]{3,2,1,0:T(8,128)S(1)}, s32[]{:T(128)}, f32[8,2,4,128,128]{4,3,2,1,0:T(8,128)}, ...), condition=%wide.region_14.16_spmd.clone, body=%wide.region_13.15_spmd.clone.sunk | while | flops 403701760 | bytes 6818407 | solution.py:32
  449.4 165.5 %while.159 = (s32[]{:T(128)}, f32[2,4,128,256]{3,2,1,0:T(8,128)S(1)}, f32[2,2,64,4,256]{4,2,3,1,0:T(8,128)}, pred[2,2,64,64,4]{3,4,2,1,0:T(4,128)(4,1)}, f32[2,2...) while((s32[]{:T(128)}, ...), condition=%wide.region_19.21_spmd.clone.clone, body=%wide.region_16.20_spmd.clone.clone.sunk | while | flops 908710336 | bytes 42334584 | solution.py:150
  463.8 39.9 %custom-call.61 = f32[2,4,1,64,64]{3,4,2,1,0:T(8,128)} custom-call(f32[2,4,1,64,64]{4,3,2,1,0:T(8,128)S(1)} %add_bitcast_fusion.5), custom_call_target="InvertDiagBlocksLowerTriangular" | custom-call | tf_op jit(solution)/shard_map/jvp(vmap())/while/body/eval_jaxpr/triangular_solve/custom-call.1 | solution.py:78
  546.3 39.9 %custom-call.61 = f32[2,4,1,64,64]{3,4,2,1,0:T(8,128)} custom-call(f32[2,4,1,64,64]{4,3,2,1,0:T(8,128)S(1)} %add_bitcast_fusion.5), custom_call_target="InvertDiagBlocksLowerTriangular" | custom-call | tf_op jit(solution)/shard_map/jvp(vmap())/while/body/eval_jaxpr/triangular_solve/custom-call.1 | solution.py:78
  616.8 4.6 multiply_convert_fusion.3
  621.6 4.8 fusion.263
  627.8 42.6 %reduce-scatter.28.cloned.1.call-done = f32[2,128,512]{2,1,0:T(8,128)} async-done(((f32[2,128,2048]{2,1,0:T(8,128)}), f32[2,128,512]{2,1,0:T(8,128)}) %reduce-scatter.28.cloned.1.call-update) | async-done | bytes 524304 | tf_op jit(solution)/shard_map/reduce_scatter | solution.py:243
  671.6 9.9 psum.56
  684.3 30.7 %all-gather.37.cloned.1.call-done = bf16[2048,1408]{1,0:T(8,128)(2,1)} async-done(((bf16[256,1408]{1,0:T(8,128)(2,1)}), bf16[2048,1408]{1,0:T(8,128)(2,1)}) %all-gather.37.cloned.1.call-update) | async-done | bytes 5767184 | tf_op jit(solution)/shard_map/all_gather | solution.py:276
  715.0 30.2 %all-gather.35.cloned.1.call-done = bf16[2,128,2048]{2,1,0:T(8,128)(2,1)} async-done(((bf16[2,128,512]{2,1,0:T(8,128)(2,1)}), bf16[2,128,2048]{2,1,0:T(8,128)(2,1)}) %all-gather.35.cloned.1.call-update) | async-done | bytes 1048592 | tf_op jit(solution)/shard_map/all_gather | solution.py:240
  745.2 5.9 fusion.332
  751.1 38.8 %all-gather.39.cloned.1.call-done = bf16[2048,1408]{1,0:T(8,128)(2,1)} async-done(((bf16[256,1408]{1,0:T(8,128)(2,1)}), bf16[2048,1408]{1,0:T(8,128)(2,1)}) %all-gather.39.cloned.1.call-update) | async-done | bytes 5767184 | tf_op jit(solution)/shard_map/all_gather | solution.py:277
  789.9 5.5 fusion.333
  795.4 24.1 %all-gather.43.cloned.1.call-done = bf16[2,128,2048]{2,1,0:T(8,128)(2,1)} async-done(((bf16[2,128,512]{2,1,0:T(8,128)(2,1)}), bf16[2,128,2048]{2,1,0:T(8,128)(2,1)}) %all-gather.43.cloned.1.call-update) | async-done | bytes 1048592 | tf_op jit(solution)/shard_map/all_gather | solution.py:240
  819.5 45.8 %all-gather.41.cloned.1.call-done = bf16[1408,2048]{1,0:T(8,128)(2,1)} async-done(((bf16[1408,256]{1,0:T(8,128)(2,1)}), bf16[1408,2048]{1,0:T(8,128)(2,1)}) %all-gather.41.cloned.1.call-update) | async-done | bytes 5767184 | tf_op jit(solution)/shard_map/all_gather | solution.py:278
  865.3 7.1 multiply_convert_fusion
  878.7 44.0 %reduce-scatter.32.cloned.1.call-done = f32[2,128,512]{2,1,0:T(8,128)} async-done(((f32[2,128,2048]{2,1,0:T(8,128)}), f32[2,128,512]{2,1,0:T(8,128)}) %reduce-scatter.32.cloned.1.call-update) | async-done | bytes 524304 | tf_op jit(solution)/shard_map/reduce_scatter | solution.py:243
  924.5 9.8 psum.57
  937.7 25.1 %all-gather.45.cloned.1.call-done = bf16[2,128,2048]{2,1,0:T(8,128)(2,1)} async-done(((bf16[2,128,512]{2,1,0:T(8,128)(2,1)}), bf16[2,128,2048]{2,1,0:T(8,128)(2,1)}) %all-gather.45.cloned.1.call-update) | async-done | bytes 1048592 | tf_op jit(solution)/shard_map/all_gather | solution.py:240
  962.8 3.8 convolution_convert_fusion.8
  973.3 100.8 %while.162 = (s32[]{:T(128)}, f32[2,4,128,256]{3,2,1,0:T(8,128)S(1)}, f32[2,2,4,1,1]{2,1,4,3,0:T(2,128)S(1)}, f32[2,2,64,4,128]{4,2,3,1,0:T(8,128)}, f32[2,2,64,...) while((s32[]{:T(128)}, ...), condition=%wide.region_30.33_spmd.clone, body=%wide.region_29.32_spmd.clone.sunk | while | flops 807350336 | bytes 10942703 | solution.py:150
  981.4 39.3 %custom-call.63 = f32[2,4,1,64,64]{3,4,2,1,0:T(8,128)S(1)} custom-call(f32[2,4,1,64,64]{4,3,2,1,0:T(8,128)S(1)} %fusion.600), custom_call_target="InvertDiagBlocksLowerTriangular" | custom-call | tf_op jit(solution)/shard_map/transpose(jvp(vmap()))/while/body/eval_jaxpr/triangular_solve/custom-call.2 | solution.py:78
  1031.8 39.3 %custom-call.63 = f32[2,4,1,64,64]{3,4,2,1,0:T(8,128)S(1)} custom-call(f32[2,4,1,64,64]{4,3,2,1,0:T(8,128)S(1)} %fusion.600), custom_call_target="InvertDiagBlocksLowerTriangular" | custom-call | tf_op jit(solution)/shard_map/transpose(jvp(vmap()))/while/body/eval_jaxpr/triangular_solve/custom-call.2 | solution.py:78
  1075.1 5.7 convolution_convert_fusion.2
  1082.5 4.4 convolution_convert_fusion.1
  1088.3 4.1 convolution_convert_fusion
  1103.0 26.1 %all-gather.53.cloned.1.call-done = f32[16,4,128,256]{3,2,1,0:T(8,128)} async-done(((f32[2,4,128,256]{3,2,1,0:T(8,128)}), f32[16,4,128,256]{3,2,1,0:T(8,128)}) %all-gather.53.cloned.1.call-update) | async-done | bytes 8388624 | tf_op jit(solution)/shard_map/all_gather | solution.py:21
  1129.1 34.7 %while.163 = (s32[]{:T(128)}, f32[2,4,128,256]{3,2,1,0:T(8,128)S(1)}, s32[]{:T(128)}, f32[8,2,4,128,128]{4,3,2,1,0:T(8,128)}, f32[8,2,4,128,256]{4,3,2,1,0:T(8,1...) while((s32[]{:T(128)}, f32[2,4,128,256]{3,2,1,0:T(8,128)S(1)}, s32[]{:T(128)}, ...), condition=%wide.region_32.35_spmd.clone, body=%wide.region_31.34_spmd.clone.sunk | while | flops 403701760 | bytes 6818469 | solution.py:32
  1142.7 3.7 fusion.604
  1167.4 245.6 %while.158 = (s32[]{:T(128)}, f32[2,4,128,256]{3,2,1,0:T(8,128)S(1)}, bf16[2,2,64,4,128]{4,2,0,3,1:T(8,128)(2,1)}, bf16[2,2,64,4,128]{4,2,0,3,1:T(8,128)(2,1)}, ...) while((s32[]{:T(128)}, ...), condition=%wide.region_42.45_spmd.clone, body=%wide.region_33.44_spmd.clone.sunk | while | flops 1842098176 | bytes 77848368 | solution.py:150
  1180.2 39.3 %custom-call.59 = f32[2,4,1,64,64]{3,4,2,1,0:T(8,128)S(1)} custom-call(f32[2,4,1,64,64]{4,3,2,1,0:T(8,128)S(1)} %fusion.545), custom_call_target="InvertDiagBlocksLowerTriangular" | custom-call | tf_op jit(solution)/shard_map/transpose(jvp(vmap()))/while/body/eval_jaxpr/triangular_solve/custom-call.2 | solution.py:78
  1236.6 40.0 %custom-call.60 = f32[2,4,1,64,64]{3,4,2,1,0:T(8,128)} custom-call(f32[2,4,1,64,64]{4,3,2,1,0:T(8,128)S(1)} %add_bitcast_fusion.4), custom_call_target="InvertDiagBlocksLowerTriangular" | custom-call | tf_op jit(solution)/shard_map/transpose(jvp(vmap()))/while/body/eval_jaxpr/triangular_solve | solution.py:78
  1302.9 39.3 %custom-call.59 = f32[2,4,1,64,64]{3,4,2,1,0:T(8,128)S(1)} custom-call(f32[2,4,1,64,64]{4,3,2,1,0:T(8,128)S(1)} %fusion.545), custom_call_target="InvertDiagBlocksLowerTriangular" | custom-call | tf_op jit(solution)/shard_map/transpose(jvp(vmap()))/while/body/eval_jaxpr/triangular_solve/custom-call.2 | solution.py:78
  1359.3 40.0 %custom-call.60 = f32[2,4,1,64,64]{3,4,2,1,0:T(8,128)} custom-call(f32[2,4,1,64,64]{4,3,2,1,0:T(8,128)S(1)} %add_bitcast_fusion.4), custom_call_target="InvertDiagBlocksLowerTriangular" | custom-call | tf_op jit(solution)/shard_map/transpose(jvp(vmap()))/while/body/eval_jaxpr/triangular_solve | solution.py:78
  1419.1 5.4 multiply_reduce_fusion.4
  1450.5 11.1 scatter-add.4
  1479.5 5.8 fusion.334
  1502.8 6.6 reduce-scatter.58.cloned.1.call-done
  1510.8 36.0 %reduce-scatter.60.cloned.1.call-done = bf16[128,4]{1,0:T(8,128)(2,1)} async-done(((bf16[1024,4]{1,0:T(8,128)(2,1)}), bf16[128,4]{1,0:T(8,128)(2,1)}) %reduce-scatter.60.cloned.1.call-update) | async-done | bytes 1040
  1548.2 36.2 %reduce-scatter.52.cloned.1.call-done = bf16[256,4]{1,0:T(8,128)(2,1)} async-done(((bf16[2048,4]{1,0:T(8,128)(2,1)}), bf16[256,4]{1,0:T(8,128)(2,1)}) %reduce-scatter.52.cloned.1.call-update) | async-done | bytes 2064
  1586.0 36.6 %reduce-scatter.54.cloned.1.call-done = bf16[256,4]{1,0:T(8,128)(2,1)} async-done(((bf16[2048,4]{1,0:T(8,128)(2,1)}), bf16[256,4]{1,0:T(8,128)(2,1)}) %reduce-scatter.54.cloned.1.call-update) | async-done | bytes 2064
  1624.1 43.0 %reduce-scatter.36.cloned.1.call-done = bf16[256,512]{1,0:T(8,128)(2,1)} async-done(((bf16[2048,512]{1,0:T(8,128)(2,1)}), bf16[256,512]{1,0:T(8,128)(2,1)}) %reduce-scatter.36.cloned.1.call-update) | async-done | bytes 262160 | tf_op jit(solution)/shard_map/reduce_scatter | solution.py:518
  1668.9 42.9 %reduce-scatter.38.cloned.1.call-done = bf16[256,512]{1,0:T(8,128)(2,1)} async-done(((bf16[2048,512]{1,0:T(8,128)(2,1)}), bf16[256,512]{1,0:T(8,128)(2,1)}) %reduce-scatter.38.cloned.1.call-update) | async-done | bytes 262160 | tf_op jit(solution)/shard_map/reduce_scatter | solution.py:521
  1713.6 44.4 %reduce-scatter.34.cloned.1.call-done = f32[2,128,512]{2,1,0:T(8,128)} async-done(((f32[2,128,2048]{2,1,0:T(8,128)}), f32[2,128,512]{2,1,0:T(8,128)}) %reduce-scatter.34.cloned.1.call-update) | async-done | bytes 524304 | tf_op jit(solution)/shard_map/reduce_scatter | solution.py:243
  1759.6 9.9 psum.58
  1769.5 42.9 %all-reduce.13 = (f32[2048]{0:T(1024)}, f32[16]{0:T(128)}, f32[16]{0:T(128)}, f32[256]{0:T(256)}, f32[2048]{0:T(1024)}) all-reduce(f32[2048]{0:T(1024)S(1)} %dynamic_update_slice.221, f32[16]{0:T(128)S(1)} %multiply_dynamic-update-slice_fusion.1, ...), channel_id=1, replica_groups=mesh['seq'=8,'shard'=4] {'seq','shard'}, use_global_device_ids=true, to_apply=%region_49.52 | all-reduce | flops 4384 | bytes 35072 | tf_op jit(solution)/shard_map/psum | solution.py:571
  1814.9 43.5 %reduce-scatter.40.cloned.1.call-done = bf16[256,1024]{1,0:T(8,128)(2,1)} async-done(((bf16[2048,1024]{1,0:T(8,128)(2,1)}), bf16[256,1024]{1,0:T(8,128)(2,1)}) %reduce-scatter.40.cloned.1.call-update) | async-done | bytes 524304 | tf_op jit(solution)/shard_map/reduce_scatter | solution.py:524
  (1024 shorter events, 460.2 us)
Async XLA Ops:
  7.2 53.5 %copy-start.135 = (f32[2048]{0:T(1024)S(1)}, f32[2048]{0:T(1024)}, u32[]{:S(2)}) copy-start(f32[2048]{0:T(1024)} %param.43) | copy-start | bytes 24580
  7.2 52.0 %all-gather.23.cloned.1.call-start = ((), (), s32[]{:S(2)}) async-start(), calls=%async_computation.17 | async-start | bytes 1310720 | tf_op jit(solution)/shard_map/all_gather | solution.py:240
  8.0 61.6 %all-gather.27.cloned.1.call-start = ((), (), s32[]{:S(2)}) async-start(), calls=%async_computation.19 | async-start | bytes 2359296 | tf_op jit(solution)/shard_map/all_gather | solution.py:267
  8.7 90.7 %all-gather.25.cloned.1.call-start = ((), (), s32[]{:S(2)}) async-start(), calls=%async_computation.18 | async-start | bytes 2359296 | tf_op jit(solution)/shard_map/all_gather | solution.py:266
  9.4 128.5 %all-gather.29.cloned.1.call-start = ((), (), s32[]{:S(2)}) async-start(), calls=%async_computation.20 | async-start | bytes 4718592 | tf_op jit(solution)/shard_map/all_gather | solution.py:268
  10.0 349.4 %all-gather.31.cloned.1.call-start = ((), (), s32[]{:S(2)}) async-start(), calls=%async_computation.21 | async-start | bytes 4718592 | tf_op jit(solution)/shard_map/all_gather | solution.py:269
  10.6 356.4 %all-gather.47.cloned.1.call-start = ((), (), s32[]{:S(2)}) async-start(), calls=%async_computation.41 | async-start | bytes 4718592 | tf_op jit(solution)/shard_map/all_gather | solution.py:21
  13.0 130.9 %copy-start.147 = (f32[4]{0:T(128)}, f32[4]{0:T(128)S(1)}, u32[]{:S(2)}) copy-start(f32[4]{0:T(128)S(1)} %fusion.325) | copy-start | bytes 52
  50.6 98.8 %copy-start.97 = (f32[2048,1]{0,1:T(1,128)}, f32[2048,1]{0,1:T(1,128)S(1)}, u32[]{:S(2)}) copy-start(f32[2048,1]{0,1:T(1,128)S(1)} %get-tuple-element.3044) | copy-start | bytes 24580
  50.7 98.8 %copy-start.99 = (f32[2048,1]{0,1:T(1,128)}, f32[2048,1]{0,1:T(1,128)S(1)}, u32[]{:S(2)}) copy-start(f32[2048,1]{0,1:T(1,128)S(1)} %get-tuple-element.3045) | copy-start | bytes 24580
  50.7 98.8 %copy-start.101 = (f32[2048,1]{0,1:T(1,128)}, f32[2048,1]{0,1:T(1,128)S(1)}, u32[]{:S(2)}) copy-start(f32[2048,1]{0,1:T(1,128)S(1)} %get-tuple-element.3046) | copy-start | bytes 24580
  50.7 98.8 %copy-start.103 = (f32[2048,1]{0,1:T(1,128)}, f32[2048,1]{0,1:T(1,128)S(1)}, u32[]{:S(2)}) copy-start(f32[2048,1]{0,1:T(1,128)S(1)} %get-tuple-element.3047) | copy-start | bytes 24580
  51.1 98.4 %copy-start.127 = (f32[2,128]{1,0:T(2,128)}, f32[2,128]{1,0:T(2,128)S(1)}, u32[]{:S(2)}) copy-start(f32[2,128]{1,0:T(2,128)S(1)} %get-tuple-element.3051) | copy-start | bytes 3076
  51.1 98.4 %copy-start.129 = (f32[2,128]{1,0:T(2,128)}, f32[2,128]{1,0:T(2,128)S(1)}, u32[]{:S(2)}) copy-start(f32[2,128]{1,0:T(2,128)S(1)} %get-tuple-element.3052) | copy-start | bytes 3076
  51.1 98.4 %copy-start.131 = (f32[2,128]{1,0:T(2,128)}, f32[2,128]{1,0:T(2,128)S(1)}, u32[]{:S(2)}) copy-start(f32[2,128]{1,0:T(2,128)S(1)} %get-tuple-element.3053) | copy-start | bytes 3076
  62.3 554.5 %copy-start.4 = (bf16[2,128,2048]{2,1,0:T(8,128)(2,1)}, bf16[2,128,2048]{2,1,0:T(8,128)(2,1)S(1)}, u32[]{:S(2)}) copy-start(bf16[2,128,2048]{2,1,0:T(8,128)(2,1)S(1)} %fusion.271) | copy-start | bytes 3145732
  62.7 82.1 %copy-start.116 = (f32[2,128,4]{1,2,0:T(4,128)}, f32[2,128,4]{1,2,0:T(4,128)S(1)}, u32[]{:S(2)}) copy-start(f32[2,128,4]{1,2,0:T(4,128)S(1)} %fusion.278) | copy-start | bytes 12292
  63.7 80.2 %copy-start.114 = (f32[2,128,4]{1,2,0:T(4,128)}, f32[2,128,4]{1,2,0:T(4,128)S(1)}, u32[]{:S(2)}) copy-start(f32[2,128,4]{1,2,0:T(4,128)S(1)} %get-tuple-element.3054) | copy-start | bytes 12292
  63.7 80.3 %copy-start.141 = (u8[128,4]{0,1:T(4,128)(4,1)}, u8[128,4]{0,1:T(4,128)(4,1)S(1)}, u32[]{:S(2)}) copy-start(u8[128,4]{0,1:T(4,128)(4,1)S(1)} %get-tuple-element.2737) | copy-start | bytes 1540
  141.5 5.3 collective-permute-start
  249.1 164.3 %all-gather.49.cloned.1.call-start = ((), (), s32[]{:S(2)}) async-start(), calls=%async_computation.42 | async-start | bytes 9437184 | tf_op jit(solution)/shard_map/all_gather | solution.py:21
  358.2 263.5 %all-gather.33.cloned.1.call-start = ((), (), s32[]{:S(2)}) async-start(), calls=%async_computation.22 | async-start | bytes 4718592 | tf_op jit(solution)/shard_map/all_gather | solution.py:275
  358.9 311.5 %reduce-scatter.28.cloned.1.call-start = ((), (), s32[]{:S(2)}) async-start(), calls=%async_computation.23 | async-start | bytes 2621440 | tf_op jit(solution)/shard_map/reduce_scatter | solution.py:243
  626.4 44.0 %copy-start.38 = (bf16[2,128,512]{2,1,0:T(8,128)(2,1)S(1)}, bf16[2,128,512]{2,1,0:T(8,128)(2,1)}, u32[]{:S(2)}) copy-start(bf16[2,128,512]{2,1,0:T(8,128)(2,1)} %param.41) | copy-start | bytes 786436
  626.4 88.5 %all-gather.37.cloned.1.call-start = ((), (), s32[]{:S(2)}) async-start(), calls=%async_computation.25 | async-start | bytes 6488064 | tf_op jit(solution)/shard_map/all_gather | solution.py:276
  627.0 118.1 %all-gather.35.cloned.1.call-start = ((), (), s32[]{:S(2)}) async-start(), calls=%async_computation.24 | async-start | bytes 1310720 | tf_op jit(solution)/shard_map/all_gather | solution.py:240
  627.8 306.5 %copy-start.105 = (f32[512]{0:T(512)}, f32[512]{0:T(512)S(1)}, u32[]{:S(2)}) copy-start(f32[512]{0:T(512)S(1)} %dynamic_slice.494) | copy-start | bytes 6148
  671.6 262.8 %copy-start.21 = (f32[2,128,512]{2,1,0:T(8,128)}, f32[2,128,512]{2,1,0:T(8,128)S(1)}, u32[]{:S(2)}) copy-start(f32[2,128,512]{2,1,0:T(8,128)S(1)} %get-tuple-element.2955) | copy-start | bytes 1572868
  681.5 252.9 %copy-start.125 = (f32[2,128]{1,0:T(2,128)}, f32[2,128]{1,0:T(2,128)S(1)}, u32[]{:S(2)}) copy-start(f32[2,128]{1,0:T(2,128)S(1)} %add_rsqrt_fusion.2) | copy-start | bytes 3076
  682.3 107.6 %all-gather.39.cloned.1.call-start = ((), (), s32[]{:S(2)}) async-start(), calls=%async_computation.26 | async-start | bytes 6488064 | tf_op jit(solution)/shard_map/all_gather | solution.py:277
  682.9 136.6 %all-gather.43.cloned.1.call-start = ((), (), s32[]{:S(2)}) async-start(), calls=%async_computation.29 | async-start | bytes 1310720 | tf_op jit(solution)/shard_map/all_gather | solution.py:240
  683.6 181.6 %all-gather.41.cloned.1.call-start = ((), (), s32[]{:S(2)}) async-start(), calls=%async_computation.27 | async-start | bytes 6488064 | tf_op jit(solution)/shard_map/all_gather | solution.py:278
  684.2 238.5 %reduce-scatter.32.cloned.1.call-start = ((), (), s32[]{:S(2)}) async-start(), calls=%async_computation.30 | async-start | bytes 2621440 | tf_op jit(solution)/shard_map/reduce_scatter | solution.py:243
  745.2 44.7 %copy-start.26 = (bf16[2,128,2048]{2,1,0:T(8,128)(2,1)S(1)}, bf16[2,128,2048]{2,1,0:T(8,128)(2,1)}, u32[]{:S(2)}) copy-start(bf16[2,128,2048]{2,1,0:T(8,128)(2,1)} %all-gather.35.cloned.1.call-done) | copy-start | bytes 3145732
  878.7 55.7 %copy-start.50 = (bf16[2,128,512]{2,1,0:T(8,128)(2,1)S(1)}, bf16[2,128,512]{2,1,0:T(8,128)(2,1)}, u32[]{:S(2)}) copy-start(bf16[2,128,512]{2,1,0:T(8,128)(2,1)} %param.61) | copy-start | bytes 786436
  878.7 57.8 %copy-start.13 = (f32[2,4,128,128]{3,2,1,0:T(8,128)S(1)}, f32[2,4,128,128]{3,2,1,0:T(8,128)}, u32[]{:S(2)}) copy-start(f32[2,4,128,128]{3,2,1,0:T(8,128)} %copy-done.12) | copy-start | bytes 1572868
  878.7 84.1 %all-gather.45.cloned.1.call-start = ((), (), s32[]{:S(2)}) async-start(), calls=%async_computation.31 | async-start | bytes 1310720 | tf_op jit(solution)/shard_map/all_gather | solution.py:240
  936.4 166.6 %all-gather.51.cloned.1.call-start = ((), (), s32[]{:S(2)}) async-start(), calls=%async_computation.43 | async-start | bytes 4718592 | tf_op jit(solution)/shard_map/all_gather | solution.py:21
  937.5 191.6 %all-gather.53.cloned.1.call-start = ((), (), s32[]{:S(2)}) async-start(), calls=%async_computation.44 | async-start | bytes 9437184 | tf_op jit(solution)/shard_map/all_gather | solution.py:21
  1075.1 414.6 %reduce-scatter.46.cloned.1.call-start = ((), (), s32[]{:S(2)}) async-start(), calls=%async_computation.38 | async-start | bytes 6488064 | tf_op jit(solution)/shard_map/reduce_scatter | solution.py:554
  1080.9 411.1 %reduce-scatter.48.cloned.1.call-start = ((), (), s32[]{:S(2)}) async-start(), calls=%async_computation.39 | async-start | bytes 6488064 | tf_op jit(solution)/shard_map/reduce_scatter | solution.py:557
  1086.9 407.4 %reduce-scatter.50.cloned.1.call-start = ((), (), s32[]{:S(2)}) async-start(), calls=%async_computation.40 | async-start | bytes 6488064 | tf_op jit(solution)/shard_map/reduce_scatter | solution.py:560
  1092.4 404.2 %reduce-scatter.42.cloned.1.call-start = ((), (), s32[]{:S(2)}) async-start(), calls=%async_computation.36 | async-start | bytes 4718592 | tf_op jit(solution)/shard_map/reduce_scatter | solution.py:527
  1098.0 400.9 %reduce-scatter.44.cloned.1.call-start = ((), (), s32[]{:S(2)}) async-start(), calls=%async_computation.37 | async-start | bytes 4718592 | tf_op jit(solution)/shard_map/reduce_scatter | solution.py:551
  1102.9 398.5 %reduce-scatter.56.cloned.1.call-start = ((), (), s32[]{:S(2)}) async-start(), calls=%async_computation.47 | async-start | bytes 147456
  1435.2 10.9 collective-permute-start.1
  1437.4 72.0 %reduce-scatter.58.cloned.1.call-start = ((), (), s32[]{:S(2)}) async-start(), calls=%async_computation.48 | async-start | bytes 147456
  1438.6 108.2 %reduce-scatter.60.cloned.1.call-start = ((), (), s32[]{:S(2)}) async-start(), calls=%async_computation.49 | async-start | bytes 294912
  1439.8 144.7 %reduce-scatter.52.cloned.1.call-start = ((), (), s32[]{:S(2)}) async-start(), calls=%async_computation.45 | async-start | bytes 589824
  1441.1 181.4 %reduce-scatter.54.cloned.1.call-start = ((), (), s32[]{:S(2)}) async-start(), calls=%async_computation.46 | async-start | bytes 589824
  1446.0 221.0 %reduce-scatter.36.cloned.1.call-start = ((), (), s32[]{:S(2)}) async-start(), calls=%async_computation.33 | async-start | bytes 2359296 | tf_op jit(solution)/shard_map/reduce_scatter | solution.py:518
  1465.2 246.6 %reduce-scatter.38.cloned.1.call-start = ((), (), s32[]{:S(2)}) async-start(), calls=%async_computation.34 | async-start | bytes 2359296 | tf_op jit(solution)/shard_map/reduce_scatter | solution.py:521
  1467.3 290.7 %reduce-scatter.34.cloned.1.call-start = ((), (), s32[]{:S(2)}) async-start(), calls=%async_computation.32 | async-start | bytes 2621440 | tf_op jit(solution)/shard_map/reduce_scatter | solution.py:243
  1478.4 333.9 %reduce-scatter.30.cloned.1.call-start = ((), (), s32[]{:S(2)}) async-start(), calls=%async_computation.28 | async-start | bytes 2621440 | tf_op jit(solution)/shard_map/reduce_scatter | solution.py:243
  1485.3 373.1 %reduce-scatter.40.cloned.1.call-start = ((), (), s32[]{:S(2)}) async-start(), calls=%async_computation.35 | async-start | bytes 4718592 | tf_op jit(solution)/shard_map/reduce_scatter | solution.py:524
  1496.6 261.4 %copy-start.39 = (bf16[2,128,512]{2,1,0:T(8,128)(2,1)S(1)}, bf16[2,128,512]{2,1,0:T(8,128)(2,1)}, u32[]{:S(2)}) copy-start(bf16[2,128,512]{2,1,0:T(8,128)(2,1)} %param.41) | copy-start | bytes 786436
  1496.6 261.4 %copy-start.134 = (f32[2,128]{1,0:T(2,128)S(1)}, f32[2,128]{1,0:T(2,128)}, u32[]{:S(2)}) copy-start(f32[2,128]{1,0:T(2,128)} %copy-done.133) | copy-start | bytes 3076
  1498.8 270.7 %copy-start.143 = (f32[256]{0:T(256)S(1)}, f32[256]{0:T(256)}, u32[]{:S(2)}) copy-start(f32[256]{0:T(256)} %get-tuple-element.2726) | copy-start | bytes 3076
  1498.8 313.5 %copy-start.22 = (f32[2,128,512]{2,1,0:T(8,128)S(1)}, f32[2,128,512]{2,1,0:T(8,128)}, u32[]{:S(2)}) copy-start(f32[2,128,512]{2,1,0:T(8,128)} %copy-done.21) | copy-start | bytes 1572868
  1498.8 313.5 %copy-start.37 = (f32[2,128,512]{2,1,0:T(8,128)S(1)}, f32[2,128,512]{2,1,0:T(8,128)}, u32[]{:S(2)}) copy-start(f32[2,128,512]{2,1,0:T(8,128)} %reduce-scatter.32.cloned.1.call-done) | copy-start | bytes 1572868
  1498.8 313.6 %copy-start.51 = (bf16[2,128,512]{2,1,0:T(8,128)(2,1)S(1)}, bf16[2,128,512]{2,1,0:T(8,128)(2,1)}, u32[]{:S(2)}) copy-start(bf16[2,128,512]{2,1,0:T(8,128)(2,1)} %param.61) | copy-start | bytes 786436
  1498.8 313.6 %copy-start.106 = (f32[512]{0:T(512)S(1)}, f32[512]{0:T(512)}, u32[]{:S(2)}) copy-start(f32[512]{0:T(512)} %copy-done.105) | copy-start | bytes 6148
  1498.8 313.6 %copy-start.126 = (f32[2,128]{1,0:T(2,128)S(1)}, f32[2,128]{1,0:T(2,128)}, u32[]{:S(2)}) copy-start(f32[2,128]{1,0:T(2,128)} %copy-done.125) | copy-start | bytes 3076
  1498.8 313.6 %copy-start.138 = (f32[2,128]{1,0:T(2,128)S(1)}, f32[2,128]{1,0:T(2,128)}, u32[]{:S(2)}) copy-start(f32[2,128]{1,0:T(2,128)} %copy-done.137) | copy-start | bytes 3076
  (180 other events, 692.9 us)
Sparse Core Ops, SparseCore 0:
  9.6 30.6 all-gather.22
  42.2 27.3 all-gather.26
  71.5 27.8 all-gather.24
  101.2 36.7 all-gather.28
  139.7 37.1 all-gather.30
  249.2 37.6 all-gather.46
  358.3 55.0 all-gather.48
  415.3 37.4 all-gather.32
  626.5 43.8 reduce-scatter.27
  672.3 42.6 all-gather.36
  717.2 27.9 all-gather.34
  747.0 42.8 all-gather.38
  791.5 27.9 all-gather.42
  821.4 43.8 all-gather.40
  878.8 43.8 reduce-scatter.31
  936.5 26.2 all-gather.44
  964.5 36.6 all-gather.50
  1075.2 53.8 all-gather.52
  1132.5 59.0 reduce-scatter.45
  1195.3 59.3 reduce-scatter.47
  1258.1 59.3 reduce-scatter.49
  1321.2 51.6 reduce-scatter.41
  1376.3 51.4 reduce-scatter.43
  1437.6 35.4 reduce-scatter.55
  1476.0 33.3 reduce-scatter.57
  1513.2 33.6 reduce-scatter.59
  1550.3 34.0 reduce-scatter.51
  1588.4 34.1 reduce-scatter.53
  1625.8 41.1 reduce-scatter.35
  1670.5 41.2 reduce-scatter.37
  1714.1 43.8 reduce-scatter.33
  1760.4 43.9 reduce-scatter.29
  1807.6 50.7 reduce-scatter.39
where the time goes:
time: 1880 us; the launch traced here: 1870 us
  waiting for transfers between devices  719 us (38%)
  other arithmetic  570 us (30%)
  matrix products  265 us (14%)
  local copies, waits for them, and re-layouts  172 us (9%)
  blocking collectives  116 us (6%)
    another operation x38, other arithmetic, block_core(): lax.linalg.triangular_solve(system, jnp.transpose(target, (1, 0, 2)), lef...  404 us
    reduce_scatter x4, waiting for transfers between devices, summed_rows(): return lax.psum_scatter(term_rows, 'shard', scatter_dimension=2, tiled=True)  131 us
    unnamed x38, waiting for transfers between devices  122 us
    all_gather x4, waiting for transfers between devices, whole_rows(): return lax.all_gather(part_rows, 'shard', axis=2, tiled=True)  79.3 us
    another operation x8, other arithmetic, block_transfer(): lax.linalg.triangular_solve(system, jnp.transpose(scaled_keys, (1, 0, 2))...  78.8 us
    all_gather x4, waiting for transfers between devices, entering(): everything = jax.tree.map(lambda part: lax.all_gather(part, axis), x)  72.5 us
    dot_general x16, matrix products, compose(): jnp.einsum('shkj,shjv->shkv', second_map[0], first_map[1], precision=EXAC...  53.6 us
    all_gather x1, waiting for transfers between devices, per_device(): lax.all_gather(down_weight, 'seq', axis=1, tiled=True)  45.8 us
  transfers between devices with their start and end apart: 35, of which 21 were waited for; matrix products, arithmetic and copies ran while one was open for 51% of the time, Pallas kernels for 0%

commit v1 on v0

v1 whole, which is shorter than its diff:
```python
import functools
import jax, jax.numpy as jnp
from jax import lax
from jax.experimental import pallas as pl
from jax.experimental.pallas import tpu as pltpu
from jax.sharding import PartitionSpec
f32=jnp.float32; bf16=jnp.bfloat16
SPAN=64
EPSILON=1e-6
HI=lax.Precision.HIGHEST

def dg(a,b,ca=1,cb=0):
    return lax.dot_general(a,b,(((ca,),(cb,)),((),())),preferred_element_type=f32)
def halves(x):
    h=x.astype(bf16)
    return h,(x-h.astype(f32)).astype(bf16)
def mm3(a,b,ca=1,cb=0):
    ah,al=halves(a); bh,bl=halves(b)
    return dg(ah,bh,ca,cb)+(dg(al,bh,ca,cb)+dg(ah,bl,ca,cb))
def mm1(a,b,ca=1,cb=0):
    return dg(a.astype(bf16),b.astype(bf16),ca,cb)
def mmx(a,b,ca=1,cb=0):
    return lax.dot_general(a,b,(((ca,),(cb,)),((),())),preferred_element_type=f32,precision=HI)

def square_masks():
    i=lax.broadcasted_iota(jnp.int32,(SPAN,SPAN),0); j=lax.broadcasted_iota(jnp.int32,(SPAN,SPAN),1)
    return i,j
def positions(base,rows,cols,axis):
    return base+lax.broadcasted_iota(jnp.int32,(rows,cols),axis)
def doc_count(starts,pos):
    n=jnp.zeros(pos.shape,jnp.int32)
    for e in range(starts.shape[0]):
        n=n+jnp.where(starts[e]<=pos,1,0)
    return n
def doc_age(starts,pos):
    s=jnp.zeros(pos.shape,jnp.int32)
    for e in range(starts.shape[0]):
        s=jnp.where(starts[e]<=pos,starts[e],s)
    return pos-s
def count_at(starts,p):
    n=jnp.int32(0)
    for e in range(starts.shape[0]):
        n=n+jnp.where(starts[e]<=p,1,0)
    return n
def sigmoid(x):
    return 1.0/(1.0+jnp.exp(-x))
def softplus(x):
    return jnp.maximum(x,0.0)+jnp.log(1.0+jnp.exp(-jnp.abs(x)))

def inverse(A):
    i,j=square_masks()
    near=(i//8)==(j//8)
    eye=jnp.where(i==j,1.0,0.0)
    X=jnp.where(near,-A,0.0); far=jnp.where(near,0.0,A)
    X2=mm3(X,X); X4=mm3(X2,X2)
    Di=eye+X; Di=Di+mm3(Di,X2); Di=Di+mm3(Di,X4)
    Y=-mm3(Di,far)
    Y2=mm3(Y,Y); Y4=mm3(Y2,Y2)
    T=Di+mm3(Y4,Di); T=T+mm3(Y2,T); T=T+mm3(Y,T)
    return T

def span_terms(n,q,k,starts,xc,xr,rate,bias):
    i,j=square_masks()
    base=n*SPAN
    docs=doc_count(starts,positions(base,SPAN,128,0))
    docr=doc_count(starts,positions(base,1,SPAN,1))
    before=count_at(starts,base-1)
    lastdoc=count_at(starts,base+SPAN-1)
    lower=jnp.where(i>=j,1.0,0.0); upper=jnp.where(i<=j,1.0,0.0)
    beta=sigmoid(xc[:,0:1])
    g=-rate*softplus(xc[:,1:2]+bias)
    gr=-rate*softplus(xr[1:2]+bias)
    G=mmx(lower,jnp.broadcast_to(g,(SPAN,128)))
    Gr=mmx(jnp.broadcast_to(gr,(8,SPAN)),upper)[0:1]
    same=docs[:,:SPAN]==docr
    incl=(i>=j)&same
    D=jnp.where(incl,jnp.exp(jnp.where(incl,G[:,:SPAN]-Gr,0.0)),0.0)
    gam=jnp.where(docs==before,jnp.exp(G),0.0)
    end=jnp.where(docs==lastdoc,jnp.exp(G[SPAN-1:SPAN]-G),0.0)
    KK=dg(k,k,1,1); QK=dg(q,k,1,1)
    return beta,g,D,gam,end,KK,QK,i,j

def conv_pre(upad,taps,age,base,rows):
    window=upad[pl.ds(base,rows+8),:]
    pre=window[8:]*taps[3:4]
    for back in range(1,4):
        ok=jnp.where(age>=back,1.0,0.0)
        pre=pre+window[8-back:8-back+rows]*ok*taps[3-back:4-back]
    return pre

def forward_kernel(u_ref,taps_ref,xc_ref,xr_ref,starts,hp,o_ref,q_ref,k_ref,v_ref,s_ref,w_ref,t_ref,qt_ref,mh_ref,ml_ref,upad,un_ref,gc_ref,on_ref):
    L=u_ref.shape[0]; NC=L//SPAN; DV=v_ref.shape[1]; DK=q_ref.shape[1]
    rate=jnp.exp(jnp.full((1,1),hp[0],f32)); bias=hp[1]
    upad[0:8]=jnp.zeros((8,upad.shape[1]),f32)
    taps=taps_ref[...]
    R=128
    def load(c,_):
        upad[pl.ds(pl.multiple_of(8+c*R,8),R),:]=u_ref[pl.ds(pl.multiple_of(c*R,R),R),:].astype(f32)
        return 0
    lax.fori_loop(0,L//R,load,0)
    def conv(c,_):
        base=pl.multiple_of(c*R,R)
        age=doc_age(starts,positions(base,R,128,0))[:,0:1]
        pre=conv_pre(upad,taps,age,base,R)
        act=pre*sigmoid(pre)
        rows=pl.ds(base,R)
        aq=act[:,:DK]; ak=act[:,DK:2*DK]
        q_ref[rows,:]=(aq*lax.rsqrt(jnp.sum(aq*aq,axis=1,keepdims=True)+EPSILON)*DK**-0.5).astype(bf16)
        k_ref[rows,:]=(ak*lax.rsqrt(jnp.sum(ak*ak,axis=1,keepdims=True)+EPSILON)).astype(bf16)
        v_ref[rows,:]=act[:,2*DK:].astype(bf16)
        return 0
    lax.fori_loop(0,L//R,conv,0)
    def local(n,_):
        rows=pl.ds(pl.multiple_of(n*SPAN,SPAN),SPAN)
        q=q_ref[rows,:]; k=k_ref[rows,:]; v=v_ref[rows,:]
        beta,g,D,gam,end,KK,QK,i,j=span_terms(n,q,k,starts,xc_ref[n],xr_ref[n],rate,bias)
        A=jnp.where(i>j,beta*D*KK,0.0)
        T=inverse(A)
        kf=k.astype(f32)
        UW=mm3(T,jnp.concatenate([beta*v.astype(f32),(beta*gam)*kf],axis=1))
        P=QK*D
        PW=mm1(P,UW)
        qt=gam*q.astype(f32)-PW[:,DV:]
        NM=mm3(end*kf,UW,0,0)
        t_ref[n]=T
        on_ref[n]=PW[:,:DV]
        w_ref[n]=UW[:,:DV]
        qt_ref[n,0:SPAN]=qt.astype(bf16)
        qt_ref[n,SPAN:]=UW[:,DV:].astype(bf16)
        un_ref[n]=NM[:,:DV]
        mh,ml=halves(NM[:,DV:])
        mh_ref[n]=mh; ml_ref[n]=ml
        gc_ref[n]=jnp.broadcast_to(gam[SPAN-1:SPAN],(8,128))
        return 0
    lax.fori_loop(0,NC,local,0,unroll=4)
    def chain(n,S):
        s_ref[n]=S
        sh,sl=halves(S); mh=mh_ref[n]; ml=ml_ref[n]
        gc=gc_ref[n][0:1]
        return jnp.concatenate([gc]*(DV//128),axis=1)*S+un_ref[n]-(dg(mh,sh)+(dg(ml,sh)+dg(mh,sl)))
    lax.fori_loop(0,NC,chain,jnp.zeros((DK,DV),f32),unroll=2)
    def emit(n,_):
        rows=pl.ds(pl.multiple_of(n*SPAN,SPAN),SPAN)
        r=dg(qt_ref[n],s_ref[n].astype(bf16))
        o_ref[rows,:]=(on_ref[n]+r[:SPAN]).astype(o_ref.dtype)
        w_ref[n]=w_ref[n]-r[SPAN:]
        return 0
    lax.fori_loop(0,NC,emit,0,unroll=4)

def backward_kernel(do_ref,u_ref,taps_ref,xc_ref,xr_ref,starts,hp,q_ref,k_ref,v_ref,s_ref,w_ref,t_ref,qt_ref,mh_ref,ml_ref,
                    du_ref,dtaps_ref,dx_ref,dh_ref,upad,dpre,ds_ref,dqkv,r_ref,gc_ref):
    L=u_ref.shape[0]; NC=L//SPAN; DV=v_ref.shape[1]; DK=q_ref.shape[1]
    rate=jnp.exp(jnp.full((1,1),hp[0],f32)); bias=hp[1]
    taps=taps_ref[...]
    R=128
    upad[0:8]=jnp.zeros((8,upad.shape[1]),f32)
    dpre[L:L+8]=jnp.zeros((8,upad.shape[1]),f32)
    def load(c,_):
        upad[pl.ds(pl.multiple_of(8+c*R,8),R),:]=u_ref[pl.ds(pl.multiple_of(c*R,R),R),:].astype(f32)
        return 0
    lax.fori_loop(0,L//R,load,0)
    def early(n,_):
        rows=pl.ds(pl.multiple_of(n*SPAN,SPAN),SPAN)
        r_ref[n]=dg(qt_ref[n][0:SPAN],do_ref[rows,:],0,0)
        base=n*SPAN
        G=jnp.sum(-rate*softplus(xc_ref[n][:,1:2]+bias),axis=0,keepdims=True)
        alive=jnp.where(count_at(starts,base+SPAN-1)==count_at(starts,base-1),1.0,0.0)
        gc_ref[n]=jnp.broadcast_to(jnp.exp(G)*alive,(8,128))
        return 0
    lax.fori_loop(0,NC,early,0,unroll=4)
    def chain(m,dS):
        n=NC-1-m
        ds_ref[n]=dS
        sh,sl=halves(dS); mh=mh_ref[n]; ml=ml_ref[n]
        gc=gc_ref[n][0:1]
        return jnp.concatenate([gc]*(DV//128),axis=1)*dS+r_ref[n]-(dg(mh,sh,0,0)+(dg(ml,sh,0,0)+dg(mh,sl,0,0)))
    lax.fori_loop(0,NC,chain,jnp.zeros((DK,DV),f32),unroll=2)
    def local(n,sums):
        rows=pl.ds(pl.multiple_of(n*SPAN,SPAN),SPAN)
        q=q_ref[rows,:]; k=k_ref[rows,:]; v=v_ref[rows,:]; dO=do_ref[rows,:]
        xc=xc_ref[n]
        beta,g,D,gam,end,KK,QK,i,j=span_terms(n,q,k,starts,xc,xr_ref[n],rate,bias)
        S0=s_ref[n]; dS1=ds_ref[n]
        S0h=S0.astype(bf16); dSh=dS1.astype(bf16)
        kf=k.astype(f32); qf=q.astype(f32); vf=v.astype(f32)
        W=w_ref[n].astype(bf16); T=t_ref[n].astype(bf16)
        P=(QK*D).astype(bf16)
        dW=dg(P,dO,0,0)+jnp.concatenate([end]*(DV//128),axis=1)*dg(k,dSh)
        Y=dg(T,dW.astype(bf16),0,0)
        dOY=jnp.concatenate([dO,Y.astype(bf16)],axis=0)
        dPA=dg(dOY,W,1,1)
        GS=dg(dOY,S0h,1,1)
        dOS=GS[:SPAN]; YS=GS[SPAN:]
        Z=dg(W,dSh,1,1)
        dPD=dPA[:SPAN]*D
        EA=jnp.where(i>j,-dPA[SPAN:]*D,0.0)
        E=beta*EA
        A1=jnp.concatenate([dPD,E],axis=0).astype(bf16)
        r1=dg(A1,k)
        r2=dg(A1,jnp.concatenate([q,k],axis=0),0,0)
        dqkv[rows,0:DK]=gam*dOS+r1[:SPAN]
        dqkv[rows,DK:2*DK]=r1[SPAN:]+r2-(beta*gam)*YS+end*Z
        dqkv[rows,2*DK:]=beta*Y
        EK=EA*KK
        kYS=jnp.sum(kf*YS,axis=1,keepdims=True)
        dbeta=jnp.sum(Y*vf,axis=1,keepdims=True)-gam*kYS+jnp.sum(EK,axis=1,keepdims=True)
        Fm=dPD*QK+beta*EK
        dgam=jnp.sum(qf*dOS,axis=1,keepdims=True)-beta*kYS
        dend=jnp.sum(kf*Z,axis=1,keepdims=True)*end
        colsum=mmx(Fm,jnp.ones((SPAN,128),f32),0,0)
        dG=jnp.sum(Fm,axis=1,keepdims=True)-colsum+dgam*gam-dend
        tail=jnp.sum(jnp.sum(S0*dS1,axis=0,keepdims=True),axis=1,keepdims=True)
        last=jnp.sum(dend,axis=0,keepdims=True)+gam[SPAN-1:SPAN]*tail
        row=lax.broadcasted_iota(jnp.int32,(SPAN,128),0)
        dG=dG+jnp.where(row==SPAN-1,last,0.0)
        upper=jnp.where(i<=j,1.0,0.0)
        dlog=mmx(upper,dG)
        dbp=(dbeta*beta*(1.0-beta))
        ddp=dlog*(-rate)*sigmoid(xc[:,1:2]+bias)
        dx_ref[n,:,0:1]=dbp[:,0:1]
        dx_ref[n,:,1:2]=ddp[:,0:1]
        sl,sb=sums
        return (sl+jnp.sum(dlog*g,axis=0,keepdims=True),sb+jnp.sum(ddp,axis=0,keepdims=True))
    zero=jnp.zeros((1,128),f32)
    sl,sb=lax.fori_loop(0,NC,local,(zero,zero),unroll=4)
    dh_ref[0:1]=sl; dh_ref[1:2]=sb
    def norms(c,dt):
        base=pl.multiple_of(c*R,R)
        age=doc_age(starts,positions(base,R,128,0))[:,0:1]
        pre=conv_pre(upad,taps,age,base,R)
        sg=sigmoid(pre); act=pre*sg
        rows=pl.ds(base,R)
        d=dqkv[rows,:]
        def unit_back(a,dd,f):
            s=lax.rsqrt(jnp.sum(a*a,axis=1,keepdims=True)+EPSILON)
            dot=jnp.sum(a*dd,axis=1,keepdims=True)
            return f*(s*dd-a*(s*s*s*dot))
        dact=jnp.concatenate([unit_back(act[:,:DK],d[:,:DK],DK**-0.5),unit_back(act[:,DK:2*DK],d[:,DK:2*DK],1.0),d[:,2*DK:]],axis=1)
        dp=dact*sg*(1.0+pre*(1.0-sg))
        dpre[rows,:]=dp
        window=upad[pl.ds(base,R+8),:]
        new=[]
        for j in range(4):
            back=3-j
            x=window[8-back:8-back+R]
            if back: x=x*jnp.where(age>=back,1.0,0.0)
            new.append(dt[j]+jnp.sum(x*dp,axis=0,keepdims=True))
        return tuple(new)
    zt=jnp.zeros((1,upad.shape[1]),f32)
    dt=lax.fori_loop(0,L//R,norms,(zt,)*4)
    for j in range(4): dtaps_ref[j:j+1]=dt[j]
    def back(c,_):
        base=pl.multiple_of(c*R,R)
        window=dpre[pl.ds(base,R+8),:]
        age=doc_age(starts,positions(base,R+8,128,0))[:,0:1]
        d=window[:R]*taps[3:4]
        for s in range(1,4):
            x=window[s:s+R]*jnp.where(age[s:s+R]>=s,1.0,0.0)
            d=d+x*taps[3-s:4-s]
        du_ref[pl.ds(base,R),:]=d.astype(bf16)
        return 0
    lax.fori_loop(0,L//R,back,0)

SM=pl.BlockSpec(memory_space=pltpu.SMEM); VM=pl.BlockSpec(memory_space=pltpu.VMEM)
def S(shape,dt=f32): return jax.ShapeDtypeStruct(shape,dt)
def forward(u,taps,xc,xr,starts,hp,DK=128,DV=256):
    L=u.shape[0]; NC=L//SPAN; CH=u.shape[1]
    return pl.pallas_call(forward_kernel,name="rec_fwd",
      out_shape=(S((L,DV),bf16),S((L,DK),bf16),S((L,DK),bf16),S((L,DV),bf16),S((NC,DK,DV)),S((NC,SPAN,DV)),S((NC,SPAN,SPAN)),S((NC,2*SPAN,DK),bf16),S((NC,DK,DK),bf16),S((NC,DK,DK),bf16)),
      in_specs=[VM,VM,VM,VM,SM,SM],out_specs=(VM,)*10,
      scratch_shapes=[pltpu.VMEM((L+8,CH),f32),pltpu.VMEM((NC,DK,DV),f32),pltpu.VMEM((NC,8,128),f32),pltpu.VMEM((NC,SPAN,DV),f32)],
      compiler_params=pltpu.CompilerParams(vmem_limit_bytes=56*2**20))(u,taps,xc,xr,starts,hp)
def backward(do,u,taps,xc,xr,starts,hp,saved):
    q,k,v,s,w,t,qt,mh,ml=saved
    L=u.shape[0]; NC=L//SPAN; CH=u.shape[1]; DK=q.shape[1]; DV=v.shape[1]
    return pl.pallas_call(backward_kernel,name="rec_bwd",
      out_shape=(S((L,CH),bf16),S((4,CH)),S((NC,SPAN,2)),S((2,128))),
      in_specs=[VM]*5+[SM]*2+[VM]*9,out_specs=(VM,)*4,
      scratch_shapes=[pltpu.VMEM((L+8,CH),f32),pltpu.VMEM((L+8,CH),f32),pltpu.VMEM((NC,DK,DV),f32),pltpu.VMEM((L,CH),f32),pltpu.VMEM((NC,DK,DV),f32),pltpu.VMEM((NC,8,128),f32)],
      compiler_params=pltpu.CompilerParams(vmem_limit_bytes=56*2**20))(do,u,taps,xc,xr,starts,hp,q,k,v,s,w,t,qt,mh,ml)


def per_device(
    tokens, doc_starts, norm_gain, query_weight, key_weight, value_weight, outgate_weight,
    beta_weight, decay_weight, query_conv, key_conv, value_conv, decay_log, decay_bias, head_gain,
    output_weight, ffn_gain, gate_weight, up_weight, down_weight, cotangent,
):
    seq_count, local_len, feature_part = tokens.shape
    row_count = seq_count * local_len
    shard_count = lax.axis_size("shard")
    shard_pos = lax.axis_index("shard")
    seq_devices = lax.axis_size("seq")
    seq_pos = lax.axis_index("seq")
    model_dim = feature_part * shard_count
    head_count = beta_weight.shape[1]
    key_dim = query_weight.shape[1] // head_count
    value_dim = value_weight.shape[1] // head_count
    tap_count = query_conv.shape[1]
    width_k = head_count * key_dim
    channels = 2 * key_dim + value_dim
    feature_start = shard_pos * feature_part
    head_start = shard_pos * head_count
    pairs = seq_count * head_count
    copies = seq_devices // pairs
    length = local_len * seq_devices
    spans = length // SPAN
    my_pair = seq_pos // copies
    my_seq = my_pair // head_count
    my_head = my_pair % head_count

    def whole_rows(part_rows):
        return lax.all_gather(part_rows, "shard", axis=2, tiled=True)

    def summed_rows(term_rows):
        return lax.psum_scatter(
            term_rows.astype(bf16), "shard", scatter_dimension=2, tiled=True
        ).astype(f32)

    def row_total(partial_rows):
        return lax.psum(partial_rows, "shard")

    def project(a, b):
        return jnp.dot(a, b, preferred_element_type=f32)

    def to_pairs(x):
        y = jnp.moveaxis(x, 2, 1).reshape((pairs,) + (local_len, x.shape[3]))
        y = jnp.repeat(y, copies, axis=0)
        y = lax.all_to_all(y, "seq", 0, 0)
        return y.reshape(length, x.shape[3])

    def from_pairs(x):
        y = x.reshape(seq_devices, local_len, x.shape[1])
        y = lax.all_to_all(y, "seq", 0, 0)[::copies]
        return jnp.moveaxis(y.reshape(seq_count, head_count, local_len, x.shape[1]), 1, 2)

    full_query, full_key, full_value, full_outgate, full_beta, full_decay = (
        lax.all_gather(w, "seq", axis=0, tiled=True)
        for w in (query_weight, key_weight, value_weight, outgate_weight, beta_weight, decay_weight)
    )
    full_qconv, full_kconv, full_vconv = (
        lax.all_gather(w, "seq", axis=0, tiled=True) for w in (query_conv, key_conv, value_conv)
    )
    full_output = lax.all_gather(output_weight, "seq", axis=1, tiled=True)
    full_gate = lax.all_gather(gate_weight, "seq", axis=0, tiled=True)
    full_up = lax.all_gather(up_weight, "seq", axis=0, tiled=True)
    full_down = lax.all_gather(down_weight, "seq", axis=1, tiled=True)

    tokens_local = tokens.astype(f32)
    whole_tokens = whole_rows(tokens).astype(f32)
    scale_one = lax.rsqrt(jnp.mean(whole_tokens * whole_tokens, axis=2, keepdims=True) + EPSILON)
    normed_one = (whole_tokens * scale_one * norm_gain).astype(bf16).reshape(row_count, model_dim)
    shape4 = (seq_count, local_len, head_count, -1)
    query_proj = project(normed_one, full_query).astype(bf16).reshape(shape4)
    key_proj = project(normed_one, full_key).astype(bf16).reshape(shape4)
    value_proj = project(normed_one, full_value).astype(bf16).reshape(shape4)
    gate_proj = project(normed_one, full_outgate).reshape(shape4)
    beta_proj = project(normed_one, full_beta).reshape(shape4)
    decay_proj = project(normed_one, full_decay).reshape(shape4)

    u = to_pairs(jnp.concatenate([query_proj, key_proj, value_proj], axis=3))
    rates = to_pairs(jnp.concatenate([beta_proj, decay_proj], axis=3)).reshape(spans, SPAN, 2)
    rates_t = jnp.swapaxes(rates, 1, 2)
    taps = jnp.concatenate(
        [
            lax.dynamic_slice_in_dim(full_qconv, my_head * key_dim, key_dim),
            lax.dynamic_slice_in_dim(full_kconv, my_head * key_dim, key_dim),
            lax.dynamic_slice_in_dim(full_vconv, my_head * value_dim, value_dim),
        ],
        axis=0,
    ).astype(f32).T
    starts = lax.dynamic_index_in_dim(doc_starts, my_seq, 0, keepdims=False)
    at_head = head_start + my_head
    decay_pair = jnp.concatenate(
        [lax.dynamic_slice_in_dim(decay_log, at_head, 1), lax.dynamic_slice_in_dim(decay_bias, at_head, 1)]
    )
    o_pair, *saved = forward(u, taps, rates, rates_t, starts, decay_pair, key_dim, value_dim)
    o = from_pairs(o_pair).astype(f32)

    rho = lax.rsqrt(jnp.mean(o * o, axis=3, keepdims=True) + EPSILON)
    gate_sig = jax.nn.sigmoid(gate_proj)
    gate_silu = gate_proj * gate_sig
    z = o * rho
    branch = (z * head_gain * gate_silu).astype(bf16).reshape(row_count, head_count * value_dim)
    attn_rows = summed_rows(project(branch, full_output).reshape(seq_count, local_len, model_dim))
    residual = tokens_local + attn_rows
    local_ffn_gain = lax.dynamic_slice_in_dim(ffn_gain, feature_start, feature_part)
    local_norm_gain = lax.dynamic_slice_in_dim(norm_gain, feature_start, feature_part)
    scale_two = lax.rsqrt(row_total(jnp.sum(residual * residual, axis=2)) / model_dim + EPSILON)[:, :, None]
    normed_two = whole_rows((residual * scale_two * local_ffn_gain).astype(bf16)).reshape(row_count, model_dim)
    gate_vals = project(normed_two, full_gate)
    up_vals = project(normed_two, full_up)
    sigmoid_gate = jax.nn.sigmoid(gate_vals)
    gate_act = gate_vals * sigmoid_gate
    hidden = (gate_act * up_vals).astype(bf16)
    output = residual + summed_rows(project(hidden, full_down).reshape(seq_count, local_len, model_dim))

    def scattered(grad, axis):
        return lax.psum_scatter(grad.astype(bf16), "seq", scatter_dimension=axis, tiled=True).astype(f32)

    cot_rows = whole_rows(cotangent).reshape(row_count, model_dim)
    grad_hidden = jnp.einsum("rd,fd->rf", cot_rows, full_down, preferred_element_type=f32)
    out_down = scattered(jnp.einsum("rf,rd->fd", hidden, cot_rows, preferred_element_type=f32), 1)
    grad_gate_vals = (grad_hidden * up_vals * sigmoid_gate * (1.0 + gate_vals * (1.0 - sigmoid_gate))).astype(bf16)
    grad_up_vals = (grad_hidden * gate_act).astype(bf16)
    out_gate = scattered(jnp.einsum("rd,rf->df", normed_two, grad_gate_vals, preferred_element_type=f32), 0)
    out_up = scattered(jnp.einsum("rd,rf->df", normed_two, grad_up_vals, preferred_element_type=f32), 0)
    grad_normed_two = jnp.einsum("rf,df->rd", grad_gate_vals, full_gate, preferred_element_type=f32) + jnp.einsum(
        "rf,df->rd", grad_up_vals, full_up, preferred_element_type=f32
    )
    grad_two = summed_rows(grad_normed_two.reshape(seq_count, local_len, model_dim))
    gained_two = local_ffn_gain * grad_two
    inner_two = row_total(jnp.sum(gained_two * residual, axis=2))[:, :, None] / model_dim
    grad_residual = cotangent.astype(f32) + scale_two * (gained_two - residual * scale_two * scale_two * inner_two)
    grad_ffn_part = jnp.sum(grad_two * residual * scale_two, axis=(0, 1))
    attn_cot = whole_rows(grad_residual.astype(bf16)).reshape(row_count, model_dim)
    out_output = scattered(jnp.einsum("rv,rd->vd", branch, attn_cot, preferred_element_type=f32), 1)
    grad_mixed = (
        jnp.einsum("rd,vd->rv", attn_cot, full_output, preferred_element_type=f32).astype(bf16).astype(f32).reshape(shape4)
    )
    grad_head_gain = jnp.sum(grad_mixed * z * gate_silu, axis=(0, 1, 2))
    dz = grad_mixed * head_gain * gate_silu
    grad_o = (rho * (dz - z * jnp.mean(dz * z, axis=3, keepdims=True))).astype(bf16)
    grad_gate_proj = (grad_mixed * z * head_gain * gate_sig * (1.0 + gate_proj * (1.0 - gate_sig))).astype(bf16)
    grad_gate_proj = grad_gate_proj.reshape(row_count, head_count * value_dim)

    du_pair, dtaps, drates, dhead = backward(
        to_pairs(grad_o), u, taps, rates, rates_t, starts, decay_pair, saved
    )
    du = from_pairs(du_pair)
    drates = from_pairs(drates.reshape(length, 2)).astype(bf16)
    grad_qproj = du[..., :key_dim].reshape(row_count, width_k)
    grad_kproj = du[..., key_dim : 2 * key_dim].reshape(row_count, width_k)
    grad_vproj = du[..., 2 * key_dim :].reshape(row_count, head_count * value_dim)
    grad_beta_proj = drates[..., 0].reshape(row_count, head_count)
    grad_decay_proj = drates[..., 1].reshape(row_count, head_count)

    def weight_grad(grad_cols):
        return scattered(jnp.einsum("rd,rc->dc", normed_one, grad_cols, preferred_element_type=f32), 0)

    def input_grad(grad_cols, weight_full):
        return jnp.einsum("rc,dc->rd", grad_cols, weight_full, preferred_element_type=f32)

    grad_normed_one = (
        input_grad(grad_qproj, full_query)
        + input_grad(grad_kproj, full_key)
        + input_grad(grad_vproj, full_value)
        + input_grad(grad_gate_proj, full_outgate)
        + input_grad(grad_beta_proj, full_beta)
        + input_grad(grad_decay_proj, full_decay)
    )
    grad_one = summed_rows(grad_normed_one.reshape(seq_count, local_len, model_dim))
    gained_one = local_norm_gain * grad_one
    inner_one = row_total(jnp.sum(gained_one * tokens_local, axis=2))[:, :, None] / model_dim
    grad_tokens = grad_residual + scale_one * (gained_one - tokens_local * scale_one * scale_one * inner_one)
    grad_norm_part = jnp.sum(grad_one * tokens_local * scale_one, axis=(0, 1))

    small = dtaps
    tap_all = lax.all_gather(small, "seq")[::copies].reshape(seq_count, head_count, tap_count, channels)
    tap_sum = jnp.sum(tap_all, axis=0)

    def own_rows(part):
        rows = jnp.swapaxes(part, 1, 2).reshape(-1, tap_count)
        count = rows.shape[0] // seq_devices
        return lax.dynamic_slice_in_dim(rows, seq_pos * count, count)

    out_qconv = own_rows(tap_sum[:, :, :key_dim])
    out_kconv = own_rows(tap_sum[:, :, key_dim : 2 * key_dim])
    out_vconv = own_rows(tap_sum[:, :, 2 * key_dim :])

    def place_into(full_length, part_vals, start_at):
        return lax.dynamic_update_slice(jnp.zeros((full_length,), f32), part_vals, (start_at,))

    total_heads = decay_log.shape[0]
    primary = jnp.where(seq_pos % copies == 0, 1.0, 0.0)
    small_sums = lax.psum(
        (
            place_into(model_dim, grad_norm_part, feature_start),
            place_into(model_dim, grad_ffn_part, feature_start),
            grad_head_gain,
            place_into(total_heads, dhead[0, :1] * primary, at_head),
            place_into(total_heads, dhead[1, :1] * primary, at_head),
        ),
        ("seq", "shard"),
    )
    return (
        output, grad_tokens, small_sums[0], weight_grad(grad_qproj), weight_grad(grad_kproj),
        weight_grad(grad_vproj), weight_grad(grad_gate_proj), weight_grad(grad_beta_proj),
        weight_grad(grad_decay_proj), out_qconv, out_kconv, out_vconv, small_sums[3], small_sums[4],
        small_sums[2], out_output, small_sums[1], out_gate, out_up, out_down,
    )


def solution(mesh):
    P = PartitionSpec
    rows, cols = P("seq", "shard"), P("shard", "seq")
    both, acts = P(("shard", "seq"), None), P(None, "seq", "shard")
    return jax.shard_map(
        per_device,
        mesh=mesh,
        in_specs=(acts, P(), P()) + (rows,) * 6 + (both,) * 3 + (P(), P(), P(), cols, P(), rows, rows, cols, acts),
        out_specs=(acts, acts, P()) + (rows,) * 6 + (both,) * 3 + (P(), P(), P(), cols, P(), rows, rows, cols),
        check_vma=False,
    )
```

time: 1880 us -> 1230 us (0.65)
  other arithmetic: 570 us -> 37.9 us
  matrix products: 265 us -> 92.2 us
  local copies, waits for them, and re-layouts: 172 us -> 37 us
  Pallas kernels: 0 us -> 75.6 us
  waiting for transfers between devices: 719 us -> 787 us
  blocking collectives: 116 us -> 157 us
    another operation x79 -> x0, other arithmetic: 487 us -> none  [the longest x38 404 us: block_core(): lax.linalg.triangular_solve(system, jnp.transpose(target, (1, 0, 2)), lef...]
    reduce_scatter x12, waiting for transfers between devices: 260 us -> 482 us  [the longest x8 401 us: scattered(): lax.psum_scatter(grad.astype(bf16), 'seq', scatter_dimension=axis, tiled=...]
    dot_general x101 -> x27, matrix products: 234 us -> 79.5 us  [the longest x10 35.1 us: project(): return jnp.dot(a, b, preferred_element_type=f32)]
    unnamed x38 -> x28, waiting for transfers between devices: 122 us -> 6.98 us
    pallas_call x0 -> x2, Pallas kernels: none -> 75.6 us  [the longest x1 42.1 us: forward(): pl.pallas_call(forward_kernel, name='rec_fwd', out_shape=(S((L, DV), bf16...]
    all_gather x12 -> x8, waiting for transfers between devices: 258 us -> 199 us  [the longest x4 84.7 us: per_device(): lax.all_gather(w, 'seq', axis=0, tiled=True)]
    while x258 -> x0, local copies, waits for them, and re-layouts: 25.6 us -> none
    all_gather x5 -> x6, blocking collectives: 44 us -> 68.1 us  [the longest x5 59.8 us: per_device(): lax.all_gather(w, 'seq', axis=0, tiled=True)]
  transfers between devices with their start and end apart: 35 -> 30, of which waited for: 21 -> 24; matrix products, arithmetic and copies ran while one was open for 51% -> 10% of each run, Pallas kernels for 0% -> 3%
where the time goes in v1:
time: 1230 us; the launch traced here: 1220 us
  waiting for transfers between devices  787 us (64%)
  blocking collectives  157 us (13%)
  matrix products  92.2 us (7%)
  Pallas kernels  75.6 us (6%)
  other arithmetic  37.9 us (3%)
  local copies, waits for them, and re-layouts  37 us (3%)
  starting transfers between devices  16.3 us (1%)
  between operations  15.2 us (1%)
    reduce_scatter x8, waiting for transfers between devices, scattered(): lax.psum_scatter(grad.astype(bf16), 'seq', scatter_dimension=axis, tiled=...  401 us
    all_gather x4, waiting for transfers between devices, whole_rows(): return lax.all_gather(part_rows, 'shard', axis=2, tiled=True)  90.8 us
    all_gather x4, waiting for transfers between devices, per_device(): lax.all_gather(w, 'seq', axis=0, tiled=True)  84.7 us
    reduce_scatter x4, waiting for transfers between devices, summed_rows(): lax.psum_scatter(term_rows.astype(bf16), 'shard', scatter_dimension=2, ti...  80.4 us
    all_gather x5, blocking collectives, per_device(): lax.all_gather(w, 'seq', axis=0, tiled=True)  59.8 us
    all_gather x1, waiting for transfers between devices, per_device(): full_down = lax.all_gather(down_weight, 'seq', axis=1, tiled=True)  45.8 us
    pallas_call x1, Pallas kernels, forward(): pl.pallas_call(forward_kernel, name='rec_fwd', out_shape=(S((L, DV), bf16...  42.1 us
    psum x1, blocking collectives, per_device(): lax.psum((place_into(model_dim, grad_norm_part, feature_start), place_int...  40 us
  transfers between devices with their start and end apart: 30, of which 24 were waited for; matrix products, arithmetic and copies ran while one was open for 10% of the time, Pallas kernels for 3%

profile of v1, /device:TPU:0, one launch (start us, length us, event | category | flops | bytes accessed | tf_op | source)
XLA Modules:
  0.0 1217.6 jit_solution(12815123973062512184)
XLA Ops:
  11.2 10.4 all_gather.65
  21.6 8.9 all_gather.64
  30.4 9.9 all-gather.17.cloned.1.call-done
  44.8 3.7 all-to-all-start.1
  48.4 21.2 %all-gather.19.cloned.1.call-done = bf16[2048,512]{1,0:T(8,128)(2,1)} async-done(((bf16[256,512]{1,0:T(8,128)(2,1)}), bf16[2048,512]{1,0:T(8,128)(2,1)}) %all-gather.19.cloned.1.call-update) | async-done | bytes 2097168 | tf_op jit(solution)/shard_map/all_gather | solution.py:337
  69.6 2.3 convolution_convert_fusion.14
  72.0 27.4 %all-gather.21.cloned.1.call-done = bf16[2048,512]{1,0:T(8,128)(2,1)} async-done(((bf16[256,512]{1,0:T(8,128)(2,1)}), bf16[2048,512]{1,0:T(8,128)(2,1)}) %all-gather.21.cloned.1.call-update) | async-done | bytes 2097168 | tf_op jit(solution)/shard_map/all_gather | solution.py:337
  99.4 2.3 convolution_convert_fusion.13
  101.8 36.1 %all-gather.23.cloned.1.call-done = bf16[2048,1024]{1,0:T(8,128)(2,1)} async-done(((bf16[256,1024]{1,0:T(8,128)(2,1)}), bf16[2048,1024]{1,0:T(8,128)(2,1)}) %all-gather.23.cloned.1.call-update) | async-done | bytes 4194320 | tf_op jit(solution)/shard_map/all_gather | solution.py:337
  137.9 3.5 convolution_convert_fusion.12
  143.6 3.6 all-to-all-start
  147.2 23.8 %all-gather.1 = bf16[8,64,4]{1,2,0:T(4,128)(2,1)S(1)} all-gather(bf16[1,64,4]{1,2,0:T(4,128)(2,1)S(1)} %bitcast.260), channel_id=1, replica_groups=mesh['seq'=8,'shard'=4] {'seq'}, dimensions={0}, use_global_device_ids=true | all-gather | bytes 4608 | tf_op jit(solution)/shard_map/all_gather | solution.py:341
  171.1 7.8 all-gather.2
  180.2 9.0 all_gather.63
  194.9 42.1 %rec_fwd.1 = (bf16[1024,256]{1,0:T(8,128)(2,1)}, bf16[1024,128]{1,0:T(8,128)(2,1)}, bf16[1024,128]{1,0:T(8,128)(2,1)}, bf16[1024,256]{1,0:T(8,128)(2,1)}, f32[16...) custom-call(bf16[1024,512]{1,0:T(8,128)(2,1)} %bitcast.213, ...), custom_call_target="tpu_custom_call" | custom-call | tf_op jit(solution)/shard_map/rec_fwd/pallas_call | solution.py:268
  237.0 3.5 all-to-all-start.2
  241.0 6.5 copy.84
  247.5 2.6 all-to-all-done.2
  250.4 4.6 fusion.23
  255.3 4.5 fusion.6
  261.3 24.8 %reduce-scatter.19.cloned.1.call-done = bf16[2,128,512]{2,1,0:T(8,128)(2,1)} async-done(((bf16[2,128,2048]{2,1,0:T(8,128)(2,1)}), bf16[2,128,512]{2,1,0:T(8,128)(2,1)}) %reduce-scatter.19.cloned.1.call-update) | async-done | bytes 262160 | tf_op jit(solution)/shard_map/reduce_scatter | solution.py:315
  287.2 9.4 psum.56
  300.4 29.8 %all-gather.31.cloned.1.call-done = bf16[2048,1408]{1,0:T(8,128)(2,1)} async-done(((bf16[256,1408]{1,0:T(8,128)(2,1)}), bf16[2048,1408]{1,0:T(8,128)(2,1)}) %all-gather.31.cloned.1.call-update) | async-done | bytes 5767184 | tf_op jit(solution)/shard_map/all_gather | solution.py:344
  330.2 30.2 %all-gather.29.cloned.1.call-done = bf16[2,128,2048]{2,1,0:T(8,128)(2,1)} async-done(((bf16[2,128,512]{2,1,0:T(8,128)(2,1)}), bf16[2,128,2048]{2,1,0:T(8,128)(2,1)}) %all-gather.29.cloned.1.call-update) | async-done | bytes 1048592 | tf_op jit(solution)/shard_map/all_gather | solution.py:312
  360.4 5.9 fusion.60
  366.3 38.8 %all-gather.33.cloned.1.call-done = bf16[2048,1408]{1,0:T(8,128)(2,1)} async-done(((bf16[256,1408]{1,0:T(8,128)(2,1)}), bf16[2048,1408]{1,0:T(8,128)(2,1)}) %all-gather.33.cloned.1.call-update) | async-done | bytes 5767184 | tf_op jit(solution)/shard_map/all_gather | solution.py:345
  405.1 5.6 fusion.61
  410.7 24.0 %all-gather.37.cloned.1.call-done = bf16[2,128,2048]{2,1,0:T(8,128)(2,1)} async-done(((bf16[2,128,512]{2,1,0:T(8,128)(2,1)}), bf16[2,128,2048]{2,1,0:T(8,128)(2,1)}) %all-gather.37.cloned.1.call-update) | async-done | bytes 1048592 | tf_op jit(solution)/shard_map/all_gather | solution.py:312
  434.7 45.8 %all-gather.35.cloned.1.call-done = bf16[1408,2048]{1,0:T(8,128)(2,1)} async-done(((bf16[1408,256]{1,0:T(8,128)(2,1)}), bf16[1408,2048]{1,0:T(8,128)(2,1)}) %all-gather.35.cloned.1.call-update) | async-done | bytes 5767184 | tf_op jit(solution)/shard_map/all_gather | solution.py:346
  480.5 7.0 multiply_convert_fusion
  490.7 2.8 fusion.4
  493.6 27.2 %reduce-scatter.23.cloned.1.call-done = bf16[2,128,512]{2,1,0:T(8,128)(2,1)} async-done(((bf16[2,128,2048]{2,1,0:T(8,128)(2,1)}), bf16[2,128,512]{2,1,0:T(8,128)(2,1)}) %reduce-scatter.23.cloned.1.call-update) | async-done | bytes 262160 | tf_op jit(solution)/shard_map/reduce_scatter | solution.py:315
  522.0 9.6 psum.57
  533.5 26.7 %all-gather.39.cloned.1.call-done = bf16[2,128,2048]{2,1,0:T(8,128)(2,1)} async-done(((bf16[2,128,512]{2,1,0:T(8,128)(2,1)}), bf16[2,128,2048]{2,1,0:T(8,128)(2,1)}) %all-gather.39.cloned.1.call-update) | async-done | bytes 1048592 | tf_op jit(solution)/shard_map/all_gather | solution.py:312
  560.2 4.8 fusion.13
  570.5 13.3 %all_to_all.30 = bf16[8,128,256]{2,1,0:T(8,128)(2,1)} all-to-all(bf16[8,128,256]{2,1,0:T(8,128)(2,1)S(1)} %bitcast.239), channel_id=1, replica_groups=mesh['seq'=8,'shard'=4] {'seq'}, dimensions={0} | all-to-all | bytes 1048576 | tf_op jit(solution)/shard_map/all_to_all | solution.py:328
  583.7 33.5 %rec_bwd.1 = (bf16[1024,512]{1,0:T(8,128)(2,1)}, f32[4,512]{1,0:T(4,128)}, f32[16,64,2]{2,1,0:T(8,128)}, f32[2,128]{1,0:T(2,128)}) custom-call(bf16[1024,256]{1,0:T(8,128)(2,1)} %bitcast.235, bf16[1024,512]{1,0:T(8,128)(2,1)} %bitcast.214, f32[4,512]{1,0:T(4,128)} %convert_bitcast_fusion.1.taps_ref, f32[16,64,2]{2,1,0:T(8,128)} %copy.83.xc_ref, ...), custom_call_target="tpu_custom_call" | custom-call | tf_op jit(solution)/shard_map/rec_bwd/pallas_call | solution.py:276
  618.5 7.0 all_to_all.31
  625.5 3.6 all-to-all-start.4
  630.7 5.0 fusion.64
  638.7 5.7 all-to-all-done.4
  653.4 5.6 convolution_convert_fusion.8
  663.4 5.5 convolution_convert_fusion.2
  668.9 5.4 convolution_convert_fusion.1
  675.4 5.4 convolution_convert_fusion
  683.1 3.4 convolution_convert_fusion.3
  687.6 3.3 convolution_convert_fusion.4
  691.0 3.3 convolution_convert_fusion.5
  695.0 8.3 all-gather.3
  710.8 28.4 %reduce-scatter.25.cloned.1.call-done = bf16[2,128,512]{2,1,0:T(8,128)(2,1)} async-done(((bf16[2,128,2048]{2,1,0:T(8,128)(2,1)}), bf16[2,128,512]{2,1,0:T(8,128)(2,1)}) %reduce-scatter.25.cloned.1.call-update) | async-done | bytes 262160 | tf_op jit(solution)/shard_map/reduce_scatter | solution.py:315
  740.7 9.4 psum.58
  750.1 40.0 %all-reduce = (f32[2048]{0:T(1024)}, f32[16]{0:T(128)}, f32[16]{0:T(128)}, f32[256]{0:T(256)}, f32[2048]{0:T(1024)}) all-reduce(f32[2048]{0:T(1024)S(1)} %dynamic_update_slice.12, f32[16]{0:T(128)S(1)} %bitcast_dynamic-update-slice_fusion.1, ...), channel_id=1, replica_groups=mesh['seq'=8,'shard'=4] {'seq','shard'}, use_global_device_ids=true, to_apply=%region_14.15 | all-reduce | flops 4384 | bytes 35072 | tf_op jit(solution)/shard_map/psum | solution.py:475
  790.1 2.5 fusion.34
  792.6 18.6 %reduce-scatter.27.cloned.1.call-done = bf16[256,512]{1,0:T(8,128)(2,1)} async-done(((bf16[2048,512]{1,0:T(8,128)(2,1)}), bf16[256,512]{1,0:T(8,128)(2,1)}) %reduce-scatter.27.cloned.1.call-update) | async-done | bytes 262160 | tf_op jit(solution)/shard_map/reduce_scatter | solution.py:398
  813.0 43.0 %reduce-scatter.29.cloned.1.call-done = bf16[256,512]{1,0:T(8,128)(2,1)} async-done(((bf16[2048,512]{1,0:T(8,128)(2,1)}), bf16[256,512]{1,0:T(8,128)(2,1)}) %reduce-scatter.29.cloned.1.call-update) | async-done | bytes 262160 | tf_op jit(solution)/shard_map/reduce_scatter | solution.py:398
  857.7 60.7 %reduce-scatter.37.cloned.1.call-done = bf16[256,1408]{1,0:T(8,128)(2,1)} async-done(((bf16[2048,1408]{1,0:T(8,128)(2,1)}), bf16[256,1408]{1,0:T(8,128)(2,1)}) %reduce-scatter.37.cloned.1.call-update) | async-done | bytes 720912 | tf_op jit(solution)/shard_map/reduce_scatter | solution.py:398
  918.5 2.3 convert_element_type.209
  920.8 60.6 %reduce-scatter.39.cloned.1.call-done = bf16[256,1408]{1,0:T(8,128)(2,1)} async-done(((bf16[2048,1408]{1,0:T(8,128)(2,1)}), bf16[256,1408]{1,0:T(8,128)(2,1)}) %reduce-scatter.39.cloned.1.call-update) | async-done | bytes 720912 | tf_op jit(solution)/shard_map/reduce_scatter | solution.py:398
  981.4 2.3 convert_element_type.211
  983.7 60.2 %reduce-scatter.41.cloned.1.call-done = bf16[1408,256]{1,0:T(8,128)(2,1)} async-done(((bf16[1408,2048]{1,0:T(8,128)(2,1)}), bf16[1408,256]{1,0:T(8,128)(2,1)}) %reduce-scatter.41.cloned.1.call-update) | async-done | bytes 720912 | tf_op jit(solution)/shard_map/reduce_scatter | solution.py:398
  1043.9 2.3 convert_element_type.213
  1046.3 52.6 %reduce-scatter.35.cloned.1.call-done = bf16[1024,256]{1,0:T(8,128)(2,1)} async-done(((bf16[1024,2048]{1,0:T(8,128)(2,1)}), bf16[1024,256]{1,0:T(8,128)(2,1)}) %reduce-scatter.35.cloned.1.call-update) | async-done | bytes 524304 | tf_op jit(solution)/shard_map/reduce_scatter | solution.py:398
  1101.0 52.6 %reduce-scatter.33.cloned.1.call-done = bf16[256,1024]{1,0:T(8,128)(2,1)} async-done(((bf16[2048,1024]{1,0:T(8,128)(2,1)}), bf16[256,1024]{1,0:T(8,128)(2,1)}) %reduce-scatter.33.cloned.1.call-update) | async-done | bytes 524304 | tf_op jit(solution)/shard_map/reduce_scatter | solution.py:398
  1155.7 52.8 %reduce-scatter.31.cloned.1.call-done = bf16[256,1024]{1,0:T(8,128)(2,1)} async-done(((bf16[2048,1024]{1,0:T(8,128)(2,1)}), bf16[256,1024]{1,0:T(8,128)(2,1)}) %reduce-scatter.31.cloned.1.call-update) | async-done | bytes 524304 | tf_op jit(solution)/shard_map/reduce_scatter | solution.py:398
  (227 shorter events, 79.9 us)
Async XLA Ops:
  7.2 183.8 %copy-start = (s32[2,16]{1,0:T(2,128)S(1)}, s32[2,16]{1,0:T(2,128)}, u32[]{:S(2)}) copy-start(s32[2,16]{1,0:T(2,128)} %param.22) | copy-start | bytes 388
  7.2 4.0 copy-start.27
  7.2 14.3 %copy-start.28 = (bf16[256,4]{0,1:T(4,128)(2,1)S(1)}, bf16[256,4]{0,1:T(4,128)(2,1)}, u32[]{:S(2)}) copy-start(bf16[256,4]{0,1:T(4,128)(2,1)} %param.28) | copy-start | bytes 6148
  7.2 34.6 %copy-start.24 = (f32[2048]{0:T(1024)S(1)}, f32[2048]{0:T(1024)}, u32[]{:S(2)}) copy-start(f32[2048]{0:T(1024)} %param.23) | copy-start | bytes 24580
  7.2 33.1 %all-gather.17.cloned.1.call-start = ((), (), s32[]{:S(2)}) async-start(), calls=%async_computation.20 | async-start | bytes 1310720 | tf_op jit(solution)/shard_map/all_gather | solution.py:312
  8.0 61.6 %all-gather.19.cloned.1.call-start = ((), (), s32[]{:S(2)}) async-start(), calls=%async_computation.21 | async-start | bytes 2359296 | tf_op jit(solution)/shard_map/all_gather | solution.py:337
  8.7 90.7 %all-gather.21.cloned.1.call-start = ((), (), s32[]{:S(2)}) async-start(), calls=%async_computation.22 | async-start | bytes 2359296 | tf_op jit(solution)/shard_map/all_gather | solution.py:337
  9.5 128.5 %all-gather.23.cloned.1.call-start = ((), (), s32[]{:S(2)}) async-start(), calls=%async_computation.23 | async-start | bytes 4718592 | tf_op jit(solution)/shard_map/all_gather | solution.py:337
  10.0 231.0 %all-gather.25.cloned.1.call-start = ((), (), s32[]{:S(2)}) async-start(), calls=%async_computation.24 | async-start | bytes 4718592 | tf_op jit(solution)/shard_map/all_gather | solution.py:337
  10.6 244.6 %all-gather.27.cloned.1.call-start = ((), (), s32[]{:S(2)}) async-start(), calls=%async_computation.25 | async-start | bytes 4718592 | tf_op jit(solution)/shard_map/all_gather | solution.py:343
  44.8 98.8 %all-to-all-start.1 = ((f32[8,128,2]{1,2,0:T(2,128)}), f32[8,128,2]{1,2,0:T(2,128)S(1)}, u32[]{:S(2)}, u32[]{:S(2)}) async-start(f32[8,128,2]{1,2,0:T(2,128)} %copy.80), calls=%async_computation.1 | async-start | bytes 16384 | tf_op jit(solution)/shard_map/all_to_all | solution.py:328
  142.3 4.9 copy-start.29
  142.3 28.8 %copy-start.30 = (bf16[64,4]{0,1:T(4,128)(2,1)S(1)}, bf16[64,4]{0,1:T(4,128)(2,1)}, u32[]{:S(2)}) copy-start(bf16[64,4]{0,1:T(4,128)(2,1)} %param.31) | copy-start | bytes 1540
  142.3 36.7 %copy-start.36 = (f32[16]{0:T(128)S(1)}, f32[16]{0:T(128)}, u32[]{:S(2)}) copy-start(f32[16]{0:T(128)} %param.33) | copy-start | bytes 196
  142.4 37.3 %copy-start.37 = (f32[16]{0:T(128)S(1)}, f32[16]{0:T(128)}, u32[]{:S(2)}) copy-start(f32[16]{0:T(128)} %param.34) | copy-start | bytes 196
  142.4 37.8 %copy-start.31 = (bf16[128,4]{0,1:T(4,128)(2,1)S(1)}, bf16[128,4]{0,1:T(4,128)(2,1)}, u32[]{:S(2)}) copy-start(bf16[128,4]{0,1:T(4,128)(2,1)} %param.32) | copy-start | bytes 3076
  143.6 50.3 %all-to-all-start = ((bf16[8,128,512]{2,1,0:T(8,128)(2,1)}), bf16[8,128,512]{2,1,0:T(8,128)(2,1)S(1)}, u32[]{:S(2)}, u32[]{:S(2)}) async-start(bf16[8,128,512]{2,1,0:T(8,128)(2,1)} %bitcast.2), calls=%async_computation | async-start | bytes 2097152 | tf_op jit(solution)/shard_map/all_to_all | solution.py:328
  237.0 13.2 %all-to-all-start.2 = ((bf16[8,128,256]{2,1,0:T(8,128)(2,1)}), bf16[8,128,256]{2,1,0:T(8,128)(2,1)S(1)}, u32[]{:S(2)}, u32[]{:S(2)}) async-start(bf16[8,128,256]{2,1,0:T(8,128)(2,1)} %bitcast.248), calls=%async_computation.2 | async-start | bytes 1048576 | tf_op jit(solution)/shard_map/all_to_all | solution.py:333
  240.5 45.6 %reduce-scatter.19.cloned.1.call-start = ((), (), s32[]{:S(2)}) async-start(), calls=%async_computation.26 | async-start | bytes 1310720 | tf_op jit(solution)/shard_map/reduce_scatter | solution.py:315
  241.0 9.4 copy-start.26
  250.1 4.8 copy-start.5
  255.0 4.8 copy-start.16
  255.3 30.8 %copy-start.2 = (bf16[2,128,512]{2,1,0:T(8,128)(2,1)S(1)}, bf16[2,128,512]{2,1,0:T(8,128)(2,1)}, u32[]{:S(2)}) copy-start(bf16[2,128,512]{2,1,0:T(8,128)(2,1)} %param.21) | copy-start | bytes 786436
  259.8 70.4 %all-gather.31.cloned.1.call-start = ((), (), s32[]{:S(2)}) async-start(), calls=%async_computation.28 | async-start | bytes 6488064 | tf_op jit(solution)/shard_map/all_gather | solution.py:344
  260.5 99.8 %all-gather.29.cloned.1.call-start = ((), (), s32[]{:S(2)}) async-start(), calls=%async_computation.27 | async-start | bytes 1310720 | tf_op jit(solution)/shard_map/all_gather | solution.py:312
  298.4 106.6 %all-gather.33.cloned.1.call-start = ((), (), s32[]{:S(2)}) async-start(), calls=%async_computation.29 | async-start | bytes 6488064 | tf_op jit(solution)/shard_map/all_gather | solution.py:345
  299.0 135.7 %all-gather.37.cloned.1.call-start = ((), (), s32[]{:S(2)}) async-start(), calls=%async_computation.32 | async-start | bytes 1310720 | tf_op jit(solution)/shard_map/all_gather | solution.py:312
  299.8 180.7 %all-gather.35.cloned.1.call-start = ((), (), s32[]{:S(2)}) async-start(), calls=%async_computation.30 | async-start | bytes 6488064 | tf_op jit(solution)/shard_map/all_gather | solution.py:346
  300.3 220.5 %reduce-scatter.23.cloned.1.call-start = ((), (), s32[]{:S(2)}) async-start(), calls=%async_computation.33 | async-start | bytes 1310720 | tf_op jit(solution)/shard_map/reduce_scatter | solution.py:315
  360.3 44.7 %copy-start.4 = (bf16[2,128,2048]{2,1,0:T(8,128)(2,1)S(1)}, bf16[2,128,2048]{2,1,0:T(8,128)(2,1)}, u32[]{:S(2)}) copy-start(bf16[2,128,2048]{2,1,0:T(8,128)(2,1)} %all-gather.29.cloned.1.call-done) | copy-start | bytes 3145732
  480.5 7.0 copy-start.33
  487.5 1.8 copy-start.23
  487.5 1.9 copy-start.22
  487.5 3.2 copy-start.34
  490.7 30.1 %copy-start.7 = (bf16[2,128,512]{2,1,0:T(8,128)(2,1)S(1)}, bf16[2,128,512]{2,1,0:T(8,128)(2,1)}, u32[]{:S(2)}) copy-start(bf16[2,128,512]{2,1,0:T(8,128)(2,1)} %reduce-scatter.19.cloned.1.call-done) | copy-start | bytes 786436
  490.7 40.9 %copy-start.11 = (bf16[2,128,512]{2,1,0:T(8,128)(2,1)S(1)}, bf16[2,128,512]{2,1,0:T(8,128)(2,1)}, u32[]{:S(2)}) copy-start(bf16[2,128,512]{2,1,0:T(8,128)(2,1)} %param.41) | copy-start | bytes 786436
  493.5 66.7 %all-gather.39.cloned.1.call-start = ((), (), s32[]{:S(2)}) async-start(), calls=%async_computation.34 | async-start | bytes 1310720 | tf_op jit(solution)/shard_map/all_gather | solution.py:312
  566.6 2.3 copy-start.6
  566.6 2.2 copy-start.9
  625.5 18.9 %all-to-all-start.4 = ((bf16[8,128,512]{2,1,0:T(8,128)(2,1)}), bf16[8,128,512]{2,1,0:T(8,128)(2,1)S(1)}, u32[]{:S(2)}, u32[]{:S(2)}) async-start(bf16[8,128,512]{2,1,0:T(8,128)(2,1)} %bitcast.244), calls=%async_computation.7 | async-start | bytes 2097152 | tf_op jit(solution)/shard_map/all_to_all | solution.py:333
  629.1 78.0 %reduce-scatter.43.cloned.1.call-start = ((), (), s32[]{:S(2)}) async-start(), calls=%async_computation.44 | async-start | bytes 589824
  630.7 5.0 copy-start.13
  637.0 72.2 %reduce-scatter.45.cloned.1.call-start = ((), (), s32[]{:S(2)}) async-start(), calls=%async_computation.45 | async-start | bytes 589824
  638.4 100.8 %reduce-scatter.25.cloned.1.call-start = ((), (), s32[]{:S(2)}) async-start(), calls=%async_computation.35 | async-start | bytes 1310720 | tf_op jit(solution)/shard_map/reduce_scatter | solution.py:315
  644.4 2.3 copy-start.35
  646.7 1.6 copy-start.15
  648.3 1.6 copy-start.18
  648.3 2.2 copy-start.19
  653.3 136.8 %reduce-scatter.21.cloned.1.call-start = ((), (), s32[]{:S(2)}) async-start(), calls=%async_computation.31 | async-start | bytes 1310720 | tf_op jit(solution)/shard_map/reduce_scatter | solution.py:315
  659.0 152.1 %reduce-scatter.27.cloned.1.call-start = ((), (), s32[]{:S(2)}) async-start(), calls=%async_computation.36 | async-start | bytes 2359296 | tf_op jit(solution)/shard_map/reduce_scatter | solution.py:398
  661.2 194.8 %reduce-scatter.29.cloned.1.call-start = ((), (), s32[]{:S(2)}) async-start(), calls=%async_computation.37 | async-start | bytes 2359296 | tf_op jit(solution)/shard_map/reduce_scatter | solution.py:398
  663.3 255.2 %reduce-scatter.37.cloned.1.call-start = ((), (), s32[]{:S(2)}) async-start(), calls=%async_computation.41 | async-start | bytes 6488064 | tf_op jit(solution)/shard_map/reduce_scatter | solution.py:398
  668.9 312.5 %reduce-scatter.39.cloned.1.call-start = ((), (), s32[]{:S(2)}) async-start(), calls=%async_computation.42 | async-start | bytes 6488064 | tf_op jit(solution)/shard_map/reduce_scatter | solution.py:398
  674.3 1.1 copy-start.20
  674.4 369.6 %reduce-scatter.41.cloned.1.call-start = ((), (), s32[]{:S(2)}) async-start(), calls=%async_computation.43 | async-start | bytes 6488064 | tf_op jit(solution)/shard_map/reduce_scatter | solution.py:398
  680.9 418.0 %reduce-scatter.35.cloned.1.call-start = ((), (), s32[]{:S(2)}) async-start(), calls=%async_computation.40 | async-start | bytes 4718592 | tf_op jit(solution)/shard_map/reduce_scatter | solution.py:398
  681.9 1.2 copy-start.21
  686.6 467.0 %reduce-scatter.33.cloned.1.call-start = ((), (), s32[]{:S(2)}) async-start(), calls=%async_computation.39 | async-start | bytes 4718592 | tf_op jit(solution)/shard_map/reduce_scatter | solution.py:398
  690.9 517.6 %reduce-scatter.31.cloned.1.call-start = ((), (), s32[]{:S(2)}) async-start(), calls=%async_computation.38 | async-start | bytes 4718592 | tf_op jit(solution)/shard_map/reduce_scatter | solution.py:398
  694.3 9.0 copy-start.32
  694.3 95.8 %copy-start.8 = (bf16[2,128,512]{2,1,0:T(8,128)(2,1)S(1)}, bf16[2,128,512]{2,1,0:T(8,128)(2,1)}, u32[]{:S(2)}) copy-start(bf16[2,128,512]{2,1,0:T(8,128)(2,1)} %reduce-scatter.19.cloned.1.call-done) | copy-start | bytes 786436
  694.3 95.8 %copy-start.10 = (bf16[2,128,512]{2,1,0:T(8,128)(2,1)S(1)}, bf16[2,128,512]{2,1,0:T(8,128)(2,1)}, u32[]{:S(2)}) copy-start(bf16[2,128,512]{2,1,0:T(8,128)(2,1)} %reduce-scatter.23.cloned.1.call-done) | copy-start | bytes 786436
  694.3 95.8 %copy-start.12 = (bf16[2,128,512]{2,1,0:T(8,128)(2,1)S(1)}, bf16[2,128,512]{2,1,0:T(8,128)(2,1)}, u32[]{:S(2)}) copy-start(bf16[2,128,512]{2,1,0:T(8,128)(2,1)} %param.41) | copy-start | bytes 786436
  1043.9 166.7 %copy-start.1 = (s32[2,16]{1,0:T(2,128)S(1)}, s32[2,16]{1,0:T(2,128)}, u32[]{:S(2)}) copy-start(s32[2,16]{1,0:T(2,128)} %param.22) | copy-start | bytes 388
  (4 other events, 3.8 us)
Sparse Core Ops, SparseCore 0:
  9.6 30.6 all-gather.16
  42.2 27.3 all-gather.18
  71.5 27.8 all-gather.20
  101.2 36.7 all-gather.22
  139.7 47.9 all-gather.24
  189.4 38.5 all-gather.26
  259.9 26.1 reduce-scatter.18
  288.1 41.9 all-gather.30
  332.4 27.9 all-gather.28
  362.2 42.8 all-gather.32
  406.7 27.9 all-gather.36
  436.6 43.8 all-gather.34
  493.6 27.1 reduce-scatter.22
  533.6 26.4 all-gather.38
  637.2 34.0 reduce-scatter.42
  675.0 34.2 reduce-scatter.44
  712.0 27.1 reduce-scatter.24
  742.0 25.8 reduce-scatter.20
  771.1 39.9 reduce-scatter.26
  814.6 41.2 reduce-scatter.28
  859.4 59.0 reduce-scatter.36
  922.3 59.0 reduce-scatter.38
  984.8 59.0 reduce-scatter.40
  1047.5 51.3 reduce-scatter.34
  1102.2 51.2 reduce-scatter.32
  1157.1 51.3 reduce-scatter.30

commit v2 on v1

--- a/solution.py
+++ b/solution.py
@@ -280,6 +280,298 @@
       compiler_params=pltpu.CompilerParams(vmem_limit_bytes=56*2**20))(do,u,taps,xc,xr,starts,hp,q,k,v,s,w,t,qt,mh,ml)
 
 
+MESH=pl.DeviceIdType.MESH
+ANY=pl.BlockSpec(memory_space=pl.ANY)
+
+def flip(s,bit):
+    return s+bit-2*bit*lax.rem(lax.div(s,bit),2)
+
+def flips(s,mask):
+    bit=1
+    while bit<=mask:
+        if mask&bit: s=flip(s,bit)
+        bit*=2
+    return s
+
+def greet(n,zc):
+    s=lax.axis_index("seq"); z=lax.axis_index("shard")
+    bar=pltpu.get_barrier_semaphore()
+    for d in range(1,n):
+        pl.semaphore_signal(bar,inc=1,device_id={"seq":lax.rem(s+d,n)},device_id_type=MESH)
+    for d in range(1,zc):
+        pl.semaphore_signal(bar,inc=1,device_id={"shard":lax.rem(z+d,zc)},device_id_type=MESH)
+    pl.semaphore_wait(bar,n-1+zc-1)
+
+def links(n):
+    return 8 if n==8 else n
+
+class SeqGather:
+    def __init__(self,n,src,dst,axis,sems,r0=0,nr=None):
+        self.n=n; self.src=src; self.dst=dst; self.axis=axis; self.send,self.recv,self.loc=sems
+        self.R,self.C=src.shape
+        self.r0=r0; self.nr=self.R if nr is None else nr
+        self.s=lax.axis_index("seq")
+        self.open=[]
+    def slot(self,t,a,b):
+        if self.axis==0:
+            return self.dst.at[pl.ds(pl.multiple_of(t*self.R+self.r0+a,16),b-a),:]
+        return self.dst.at[pl.ds(self.r0+a,b-a),pl.ds(pl.multiple_of(t*self.C,128),self.C)]
+    def copy(self,src,t,a,b,k,to):
+        c=pltpu.make_async_remote_copy(src_ref=src,dst_ref=self.slot(t,a,b),send_sem=self.send.at[k],recv_sem=self.recv.at[k],device_id={"seq":to},device_id_type=MESH)
+        c.start()
+        return c
+    def pass_on(self,t,a,b,k,to):
+        return self.copy(self.slot(t,a,b),t,a,b,k,to)
+    def start(self):
+        s=self.s; nr=self.nr
+        mine=self.src.at[pl.ds(self.r0,nr),:]
+        self.own=pltpu.make_async_copy(mine,self.slot(s,0,nr),self.loc)
+        self.own.start()
+        masks=(2,4) if self.n==8 else range(2,self.n,2)
+        self.direct=[self.copy(mine,s,0,nr,i+1,flips(s,m)) for i,m in enumerate(masks)]
+        self.open.append(self.copy(mine,s,0,nr,0,flip(s,1)))
+    def middle(self):
+        s=self.s; nr=self.nr; h=nr//2
+        if self.n!=8: return
+        x,y=flip(s,2),flip(s,4)
+        self.direct[0].wait_recv()
+        fa=self.pass_on(x,0,h,3,y)
+        self.open.append(self.pass_on(x,0,nr,5,flip(s,1)))
+        self.direct[1].wait_recv()
+        fb=self.pass_on(y,h,nr,4,x)
+        self.open.append(self.pass_on(y,0,nr,6,flip(s,1)))
+        self.diag=(fa,fb)
+    def late(self):
+        s=self.s; nr=self.nr
+        if self.n==8:
+            for f in self.diag: f.wait_recv()
+            self.open.append(self.pass_on(flips(s,6),0,nr,7,flip(s,1)))
+            for f in self.diag: f.wait_send()
+        else:
+            for i,m in enumerate(range(2,self.n,2)):
+                self.direct[i].wait_recv()
+                self.open.append(self.pass_on(flips(s,m),0,nr,self.n//2+i,flip(s,1)))
+        for f in self.direct: f.wait_send()
+    def finish(self):
+        for f in self.open: f.wait()
+        self.own.wait()
+
+class ShardGather:
+    def __init__(self,zc,src,dst,send,recv):
+        self.zc=zc; self.src=src; self.dst=dst; self.send=send; self.recv=recv
+        self.z=lax.axis_index("shard"); self.C=src.shape[1]
+    def slot(self):
+        return self.dst.at[:,pl.ds(pl.multiple_of(self.z*self.C,128),self.C)]
+    def start(self):
+        self.own=pltpu.make_async_copy(self.src,self.slot(),self.recv.at[0]); self.own.start()
+        self.cs=[]
+        for d in range(1,self.zc):
+            c=pltpu.make_async_remote_copy(src_ref=self.src,dst_ref=self.slot(),send_sem=self.send.at[d],recv_sem=self.recv.at[d],device_id={"shard":lax.rem(self.z+d,self.zc)},device_id_type=MESH)
+            c.start(); self.cs.append(c)
+    def finish(self):
+        for c in self.cs: c.wait()
+        self.own.wait()
+
+class ShardSplit:
+    def __init__(self,zc,src,box,send,recv):
+        self.zc=zc; self.src=src; self.box=box; self.send=send; self.recv=recv
+        self.z=lax.axis_index("shard"); self.C=box.shape[2]
+    def start(self):
+        C=self.C
+        self.own=pltpu.make_async_copy(self.src.at[:,pl.ds(pl.multiple_of(self.z*C,128),C)],self.box.at[0],self.recv.at[0]); self.own.start()
+        self.cs=[]
+        for d in range(1,self.zc):
+            to=lax.rem(self.z+d,self.zc)
+            c=pltpu.make_async_remote_copy(src_ref=self.src.at[:,pl.ds(pl.multiple_of(to*C,128),C)],dst_ref=self.box.at[d],send_sem=self.send.at[d],recv_sem=self.recv.at[d],device_id={"shard":to},device_id_type=MESH)
+            c.start(); self.cs.append(c)
+    def finish(self):
+        for c in self.cs: c.wait()
+        self.own.wait()
+
+class ShardAll:
+    def __init__(self,axis,n,box,send,recv):
+        self.axis=axis; self.n=n; self.box=box; self.send=send; self.recv=recv; self.me=lax.axis_index(axis)
+    def start(self):
+        self.cs=[]
+        for d in range(1,self.n):
+            c=pltpu.make_async_remote_copy(src_ref=self.box.at[self.me],dst_ref=self.box.at[self.me],send_sem=self.send.at[d],recv_sem=self.recv.at[d],device_id={self.axis:lax.rem(self.me+d,self.n)},device_id_type=MESH)
+            c.start(); self.cs.append(c)
+    def finish(self):
+        for c in self.cs: c.wait()
+
+class ColumnSplit:
+    def __init__(self,n,src,dst,send,recv):
+        self.n=n; self.src=src; self.dst=dst; self.send=send; self.recv=recv
+        self.s=lax.axis_index("seq"); self.C=dst.shape[1]; self.R=src.shape[0]
+    def start(self):
+        n,s,C,R=self.n,self.s,self.C,self.R
+        to_rows=self.dst.at[pl.ds(pl.multiple_of(s*R,16),R),:]
+        block=lambda t: self.src.at[:,pl.ds(pl.multiple_of(t*C,128),C)]
+        self.own=pltpu.make_async_copy(block(s),to_rows,self.recv.at[0]); self.own.start()
+        self.cs=[]
+        for d in range(1,n):
+            t=lax.rem(s+d,n)
+            c=pltpu.make_async_remote_copy(src_ref=block(t),dst_ref=to_rows,send_sem=self.send.at[d],recv_sem=self.recv.at[d],device_id={"seq":t},device_id_type=MESH)
+            c.start(); self.cs.append(c)
+    def finish(self):
+        for c in self.cs: c.wait()
+        self.own.wait()
+
+def row_form(cols):
+    return mmx(jnp.ones((8,cols.shape[1]),f32),cols,1,1)
+
+def col_form(rows):
+    r=rows.shape[1]
+    i=lax.broadcasted_iota(jnp.int32,(r,r),0); j=lax.broadcasted_iota(jnp.int32,(r,r),1)
+    return mmx(jnp.where(i==j,1.0,0.0),rows,1,1)
+
+def gathers(n,pairs,sems):
+    send,recv,loc=sems
+    return [SeqGather(n,src,dst,axis,(send.at[i],recv.at[i],loc.at[i])) for i,(src,dst,axis) in enumerate(pairs)]
+def gather_sems(n,k):
+    return [pltpu.SemaphoreType.DMA((k,links(n))),pltpu.SemaphoreType.DMA((k,links(n))),pltpu.SemaphoreType.DMA((k,))]
+def pair_sems(k):
+    return [pltpu.SemaphoreType.DMA((k,)),pltpu.SemaphoreType.DMA((k,))]
+def each(ops,name):
+    for o in ops: getattr(o,name)()
+
+def front_kernel(n,zc,tok,cot,gain,w,wo,normed,scale,cotfull,wfull,wofull,tokfull,zs,zr,cs,cr,*gs):
+    greet(n,zc)
+    zt=ShardGather(zc,tok,tokfull,zs,zr); zt.start()
+    gw=gathers(n,[(w,wfull,0),(wo,wofull,1)],gs)
+    each(gw,"start")
+    zt.finish()
+    zk=ShardGather(zc,cot,cotfull,cs,cr); zk.start()
+    rows=tokfull.shape[0]; D=tokfull.shape[1]
+    def norm(c,_):
+        r=pl.ds(pl.multiple_of(c*32,32),32)
+        x=tokfull[r,:].astype(f32)
+        sc=lax.rsqrt(jnp.sum(x*x,axis=1,keepdims=True)/D+EPSILON)
+        normed[r,:]=(x*sc*gain[...]).astype(bf16)
+        scale[r,:]=jnp.broadcast_to(sc,(32,128))
+        return 0
+    lax.fori_loop(0,rows//32,norm,0)
+    each(gw,"middle"); each(gw,"late")
+    zk.finish()
+    each(gw,"finish")
+
+def attn_out_kernel(n,zc,part,tok,gain,wg,wu,wd,n1,res,scale,nfull,wgfull,wufull,wdfull,n1c,box,sums,nloc,as_,ar,bs,br,cs,cr,es,er,*gs):
+    greet(n,zc)
+    D=part.shape[1]
+    split=ShardSplit(zc,part,box,as_,ar); split.start()
+    gw=gathers(n,[(wg,wgfull,0),(wu,wufull,0),(wd,wdfull,1)],gs)
+    each(gw,"start")
+    cols=ColumnSplit(n,n1,n1c,es,er); cols.start()
+    split.finish()
+    r=tok[...].astype(f32)
+    for d in range(zc): r=r+box[d].astype(f32)
+    res[...]=r
+    sums[lax.axis_index("shard")]=row_form(r*r)
+    tot=ShardAll("shard",zc,sums,bs,br); tot.start(); tot.finish()
+    t=sums[0]
+    for d in range(1,zc): t=t+sums[d]
+    sc=lax.rsqrt(col_form(t)[:,0:1]/D+EPSILON)
+    scale[...]=jnp.broadcast_to(sc,scale.shape)
+    nloc[...]=(r*sc*gain[...]).astype(bf16)
+    zg=ShardGather(zc,nloc,nfull,cs,cr); zg.start()
+    each(gw,"middle")
+    zg.finish()
+    each(gw,"late"); cols.finish(); each(gw,"finish")
+
+def ffn_back_kernel(n,zc,part,res,scale,cot,gain,dg_,du_,hid,bra,n2,gres,afull,gffn,dgfull,dufull,hidfull,brafull,n2c,box,sums,aloc,as_,ar,bs,br,cs,cr,es,er,*gs):
+    greet(n,zc)
+    D=part.shape[1]
+    split=ShardSplit(zc,part,box,as_,ar); split.start()
+    gw=gathers(n,[(dg_,dgfull,0),(du_,dufull,0),(hid,hidfull,0),(bra,brafull,0)],gs)
+    each(gw,"start")
+    cols=ColumnSplit(n,n2,n2c,es,er); cols.start()
+    split.finish()
+    g=box[0].astype(f32)
+    for d in range(1,zc): g=g+box[d].astype(f32)
+    r=res[...]; sc=scale[...][:,0:1]
+    gained=gain[...]*g
+    sums[lax.axis_index("shard")]=row_form(gained*r)
+    tot=ShardAll("shard",zc,sums,bs,br); tot.start()
+    gffn[...]=jnp.broadcast_to(jnp.sum(g*r*sc,axis=0,keepdims=True),gffn.shape)
+    tot.finish()
+    t=sums[0]
+    for d in range(1,zc): t=t+sums[d]
+    inner=col_form(t)[:,0:1]/D
+    gr=cot[...].astype(f32)+sc*(gained-r*(sc*sc*inner))
+    gres[...]=gr
+    aloc[...]=gr.astype(bf16)
+    zg=ShardGather(zc,aloc,afull,cs,cr); zg.start()
+    each(gw,"middle")
+    zg.finish()
+    each(gw,"late"); cols.finish(); each(gw,"finish")
+
+def tail_kernel(n,zc,partdx,partout,res,gres,tok,scale,gain,small,dy,cot,att,output,gtok,dyfull,cotc,attc,smalls,totals,box,boxo,sums,as_,ar,bs,br,cs,cr,ds_,dr,es,er,fs,fr,hs,hr,*gs):
+    greet(n,zc)
+    D=partdx.shape[1]
+    split=ShardSplit(zc,partdx,box,as_,ar); split.start()
+    gw=gathers(n,[(dy,dyfull,0)],gs)
+    each(gw,"start")
+    cc=ColumnSplit(n,cot,cotc,ds_,dr); cc.start()
+    ca=ColumnSplit(n,att,attc,es,er); ca.start()
+    split.finish()
+    so=ShardSplit(zc,partout,boxo,fs,fr); so.start()
+    g=box[0].astype(f32)
+    for d in range(1,zc): g=g+box[d].astype(f32)
+    x=tok[...].astype(f32); sc=scale[...][:,0:1]
+    gained=gain[...]*g
+    sums[lax.axis_index("shard")]=row_form(gained*x)
+    tot=ShardAll("shard",zc,sums,bs,br); tot.start()
+    me=lax.axis_index("seq")
+    smalls[me]=small[...]
+    smalls[me,0:1,0:g.shape[1]]=jnp.sum(g*x*sc,axis=0,keepdims=True)
+    sa=ShardAll("seq",n,smalls,cs,cr); sa.start()
+    tot.finish()
+    t=sums[0]
+    for d in range(1,zc): t=t+sums[d]
+    inner=col_form(t)[:,0:1]/D
+    gtok[...]=gres[...]+sc*(gained-x*(sc*sc*inner))
+    sa.finish()
+    t=smalls[0]
+    for d in range(1,n): t=t+smalls[d]
+    totals[lax.axis_index("shard")]=t
+    za=ShardAll("shard",zc,totals,hs,hr); za.start()
+    each(gw,"middle")
+    so.finish()
+    o=res[...]
+    for d in range(zc): o=o+boxo[d].astype(f32)
+    output[...]=o
+    za.finish()
+    each(gw,"late"); cc.finish(); ca.finish(); each(gw,"finish")
+
+def call(name,cid,kernel,args,specs,outs,ospecs,scratch):
+    return pl.pallas_call(kernel,name=name,out_shape=tuple(outs),in_specs=specs,out_specs=tuple(ospecs),scratch_shapes=scratch,
+      compiler_params=pltpu.CompilerParams(collective_id=cid,has_side_effects=True,vmem_limit_bytes=56*2**20))(*args)
+
+def front(n,zc,tok,cot,gain,w,wo):
+    R,F=tok.shape; D=F*zc
+    return call("front",1,functools.partial(front_kernel,n,zc),(tok,cot,gain,w,wo),[VM,VM,VM,ANY,ANY],
+      [S((R,D),bf16),S((R,128)),S((R,D),bf16),S((w.shape[0]*n,w.shape[1]),bf16),S((wo.shape[0],wo.shape[1]*n),bf16)],[VM,VM,ANY,ANY,ANY],
+      [pltpu.VMEM((R,D),bf16)]+pair_sems(zc)*2+gather_sems(n,2))
+def attn_out(n,zc,part,tok,gain,wg,wu,wd,n1):
+    R,F=tok.shape; D=F*zc
+    return call("attn_out",2,functools.partial(attn_out_kernel,n,zc),(part,tok,gain,wg,wu,wd,n1),[ANY,VM,VM]+[ANY]*4,
+      [S((R,F)),S((R,128)),S((R,D),bf16),S((wg.shape[0]*n,wg.shape[1]),bf16),S((wu.shape[0]*n,wu.shape[1]),bf16),S((wd.shape[0],wd.shape[1]*n),bf16),S((R*n,D//n),bf16)],
+      [VM,VM,VM,ANY,ANY,ANY,ANY],
+      [pltpu.VMEM((zc,R,F),bf16),pltpu.VMEM((zc,8,R),f32),pltpu.VMEM((R,F),bf16)]+pair_sems(zc)*3+pair_sems(n)+gather_sems(n,3))
+def ffn_back(n,zc,part,res,scale,cot,gain,dg_,du_,hid,bra,n2):
+    R,F=cot.shape; D=F*zc
+    full=lambda a: S((a.shape[0]*n,a.shape[1]),bf16)
+    return call("ffn_back",3,functools.partial(ffn_back_kernel,n,zc),(part,res,scale,cot,gain,dg_,du_,hid,bra,n2),[ANY,VM,VM,VM,VM]+[ANY]*5,
+      [S((R,F)),S((R,D),bf16),S((8,F)),full(dg_),full(du_),full(hid),full(bra),S((R*n,D//n),bf16)],[VM,VM,VM]+[ANY]*5,
+      [pltpu.VMEM((zc,R,F),bf16),pltpu.VMEM((zc,8,R),f32),pltpu.VMEM((R,F),bf16)]+pair_sems(zc)*3+pair_sems(n)+gather_sems(n,4))
+def tail(n,zc,partdx,partout,res,gres,tok,scale,gain,small,dy,cot,att):
+    R,F=tok.shape; D=F*zc
+    return call("tail",4,functools.partial(tail_kernel,n,zc),(partdx,partout,res,gres,tok,scale,gain,small,dy,cot,att),[ANY,ANY]+[VM]*6+[ANY]*3,
+      [S((R,F)),S((R,F)),S((dy.shape[0]*n,dy.shape[1]),bf16),S((R*n,D//n),bf16),S((R*n,D//n),bf16),S((n,)+small.shape),S((zc,)+small.shape)],
+      [VM,VM,ANY,ANY,ANY,VM,VM],
+      [pltpu.VMEM((zc,R,F),bf16),pltpu.VMEM((zc,R,F),bf16),pltpu.VMEM((zc,8,R),f32)]+pair_sems(zc)*2+pair_sems(n)*3+pair_sems(zc)*2+gather_sems(n,1))
+
+
 def per_device(
     tokens, doc_starts, norm_gain, query_weight, key_weight, value_weight, outgate_weight,
     beta_weight, decay_weight, query_conv, key_conv, value_conv, decay_log, decay_bias, head_gain,
@@ -308,17 +600,6 @@
     my_seq = my_pair // head_count
     my_head = my_pair % head_count
 
-    def whole_rows(part_rows):
-        return lax.all_gather(part_rows, "shard", axis=2, tiled=True)
-
-    def summed_rows(term_rows):
-        return lax.psum_scatter(
-            term_rows.astype(bf16), "shard", scatter_dimension=2, tiled=True
-        ).astype(f32)
-
-    def row_total(partial_rows):
-        return lax.psum(partial_rows, "shard")
-
     def project(a, b):
         return jnp.dot(a, b, preferred_element_type=f32)
 
@@ -333,29 +614,34 @@
         y = lax.all_to_all(y, "seq", 0, 0)[::copies]
         return jnp.moveaxis(y.reshape(seq_count, head_count, local_len, x.shape[1]), 1, 2)
 
-    full_query, full_key, full_value, full_outgate, full_beta, full_decay = (
-        lax.all_gather(w, "seq", axis=0, tiled=True)
-        for w in (query_weight, key_weight, value_weight, outgate_weight, beta_weight, decay_weight)
-    )
-    full_qconv, full_kconv, full_vconv = (
-        lax.all_gather(w, "seq", axis=0, tiled=True) for w in (query_conv, key_conv, value_conv)
-    )
-    full_output = lax.all_gather(output_weight, "seq", axis=1, tiled=True)
-    full_gate = lax.all_gather(gate_weight, "seq", axis=0, tiled=True)
-    full_up = lax.all_gather(up_weight, "seq", axis=0, tiled=True)
-    full_down = lax.all_gather(down_weight, "seq", axis=1, tiled=True)
-
-    tokens_local = tokens.astype(f32)
-    whole_tokens = whole_rows(tokens).astype(f32)
-    scale_one = lax.rsqrt(jnp.mean(whole_tokens * whole_tokens, axis=2, keepdims=True) + EPSILON)
-    normed_one = (whole_tokens * scale_one * norm_gain).astype(bf16).reshape(row_count, model_dim)
+    taps_local = jnp.concatenate([query_conv, key_conv, value_conv], axis=0)
+    tap_rows = taps_local.shape[0]
+    width_v = head_count * value_dim
+    widths = [width_k, width_k, width_v, width_v, head_count, head_count]
+    edges = [sum(widths[:i]) for i in range(7)]
+    filled = edges[6] + tap_count
+    padding = -filled % 128
+    taps_padded = jnp.pad(taps_local, ((0, query_weight.shape[0] - tap_rows), (0, padding)))
+    weights_one = jnp.concatenate(
+        [query_weight, key_weight, value_weight, outgate_weight, beta_weight, decay_weight, taps_padded], axis=1
+    )
+    flat = lambda x: x.reshape(row_count, x.shape[2])
+    local_ffn_gain = lax.dynamic_slice_in_dim(ffn_gain, feature_start, feature_part)[None]
+    local_norm_gain = lax.dynamic_slice_in_dim(norm_gain, feature_start, feature_part)[None]
+    tokens_flat, cot_flat = flat(tokens), flat(cotangent)
+    normed_one, scale_one, cot_rows, full_one, full_output = front(
+        seq_devices, shard_count, tokens_flat, cot_flat, norm_gain[None], weights_one, output_weight
+    )
+    proj = project(normed_one, full_one)
     shape4 = (seq_count, local_len, head_count, -1)
-    query_proj = project(normed_one, full_query).astype(bf16).reshape(shape4)
-    key_proj = project(normed_one, full_key).astype(bf16).reshape(shape4)
-    value_proj = project(normed_one, full_value).astype(bf16).reshape(shape4)
-    gate_proj = project(normed_one, full_outgate).reshape(shape4)
-    beta_proj = project(normed_one, full_beta).reshape(shape4)
-    decay_proj = project(normed_one, full_decay).reshape(shape4)
+    part = lambda i: proj[:, edges[i] : edges[i + 1]].reshape(shape4)
+    query_proj, key_proj, value_proj = (part(i).astype(bf16) for i in range(3))
+    gate_proj, beta_proj, decay_proj = (part(i) for i in range(3, 6))
+    all_taps = full_one[:, edges[6] : filled].reshape(seq_devices, -1, tap_count)
+    count_q, count_v = query_conv.shape[0], value_conv.shape[0]
+    full_qconv = all_taps[:, :count_q].reshape(-1, tap_count)
+    full_kconv = all_taps[:, count_q : 2 * count_q].reshape(-1, tap_count)
+    full_vconv = all_taps[:, 2 * count_q : tap_rows].reshape(-1, tap_count)
 
     u = to_pairs(jnp.concatenate([query_proj, key_proj, value_proj], axis=3))
     rates = to_pairs(jnp.concatenate([beta_proj, decay_proj], axis=3)).reshape(spans, SPAN, 2)
@@ -380,42 +666,35 @@
     gate_sig = jax.nn.sigmoid(gate_proj)
     gate_silu = gate_proj * gate_sig
     z = o * rho
-    branch = (z * head_gain * gate_silu).astype(bf16).reshape(row_count, head_count * value_dim)
-    attn_rows = summed_rows(project(branch, full_output).reshape(seq_count, local_len, model_dim))
-    residual = tokens_local + attn_rows
-    local_ffn_gain = lax.dynamic_slice_in_dim(ffn_gain, feature_start, feature_part)
-    local_norm_gain = lax.dynamic_slice_in_dim(norm_gain, feature_start, feature_part)
-    scale_two = lax.rsqrt(row_total(jnp.sum(residual * residual, axis=2)) / model_dim + EPSILON)[:, :, None]
-    normed_two = whole_rows((residual * scale_two * local_ffn_gain).astype(bf16)).reshape(row_count, model_dim)
+    branch = (z * head_gain * gate_silu).astype(bf16).reshape(row_count, width_v)
+    attn_part = project(branch, full_output).astype(bf16)
+    residual, scale_two, normed_two, full_gate, full_up, full_down, normed_one_cols = attn_out(
+        seq_devices, shard_count, attn_part, tokens_flat, local_ffn_gain, gate_weight, up_weight, down_weight, normed_one
+    )
     gate_vals = project(normed_two, full_gate)
     up_vals = project(normed_two, full_up)
     sigmoid_gate = jax.nn.sigmoid(gate_vals)
     gate_act = gate_vals * sigmoid_gate
     hidden = (gate_act * up_vals).astype(bf16)
-    output = residual + summed_rows(project(hidden, full_down).reshape(seq_count, local_len, model_dim))
-
-    def scattered(grad, axis):
-        return lax.psum_scatter(grad.astype(bf16), "seq", scatter_dimension=axis, tiled=True).astype(f32)
-
-    cot_rows = whole_rows(cotangent).reshape(row_count, model_dim)
-    grad_hidden = jnp.einsum("rd,fd->rf", cot_rows, full_down, preferred_element_type=f32)
-    out_down = scattered(jnp.einsum("rf,rd->fd", hidden, cot_rows, preferred_element_type=f32), 1)
+    out_part = project(hidden, full_down).astype(bf16)
+
+    def back(cols, weight):
+        return jnp.einsum("rc,dc->rd", cols, weight, preferred_element_type=f32)
+
+    def grad(left, right):
+        return jnp.einsum("rd,rc->dc", left, right, preferred_element_type=f32)
+
+    grad_hidden = back(cot_rows, full_down)
     grad_gate_vals = (grad_hidden * up_vals * sigmoid_gate * (1.0 + gate_vals * (1.0 - sigmoid_gate))).astype(bf16)
     grad_up_vals = (grad_hidden * gate_act).astype(bf16)
-    out_gate = scattered(jnp.einsum("rd,rf->df", normed_two, grad_gate_vals, preferred_element_type=f32), 0)
-    out_up = scattered(jnp.einsum("rd,rf->df", normed_two, grad_up_vals, preferred_element_type=f32), 0)
-    grad_normed_two = jnp.einsum("rf,df->rd", grad_gate_vals, full_gate, preferred_element_type=f32) + jnp.einsum(
-        "rf,df->rd", grad_up_vals, full_up, preferred_element_type=f32
-    )
-    grad_two = summed_rows(grad_normed_two.reshape(seq_count, local_len, model_dim))
-    gained_two = local_ffn_gain * grad_two
-    inner_two = row_total(jnp.sum(gained_two * residual, axis=2))[:, :, None] / model_dim
-    grad_residual = cotangent.astype(f32) + scale_two * (gained_two - residual * scale_two * scale_two * inner_two)
-    grad_ffn_part = jnp.sum(grad_two * residual * scale_two, axis=(0, 1))
-    attn_cot = whole_rows(grad_residual.astype(bf16)).reshape(row_count, model_dim)
-    out_output = scattered(jnp.einsum("rv,rd->vd", branch, attn_cot, preferred_element_type=f32), 1)
+    two_part = (back(grad_gate_vals, full_gate) + back(grad_up_vals, full_up)).astype(bf16)
+    grad_residual, attn_cot, grad_ffn_part, dgate_all, dup_all, hidden_all, branch_all, normed_two_cols = ffn_back(
+        seq_devices, shard_count, two_part, residual, scale_two, cot_flat, local_ffn_gain,
+        grad_gate_vals, grad_up_vals, hidden, branch, normed_two,
+    )
+    out_gate, out_up = grad(normed_two_cols, dgate_all), grad(normed_two_cols, dup_all)
     grad_mixed = (
-        jnp.einsum("rd,vd->rv", attn_cot, full_output, preferred_element_type=f32).astype(bf16).astype(f32).reshape(shape4)
+        back(attn_cot, full_output).astype(bf16).astype(f32).reshape(shape4)
     )
     grad_head_gain = jnp.sum(grad_mixed * z * gate_silu, axis=(0, 1, 2))
     dz = grad_mixed * head_gain * gate_silu
@@ -434,59 +713,53 @@
     grad_beta_proj = drates[..., 0].reshape(row_count, head_count)
     grad_decay_proj = drates[..., 1].reshape(row_count, head_count)
 
-    def weight_grad(grad_cols):
-        return scattered(jnp.einsum("rd,rc->dc", normed_one, grad_cols, preferred_element_type=f32), 0)
-
-    def input_grad(grad_cols, weight_full):
-        return jnp.einsum("rc,dc->rd", grad_cols, weight_full, preferred_element_type=f32)
-
-    grad_normed_one = (
-        input_grad(grad_qproj, full_query)
-        + input_grad(grad_kproj, full_key)
-        + input_grad(grad_vproj, full_value)
-        + input_grad(grad_gate_proj, full_outgate)
-        + input_grad(grad_beta_proj, full_beta)
-        + input_grad(grad_decay_proj, full_decay)
-    )
-    grad_one = summed_rows(grad_normed_one.reshape(seq_count, local_len, model_dim))
-    gained_one = local_norm_gain * grad_one
-    inner_one = row_total(jnp.sum(gained_one * tokens_local, axis=2))[:, :, None] / model_dim
-    grad_tokens = grad_residual + scale_one * (gained_one - tokens_local * scale_one * scale_one * inner_one)
-    grad_norm_part = jnp.sum(grad_one * tokens_local * scale_one, axis=(0, 1))
-
-    small = dtaps
-    tap_all = lax.all_gather(small, "seq")[::copies].reshape(seq_count, head_count, tap_count, channels)
-    tap_sum = jnp.sum(tap_all, axis=0)
-
-    def own_rows(part):
-        rows = jnp.swapaxes(part, 1, 2).reshape(-1, tap_count)
+    grad_one = jnp.concatenate(
+        [
+            grad_qproj, grad_kproj, grad_vproj, grad_gate_proj, grad_beta_proj, grad_decay_proj,
+            jnp.zeros((row_count, tap_count + padding), bf16),
+        ],
+        axis=1,
+    )
+    one_part = back(grad_one, full_one).astype(bf16)
+    primary = jnp.where(seq_pos % copies == 0, 1.0, 0.0)
+    total_heads = decay_log.shape[0]
+    width_s = max(feature_part, channels)
+    widen = lambda x: jnp.pad(x, ((0, 0), (0, width_s - x.shape[1])))
+    heads_row = lax.dynamic_update_slice(
+        lax.dynamic_update_slice(jnp.zeros((1, width_s), f32), dhead[0:1, :1] * primary, (0, at_head)),
+        dhead[1:2, :1] * primary,
+        (0, total_heads + at_head),
+    )
+    small = jnp.concatenate(
+        [jnp.zeros((1, width_s), f32), widen(grad_ffn_part[:1]), widen(grad_head_gain[None]), heads_row, widen(dtaps)], axis=0
+    )
+    output, grad_tokens, one_all, cot_cols, attn_cols, smalls, totals = tail(
+        seq_devices, shard_count, one_part, out_part, residual, grad_residual, tokens_flat, scale_one,
+        local_norm_gain, small, grad_one, cot_rows, attn_cot,
+    )
+    outs_one = [grad(normed_one_cols, one_all[:, edges[i] : edges[i + 1]]) for i in range(6)]
+    out_down = grad(hidden_all, cot_cols)
+    out_output = grad(branch_all, attn_cols)
+    tap_sum = jnp.sum(smalls[::copies, 4:].reshape(seq_count, head_count, tap_count, width_s), axis=0)
+
+    def own_rows(taps_part):
+        rows = jnp.swapaxes(taps_part, 1, 2).reshape(-1, tap_count)
         count = rows.shape[0] // seq_devices
         return lax.dynamic_slice_in_dim(rows, seq_pos * count, count)
 
     out_qconv = own_rows(tap_sum[:, :, :key_dim])
     out_kconv = own_rows(tap_sum[:, :, key_dim : 2 * key_dim])
-    out_vconv = own_rows(tap_sum[:, :, 2 * key_dim :])
-
-    def place_into(full_length, part_vals, start_at):
-        return lax.dynamic_update_slice(jnp.zeros((full_length,), f32), part_vals, (start_at,))
-
-    total_heads = decay_log.shape[0]
-    primary = jnp.where(seq_pos % copies == 0, 1.0, 0.0)
-    small_sums = lax.psum(
-        (
-            place_into(model_dim, grad_norm_part, feature_start),
-            place_into(model_dim, grad_ffn_part, feature_start),
-            grad_head_gain,
-            place_into(total_heads, dhead[0, :1] * primary, at_head),
-            place_into(total_heads, dhead[1, :1] * primary, at_head),
-        ),
-        ("seq", "shard"),
-    )
+    out_vconv = own_rows(tap_sum[:, :, 2 * key_dim : channels])
+    out_norm = totals[:, 0, :feature_part].reshape(-1)
+    out_ffn = totals[:, 1, :feature_part].reshape(-1)
+    totals_all = jnp.sum(totals, axis=0)
+    out_head = totals_all[2, :value_dim]
+    out_log = totals_all[3, :total_heads]
+    out_bias = totals_all[3, total_heads : 2 * total_heads]
+    shape3 = (seq_count, local_len, feature_part)
     return (
-        output, grad_tokens, small_sums[0], weight_grad(grad_qproj), weight_grad(grad_kproj),
-        weight_grad(grad_vproj), weight_grad(grad_gate_proj), weight_grad(grad_beta_proj),
-        weight_grad(grad_decay_proj), out_qconv, out_kconv, out_vconv, small_sums[3], small_sums[4],
-        small_sums[2], out_output, small_sums[1], out_gate, out_up, out_down,
+        output.reshape(shape3), grad_tokens.reshape(shape3), out_norm, *outs_one, out_qconv, out_kconv, out_vconv,
+        out_log, out_bias, out_head, out_output, out_ffn, out_gate, out_up, out_down,
     )
 
 

time: 1230 us -> 633 us (0.51)
  waiting for transfers between devices: 787 us -> 27.4 us
  Pallas kernels: 75.6 us -> 443 us
  blocking collectives: 157 us -> 0 us
  other arithmetic: 37.9 us -> 7.66 us
  between operations: 15.2 us -> 1.64 us
  matrix products: 92.2 us -> 79.2 us
    reduce_scatter x12 -> x0, waiting for transfers between devices: 482 us -> none  [the longest x8 401 us: scattered(): lax.psum_scatter(grad.astype(bf16), 'seq', scatter_dimension=axis, tiled=...]
    pallas_call x0 -> x4, Pallas kernels: none -> 368 us  [call(): pl.pallas_call(kernel, name=name, out_shape=tuple(outs), in_specs=specs,...]
    all_gather x12 -> x0, waiting for transfers between devices: 290 us -> none  [the longest x4 90.8 us: whole_rows(): return lax.all_gather(part_rows, 'shard', axis=2, tiled=True)]
    psum x4 -> x0, blocking collectives: 68.4 us -> none  [the longest x1 40 us: per_device(): lax.psum((place_into(model_dim, grad_norm_part, feature_start), place_int...]
    all_gather x6 -> x0, blocking collectives: 68.1 us -> none  [the longest x5 59.8 us: per_device(): lax.all_gather(w, 'seq', axis=0, tiled=True)]
    convert_element_type x14 -> x2, other arithmetic: 24.9 us -> 1.99 us  [the longest x1 1.59 us: per_device(): (grad_mixed * z * head_gain * gate_sig * (1.0 + gate_proj * (1.0 - gate_s...]
    all_to_all x2 -> x0, blocking collectives: 20.3 us -> none  [the longest x1 13.3 us: to_pairs(): y = lax.all_to_all(y, 'seq', 0, 0)]
    all_to_all x2 -> x3, waiting for transfers between devices: 0.01 us -> 18.4 us  [to_pairs(): y = lax.all_to_all(y, 'seq', 0, 0)]
  transfers between devices with their start and end apart: 30 -> 6, of which waited for: 24 -> 5; matrix products, arithmetic and copies ran while one was open for 10% -> 5% of each run, Pallas kernels for 3% -> 0%
where the time goes in v2:
time: 633 us; the launch traced here: 625 us
  Pallas kernels  443 us (70%)
  matrix products  79.2 us (13%)
  local copies, waits for them, and re-layouts  43.8 us (7%)
  waiting for transfers between devices  27.4 us (4%)
  starting transfers between devices  22 us (3%)
  other arithmetic  7.66 us (1%)
    pallas_call x4, Pallas kernels, call(): pl.pallas_call(kernel, name=name, out_shape=tuple(outs), in_specs=specs,...  368 us
    pallas_call x1, Pallas kernels, forward(): pl.pallas_call(forward_kernel, name='rec_fwd', out_shape=(S((L, DV), bf16...  42 us
    pallas_call x1, Pallas kernels, backward(): pl.pallas_call(backward_kernel, name='rec_bwd', out_shape=(S((L, CH), bf1...  33.6 us
    dot_general x10, matrix products, grad(): return jnp.einsum('rd,rc->dc', left, right, preferred_element_type=f32)  33.2 us
    dot_general x5, matrix products, project(): return jnp.dot(a, b, preferred_element_type=f32)  23.2 us
    dot_general x5, matrix products, back(): return jnp.einsum('rc,dc->rd', cols, weight, preferred_element_type=f32)  22.8 us
    all_to_all x3, waiting for transfers between devices, to_pairs(): y = lax.all_to_all(y, 'seq', 0, 0)  18.4 us
  transfers between devices with their start and end apart: 6, of which 5 were waited for; matrix products, arithmetic and copies ran while one was open for 5% of the time, Pallas kernels for 0%

profile of v2, /device:TPU:0, one launch (start us, length us, event | category | flops | bytes accessed | tf_op | source)
XLA Modules:
  0.0 624.8 jit_solution(13316819207505072938)
XLA Ops:
  0.7 0.8 pad_maximum_fusion.1
  1.6 0.8 copy.80
  2.4 0.8 copy.81
  3.3 3.8 concatenate.25.w
  7.1 81.3 %front.1 = (bf16[256,2048]{1,0:T(8,128)(2,1)}, f32[256,128]{1,0:T(8,128)}, bf16[256,2048]{1,0:T(8,128)(2,1)}, bf16[2048,3200]{1,0:T(8,128)(2,1)}, bf16[1024,2048]{1,0:T(8,128)(2,1)}) custom-call(bf16[256,512]{1,0:T(8,128)(2,1)} %bitcast.160, bf16[256,512]{1,0:T(8,128)(2,1)} %bitcast.179, f32[1,2048]{1,0:T(1,128)} %bitcast.200, ...), custom_call_target="tpu_custom_call" | custom-call | tf_op jit(solution)/shard_map/front/pallas_call | solution.py:547
  88.3 7.5 %fusion.37 = (bf16[256,3200]{1,0:T(8,128)(2,1)S(1)}, f32[256,3200]{1,0:T(8,128)S(1)}) fusion(bf16[256,2048]{1,0:T(8,128)(2,1)} %get-tuple-element.61.n1, bf16[2048,3200]{1,0:T(8,128)(2,1)} %get-tuple-element.62), kind=kOutput, calls=%fused_computation.72 | convolution fusion | flops 3356262400 | bytes 19070976 | tf_op jit(solution)/shard_map/dot_general | solution.py:604
  95.8 1.6 copy-done.12
  98.4 3.3 all-to-all-start.1
  102.9 1.2 copy.82
  104.0 2.3 all-to-all-done.1
  106.3 3.6 all-to-all-start
  109.9 1.2 slice.105
  112.8 1.9 pad_maximum_fusion.2.hp
  116.5 1.0 copy.91.xc_ref
  117.5 7.7 %all-to-all-done = bf16[8,128,512]{2,1,0:T(8,128)(2,1)S(1)} async-done(((bf16[8,128,512]{2,1,0:T(8,128)(2,1)}), bf16[8,128,512]{2,1,0:T(8,128)(2,1)S(1)}, u32[]{:S(2)}, u32[]{:S(2)}) %all-to-all-start) | async-done | bytes 1048608 | tf_op jit(solution)/shard_map/all_to_all | solution.py:609
  125.2 1.0 copy-done.3
  126.2 42.0 %rec_fwd.1 = (bf16[1024,256]{1,0:T(8,128)(2,1)}, bf16[1024,128]{1,0:T(8,128)(2,1)}, bf16[1024,128]{1,0:T(8,128)(2,1)}, bf16[1024,256]{1,0:T(8,128)(2,1)}, f32[16...) custom-call(bf16[1024,512]{1,0:T(8,128)(2,1)} %bitcast.158, ...), custom_call_target="tpu_custom_call" | custom-call | tf_op jit(solution)/shard_map/rec_fwd/pallas_call | solution.py:268
  168.2 4.0 all-to-all-start.2
  172.2 1.3 slice.143
  174.0 1.3 dynamic_slice.40
  175.3 6.5 %all-to-all-done.2 = bf16[8,128,256]{2,1,0:T(8,128)(2,1)S(1)} async-done(((bf16[8,128,256]{2,1,0:T(8,128)(2,1)}), bf16[8,128,256]{2,1,0:T(8,128)(2,1)S(1)}, u32[]{:S(2)}, u32[]{:S(2)}) %all-to-all-start.2) | async-done | bytes 524320 | tf_op jit(solution)/shard_map/all_to_all | solution.py:614
  183.0 1.2 copy-done.19
  184.2 2.2 convolution_convert_fusion.part
  186.5 89.5 %attn_out.1 = (f32[256,512]{1,0:T(8,128)}, f32[256,128]{1,0:T(8,128)}, bf16[256,2048]{1,0:T(8,128)(2,1)}, bf16[2048,1408]{1,0:T(8,128)(2,1)}, bf16[2048,1408]{1,...) custom-call(bf16[256,2048]{1,0:T(8,128)(2,1)} %convolution_convert_fusion.part, ...), custom_call_target="tpu_custom_call" | custom-call | tf_op jit(solution)/shard_map/attn_out/pallas_call | solution.py:547
  276.0 4.6 fusion.38
  280.6 4.6 fusion.39
  285.3 3.1 multiply_convert_fusion
  288.4 1.8 fusion.40
  290.3 2.9 fusion.4.part
  293.1 107.6 %ffn_back.1 = (f32[256,512]{1,0:T(8,128)}, bf16[256,2048]{1,0:T(8,128)(2,1)}, f32[8,512]{1,0:T(8,128)}, bf16[2048,1408]{1,0:T(8,128)(2,1)}, bf16[2048,1408]{1,0:...) custom-call(bf16[256,2048]{1,0:T(8,128)(2,1)} %fusion.4.part, ...), custom_call_target="tpu_custom_call" | custom-call | tf_op jit(solution)/shard_map/ffn_back/pallas_call | solution.py:547
  400.7 3.5 fusion.10
  404.2 1.7 reshape.173
  406.7 1.6 multiply_convert_fusion.3
  408.3 3.5 all-to-all-start.3
  411.8 1.3 dynamic_slice.41
  413.1 8.3 %all-to-all-done.3 = bf16[8,128,256]{2,1,0:T(8,128)(2,1)S(1)} async-done(((bf16[8,128,256]{2,1,0:T(8,128)(2,1)}), bf16[8,128,256]{2,1,0:T(8,128)(2,1)S(1)}, u32[]{:S(2)}, u32[]{:S(2)}) %all-to-all-start.3) | async-done | bytes 524320 | tf_op jit(solution)/shard_map/all_to_all | solution.py:609
  421.5 0.8 copy-done.6
  422.3 33.6 %rec_bwd.1 = (bf16[1024,512]{1,0:T(8,128)(2,1)}, f32[4,512]{1,0:T(4,128)}, f32[16,64,2]{2,1,0:T(8,128)}, f32[2,128]{1,0:T(2,128)}) custom-call(bf16[1024,256]{1,0:T(8,128)(2,1)} %bitcast.163, bf16[1024,512]{1,0:T(8,128)(2,1)} %bitcast.159, f32[4,512]{1,0:T(4,128)} %convert_bitcast_fusion.1.taps_ref, f32[16,64,2]{2,1,0:T(8,128)} %copy.91.xc_ref, ...), custom_call_target="tpu_custom_call" | custom-call | tf_op jit(solution)/shard_map/rec_bwd/pallas_call | solution.py:276
  455.9 1.8 copy.103
  457.7 3.3 all-to-all-start.5
  461.0 5.6 fusion.42
  466.6 4.4 all-to-all-start.4
  471.0 5.8 convolution_convert_fusion.1.partout
  478.0 2.9 fusion.43
  482.2 0.8 dynamic_update_slice.7
  483.9 2.5 all-to-all-done.4
  486.4 1.1 slice.146
  487.5 1.1 fusion.32
  490.3 2.2 concatenate.30.dy
  492.6 10.0 %convolution_convert_fusion.2.partdx = bf16[256,2048]{1,0:T(8,128)(2,1)} fusion(bf16[256,3200]{1,0:T(8,128)(2,1)S(1)} %concatenate.30.dy, bf16[2048,3200]{1,0:T(8,128)(2,1)} %get-tuple-element.62), kind=kOutput, calls=%fused_computation.8 | convolution fusion | flops 3355967488 | bytes 15794176 | tf_op jit(solution)/shard_map/rc,dc->rd/dot_general | solution.py:682
  502.6 89.2 %tail.1 = (f32[256,512]{1,0:T(8,128)}, f32[256,512]{1,0:T(8,128)}, bf16[2048,3200]{1,0:T(8,128)(2,1)}, bf16[2048,256]{1,0:T(8,128)(2,1)}, bf16[2048,256]{1,0:T(8...) custom-call(bf16[256,2048]{1,0:T(8,128)(2,1)} %convolution_convert_fusion.2.partdx, ...), custom_call_target="tpu_custom_call" | custom-call | tf_op jit(solution)/shard_map/tail/pallas_call | solution.py:547
  591.8 2.3 fusion.25
  594.1 2.0 fusion.27
  596.0 1.5 fusion.34
  597.6 0.8 reduce_sum.49
  599.6 0.9 slice.127
  600.5 3.1 fusion.5
  603.7 3.1 fusion.7
  606.8 4.6 fusion
  611.3 4.6 fusion.2
  617.3 2.8 fusion.44
  620.1 2.3 fusion.41
  623.0 0.8 copy.154
  623.8 0.8 copy.155
  (133 shorter events, 16.1 us)
Async XLA Ops:
  0.7 114.0 %copy-start = (s32[2,16]{1,0:T(2,128)S(1)}, s32[2,16]{1,0:T(2,128)}, u32[]{:S(2)}) copy-start(s32[2,16]{1,0:T(2,128)} %param.22) | copy-start | bytes 388
  95.8 1.7 copy-start.12
  98.4 8.0 %all-to-all-start.1 = ((f32[8,128,2]{1,2,0:T(2,128)}), f32[8,128,2]{1,2,0:T(2,128)S(1)}, u32[]{:S(2)}, u32[]{:S(2)}) async-start(f32[8,128,2]{1,2,0:T(2,128)} %copy.88), calls=%async_computation.1 | async-start | bytes 16384 | tf_op jit(solution)/shard_map/all_to_all | solution.py:609
  102.3 8.9 %copy-start.24 = (f32[16]{0:T(128)S(1)}, f32[16]{0:T(128)}, u32[]{:S(2)}) copy-start(f32[16]{0:T(128)} %param.34) | copy-start | bytes 196
  102.3 9.5 %copy-start.25 = (f32[16]{0:T(128)S(1)}, f32[16]{0:T(128)}, u32[]{:S(2)}) copy-start(f32[16]{0:T(128)} %param.33) | copy-start | bytes 196
  106.3 18.9 %all-to-all-start = ((bf16[8,128,512]{2,1,0:T(8,128)(2,1)}), bf16[8,128,512]{2,1,0:T(8,128)(2,1)S(1)}, u32[]{:S(2)}, u32[]{:S(2)}) async-start(bf16[8,128,512]{2,1,0:T(8,128)(2,1)} %bitcast.4), calls=%async_computation | async-start | bytes 2097152 | tf_op jit(solution)/shard_map/all_to_all | solution.py:609
  112.4 69.6 %copy-start.16 = (f32[256]{0:T(256)S(1)}, f32[256]{0:T(256)}, u32[]{:S(2)}) copy-start(f32[256]{0:T(256)} %param.35) | copy-start | bytes 3076
  125.2 1.0 copy-start.3
  168.2 13.6 %all-to-all-start.2 = ((bf16[8,128,256]{2,1,0:T(8,128)(2,1)}), bf16[8,128,256]{2,1,0:T(8,128)(2,1)S(1)}, u32[]{:S(2)}, u32[]{:S(2)}) async-start(bf16[8,128,256]{2,1,0:T(8,128)(2,1)} %bitcast.183), calls=%async_computation.2 | async-start | bytes 1048576 | tf_op jit(solution)/shard_map/all_to_all | solution.py:614
  181.8 2.4 copy-start.19
  183.0 93.0 %copy-start.7 = (bf16[32,8,4,256]{3,1,2,0:T(8,128)(2,1)}, bf16[32,8,4,256]{3,1,2,0:T(8,128)(2,1)S(1)}, u32[]{:S(2)}) copy-start(bf16[32,8,4,256]{3,1,2,0:T(8,128)(2,1)S(1)} %copy.116) | copy-start | bytes 1572868
  184.2 91.8 %copy-start.8 = (bf16[256,2048]{1,0:T(8,128)(2,1)S(1)}, bf16[256,2048]{1,0:T(8,128)(2,1)}, u32[]{:S(2)}) copy-start(bf16[256,2048]{1,0:T(8,128)(2,1)} %get-tuple-element.64.cot) | copy-start | bytes 3145732
  276.0 4.6 copy-start.9
  276.0 9.3 %slice-start.5 = ((s8[5767168]{0:T(1024)(128)(4,1)}), s8[4194304]{0:T(1024)(128)(4,1)S(1)}, s32[]{:S(2)}) async-start(s8[5767168]{0:T(1024)(128)(4,1)} %bitcast.208), calls=%async_computation.11 | async-start | bytes 8388608
  280.6 4.7 slice-start.6
  280.6 7.8 %slice-start.7 = ((s8[5767168]{0:T(1024)(128)(4,1)}), s8[4194304]{0:T(1024)(128)(4,1)S(1)}, s32[]{:S(2)}) async-start(s8[5767168]{0:T(1024)(128)(4,1)} %bitcast.210), calls=%async_computation.13 | async-start | bytes 8388608
  285.3 3.1 slice-start.8
  288.4 1.9 copy-start.10
  288.4 1.9 copy-start.11
  293.1 107.6 %copy-start.20 = (bf16[1024,2048]{1,0:T(8,128)(2,1)S(1)}, bf16[1024,2048]{1,0:T(8,128)(2,1)}, u32[]{:S(2)}) copy-start(bf16[1024,2048]{1,0:T(8,128)(2,1)} %get-tuple-element.65) | copy-start | bytes 12582916
  408.3 13.2 %all-to-all-start.3 = ((bf16[8,128,256]{2,1,0:T(8,128)(2,1)}), bf16[8,128,256]{2,1,0:T(8,128)(2,1)S(1)}, u32[]{:S(2)}, u32[]{:S(2)}) async-start(bf16[8,128,256]{2,1,0:T(8,128)(2,1)} %bitcast.170), calls=%async_computation.3 | async-start | bytes 1048576 | tf_op jit(solution)/shard_map/all_to_all | solution.py:609
  421.5 0.8 copy-start.6
  422.3 38.7 %copy-start.2 = (bf16[2048,256]{1,0:T(8,128)(2,1)S(1)}, bf16[2048,256]{1,0:T(8,128)(2,1)}, u32[]{:S(2)}) copy-start(bf16[2048,256]{1,0:T(8,128)(2,1)} %get-tuple-element.97) | copy-start | bytes 3145732
  457.7 8.9 %all-to-all-start.5 = ((bf16[8,128,2]{1,2,0:T(2,128)(2,1)}), bf16[8,128,2]{1,2,0:T(2,128)(2,1)S(1)}, u32[]{:S(2)}, u32[]{:S(2)}) async-start(bf16[8,128,2]{1,2,0:T(2,128)(2,1)} %copy.103), calls=%async_computation.5 | async-start | bytes 8192 | tf_op jit(solution)/shard_map/all_to_all | solution.py:614
  466.6 11.4 %slice-start = ((s8[5767168]{0:T(1024)(128)(4,1)}), s8[1572864]{0:T(1024)(128)(4,1)S(1)}, s32[]{:S(2)}) async-start(s8[5767168]{0:T(1024)(128)(4,1)} %bitcast.154), calls=%async_computation.6 | async-start | bytes 3145728
  466.6 19.8 %all-to-all-start.4 = ((bf16[8,128,512]{2,1,0:T(8,128)(2,1)}), bf16[8,128,512]{2,1,0:T(8,128)(2,1)}, u32[]{:S(2)}, u32[]{:S(2)}) async-start(bf16[8,128,512]{2,1,0:T(8,128)(2,1)} %bitcast.174), calls=%async_computation.4 | async-start | bytes 2097152 | tf_op jit(solution)/shard_map/all_to_all | solution.py:614
  471.0 7.0 %slice-start.1 = ((s8[5767168]{0:T(1024)(128)(4,1)}), s8[4194304]{0:T(1024)(128)(4,1)S(1)}, s32[]{:S(2)}) async-start(s8[5767168]{0:T(1024)(128)(4,1)} %bitcast.154), calls=%async_computation.7 | async-start | bytes 8388608
  478.0 3.0 copy-start.18
  478.0 4.9 copy-start.17
  492.5 10.0 %copy-start.4 = (bf16[256,3200]{1,0:T(8,128)(2,1)}, bf16[256,3200]{1,0:T(8,128)(2,1)S(1)}, u32[]{:S(2)}) copy-start(bf16[256,3200]{1,0:T(8,128)(2,1)S(1)} %concatenate.30.dy) | copy-start | bytes 4915204
  502.6 89.2 %copy-start.5 = (bf16[2048,256]{1,0:T(8,128)(2,1)S(1)}, bf16[2048,256]{1,0:T(8,128)(2,1)}, u32[]{:S(2)}) copy-start(bf16[2048,256]{1,0:T(8,128)(2,1)} %get-tuple-element.92) | copy-start | bytes 3145732
  600.5 6.2 %copy-start.15 = (f32[4,4,512]{2,1,0:T(4,128)}, f32[4,4,512]{2,1,0:T(4,128)S(1)}, u32[]{:S(2)}) copy-start(f32[4,4,512]{2,1,0:T(4,128)S(1)} %reduce_sum.48) | copy-start | bytes 98308
  606.8 10.5 %slice-start.3 = ((s8[5767168]{0:T(1024)(128)(4,1)}), s8[4194304]{0:T(1024)(128)(4,1)S(1)}, s32[]{:S(2)}) async-start(s8[5767168]{0:T(1024)(128)(4,1)} %bitcast.206), calls=%async_computation.9 | async-start | bytes 8388608
  611.3 5.9 slice-start.4
  611.3 5.9 copy-start.23
  617.2 2.9 copy-start.21
  617.2 2.9 copy-start.22
  620.1 4.5 copy-start.1
  620.1 2.3 slice-start.2
  620.1 2.9 copy-start.14
  620.1 3.6 copy-start.13

commit v3 on v2

--- a/solution.py
+++ b/solution.py
@@ -69,7 +69,7 @@
     lower=jnp.where(i>=j,1.0,0.0); upper=jnp.where(i<=j,1.0,0.0)
     beta=sigmoid(xc[:,0:1])
     g=-rate*softplus(xc[:,1:2]+bias)
-    gr=-rate*softplus(xr[1:2]+bias)
+    gr=-rate*softplus(xr+bias)
     G=mmx(lower,jnp.broadcast_to(g,(SPAN,128)))
     Gr=mmx(jnp.broadcast_to(gr,(8,SPAN)),upper)[0:1]
     same=docs[:,:SPAN]==docr
@@ -88,10 +88,22 @@
         pre=pre+window[8-back:8-back+rows]*ok*taps[3-back:4-back]
     return pre
 
-def forward_kernel(u_ref,taps_ref,xc_ref,xr_ref,starts,hp,o_ref,q_ref,k_ref,v_ref,s_ref,w_ref,t_ref,qt_ref,mh_ref,ml_ref,upad,un_ref,gc_ref,on_ref):
-    L=u_ref.shape[0]; NC=L//SPAN; DV=v_ref.shape[1]; DK=q_ref.shape[1]
+def forward_kernel(n,copies,heads,proj,rows_in,taps_ref,starts,hp,wg,wo,n1,
+                   oall,u_ref,xr_ref,xc_ref,q_ref,k_ref,v_ref,s_ref,w_ref,t_ref,qt_ref,mh_ref,ml_ref,wgfull,wofull,n1c,
+                   upad,un_ref,gc_ref,on_ref,o_ref,is_,ir,os_,or_,es,er,*gs):
+    L=u_ref.shape[0]; NC=L//SPAN; DV=v_ref.shape[1]; DK=q_ref.shape[1]; local_len=L//n; per=local_len//SPAN
+    greet(n,1)
+    inward=ToPairs(n,copies,heads,local_len,proj,rows_in,u_ref,xr_ref,DK,DV,is_,ir); inward.start()
+    gw=gathers(n,[(wg,wgfull,0),(wo,wofull,1)],gs)
+    inward.finish()
+    each(gw,"start")
+    cols=ColumnSplit(n,n1,n1c,es,er); cols.start()
     rate=jnp.exp(jnp.full((1,1),hp[0],f32)); bias=hp[1]
     upad[0:8]=jnp.zeros((8,upad.shape[1]),f32)
+    def turn(m,_):
+        xc_ref[pl.ds(pl.multiple_of(m*local_len,local_len),local_len),:]=col_form(xr_ref[pl.ds(pl.multiple_of(m*8,8),8),:])
+        return 0
+    lax.fori_loop(0,n,turn,0,unroll=2)
     taps=taps_ref[...]
     R=128
     def load(c,_):
@@ -110,10 +122,10 @@
         v_ref[rows,:]=act[:,2*DK:].astype(bf16)
         return 0
     lax.fori_loop(0,L//R,conv,0)
-    def local(n,_):
+    def one_span(n,xr):
         rows=pl.ds(pl.multiple_of(n*SPAN,SPAN),SPAN)
         q=q_ref[rows,:]; k=k_ref[rows,:]; v=v_ref[rows,:]
-        beta,g,D,gam,end,KK,QK,i,j=span_terms(n,q,k,starts,xc_ref[n],xr_ref[n],rate,bias)
+        beta,g,D,gam,end,KK,QK,i,j=span_terms(n,q,k,starts,xc_ref[rows,:],xr,rate,bias)
         A=jnp.where(i>j,beta*D*KK,0.0)
         T=inverse(A)
         kf=k.astype(f32)
@@ -131,8 +143,12 @@
         mh,ml=halves(NM[:,DV:])
         mh_ref[n]=mh; ml_ref[n]=ml
         gc_ref[n]=jnp.broadcast_to(gam[SPAN-1:SPAN],(8,128))
-        return 0
-    lax.fori_loop(0,NC,local,0,unroll=4)
+    def local(m,_):
+        xr=xr_ref[pl.ds(pl.multiple_of(m*8,8),8),:]
+        for e in range(per): one_span(m*per+e,xr[1:2,e*SPAN:(e+1)*SPAN])
+        return 0
+    lax.fori_loop(0,n,local,0,unroll=2)
+    each(gw,"middle")
     def chain(n,S):
         s_ref[n]=S
         sh,sl=halves(S); mh=mh_ref[n]; ml=ml_ref[n]
@@ -146,10 +162,17 @@
         w_ref[n]=w_ref[n]-r[SPAN:]
         return 0
     lax.fori_loop(0,NC,emit,0,unroll=4)
-
-def backward_kernel(do_ref,u_ref,taps_ref,xc_ref,xr_ref,starts,hp,q_ref,k_ref,v_ref,s_ref,w_ref,t_ref,qt_ref,mh_ref,ml_ref,
-                    du_ref,dtaps_ref,dx_ref,dh_ref,upad,dpre,ds_ref,dqkv,r_ref,gc_ref):
-    L=u_ref.shape[0]; NC=L//SPAN; DV=v_ref.shape[1]; DK=q_ref.shape[1]
+    outward=FromPairs(n,copies,heads,local_len,[(o_ref,lambda t: (pl.ds(pl.multiple_of(t*local_len,local_len),local_len),slice(None)),
+        oall,lambda seq,head: (pl.ds(pl.multiple_of(seq*local_len,local_len),local_len),pl.ds(pl.multiple_of(head*DV,128),DV)))],os_,or_)
+    outward.start()
+    each(gw,"late"); outward.finish(); cols.finish(); each(gw,"finish")
+
+def backward_kernel(n,copies,heads,dall,u_ref,taps_ref,xc_ref,xr_ref,starts,hp,q_ref,k_ref,v_ref,s_ref,w_ref,t_ref,qt_ref,mh_ref,ml_ref,hid,bra,dgp,
+                    duall,rows_out,dtaps_ref,dh_ref,hidfull,brafull,dgpfull,upad,dpre,ds_ref,dqkv,r_ref,gc_ref,do_ref,du_ref,dx_ref,dxr,is_,ir,os_,or_,*gs):
+    L=u_ref.shape[0]; NC=L//SPAN; DV=v_ref.shape[1]; DK=q_ref.shape[1]; local_len=L//n; per=local_len//SPAN
+    greet(n,1)
+    inward=ToPairs(n,copies,heads,local_len,dall,None,do_ref,None,DK,DV,is_,ir); inward.start()
+    gw=gathers(n,[(hid,hidfull,0),(bra,brafull,0),(dgp,dgpfull,0)],gs)
     rate=jnp.exp(jnp.full((1,1),hp[0],f32)); bias=hp[1]
     taps=taps_ref[...]
     R=128
@@ -159,11 +182,14 @@
         upad[pl.ds(pl.multiple_of(8+c*R,8),R),:]=u_ref[pl.ds(pl.multiple_of(c*R,R),R),:].astype(f32)
         return 0
     lax.fori_loop(0,L//R,load,0)
+    inward.finish()
+    each(gw,"start")
+    dx_ref[...]=jnp.zeros(dx_ref.shape,f32)
     def early(n,_):
         rows=pl.ds(pl.multiple_of(n*SPAN,SPAN),SPAN)
         r_ref[n]=dg(qt_ref[n][0:SPAN],do_ref[rows,:],0,0)
         base=n*SPAN
-        G=jnp.sum(-rate*softplus(xc_ref[n][:,1:2]+bias),axis=0,keepdims=True)
+        G=jnp.sum(-rate*softplus(xc_ref[rows,1:2]+bias),axis=0,keepdims=True)
         alive=jnp.where(count_at(starts,base+SPAN-1)==count_at(starts,base-1),1.0,0.0)
         gc_ref[n]=jnp.broadcast_to(jnp.exp(G)*alive,(8,128))
         return 0
@@ -175,11 +201,12 @@
         gc=gc_ref[n][0:1]
         return jnp.concatenate([gc]*(DV//128),axis=1)*dS+r_ref[n]-(dg(mh,sh,0,0)+(dg(ml,sh,0,0)+dg(mh,sl,0,0)))
     lax.fori_loop(0,NC,chain,jnp.zeros((DK,DV),f32),unroll=2)
-    def local(n,sums):
+    each(gw,"middle")
+    def one_span(n,xr,sums):
         rows=pl.ds(pl.multiple_of(n*SPAN,SPAN),SPAN)
         q=q_ref[rows,:]; k=k_ref[rows,:]; v=v_ref[rows,:]; dO=do_ref[rows,:]
-        xc=xc_ref[n]
-        beta,g,D,gam,end,KK,QK,i,j=span_terms(n,q,k,starts,xc,xr_ref[n],rate,bias)
+        xc=xc_ref[rows,:]
+        beta,g,D,gam,end,KK,QK,i,j=span_terms(n,q,k,starts,xc,xr,rate,bias)
         S0=s_ref[n]; dS1=ds_ref[n]
         S0h=S0.astype(bf16); dSh=dS1.astype(bf16)
         kf=k.astype(f32); qf=q.astype(f32); vf=v.astype(f32)
@@ -217,12 +244,20 @@
         dlog=mmx(upper,dG)
         dbp=(dbeta*beta*(1.0-beta))
         ddp=dlog*(-rate)*sigmoid(xc[:,1:2]+bias)
-        dx_ref[n,:,0:1]=dbp[:,0:1]
-        dx_ref[n,:,1:2]=ddp[:,0:1]
+        dx_ref[rows,0:1]=dbp[:,0:1]
+        dx_ref[rows,1:2]=ddp[:,0:1]
         sl,sb=sums
         return (sl+jnp.sum(dlog*g,axis=0,keepdims=True),sb+jnp.sum(ddp,axis=0,keepdims=True))
+    def local(m,sums):
+        xr=xr_ref[pl.ds(pl.multiple_of(m*8,8),8),:]
+        for e in range(per): sums=one_span(m*per+e,xr[1:2,e*SPAN:(e+1)*SPAN],sums)
+        return sums
     zero=jnp.zeros((1,128),f32)
-    sl,sb=lax.fori_loop(0,NC,local,(zero,zero),unroll=4)
+    sl,sb=lax.fori_loop(0,n,local,(zero,zero),unroll=2)
+    def turn(m,_):
+        dxr[pl.ds(pl.multiple_of(m*8,8),8),:]=flat_form(dx_ref[pl.ds(pl.multiple_of(m*local_len,local_len),local_len),:])
+        return 0
+    lax.fori_loop(0,n,turn,0,unroll=2)
     dh_ref[0:1]=sl; dh_ref[1:2]=sb
     def norms(c,dt):
         base=pl.multiple_of(c*R,R)
@@ -260,24 +295,34 @@
         du_ref[pl.ds(base,R),:]=d.astype(bf16)
         return 0
     lax.fori_loop(0,L//R,back,0)
+    wk=heads*DK
+    at=lambda start,width: (lambda t: (pl.ds(pl.multiple_of(t*local_len,local_len),local_len),pl.ds(start,width)))
+    to=lambda start,width: (lambda seq,head: (pl.ds(pl.multiple_of(seq*local_len,local_len),local_len),pl.ds(pl.multiple_of(start+head*width,128),width)))
+    outward=FromPairs(n,copies,heads,local_len,[(du_ref,at(0,DK),duall,to(0,DK)),(du_ref,at(DK,DK),duall,to(wk,DK)),(du_ref,at(2*DK,DV),duall,to(2*wk,DV)),
+        (dxr,lambda t: (pl.ds(pl.multiple_of(t*8,8),8),slice(None)),rows_out,lambda seq,head: (pl.ds(pl.multiple_of((seq*heads+head)*8,8),8),slice(None)))],os_,or_)
+    outward.start()
+    each(gw,"late"); outward.finish(); each(gw,"finish")
 
 SM=pl.BlockSpec(memory_space=pltpu.SMEM); VM=pl.BlockSpec(memory_space=pltpu.VMEM)
 def S(shape,dt=f32): return jax.ShapeDtypeStruct(shape,dt)
-def forward(u,taps,xc,xr,starts,hp,DK=128,DV=256):
-    L=u.shape[0]; NC=L//SPAN; CH=u.shape[1]
-    return pl.pallas_call(forward_kernel,name="rec_fwd",
-      out_shape=(S((L,DV),bf16),S((L,DK),bf16),S((L,DK),bf16),S((L,DV),bf16),S((NC,DK,DV)),S((NC,SPAN,DV)),S((NC,SPAN,SPAN)),S((NC,2*SPAN,DK),bf16),S((NC,DK,DK),bf16),S((NC,DK,DK),bf16)),
-      in_specs=[VM,VM,VM,VM,SM,SM],out_specs=(VM,)*10,
-      scratch_shapes=[pltpu.VMEM((L+8,CH),f32),pltpu.VMEM((NC,DK,DV),f32),pltpu.VMEM((NC,8,128),f32),pltpu.VMEM((NC,SPAN,DV),f32)],
-      compiler_params=pltpu.CompilerParams(vmem_limit_bytes=56*2**20))(u,taps,xc,xr,starts,hp)
-def backward(do,u,taps,xc,xr,starts,hp,saved):
-    q,k,v,s,w,t,qt,mh,ml=saved
-    L=u.shape[0]; NC=L//SPAN; CH=u.shape[1]; DK=q.shape[1]; DV=v.shape[1]
-    return pl.pallas_call(backward_kernel,name="rec_bwd",
-      out_shape=(S((L,CH),bf16),S((4,CH)),S((NC,SPAN,2)),S((2,128))),
-      in_specs=[VM]*5+[SM]*2+[VM]*9,out_specs=(VM,)*4,
-      scratch_shapes=[pltpu.VMEM((L+8,CH),f32),pltpu.VMEM((L+8,CH),f32),pltpu.VMEM((NC,DK,DV),f32),pltpu.VMEM((L,CH),f32),pltpu.VMEM((NC,DK,DV),f32),pltpu.VMEM((NC,8,128),f32)],
-      compiler_params=pltpu.CompilerParams(vmem_limit_bytes=56*2**20))(do,u,taps,xc,xr,starts,hp,q,k,v,s,w,t,qt,mh,ml)
+def forward(n,copies,heads,proj,rows_in,taps,starts,hp,wg,wo,n1,DK,DV):
+    R=proj.shape[0]; CH=taps.shape[1]; local_len=rows_in.shape[1]; L=n*local_len; NC=L//SPAN; pairs=rows_in.shape[0]//8
+    full=lambda a: S((a.shape[0]*n,a.shape[1]),bf16)
+    return call("rec_fwd",5,functools.partial(forward_kernel,n,copies,heads),(proj,rows_in,taps,starts,hp,wg,wo,n1),[ANY,ANY,VM,SM,SM,ANY,ANY,ANY],
+      [S((R,heads*DV),bf16),S((L,CH),bf16),S((n*8,local_len)),S((L,8)),S((L,DK),bf16),S((L,DK),bf16),S((L,DV),bf16),S((NC,DK,DV)),S((NC,SPAN,DV)),S((NC,SPAN,SPAN)),
+       S((NC,2*SPAN,DK),bf16),S((NC,DK,DK),bf16),S((NC,DK,DK),bf16),full(wg),S((wo.shape[0],wo.shape[1]*n),bf16),S((R*n,n1.shape[1]//n),bf16)],
+      [ANY]+[VM]*12+[ANY]*3,
+      [pltpu.VMEM((L+8,CH),f32),pltpu.VMEM((NC,DK,DV),f32),pltpu.VMEM((NC,8,128),f32),pltpu.VMEM((NC,SPAN,DV),f32),pltpu.VMEM((L,DV),bf16),
+       pltpu.SemaphoreType.DMA((4,n)),pltpu.SemaphoreType.DMA((4,n)),pltpu.SemaphoreType.DMA((1,pairs)),pltpu.SemaphoreType.DMA((1,pairs))]+pair_sems(n)+gather_sems(n,2))
+def backward(n,copies,heads,dall,taps,starts,hp,saved,hid,bra,dgp):
+    u,xr,xc,q,k,v,s,w,t,qt,mh,ml=saved
+    L,CH=u.shape; NC=L//SPAN; DK=q.shape[1]; DV=v.shape[1]; local_len=L//n; pairs=n//copies; R=dall.shape[0]
+    full=lambda a: S((a.shape[0]*n,a.shape[1]),bf16)
+    return call("rec_bwd",6,functools.partial(backward_kernel,n,copies,heads),(dall,u,taps,xc,xr,starts,hp,q,k,v,s,w,t,qt,mh,ml,hid,bra,dgp),[ANY]+[VM]*4+[SM]*2+[VM]*9+[ANY]*3,
+      [S((R,heads*CH),bf16),S((pairs*8,local_len)),S((4,CH)),S((2,128)),full(hid),full(bra),full(dgp)],[ANY,ANY,VM,VM,ANY,ANY,ANY],
+      [pltpu.VMEM((L+8,CH),f32),pltpu.VMEM((L+8,CH),f32),pltpu.VMEM((NC,DK,DV),f32),pltpu.VMEM((L,CH),f32),pltpu.VMEM((NC,DK,DV),f32),pltpu.VMEM((NC,8,128),f32),
+       pltpu.VMEM((L,DV),bf16),pltpu.VMEM((L,CH),bf16),pltpu.VMEM((L,8),f32),pltpu.VMEM((n*8,local_len),f32),
+       pltpu.SemaphoreType.DMA((4,n)),pltpu.SemaphoreType.DMA((4,n)),pltpu.SemaphoreType.DMA((4,pairs)),pltpu.SemaphoreType.DMA((4,pairs))]+gather_sems(n,3))
 
 
 MESH=pl.DeviceIdType.MESH
@@ -306,15 +351,15 @@
     return 8 if n==8 else n
 
 class SeqGather:
-    def __init__(self,n,src,dst,axis,sems,r0=0,nr=None):
+    def __init__(self,n,src,dst,axis,sems,c0=0):
         self.n=n; self.src=src; self.dst=dst; self.axis=axis; self.send,self.recv,self.loc=sems
         self.R,self.C=src.shape
-        self.r0=r0; self.nr=self.R if nr is None else nr
+        self.r0=0; self.nr=self.R; self.c0=c0
         self.s=lax.axis_index("seq")
         self.open=[]
     def slot(self,t,a,b):
         if self.axis==0:
-            return self.dst.at[pl.ds(pl.multiple_of(t*self.R+self.r0+a,16),b-a),:]
+            return self.dst.at[pl.ds(pl.multiple_of(t*self.R+self.r0+a,16),b-a),pl.ds(self.c0,self.C)]
         return self.dst.at[pl.ds(self.r0+a,b-a),pl.ds(pl.multiple_of(t*self.C,128),self.C)]
     def copy(self,src,t,a,b,k,to):
         c=pltpu.make_async_remote_copy(src_ref=src,dst_ref=self.slot(t,a,b),send_sem=self.send.at[k],recv_sem=self.recv.at[k],device_id={"seq":to},device_id_type=MESH)
@@ -417,6 +462,53 @@
         for c in self.cs: c.wait()
         self.own.wait()
 
+class ToPairs:
+    def __init__(self,n,copies,heads,local_len,src,rows_src,dst,rows_dst,DK,DV,send,recv):
+        self.__dict__.update(n=n,copies=copies,heads=heads,ll=local_len,src=src,rows_src=rows_src,dst=dst,rows_dst=rows_dst,DK=DK,DV=DV,send=send,recv=recv)
+    def parts(self,t):
+        s=lax.axis_index("seq"); ll,DK,DV,heads=self.ll,self.DK,self.DV,self.heads
+        pair=lax.div(t,self.copies); seq=lax.div(pair,heads); head=lax.rem(pair,heads)
+        rows=pl.ds(pl.multiple_of(seq*ll,ll),ll); to=pl.ds(pl.multiple_of(s*ll,ll),ll)
+        if self.rows_src is None:
+            return [(self.src.at[rows,pl.ds(pl.multiple_of(head*DV,128),DV)],self.dst.at[to,:])]
+        wk=heads*DK
+        out=[]
+        for start,width,at in ((0,DK,0),(wk,DK,DK),(2*wk,DV,2*DK)):
+            out.append((self.src.at[rows,pl.ds(pl.multiple_of(start+head*width,128),width)],self.dst.at[to,pl.ds(at,width)]))
+        out.append((self.rows_src.at[pl.ds(pl.multiple_of(pair*8,8),8),:],self.rows_dst.at[pl.ds(pl.multiple_of(s*8,8),8),:]))
+        return out
+    def start(self):
+        s=lax.axis_index("seq"); self.cs=[]
+        for d in range(self.n):
+            t=lax.rem(s+d,self.n)
+            for i,(a,b) in enumerate(self.parts(t)):
+                if d==0: c=pltpu.make_async_copy(a,b,self.recv.at[i,0])
+                else: c=pltpu.make_async_remote_copy(src_ref=a,dst_ref=b,send_sem=self.send.at[i,d],recv_sem=self.recv.at[i,d],device_id={"seq":t},device_id_type=MESH)
+                c.start(); self.cs.append(c)
+    def finish(self):
+        for c in self.cs: c.wait()
+
+class FromPairs:
+    def __init__(self,n,copies,heads,local_len,items,send,recv):
+        self.__dict__.update(n=n,copies=copies,heads=heads,items=items,send=send,recv=recv)
+    def start(self):
+        s=lax.axis_index("seq"); pairs=self.n//self.copies; p=lax.div(s,self.copies); r=lax.rem(s,self.copies)
+        seq=lax.div(p,self.heads); head=lax.rem(p,self.heads); self.cs=[]
+        for d in range(pairs):
+            t=lax.rem(p+d,pairs)*self.copies+r
+            for i,(src,at,dst,to) in enumerate(self.items):
+                a=src.at[at(t)]; b=dst.at[to(seq,head)]
+                if d==0: c=pltpu.make_async_copy(a,b,self.recv.at[i,0])
+                else: c=pltpu.make_async_remote_copy(src_ref=a,dst_ref=b,send_sem=self.send.at[i,d],recv_sem=self.recv.at[i,d],device_id={"seq":t},device_id_type=MESH)
+                c.start(); self.cs.append(c)
+    def finish(self):
+        for c in self.cs: c.wait()
+
+def flat_form(cols):
+    r=cols.shape[0]
+    i=lax.broadcasted_iota(jnp.int32,(r,r),0); j=lax.broadcasted_iota(jnp.int32,(r,r),1)
+    return mmx(cols,jnp.where(i==j,1.0,0.0),0,0)
+
 def row_form(cols):
     return mmx(jnp.ones((8,cols.shape[1]),f32),cols,1,1)
 
@@ -427,7 +519,7 @@
 
 def gathers(n,pairs,sems):
     send,recv,loc=sems
-    return [SeqGather(n,src,dst,axis,(send.at[i],recv.at[i],loc.at[i])) for i,(src,dst,axis) in enumerate(pairs)]
+    return [SeqGather(n,src,dst,axis,(send.at[i],recv.at[i],loc.at[i]),*c0) for i,(src,dst,axis,*c0) in enumerate(pairs)]
 def gather_sems(n,k):
     return [pltpu.SemaphoreType.DMA((k,links(n))),pltpu.SemaphoreType.DMA((k,links(n))),pltpu.SemaphoreType.DMA((k,))]
 def pair_sems(k):
@@ -435,10 +527,11 @@
 def each(ops,name):
     for o in ops: getattr(o,name)()
 
-def front_kernel(n,zc,tok,cot,gain,w,wo,normed,scale,cotfull,wfull,wofull,tokfull,zs,zr,cs,cr,*gs):
+def front_kernel(n,zc,tok,cot,gain,wq,wk,wv,ws,normed,scale,cotfull,wfull,cotc,tokfull,zs,zr,cs,cr,es,er,*gs):
     greet(n,zc)
     zt=ShardGather(zc,tok,tokfull,zs,zr); zt.start()
-    gw=gathers(n,[(w,wfull,0),(wo,wofull,1)],gs)
+    parts=(wq,wk,wv,ws); at=[sum(w.shape[1] for w in parts[:i]) for i in range(4)]
+    gw=gathers(n,[(w,wfull,0,a) for w,a in zip(parts,at)],gs)
     each(gw,"start")
     zt.finish()
     zk=ShardGather(zc,cot,cotfull,cs,cr); zk.start()
@@ -453,15 +546,15 @@
     lax.fori_loop(0,rows//32,norm,0)
     each(gw,"middle"); each(gw,"late")
     zk.finish()
+    cc=ColumnSplit(n,cotfull,cotc,es,er); cc.start(); cc.finish()
     each(gw,"finish")
 
-def attn_out_kernel(n,zc,part,tok,gain,wg,wu,wd,n1,res,scale,nfull,wgfull,wufull,wdfull,n1c,box,sums,nloc,as_,ar,bs,br,cs,cr,es,er,*gs):
+def attn_out_kernel(n,zc,part,tok,gain,wg,wu,wd,res,scale,nfull,wgfull,wufull,wdfull,box,sums,nloc,as_,ar,bs,br,cs,cr,*gs):
     greet(n,zc)
     D=part.shape[1]
     split=ShardSplit(zc,part,box,as_,ar); split.start()
     gw=gathers(n,[(wg,wgfull,0),(wu,wufull,0),(wd,wdfull,1)],gs)
     each(gw,"start")
-    cols=ColumnSplit(n,n1,n1c,es,er); cols.start()
     split.finish()
     r=tok[...].astype(f32)
     for d in range(zc): r=r+box[d].astype(f32)
@@ -476,13 +569,13 @@
     zg=ShardGather(zc,nloc,nfull,cs,cr); zg.start()
     each(gw,"middle")
     zg.finish()
-    each(gw,"late"); cols.finish(); each(gw,"finish")
-
-def ffn_back_kernel(n,zc,part,res,scale,cot,gain,dg_,du_,hid,bra,n2,gres,afull,gffn,dgfull,dufull,hidfull,brafull,n2c,box,sums,aloc,as_,ar,bs,br,cs,cr,es,er,*gs):
+    each(gw,"late"); each(gw,"finish")
+
+def ffn_back_kernel(n,zc,part,res,scale,cot,gain,dg_,du_,n2,gres,afull,gffn,dgfull,dufull,n2c,box,sums,aloc,as_,ar,bs,br,cs,cr,es,er,*gs):
     greet(n,zc)
     D=part.shape[1]
     split=ShardSplit(zc,part,box,as_,ar); split.start()
-    gw=gathers(n,[(dg_,dgfull,0),(du_,dufull,0),(hid,hidfull,0),(bra,brafull,0)],gs)
+    gw=gathers(n,[(dg_,dgfull,0),(du_,dufull,0)],gs)
     each(gw,"start")
     cols=ColumnSplit(n,n2,n2c,es,er); cols.start()
     split.finish()
@@ -505,13 +598,12 @@
     zg.finish()
     each(gw,"late"); cols.finish(); each(gw,"finish")
 
-def tail_kernel(n,zc,partdx,partout,res,gres,tok,scale,gain,small,dy,cot,att,output,gtok,dyfull,cotc,attc,smalls,totals,box,boxo,sums,as_,ar,bs,br,cs,cr,ds_,dr,es,er,fs,fr,hs,hr,*gs):
+def tail_kernel(n,zc,partdx,partout,res,gres,tok,scale,gain,small,dy,dsm,att,output,gtok,dyfull,dsmfull,attc,smalls,totals,box,boxo,sums,as_,ar,bs,br,cs,cr,es,er,fs,fr,hs,hr,*gs):
     greet(n,zc)
     D=partdx.shape[1]
     split=ShardSplit(zc,partdx,box,as_,ar); split.start()
-    gw=gathers(n,[(dy,dyfull,0)],gs)
+    gw=gathers(n,[(dy,dyfull,0),(dsm,dsmfull,0)],gs)
     each(gw,"start")
-    cc=ColumnSplit(n,cot,cotc,ds_,dr); cc.start()
     ca=ColumnSplit(n,att,attc,es,er); ca.start()
     split.finish()
     so=ShardSplit(zc,partout,boxo,fs,fr); so.start()
@@ -541,35 +633,36 @@
     for d in range(zc): o=o+boxo[d].astype(f32)
     output[...]=o
     za.finish()
-    each(gw,"late"); cc.finish(); ca.finish(); each(gw,"finish")
+    each(gw,"late"); ca.finish(); each(gw,"finish")
 
 def call(name,cid,kernel,args,specs,outs,ospecs,scratch):
     return pl.pallas_call(kernel,name=name,out_shape=tuple(outs),in_specs=specs,out_specs=tuple(ospecs),scratch_shapes=scratch,
       compiler_params=pltpu.CompilerParams(collective_id=cid,has_side_effects=True,vmem_limit_bytes=56*2**20))(*args)
 
-def front(n,zc,tok,cot,gain,w,wo):
+def front(n,zc,tok,cot,gain,*ws):
     R,F=tok.shape; D=F*zc
-    return call("front",1,functools.partial(front_kernel,n,zc),(tok,cot,gain,w,wo),[VM,VM,VM,ANY,ANY],
-      [S((R,D),bf16),S((R,128)),S((R,D),bf16),S((w.shape[0]*n,w.shape[1]),bf16),S((wo.shape[0],wo.shape[1]*n),bf16)],[VM,VM,ANY,ANY,ANY],
-      [pltpu.VMEM((R,D),bf16)]+pair_sems(zc)*2+gather_sems(n,2))
-def attn_out(n,zc,part,tok,gain,wg,wu,wd,n1):
+    return call("front",1,functools.partial(front_kernel,n,zc),(tok,cot,gain)+ws,[VM,VM,VM]+[ANY]*4,
+      [S((R,D),bf16),S((R,128)),S((R,D),bf16),S((ws[0].shape[0]*n,sum(w.shape[1] for w in ws)),bf16),S((R*n,D//n),bf16)],[VM,VM,ANY,ANY,ANY],
+      [pltpu.VMEM((R,D),bf16)]+pair_sems(zc)*2+pair_sems(n)+gather_sems(n,4))
+def attn_out(n,zc,part,tok,gain,wg,wu,wd):
     R,F=tok.shape; D=F*zc
-    return call("attn_out",2,functools.partial(attn_out_kernel,n,zc),(part,tok,gain,wg,wu,wd,n1),[ANY,VM,VM]+[ANY]*4,
-      [S((R,F)),S((R,128)),S((R,D),bf16),S((wg.shape[0]*n,wg.shape[1]),bf16),S((wu.shape[0]*n,wu.shape[1]),bf16),S((wd.shape[0],wd.shape[1]*n),bf16),S((R*n,D//n),bf16)],
-      [VM,VM,VM,ANY,ANY,ANY,ANY],
-      [pltpu.VMEM((zc,R,F),bf16),pltpu.VMEM((zc,8,R),f32),pltpu.VMEM((R,F),bf16)]+pair_sems(zc)*3+pair_sems(n)+gather_sems(n,3))
-def ffn_back(n,zc,part,res,scale,cot,gain,dg_,du_,hid,bra,n2):
+    return call("attn_out",2,functools.partial(attn_out_kernel,n,zc),(part,tok,gain,wg,wu,wd),[ANY,VM,VM]+[ANY]*3,
+      [S((R,F)),S((R,128)),S((R,D),bf16),S((wg.shape[0]*n,wg.shape[1]),bf16),S((wu.shape[0]*n,wu.shape[1]),bf16),S((wd.shape[0],wd.shape[1]*n),bf16)],
+      [VM,VM,VM,ANY,ANY,ANY],
+      [pltpu.VMEM((zc,R,F),bf16),pltpu.VMEM((zc,8,R),f32),pltpu.VMEM((R,F),bf16)]+pair_sems(zc)*3+gather_sems(n,3))
+def ffn_back(n,zc,part,res,scale,cot,gain,dg_,du_,n2):
     R,F=cot.shape; D=F*zc
     full=lambda a: S((a.shape[0]*n,a.shape[1]),bf16)
-    return call("ffn_back",3,functools.partial(ffn_back_kernel,n,zc),(part,res,scale,cot,gain,dg_,du_,hid,bra,n2),[ANY,VM,VM,VM,VM]+[ANY]*5,
-      [S((R,F)),S((R,D),bf16),S((8,F)),full(dg_),full(du_),full(hid),full(bra),S((R*n,D//n),bf16)],[VM,VM,VM]+[ANY]*5,
-      [pltpu.VMEM((zc,R,F),bf16),pltpu.VMEM((zc,8,R),f32),pltpu.VMEM((R,F),bf16)]+pair_sems(zc)*3+pair_sems(n)+gather_sems(n,4))
-def tail(n,zc,partdx,partout,res,gres,tok,scale,gain,small,dy,cot,att):
+    return call("ffn_back",3,functools.partial(ffn_back_kernel,n,zc),(part,res,scale,cot,gain,dg_,du_,n2),[ANY,VM,VM,VM,VM]+[ANY]*3,
+      [S((R,F)),S((R,D),bf16),S((8,F)),full(dg_),full(du_),S((R*n,D//n),bf16)],[VM,VM,VM]+[ANY]*3,
+      [pltpu.VMEM((zc,R,F),bf16),pltpu.VMEM((zc,8,R),f32),pltpu.VMEM((R,F),bf16)]+pair_sems(zc)*3+pair_sems(n)+gather_sems(n,2))
+def tail(n,zc,partdx,partout,res,gres,tok,scale,gain,small,dy,dsm,att):
     R,F=tok.shape; D=F*zc
-    return call("tail",4,functools.partial(tail_kernel,n,zc),(partdx,partout,res,gres,tok,scale,gain,small,dy,cot,att),[ANY,ANY]+[VM]*6+[ANY]*3,
-      [S((R,F)),S((R,F)),S((dy.shape[0]*n,dy.shape[1]),bf16),S((R*n,D//n),bf16),S((R*n,D//n),bf16),S((n,)+small.shape),S((zc,)+small.shape)],
+    full=lambda a: S((a.shape[0]*n,a.shape[1]),bf16)
+    return call("tail",4,functools.partial(tail_kernel,n,zc),(partdx,partout,res,gres,tok,scale,gain,small,dy,dsm,att),[ANY,ANY]+[VM]*6+[ANY]*3,
+      [S((R,F)),S((R,F)),full(dy),full(dsm),S((R*n,D//n),bf16),S((n,)+small.shape),S((zc,)+small.shape)],
       [VM,VM,ANY,ANY,ANY,VM,VM],
-      [pltpu.VMEM((zc,R,F),bf16),pltpu.VMEM((zc,R,F),bf16),pltpu.VMEM((zc,8,R),f32)]+pair_sems(zc)*2+pair_sems(n)*3+pair_sems(zc)*2+gather_sems(n,1))
+      [pltpu.VMEM((zc,R,F),bf16),pltpu.VMEM((zc,R,F),bf16),pltpu.VMEM((zc,8,R),f32)]+pair_sems(zc)*2+pair_sems(n)*2+pair_sems(zc)*2+gather_sems(n,2))
 
 
 def per_device(
@@ -603,49 +696,30 @@
     def project(a, b):
         return jnp.dot(a, b, preferred_element_type=f32)
 
-    def to_pairs(x):
-        y = jnp.moveaxis(x, 2, 1).reshape((pairs,) + (local_len, x.shape[3]))
-        y = jnp.repeat(y, copies, axis=0)
-        y = lax.all_to_all(y, "seq", 0, 0)
-        return y.reshape(length, x.shape[3])
-
-    def from_pairs(x):
-        y = x.reshape(seq_devices, local_len, x.shape[1])
-        y = lax.all_to_all(y, "seq", 0, 0)[::copies]
-        return jnp.moveaxis(y.reshape(seq_count, head_count, local_len, x.shape[1]), 1, 2)
-
     taps_local = jnp.concatenate([query_conv, key_conv, value_conv], axis=0)
     tap_rows = taps_local.shape[0]
     width_v = head_count * value_dim
-    widths = [width_k, width_k, width_v, width_v, head_count, head_count]
-    edges = [sum(widths[:i]) for i in range(7)]
-    filled = edges[6] + tap_count
-    padding = -filled % 128
+    padding = -(2 * head_count + tap_count) % 128
     taps_padded = jnp.pad(taps_local, ((0, query_weight.shape[0] - tap_rows), (0, padding)))
-    weights_one = jnp.concatenate(
-        [query_weight, key_weight, value_weight, outgate_weight, beta_weight, decay_weight, taps_padded], axis=1
-    )
+    weights_small = jnp.concatenate([beta_weight, decay_weight, taps_padded], axis=1)
+    edges = [0, width_k, 2 * width_k, 2 * width_k + width_v]
     flat = lambda x: x.reshape(row_count, x.shape[2])
     local_ffn_gain = lax.dynamic_slice_in_dim(ffn_gain, feature_start, feature_part)[None]
     local_norm_gain = lax.dynamic_slice_in_dim(norm_gain, feature_start, feature_part)[None]
     tokens_flat, cot_flat = flat(tokens), flat(cotangent)
-    normed_one, scale_one, cot_rows, full_one, full_output = front(
-        seq_devices, shard_count, tokens_flat, cot_flat, norm_gain[None], weights_one, output_weight
+    normed_one, scale_one, cot_rows, full_one, cot_cols = front(
+        seq_devices, shard_count, tokens_flat, cot_flat, norm_gain[None], query_weight, key_weight, value_weight, weights_small
     )
     proj = project(normed_one, full_one)
+    proj_qkv = proj[:, : edges[3]].astype(bf16)
+    proj_rates = proj[:, edges[3] : edges[3] + 2 * head_count].reshape(seq_count, local_len, 2, head_count)
+    rates_in = jnp.pad(jnp.transpose(proj_rates, (0, 3, 2, 1)), ((0, 0), (0, 0), (0, 6), (0, 0))).reshape(pairs * 8, local_len)
     shape4 = (seq_count, local_len, head_count, -1)
-    part = lambda i: proj[:, edges[i] : edges[i + 1]].reshape(shape4)
-    query_proj, key_proj, value_proj = (part(i).astype(bf16) for i in range(3))
-    gate_proj, beta_proj, decay_proj = (part(i) for i in range(3, 6))
-    all_taps = full_one[:, edges[6] : filled].reshape(seq_devices, -1, tap_count)
-    count_q, count_v = query_conv.shape[0], value_conv.shape[0]
+    all_taps = full_one[:, edges[3] + 2 * head_count :][:, :tap_count].reshape(seq_devices, -1, tap_count)
+    count_q = query_conv.shape[0]
     full_qconv = all_taps[:, :count_q].reshape(-1, tap_count)
     full_kconv = all_taps[:, count_q : 2 * count_q].reshape(-1, tap_count)
     full_vconv = all_taps[:, 2 * count_q : tap_rows].reshape(-1, tap_count)
-
-    u = to_pairs(jnp.concatenate([query_proj, key_proj, value_proj], axis=3))
-    rates = to_pairs(jnp.concatenate([beta_proj, decay_proj], axis=3)).reshape(spans, SPAN, 2)
-    rates_t = jnp.swapaxes(rates, 1, 2)
     taps = jnp.concatenate(
         [
             lax.dynamic_slice_in_dim(full_qconv, my_head * key_dim, key_dim),
@@ -659,8 +733,13 @@
     decay_pair = jnp.concatenate(
         [lax.dynamic_slice_in_dim(decay_log, at_head, 1), lax.dynamic_slice_in_dim(decay_bias, at_head, 1)]
     )
-    o_pair, *saved = forward(u, taps, rates, rates_t, starts, decay_pair, key_dim, value_dim)
-    o = from_pairs(o_pair).astype(f32)
+    o_flat, *saved = forward(
+        seq_devices, copies, head_count, proj_qkv, rates_in, taps, starts, decay_pair,
+        outgate_weight, output_weight, normed_one, key_dim, value_dim,
+    )
+    saved, (full_outgate, full_output, normed_one_cols) = saved[:12], saved[12:]
+    gate_proj = project(normed_one, full_outgate).reshape(shape4)
+    o = o_flat.astype(f32).reshape(shape4)
 
     rho = lax.rsqrt(jnp.mean(o * o, axis=3, keepdims=True) + EPSILON)
     gate_sig = jax.nn.sigmoid(gate_proj)
@@ -668,8 +747,8 @@
     z = o * rho
     branch = (z * head_gain * gate_silu).astype(bf16).reshape(row_count, width_v)
     attn_part = project(branch, full_output).astype(bf16)
-    residual, scale_two, normed_two, full_gate, full_up, full_down, normed_one_cols = attn_out(
-        seq_devices, shard_count, attn_part, tokens_flat, local_ffn_gain, gate_weight, up_weight, down_weight, normed_one
+    residual, scale_two, normed_two, full_gate, full_up, full_down = attn_out(
+        seq_devices, shard_count, attn_part, tokens_flat, local_ffn_gain, gate_weight, up_weight, down_weight
     )
     gate_vals = project(normed_two, full_gate)
     up_vals = project(normed_two, full_up)
@@ -688,9 +767,9 @@
     grad_gate_vals = (grad_hidden * up_vals * sigmoid_gate * (1.0 + gate_vals * (1.0 - sigmoid_gate))).astype(bf16)
     grad_up_vals = (grad_hidden * gate_act).astype(bf16)
     two_part = (back(grad_gate_vals, full_gate) + back(grad_up_vals, full_up)).astype(bf16)
-    grad_residual, attn_cot, grad_ffn_part, dgate_all, dup_all, hidden_all, branch_all, normed_two_cols = ffn_back(
+    grad_residual, attn_cot, grad_ffn_part, dgate_all, dup_all, normed_two_cols = ffn_back(
         seq_devices, shard_count, two_part, residual, scale_two, cot_flat, local_ffn_gain,
-        grad_gate_vals, grad_up_vals, hidden, branch, normed_two,
+        grad_gate_vals, grad_up_vals, normed_two,
     )
     out_gate, out_up = grad(normed_two_cols, dgate_all), grad(normed_two_cols, dup_all)
     grad_mixed = (
@@ -702,25 +781,15 @@
     grad_gate_proj = (grad_mixed * z * head_gain * gate_sig * (1.0 + gate_proj * (1.0 - gate_sig))).astype(bf16)
     grad_gate_proj = grad_gate_proj.reshape(row_count, head_count * value_dim)
 
-    du_pair, dtaps, drates, dhead = backward(
-        to_pairs(grad_o), u, taps, rates, rates_t, starts, decay_pair, saved
-    )
-    du = from_pairs(du_pair)
-    drates = from_pairs(drates.reshape(length, 2)).astype(bf16)
-    grad_qproj = du[..., :key_dim].reshape(row_count, width_k)
-    grad_kproj = du[..., key_dim : 2 * key_dim].reshape(row_count, width_k)
-    grad_vproj = du[..., 2 * key_dim :].reshape(row_count, head_count * value_dim)
-    grad_beta_proj = drates[..., 0].reshape(row_count, head_count)
-    grad_decay_proj = drates[..., 1].reshape(row_count, head_count)
-
-    grad_one = jnp.concatenate(
-        [
-            grad_qproj, grad_kproj, grad_vproj, grad_gate_proj, grad_beta_proj, grad_decay_proj,
-            jnp.zeros((row_count, tap_count + padding), bf16),
-        ],
-        axis=1,
-    )
-    one_part = back(grad_one, full_one).astype(bf16)
+    grad_qkv, drates, dtaps, dhead, hidden_all, branch_all, dgate_proj_all = backward(
+        seq_devices, copies, head_count, grad_o.reshape(row_count, width_v), taps, starts, decay_pair, saved,
+        hidden, branch, grad_gate_proj,
+    )
+    drates = jnp.transpose(drates.reshape(seq_count, head_count, 8, local_len)[:, :, :2], (0, 3, 2, 1))
+    grad_small = jnp.pad(drates.reshape(row_count, 2 * head_count).astype(bf16), ((0, 0), (0, tap_count + padding)))
+    one_part = (
+        back(grad_qkv, full_one[:, : edges[3]]) + back(grad_small, full_one[:, edges[3] :]) + back(grad_gate_proj, full_outgate)
+    ).astype(bf16)
     primary = jnp.where(seq_pos % copies == 0, 1.0, 0.0)
     total_heads = decay_log.shape[0]
     width_s = max(feature_part, channels)
@@ -733,11 +802,15 @@
     small = jnp.concatenate(
         [jnp.zeros((1, width_s), f32), widen(grad_ffn_part[:1]), widen(grad_head_gain[None]), heads_row, widen(dtaps)], axis=0
     )
-    output, grad_tokens, one_all, cot_cols, attn_cols, smalls, totals = tail(
+    output, grad_tokens, qkv_all, small_all, attn_cols, smalls, totals = tail(
         seq_devices, shard_count, one_part, out_part, residual, grad_residual, tokens_flat, scale_one,
-        local_norm_gain, small, grad_one, cot_rows, attn_cot,
-    )
-    outs_one = [grad(normed_one_cols, one_all[:, edges[i] : edges[i + 1]]) for i in range(6)]
+        local_norm_gain, small, grad_qkv, grad_small, attn_cot,
+    )
+    outs_one = [grad(normed_one_cols, qkv_all[:, edges[i] : edges[i + 1]]) for i in range(3)]
+    outs_small = grad(normed_one_cols, small_all)
+    outs_one += [
+        grad(normed_one_cols, dgate_proj_all), outs_small[:, :head_count], outs_small[:, head_count : 2 * head_count]
+    ]
     out_down = grad(hidden_all, cot_cols)
     out_output = grad(branch_all, attn_cols)
     tap_sum = jnp.sum(smalls[::copies, 4:].reshape(seq_count, head_count, tap_count, width_s), axis=0)

time: 633 us -> 571 us (0.902)
  waiting for transfers between devices: 27.4 us -> 0 us
  starting transfers between devices: 22 us -> 0 us
  local copies, waits for them, and re-layouts: 43.8 us -> 28.4 us
  Pallas kernels: 443 us -> 452 us
    pallas_call x4 -> x6, Pallas kernels: 368 us -> 452 us  [call(): pl.pallas_call(kernel, name=name, out_shape=tuple(outs), in_specs=specs,...]
    pallas_call x2 -> x0, Pallas kernels: 75.6 us -> none  [the longest x1 42 us: forward(): pl.pallas_call(forward_kernel, name='rec_fwd', out_shape=(S((L, DV), bf16...]
    all_to_all x6 -> x0, waiting for transfers between devices: 27.4 us -> none  [the longest x3 18.4 us: to_pairs(): y = lax.all_to_all(y, 'seq', 0, 0)]
    all_to_all x6 -> x0, starting transfers between devices: 22 us -> none  [the longest x3 11.6 us: from_pairs(): y = lax.all_to_all(y, 'seq', 0, 0)[::copies]]
    dot_general x10 -> x9, matrix products: 33.2 us -> 27.3 us  [grad(): return jnp.einsum('rd,rc->dc', left, right, preferred_element_type=f32)]
    dot_general x5 -> x6, matrix products: 23.2 us -> 24.4 us  [project(): return jnp.dot(a, b, preferred_element_type=f32)]
    dot_general x5 -> x7, matrix products: 22.8 us -> 22.4 us  [back(): return jnp.einsum('rc,dc->rd', cols, weight, preferred_element_type=f32)]
  transfers between devices with their start and end apart: 6 -> 0, of which waited for: 5 -> 0; matrix products, arithmetic and copies ran while one was open for 5% -> 0% of each run, Pallas kernels for 0% -> 0%
where the time goes in v3:
time: 571 us; the launch traced here: 564 us
  Pallas kernels  452 us (79%)
  matrix products  74.1 us (13%)
  local copies, waits for them, and re-layouts  28.4 us (5%)
  other arithmetic  7.32 us (1%)
    pallas_call x6, Pallas kernels, call(): pl.pallas_call(kernel, name=name, out_shape=tuple(outs), in_specs=specs,...  452 us
    dot_general x9, matrix products, grad(): return jnp.einsum('rd,rc->dc', left, right, preferred_element_type=f32)  27.3 us
    dot_general x6, matrix products, project(): return jnp.dot(a, b, preferred_element_type=f32)  24.4 us
    dot_general x7, matrix products, back(): return jnp.einsum('rc,dc->rd', cols, weight, preferred_element_type=f32)  22.4 us

profile of v3, /device:TPU:0, one launch (start us, length us, event | category | flops | bytes accessed | tf_op | source)
XLA Modules:
  0.0 563.8 jit_solution(10566908774756762121)
XLA Ops:
  0.7 0.8 pad_maximum_fusion
  1.7 0.8 copy.74
  2.5 0.8 copy.75
  3.3 0.7 fusion.19.ws
  4.0 61.0 %front.1 = (bf16[256,2048]{1,0:T(8,128)(2,1)}, f32[256,128]{1,0:T(8,128)}, bf16[256,2048]{1,0:T(8,128)(2,1)}, bf16[2048,2176]{1,0:T(8,128)(2,1)}, bf16[2048,256]{1,0:T(8,128)(2,1)}) custom-call(bf16[256,512]{1,0:T(8,128)(2,1)} %bitcast.95, bf16[256,512]{1,0:T(8,128)(2,1)} %bitcast.100, f32[1,2048]{1,0:T(1,128)} %bitcast.117, bf16[256,512]{1,0:T(8,128)(2,1)} %wq.1, ...), custom_call_target="tpu_custom_call" | custom-call | tf_op jit(solution)/shard_map/front/pallas_call | solution.py:639
  65.1 1.2 slice.84
  66.7 0.6 convert_bitcast_fusion.taps_ref
  67.3 0.6 dynamic_slice.38
  67.9 0.6 dynamic_slice.39
  68.5 1.9 pad_maximum_fusion.1.hp
  70.4 0.5 fusion.20.starts
  70.9 6.5 %fusion.27 = f32[256,2176]{1,0:T(8,128)S(1)} fusion(bf16[256,2048]{1,0:T(8,128)(2,1)} %get-tuple-element.67.n1, bf16[2048,2176]{1,0:T(8,128)(2,1)} %get-tuple-element.68), kind=kOutput, calls=%fused_computation.63 | convolution fusion | flops 2281701376 | bytes 12189696 | tf_op jit(solution)/shard_map/dot_general | solution.py:697
  77.4 1.1 slice.137.proj
  78.6 0.6 pad.17.clone
  79.2 73.5 %rec_fwd.1 = (bf16[256,1024]{1,0:T(8,128)(2,1)}, bf16[1024,512]{1,0:T(8,128)(2,1)}, f32[64,128]{1,0:T(8,128)}, f32[1024,8]{1,0:T(8,128)}, bf16[1024,128]{1,0:T(8...) custom-call(bf16[256,2048]{1,0:T(8,128)(2,1)} %slice.137.proj, ...), custom_call_target="tpu_custom_call" | custom-call | tf_op jit(solution)/shard_map/rec_fwd/pallas_call | solution.py:639
  152.8 1.6 reshape.131
  155.3 1.6 copy-done.28
  156.9 2.4 multiply_convert_fusion.5
  159.3 2.3 convolution_convert_fusion.part
  161.6 1.3 dynamic_slice.40
  162.9 86.6 %attn_out.1 = (f32[256,512]{1,0:T(8,128)}, f32[256,128]{1,0:T(8,128)}, bf16[256,2048]{1,0:T(8,128)(2,1)}, bf16[2048,1408]{1,0:T(8,128)(2,1)}, bf16[2048,1408]{1,0:T(8,128)(2,1)}, /*index=5*/bf16[1408,2048]{1,0:T(8,128)(2,1)}) custom-call(bf16[256,2048]{1,0:T(8,128)(2,1)} %convolution_convert_fusion.part, bf16[256,512]{1,0:T(8,128)(2,1)} %bitcast.96, ...), custom_call_target="tpu_custom_call" | custom-call | tf_op jit(solution)/shard_map/attn_out/pallas_call | solution.py:639
  249.5 4.7 fusion.28
  254.3 4.6 fusion.29
  258.9 3.1 multiply_convert_fusion
  262.1 1.8 fusion.30
  264.0 2.8 fusion.5.part
  266.7 67.1 %ffn_back.1 = (f32[256,512]{1,0:T(8,128)}, bf16[256,2048]{1,0:T(8,128)(2,1)}, f32[8,512]{1,0:T(8,128)}, bf16[2048,1408]{1,0:T(8,128)(2,1)}, bf16[2048,1408]{1,0:T(8,128)(2,1)}, /*index=5*/bf16[2048,256]{1,0:T(8,128)(2,1)}) custom-call(bf16[256,2048]{1,0:T(8,128)(2,1)} %fusion.5.part, f32[256,512]{1,0:T(8,128)} %get-tuple-element.77.res, ...), custom_call_target="tpu_custom_call" | custom-call | tf_op jit(solution)/shard_map/ffn_back/pallas_call | solution.py:639
  333.9 6.0 %fusion.36 = f32[256,1408]{1,0:T(8,128)} fusion(bf16[2048,256]{1,0:T(8,128)(2,1)} %get-tuple-element.109, bf16[2048,1408]{1,0:T(8,128)(2,1)} %get-tuple-element.111), kind=kOutput, calls=%fused_computation.72 | convolution fusion | flops 1476395008 | bytes 8257536 | tf_op jit(solution)/shard_map/rd,rc->dc/dot_general | solution.py:764
  339.9 2.9 fusion.35
  342.9 1.3 fusion.12
  344.2 0.5 reshape.132
  344.7 0.5 copy-done.7
  345.1 1.7 reshape.133
  346.9 1.1 fusion.16
  348.8 1.8 multiply_convert_fusion.4
  350.6 92.0 %rec_bwd.1 = (bf16[256,2048]{1,0:T(8,128)(2,1)}, f32[64,128]{1,0:T(8,128)}, f32[4,512]{1,0:T(4,128)}, f32[2,128]{1,0:T(2,128)}, bf16[2048,1408]{1,0:T(8,128)(2,1...) custom-call(bf16[256,1024]{1,0:T(8,128)(2,1)} %get-tuple-element.114.dall, ...), custom_call_target="tpu_custom_call" | custom-call | tf_op jit(solution)/shard_map/rec_bwd/pallas_call | solution.py:639
  442.6 1.3 fusion.25
  443.9 0.7 dynamic_update_slice.6
  444.6 0.9 dynamic_update_slice.7
  445.6 0.7 slice.91
  446.3 1.3 concatenate.19.small
  447.6 5.6 convolution_convert_fusion.1.partout
  453.2 5.8 %fusion = f32[256,2048]{1,0:T(8,128)S(1)} fusion(bf16[256,2048]{1,0:T(8,128)(2,1)S(1)} %copy-done.15, bf16[2048,2176]{1,0:T(8,128)(2,1)} %get-tuple-element.68), kind=kOutput, calls=%fused_computation | convolution fusion | flops 2147483648 | bytes 11534336 | tf_op jit(solution)/shard_map/rc,dc->rd/dot_general | solution.py:761
  459.2 3.5 fusion.31
  462.7 2.5 fusion.6.partdx
  465.2 0.6 pad.18.dsm
  465.8 1.3 dynamic_slice.41
  467.2 72.1 %tail.1 = (f32[256,512]{1,0:T(8,128)}, f32[256,512]{1,0:T(8,128)}, bf16[2048,2048]{1,0:T(8,128)(2,1)}, bf16[2048,128]{1,0:T(8,128)(2,1)}, bf16[2048,256]{1,0:T(8...) custom-call(bf16[256,2048]{1,0:T(8,128)(2,1)} %fusion.6.partdx, ...), custom_call_target="tpu_custom_call" | custom-call | tf_op jit(solution)/shard_map/tail/pallas_call | solution.py:639
  539.4 4.9 fusion.34
  544.3 0.4 fusion.33
  544.6 0.6 fusion.23
  545.2 2.3 fusion.32
  547.5 2.2 fusion.2
  549.7 1.5 fusion.7
  551.2 1.5 fusion.9
  552.8 0.7 constant_dynamic-slice_fusion.1
  553.5 0.6 constant_dynamic-slice_fusion.2
  554.1 0.6 constant_dynamic-slice_fusion
  554.7 0.6 slice_bitcast_fusion.2
  555.3 0.6 slice.121
  555.9 0.6 fusion.24
  556.5 5.5 fusion.37
  562.1 0.8 copy.106
  562.9 0.8 copy.107
  (119 shorter events, 2.7 us)
Async XLA Ops:
  0.7 69.7 %copy-start = (s32[2,16]{1,0:T(2,128)S(1)}, s32[2,16]{1,0:T(2,128)}, u32[]{:S(2)}) copy-start(s32[2,16]{1,0:T(2,128)} %param.22) | copy-start | bytes 388
  0.7 66.7 %copy-start.34 = (f32[16]{0:T(128)S(1)}, f32[16]{0:T(128)}, u32[]{:S(2)}) copy-start(f32[16]{0:T(128)} %param.33) | copy-start | bytes 196
  0.7 67.2 %copy-start.35 = (f32[16]{0:T(128)S(1)}, f32[16]{0:T(128)}, u32[]{:S(2)}) copy-start(f32[16]{0:T(128)} %param.34) | copy-start | bytes 196
  79.2 76.1 %copy-start.27 = (f32[256]{0:T(256)S(1)}, f32[256]{0:T(256)}, u32[]{:S(2)}) copy-start(f32[256]{0:T(256)} %param.35) | copy-start | bytes 3076
  79.2 76.1 %copy-start.12 = (bf16[256,2048]{1,0:T(8,128)(2,1)S(1)}, bf16[256,2048]{1,0:T(8,128)(2,1)}, u32[]{:S(2)}) copy-start(bf16[256,2048]{1,0:T(8,128)(2,1)} %get-tuple-element.67.n1) | copy-start | bytes 3145732
  152.8 2.6 copy-start.9
  154.3 2.6 copy-start.28
  155.3 4.0 copy-start.4
  156.9 2.4 copy-start.30
  159.3 90.2 %copy-start.20 = (bf16[256,1024]{1,0:T(8,128)(2,1)}, bf16[256,1024]{1,0:T(8,128)(2,1)S(1)}, u32[]{:S(2)}) copy-start(bf16[256,1024]{1,0:T(8,128)(2,1)S(1)} %get-tuple-element.132.bra) | copy-start | bytes 1572868
  159.3 90.2 %copy-start.33 = (bf16[256,2048]{1,0:T(8,128)(2,1)S(1)}, bf16[256,2048]{1,0:T(8,128)(2,1)}, u32[]{:S(2)}) copy-start(bf16[256,2048]{1,0:T(8,128)(2,1)} %get-tuple-element.70) | copy-start | bytes 3145732
  249.5 4.8 copy-start.16
  249.5 9.4 %slice-start.2 = ((s8[5767168]{0:T(1024)(128)(4,1)}), s8[4194304]{0:T(1024)(128)(4,1)S(1)}, s32[]{:S(2)}) async-start(s8[5767168]{0:T(1024)(128)(4,1)} %bitcast.125), calls=%async_computation.2 | async-start | bytes 8388608
  254.3 4.6 slice-start.3
  254.3 7.8 %slice-start.4 = ((s8[5767168]{0:T(1024)(128)(4,1)}), s8[4194304]{0:T(1024)(128)(4,1)S(1)}, s32[]{:S(2)}) async-start(s8[5767168]{0:T(1024)(128)(4,1)} %bitcast.127), calls=%async_computation.4 | async-start | bytes 8388608
  258.9 3.1 slice-start.5
  262.1 1.9 copy-start.18
  262.1 1.9 copy-start.19
  333.9 6.0 %copy-start.2 = (bf16[2048,1408]{1,0:T(8,128)(2,1)S(1)}, bf16[2048,1408]{1,0:T(8,128)(2,1)}, u32[]{:S(2)}) copy-start(bf16[2048,1408]{1,0:T(8,128)(2,1)} %get-tuple-element.110) | copy-start | bytes 17301508
  333.9 6.0 %copy-start.3 = (bf16[2048,256]{1,0:T(8,128)(2,1)S(1)}, bf16[2048,256]{1,0:T(8,128)(2,1)}, u32[]{:S(2)}) copy-start(bf16[2048,256]{1,0:T(8,128)(2,1)} %get-tuple-element.109) | copy-start | bytes 3145732
  339.9 2.9 copy-start.14
  339.9 2.9 copy-start.31
  344.2 1.0 copy-start.7
  346.8 1.7 copy-start.5
  346.9 1.7 copy-start.6
  346.9 1.8 copy-start.8
  346.9 2.0 copy-start.10
  350.6 97.0 %copy-start.17 = (bf16[256,1408]{1,0:T(8,128)(2,1)S(1)}, bf16[256,1408]{1,0:T(8,128)(2,1)}, u32[]{:S(2)}) copy-start(bf16[256,1408]{1,0:T(8,128)(2,1)} %get-tuple-element.117.hid) | copy-start | bytes 2162692
  447.6 5.6 copy-start.15
  453.2 5.8 %copy-start.25 = (f32[64,128]{1,0:T(8,128)S(1)}, f32[64,128]{1,0:T(8,128)}, u32[]{:S(2)}) copy-start(f32[64,128]{1,0:T(8,128)} %get-tuple-element.93) | copy-start | bytes 98308
  453.2 6.0 %copy-start.11 = (bf16[256,1024]{1,0:T(8,128)(2,1)S(1)}, bf16[256,1024]{1,0:T(8,128)(2,1)}, u32[]{:S(2)}) copy-start(bf16[256,1024]{1,0:T(8,128)(2,1)} %get-tuple-element.115.dgp) | copy-start | bytes 1572868
  467.2 78.1 %copy-start.29 = (bf16[2048,1024]{1,0:T(8,128)(2,1)S(1)}, bf16[2048,1024]{1,0:T(8,128)(2,1)}, u32[]{:S(2)}) copy-start(bf16[2048,1024]{1,0:T(8,128)(2,1)} %get-tuple-element.104) | copy-start | bytes 12582916
  539.3 8.2 %slice-start = ((s8[8388608]{0:T(1024)(128)(4,1)}), s8[4194304]{0:T(1024)(128)(4,1)S(1)}, s32[]{:S(2)}) async-start(s8[8388608]{0:T(1024)(128)(4,1)} %bitcast.123), calls=%async_computation | async-start | bytes 8388608
  539.3 4.9 copy-start.13
  539.3 4.9 copy-start.23
  539.3 8.1 %slice-start.1 = ((s8[8388608]{0:T(1024)(128)(4,1)}), s8[4194304]{0:T(1024)(128)(4,1)S(1)}, s32[]{:S(2)}) async-start(s8[8388608]{0:T(1024)(128)(4,1)} %bitcast.123), calls=%async_computation.1 | async-start | bytes 8388608
  549.7 3.1 copy-start.26
  549.7 5.0 copy-start.24
  549.7 6.8 %copy-start.32 = (bf16[2048,256]{1,0:T(8,128)(2,1)S(1)}, bf16[2048,256]{1,0:T(8,128)(2,1)}, u32[]{:S(2)}) copy-start(bf16[2048,256]{1,0:T(8,128)(2,1)} %get-tuple-element.113) | copy-start | bytes 3145732
  556.5 5.6 copy-start.22
  556.5 6.4 %copy-start.21 = (f32[256,512]{1,0:T(8,128)S(1)}, f32[256,512]{1,0:T(8,128)}, u32[]{:S(2)}) copy-start(f32[256,512]{1,0:T(8,128)} %get-tuple-element.100) | copy-start | bytes 1572868
  556.5 7.2 %copy-start.1 = (s32[2,16]{1,0:T(2,128)S(1)}, s32[2,16]{1,0:T(2,128)}, u32[]{:S(2)}) copy-start(s32[2,16]{1,0:T(2,128)} %param.22) | copy-start | bytes 388

commit v4 on v3

--- a/solution.py
+++ b/solution.py
@@ -27,6 +27,12 @@
     return i,j
 def positions(base,rows,cols,axis):
     return base+lax.broadcasted_iota(jnp.int32,(rows,cols),axis)
+class Row:
+    def __init__(self,ref,row):
+        self.ref=ref; self.row=row; self.shape=ref.shape[1:]
+    def __getitem__(self,e):
+        return self.ref[self.row,e]
+
 def doc_count(starts,pos):
     n=jnp.zeros(pos.shape,jnp.int32)
     for e in range(starts.shape[0]):
@@ -88,17 +94,70 @@
         pre=pre+window[8-back:8-back+rows]*ok*taps[3-back:4-back]
     return pre
 
-def forward_kernel(n,copies,heads,proj,rows_in,taps_ref,starts,hp,wg,wo,n1,
-                   oall,u_ref,xr_ref,xc_ref,q_ref,k_ref,v_ref,s_ref,w_ref,t_ref,qt_ref,mh_ref,ml_ref,wgfull,wofull,n1c,
-                   upad,un_ref,gc_ref,on_ref,o_ref,is_,ir,os_,or_,es,er,*gs):
-    L=u_ref.shape[0]; NC=L//SPAN; DV=v_ref.shape[1]; DK=q_ref.shape[1]; local_len=L//n; per=local_len//SPAN
-    greet(n,1)
-    inward=ToPairs(n,copies,heads,local_len,proj,rows_in,u_ref,xr_ref,DK,DV,is_,ir); inward.start()
-    gw=gathers(n,[(wg,wgfull,0),(wo,wofull,1)],gs)
+def forward_kernel(n,zc,copies,heads,DK,DV,tok,cot,gain,hgain,starts2,dlog,dbias,wq,wk,wv,ws,wg,wo,
+                   normed,scale,cotfull,wfull,wgfull,wofull,cotc,n1c,gate_ref,oall,branch,part,taps_ref,u_ref,xr_ref,xc_ref,q_ref,k_ref,v_ref,s_ref,w_ref,t_ref,qt_ref,mh_ref,ml_ref,
+                   tokfull,wbuf,sbuf,pbuf,rbuf,tbuf,upad,un_ref,gc_ref,on_ref,o_ref,zs,zr,cs,cr,ks,kr,es,er,is_,ir,os_,or_,ld,*gs):
+    L=u_ref.shape[0]; NC=L//SPAN; local_len=L//n; per=local_len//SPAN
+    greet(n,zc)
+    zt=ShardGather(zc,tok,tokfull,zs,zr); zt.start()
+    ws_all=(ws,wq,wk,wv); at=(wq.shape[1]*2+wv.shape[1],0,wq.shape[1],wq.shape[1]*2)
+    g1,g2=gs[:3],gs[3:]
+    gw=gathers(n,[(w,wfull,0,a) for w,a in zip(ws_all,at)],g1)
+    gb=gathers(n,[(wg,wgfull,0),(wo,wofull,1)],g2)
+    each(gw,"start")
+    zt.finish()
+    zk=ShardGather(zc,cot,cotfull,cs,cr); zk.start()
+    rows=tokfull.shape[0]; D=tokfull.shape[1]
+    def norm(c,_):
+        r=pl.ds(pl.multiple_of(c*32,32),32)
+        x=tokfull[r,:].astype(f32)
+        sc=lax.rsqrt(jnp.sum(x*x,axis=1,keepdims=True)/D+EPSILON)
+        normed[r,:]=(x*sc*gain[...]).astype(bf16)
+        scale[r,:]=jnp.broadcast_to(sc,(32,128))
+        return 0
+    lax.fori_loop(0,rows//32,norm,0)
+    rbuf[...]=jnp.zeros(rbuf.shape,f32)
+    each(gw,"middle")
+    pair=lax.div(lax.axis_index("seq"),copies); my_seq=lax.div(pair,heads); my_head=lax.rem(pair,heads)
+    for i,g in enumerate(gw):
+        g.late(); g.finish()
+        if i==0: each(gb,"start")
+        width=ws_all[i].shape[1]
+        buf=sbuf if i==0 else wbuf.at[:,pl.ds(0,width)]
+        c=pltpu.make_async_copy(wfull.at[:,pl.ds(at[i],width)],buf,ld.at[0]); c.start(); c.wait()
+        if i==0:
+            small=jnp.dot(normed[...],sbuf[...],preferred_element_type=f32)
+            for sq in range(rows//local_len):
+                fl=flat_form(small[sq*local_len:(sq+1)*local_len,0:8*((2*heads+7)//8)])
+                for h in range(heads):
+                    base=(sq*heads+h)*8
+                    rbuf[base:base+1]=fl[h:h+1]
+                    rbuf[base+1:base+2]=fl[heads+h:heads+h+1]
+            cq=heads*DK//n; cv=heads*DV//n; step=sbuf.shape[0]//n
+            for kind,(width_c,count,skip) in enumerate(((cq,DK,0),(cq,DK,cq),(cv,DV,2*cq))):
+                for j in range(count//width_c):
+                    dev=my_head*(count//width_c)+j
+                    to=(0,DK,2*DK)[kind]+j*width_c
+                    tbuf[to:to+width_c]=sbuf[pl.ds(pl.multiple_of(dev*step+skip,16),width_c),:]
+            ch=tbuf.shape[0]
+            ident=jnp.where(lax.broadcasted_iota(jnp.int32,(ch,ch),0)==lax.broadcasted_iota(jnp.int32,(ch,ch),1),1.0,0.0).astype(bf16)
+            tt=dg(tbuf[...],ident,0,0)
+            taps_ref[...]=tt[2*heads:2*heads+4]
+        else:
+            tile=min(width,256)
+            def column(j,_,i=i,tile=tile):
+                cc=pl.ds(pl.multiple_of(j*tile,128),tile)
+                pbuf[:,pl.ds(pl.multiple_of(at[i]+j*tile,128),tile)]=jnp.dot(normed[...],wbuf[:,cc],preferred_element_type=f32).astype(bf16)
+                return 0
+            lax.fori_loop(0,width//tile,column,0)
+    inward=ToPairs(n,copies,heads,local_len,pbuf,rbuf,u_ref,xr_ref,DK,DV,is_,ir); inward.start()
+    starts=Row(starts2,my_seq)
+    at_head=lax.axis_index("shard")*heads+my_head
+    rate=jnp.exp(jnp.full((1,1),dlog[at_head],f32)); bias=dbias[at_head]
+    zk.finish()
+    cols=ColumnSplit(n,normed,n1c,es,er); cols.start()
+    ccol=ColumnSplit(n,cotfull,cotc,ks,kr); ccol.start()
     inward.finish()
-    each(gw,"start")
-    cols=ColumnSplit(n,n1,n1c,es,er); cols.start()
-    rate=jnp.exp(jnp.full((1,1),hp[0],f32)); bias=hp[1]
     upad[0:8]=jnp.zeros((8,upad.shape[1]),f32)
     def turn(m,_):
         xc_ref[pl.ds(pl.multiple_of(m*local_len,local_len),local_len),:]=col_form(xr_ref[pl.ds(pl.multiple_of(m*8,8),8),:])
@@ -148,7 +207,7 @@
         for e in range(per): one_span(m*per+e,xr[1:2,e*SPAN:(e+1)*SPAN])
         return 0
     lax.fori_loop(0,n,local,0,unroll=2)
-    each(gw,"middle")
+    each(gb,"middle")
     def chain(n,S):
         s_ref[n]=S
         sh,sl=halves(S); mh=mh_ref[n]; ml=ml_ref[n]
@@ -165,15 +224,45 @@
     outward=FromPairs(n,copies,heads,local_len,[(o_ref,lambda t: (pl.ds(pl.multiple_of(t*local_len,local_len),local_len),slice(None)),
         oall,lambda seq,head: (pl.ds(pl.multiple_of(seq*local_len,local_len),local_len),pl.ds(pl.multiple_of(head*DV,128),DV)))],os_,or_)
     outward.start()
-    each(gw,"late"); outward.finish(); cols.finish(); each(gw,"finish")
-
-def backward_kernel(n,copies,heads,dall,u_ref,taps_ref,xc_ref,xr_ref,starts,hp,q_ref,k_ref,v_ref,s_ref,w_ref,t_ref,qt_ref,mh_ref,ml_ref,hid,bra,dgp,
+    each(gb,"late"); cols.finish(); ccol.finish(); gb[0].finish()
+    width=wg.shape[1]
+    c=pltpu.make_async_copy(wgfull,wbuf.at[:,pl.ds(0,width)],ld.at[0]); c.start(); c.wait()
+    def column(j,_):
+        cc=pl.ds(pl.multiple_of(j*256,256),256)
+        gate_ref[:,cc]=jnp.dot(normed[...],wbuf[:,cc],preferred_element_type=f32)
+        return 0
+    lax.fori_loop(0,width//256,column,0)
+    gb[1].finish()
+    for j in range(D//wbuf.shape[1]):
+        c=pltpu.make_async_copy(wofull.at[:,pl.ds(j*wbuf.shape[1],wbuf.shape[1])],wbuf.at[pl.ds(j*wofull.shape[0],wofull.shape[0]),:],ld.at[j]); c.start()
+        c.wait()
+    outward.finish()
+    def mix(c,_):
+        r=pl.ds(pl.multiple_of(c*32,32),32)
+        for h in range(heads):
+            cc=pl.ds(h*DV,DV)
+            o=oall[r,cc].astype(f32); g=gate_ref[r,cc]
+            rho=lax.rsqrt(jnp.sum(o*o,axis=1,keepdims=True)/DV+EPSILON)
+            branch[r,cc]=(o*rho*hgain[...]*(g*sigmoid(g))).astype(bf16)
+        return 0
+    lax.fori_loop(0,rows//32,mix,0)
+    tiles=wbuf.shape[1]//256
+    def column(j,_):
+        blk=lax.div(j,tiles); inner=lax.rem(j,tiles)
+        w=wbuf[pl.ds(pl.multiple_of(blk*wofull.shape[0],16),wofull.shape[0]),pl.ds(pl.multiple_of(inner*256,256),256)]
+        part[:,pl.ds(pl.multiple_of(j*256,256),256)]=jnp.dot(branch[...],w,preferred_element_type=f32).astype(bf16)
+        return 0
+    lax.fori_loop(0,D//256,column,0)
+
+def backward_kernel(n,copies,heads,dall,u_ref,taps_ref,xc_ref,xr_ref,starts2,dlog,dbias,q_ref,k_ref,v_ref,s_ref,w_ref,t_ref,qt_ref,mh_ref,ml_ref,hid,bra,dgp,
                     duall,rows_out,dtaps_ref,dh_ref,hidfull,brafull,dgpfull,upad,dpre,ds_ref,dqkv,r_ref,gc_ref,do_ref,du_ref,dx_ref,dxr,is_,ir,os_,or_,*gs):
     L=u_ref.shape[0]; NC=L//SPAN; DV=v_ref.shape[1]; DK=q_ref.shape[1]; local_len=L//n; per=local_len//SPAN
     greet(n,1)
     inward=ToPairs(n,copies,heads,local_len,dall,None,do_ref,None,DK,DV,is_,ir); inward.start()
     gw=gathers(n,[(hid,hidfull,0),(bra,brafull,0),(dgp,dgpfull,0)],gs)
-    rate=jnp.exp(jnp.full((1,1),hp[0],f32)); bias=hp[1]
+    pair=lax.div(lax.axis_index("seq"),copies)
+    starts=Row(starts2,lax.div(pair,heads)); at_head=lax.axis_index("shard")*heads+lax.rem(pair,heads)
+    rate=jnp.exp(jnp.full((1,1),dlog[at_head],f32)); bias=dbias[at_head]
     taps=taps_ref[...]
     R=128
     upad[0:8]=jnp.zeros((8,upad.shape[1]),f32)
@@ -305,20 +394,25 @@
 
 SM=pl.BlockSpec(memory_space=pltpu.SMEM); VM=pl.BlockSpec(memory_space=pltpu.VMEM)
 def S(shape,dt=f32): return jax.ShapeDtypeStruct(shape,dt)
-def forward(n,copies,heads,proj,rows_in,taps,starts,hp,wg,wo,n1,DK,DV):
-    R=proj.shape[0]; CH=taps.shape[1]; local_len=rows_in.shape[1]; L=n*local_len; NC=L//SPAN; pairs=rows_in.shape[0]//8
-    full=lambda a: S((a.shape[0]*n,a.shape[1]),bf16)
-    return call("rec_fwd",5,functools.partial(forward_kernel,n,copies,heads),(proj,rows_in,taps,starts,hp,wg,wo,n1),[ANY,ANY,VM,SM,SM,ANY,ANY,ANY],
-      [S((R,heads*DV),bf16),S((L,CH),bf16),S((n*8,local_len)),S((L,8)),S((L,DK),bf16),S((L,DK),bf16),S((L,DV),bf16),S((NC,DK,DV)),S((NC,SPAN,DV)),S((NC,SPAN,SPAN)),
-       S((NC,2*SPAN,DK),bf16),S((NC,DK,DK),bf16),S((NC,DK,DK),bf16),full(wg),S((wo.shape[0],wo.shape[1]*n),bf16),S((R*n,n1.shape[1]//n),bf16)],
-      [ANY]+[VM]*12+[ANY]*3,
-      [pltpu.VMEM((L+8,CH),f32),pltpu.VMEM((NC,DK,DV),f32),pltpu.VMEM((NC,8,128),f32),pltpu.VMEM((NC,SPAN,DV),f32),pltpu.VMEM((L,DV),bf16),
-       pltpu.SemaphoreType.DMA((4,n)),pltpu.SemaphoreType.DMA((4,n)),pltpu.SemaphoreType.DMA((1,pairs)),pltpu.SemaphoreType.DMA((1,pairs))]+pair_sems(n)+gather_sems(n,2))
-def backward(n,copies,heads,dall,taps,starts,hp,saved,hid,bra,dgp):
+def forward(n,zc,copies,heads,tok,cot,gain,hgain,starts,dlog,dbias,wq,wk,wv,ws,wg,wo,DK,DV):
+    R,F=tok.shape; D=F*zc; local_len=R//starts.shape[0]; L=n*local_len; NC=L//SPAN; pairs=n//copies; CH=2*DK+DV; HV=heads*DV
+    rows=lambda *w: S((w[0].shape[0]*n,sum(x.shape[1] for x in w)),bf16)
+    wide=max(wv.shape[1],wg.shape[1])
+    return call("mixer",5,functools.partial(forward_kernel,n,zc,copies,heads,DK,DV),(tok,cot,gain,hgain,starts,dlog,dbias,wq,wk,wv,ws,wg,wo),[VM,VM,VM,VM,SM,SM,SM]+[ANY]*6,
+      [S((R,D),bf16),S((R,128)),S((R,D),bf16),rows(wq,wk,wv,ws),rows(wg),S((wo.shape[0],wo.shape[1]*n),bf16),S((R*n,D//n),bf16),S((R*n,D//n),bf16),
+       S((R,HV)),S((R,HV),bf16),S((R,HV),bf16),S((R,D),bf16),S((4,CH)),
+       S((L,CH),bf16),S((n*8,local_len)),S((L,8)),S((L,DK),bf16),S((L,DK),bf16),S((L,DV),bf16),S((NC,DK,DV)),S((NC,SPAN,DV)),S((NC,SPAN,SPAN)),
+       S((NC,2*SPAN,DK),bf16),S((NC,DK,DK),bf16),S((NC,DK,DK),bf16)],
+      [VM,VM]+[ANY]*6+[VM]*17,
+      [pltpu.VMEM((R,D),bf16),pltpu.VMEM((D,wide),bf16),pltpu.VMEM((D,ws.shape[1]),bf16),pltpu.VMEM((R,heads*CH),bf16),pltpu.VMEM((pairs*8,local_len),f32),pltpu.VMEM((CH,128),bf16),
+       pltpu.VMEM((L+8,CH),f32),pltpu.VMEM((NC,DK,DV),f32),pltpu.VMEM((NC,8,128),f32),pltpu.VMEM((NC,SPAN,DV),f32),pltpu.VMEM((L,DV),bf16)]
+      +pair_sems(zc)*2+pair_sems(n)*2+[pltpu.SemaphoreType.DMA((4,n)),pltpu.SemaphoreType.DMA((4,n)),pltpu.SemaphoreType.DMA((1,pairs)),pltpu.SemaphoreType.DMA((1,pairs)),pltpu.SemaphoreType.DMA((D//wide,))]
+      +gather_sems(n,4)+gather_sems(n,2))
+def backward(n,copies,heads,dall,taps,starts,dlog,dbias,saved,hid,bra,dgp):
     u,xr,xc,q,k,v,s,w,t,qt,mh,ml=saved
     L,CH=u.shape; NC=L//SPAN; DK=q.shape[1]; DV=v.shape[1]; local_len=L//n; pairs=n//copies; R=dall.shape[0]
     full=lambda a: S((a.shape[0]*n,a.shape[1]),bf16)
-    return call("rec_bwd",6,functools.partial(backward_kernel,n,copies,heads),(dall,u,taps,xc,xr,starts,hp,q,k,v,s,w,t,qt,mh,ml,hid,bra,dgp),[ANY]+[VM]*4+[SM]*2+[VM]*9+[ANY]*3,
+    return call("rec_bwd",6,functools.partial(backward_kernel,n,copies,heads),(dall,u,taps,xc,xr,starts,dlog,dbias,q,k,v,s,w,t,qt,mh,ml,hid,bra,dgp),[ANY]+[VM]*4+[SM]*3+[VM]*9+[ANY]*3,
       [S((R,heads*CH),bf16),S((pairs*8,local_len)),S((4,CH)),S((2,128)),full(hid),full(bra),full(dgp)],[ANY,ANY,VM,VM,ANY,ANY,ANY],
       [pltpu.VMEM((L+8,CH),f32),pltpu.VMEM((L+8,CH),f32),pltpu.VMEM((NC,DK,DV),f32),pltpu.VMEM((L,CH),f32),pltpu.VMEM((NC,DK,DV),f32),pltpu.VMEM((NC,8,128),f32),
        pltpu.VMEM((L,DV),bf16),pltpu.VMEM((L,CH),bf16),pltpu.VMEM((L,8),f32),pltpu.VMEM((n*8,local_len),f32),
@@ -527,76 +621,78 @@
 def each(ops,name):
     for o in ops: getattr(o,name)()
 
-def front_kernel(n,zc,tok,cot,gain,wq,wk,wv,ws,normed,scale,cotfull,wfull,cotc,tokfull,zs,zr,cs,cr,es,er,*gs):
+def ffn_kernel(n,zc,part,tok,cot,cotfull,gain,wg,wu,wd,res,gres,afull,gffn,outpart,hidden,dgfull,dufull,n2c,
+               box,sums,nloc,nfull,gw_,uw_,dw_,gv,uv,dgate,dup,two,as_,ar,bs,br,cs,cr,ds_,dr,es,er,fs,fr,hs,hr,*gs):
     greet(n,zc)
-    zt=ShardGather(zc,tok,tokfull,zs,zr); zt.start()
-    parts=(wq,wk,wv,ws); at=[sum(w.shape[1] for w in parts[:i]) for i in range(4)]
-    gw=gathers(n,[(w,wfull,0,a) for w,a in zip(parts,at)],gs)
-    each(gw,"start")
-    zt.finish()
-    zk=ShardGather(zc,cot,cotfull,cs,cr); zk.start()
-    rows=tokfull.shape[0]; D=tokfull.shape[1]
-    def norm(c,_):
-        r=pl.ds(pl.multiple_of(c*32,32),32)
-        x=tokfull[r,:].astype(f32)
-        sc=lax.rsqrt(jnp.sum(x*x,axis=1,keepdims=True)/D+EPSILON)
-        normed[r,:]=(x*sc*gain[...]).astype(bf16)
-        scale[r,:]=jnp.broadcast_to(sc,(32,128))
-        return 0
-    lax.fori_loop(0,rows//32,norm,0)
-    each(gw,"middle"); each(gw,"late")
-    zk.finish()
-    cc=ColumnSplit(n,cotfull,cotc,es,er); cc.start(); cc.finish()
-    each(gw,"finish")
-
-def attn_out_kernel(n,zc,part,tok,gain,wg,wu,wd,res,scale,nfull,wgfull,wufull,wdfull,box,sums,nloc,as_,ar,bs,br,cs,cr,*gs):
-    greet(n,zc)
-    D=part.shape[1]
+    D=part.shape[1]; R=part.shape[0]; FF=gv.shape[1]; z=lax.axis_index("shard")
     split=ShardSplit(zc,part,box,as_,ar); split.start()
-    gw=gathers(n,[(wg,wgfull,0),(wu,wufull,0),(wd,wdfull,1)],gs)
+    g1,g2=gs[:3],gs[3:]
+    gw=gathers(n,[(wg,gw_,0),(wu,uw_,0),(wd,dw_,1)],g1)
     each(gw,"start")
     split.finish()
     r=tok[...].astype(f32)
     for d in range(zc): r=r+box[d].astype(f32)
     res[...]=r
-    sums[lax.axis_index("shard")]=row_form(r*r)
+    sums[z]=row_form(r*r)
     tot=ShardAll("shard",zc,sums,bs,br); tot.start(); tot.finish()
     t=sums[0]
     for d in range(1,zc): t=t+sums[d]
     sc=lax.rsqrt(col_form(t)[:,0:1]/D+EPSILON)
-    scale[...]=jnp.broadcast_to(sc,scale.shape)
     nloc[...]=(r*sc*gain[...]).astype(bf16)
     zg=ShardGather(zc,nloc,nfull,cs,cr); zg.start()
     each(gw,"middle")
     zg.finish()
-    each(gw,"late"); each(gw,"finish")
-
-def ffn_back_kernel(n,zc,part,res,scale,cot,gain,dg_,du_,n2,gres,afull,gffn,dgfull,dufull,n2c,box,sums,aloc,as_,ar,bs,br,cs,cr,es,er,*gs):
-    greet(n,zc)
-    D=part.shape[1]
-    split=ShardSplit(zc,part,box,as_,ar); split.start()
-    gw=gathers(n,[(dg_,dgfull,0),(du_,dufull,0)],gs)
-    each(gw,"start")
-    cols=ColumnSplit(n,n2,n2c,es,er); cols.start()
+    cols=ColumnSplit(n,nfull,n2c,es,er); cols.start()
+    tiles=[(a,min(a+512,FF)) for a in range(0,FF,512)]
+    gw[0].late(); gw[0].finish()
+    for a,b in tiles: gv[:,a:b]=jnp.dot(nfull[...],gw_[:,a:b],preferred_element_type=f32)
+    gw[1].late(); gw[1].finish()
+    for a,b in tiles: uv[:,a:b]=jnp.dot(nfull[...],uw_[:,a:b],preferred_element_type=f32)
+    def act(c,_):
+        rr=pl.ds(pl.multiple_of(c*32,32),32)
+        g=gv[rr,:]
+        hidden[rr,:]=(g*sigmoid(g)*uv[rr,:]).astype(bf16)
+        return 0
+    lax.fori_loop(0,R//32,act,0)
+    gw[2].late(); gw[2].finish()
+    for a,b in tiles:
+        dh=dg(cotfull[...],dw_[a:b,:],1,1)
+        g=gv[:,a:b]; sg=sigmoid(g)
+        dgate[:,a:b]=(dh*uv[:,a:b]*sg*(1.0+g*(1.0-sg))).astype(bf16)
+        dup[:,a:b]=(dh*(g*sg)).astype(bf16)
+    gd=gathers(n,[(dgate,dgfull,0),(dup,dufull,0)],g2)
+    each(gd,"start")
+    def back(j,_):
+        rr=pl.ds(pl.multiple_of(j*256,256),256)
+        two[:,rr]=(dg(dgate[...],gw_[rr,:],1,1)+dg(dup[...],uw_[rr,:],1,1)).astype(bf16)
+        return 0
+    lax.fori_loop(0,D//256,back,0)
+    split=ShardSplit(zc,two,box,fs,fr)
+    split.start()
+    def outp(j,_):
+        cc=pl.ds(pl.multiple_of(j*256,256),256)
+        outpart[:,cc]=jnp.dot(hidden[...],dw_[:,cc],preferred_element_type=f32).astype(bf16)
+        return 0
+    lax.fori_loop(0,D//256,outp,0)
     split.finish()
     g=box[0].astype(f32)
     for d in range(1,zc): g=g+box[d].astype(f32)
-    r=res[...]; sc=scale[...][:,0:1]
+    r=res[...]
     gained=gain[...]*g
-    sums[lax.axis_index("shard")]=row_form(gained*r)
-    tot=ShardAll("shard",zc,sums,bs,br); tot.start()
+    sums[zc+z]=row_form(gained*r)
+    tot=ShardAll("shard",zc,sums.at[pl.ds(zc,zc)],ds_,dr); tot.start()
     gffn[...]=jnp.broadcast_to(jnp.sum(g*r*sc,axis=0,keepdims=True),gffn.shape)
     tot.finish()
-    t=sums[0]
-    for d in range(1,zc): t=t+sums[d]
+    t=sums[zc]
+    for d in range(1,zc): t=t+sums[zc+d]
     inner=col_form(t)[:,0:1]/D
     gr=cot[...].astype(f32)+sc*(gained-r*(sc*sc*inner))
     gres[...]=gr
-    aloc[...]=gr.astype(bf16)
-    zg=ShardGather(zc,aloc,afull,cs,cr); zg.start()
-    each(gw,"middle")
+    nloc[...]=gr.astype(bf16)
+    zg=ShardGather(zc,nloc,afull,hs,hr); zg.start()
+    each(gd,"middle")
     zg.finish()
-    each(gw,"late"); cols.finish(); each(gw,"finish")
+    each(gd,"late"); cols.finish(); each(gd,"finish")
 
 def tail_kernel(n,zc,partdx,partout,res,gres,tok,scale,gain,small,dy,dsm,att,output,gtok,dyfull,dsmfull,attc,smalls,totals,box,boxo,sums,as_,ar,bs,br,cs,cr,es,er,fs,fr,hs,hr,*gs):
     greet(n,zc)
@@ -639,23 +735,14 @@
     return pl.pallas_call(kernel,name=name,out_shape=tuple(outs),in_specs=specs,out_specs=tuple(ospecs),scratch_shapes=scratch,
       compiler_params=pltpu.CompilerParams(collective_id=cid,has_side_effects=True,vmem_limit_bytes=56*2**20))(*args)
 
-def front(n,zc,tok,cot,gain,*ws):
-    R,F=tok.shape; D=F*zc
-    return call("front",1,functools.partial(front_kernel,n,zc),(tok,cot,gain)+ws,[VM,VM,VM]+[ANY]*4,
-      [S((R,D),bf16),S((R,128)),S((R,D),bf16),S((ws[0].shape[0]*n,sum(w.shape[1] for w in ws)),bf16),S((R*n,D//n),bf16)],[VM,VM,ANY,ANY,ANY],
-      [pltpu.VMEM((R,D),bf16)]+pair_sems(zc)*2+pair_sems(n)+gather_sems(n,4))
-def attn_out(n,zc,part,tok,gain,wg,wu,wd):
-    R,F=tok.shape; D=F*zc
-    return call("attn_out",2,functools.partial(attn_out_kernel,n,zc),(part,tok,gain,wg,wu,wd),[ANY,VM,VM]+[ANY]*3,
-      [S((R,F)),S((R,128)),S((R,D),bf16),S((wg.shape[0]*n,wg.shape[1]),bf16),S((wu.shape[0]*n,wu.shape[1]),bf16),S((wd.shape[0],wd.shape[1]*n),bf16)],
-      [VM,VM,VM,ANY,ANY,ANY],
-      [pltpu.VMEM((zc,R,F),bf16),pltpu.VMEM((zc,8,R),f32),pltpu.VMEM((R,F),bf16)]+pair_sems(zc)*3+gather_sems(n,3))
-def ffn_back(n,zc,part,res,scale,cot,gain,dg_,du_,n2):
-    R,F=cot.shape; D=F*zc
-    full=lambda a: S((a.shape[0]*n,a.shape[1]),bf16)
-    return call("ffn_back",3,functools.partial(ffn_back_kernel,n,zc),(part,res,scale,cot,gain,dg_,du_,n2),[ANY,VM,VM,VM,VM]+[ANY]*3,
-      [S((R,F)),S((R,D),bf16),S((8,F)),full(dg_),full(du_),S((R*n,D//n),bf16)],[VM,VM,VM]+[ANY]*3,
-      [pltpu.VMEM((zc,R,F),bf16),pltpu.VMEM((zc,8,R),f32),pltpu.VMEM((R,F),bf16)]+pair_sems(zc)*3+pair_sems(n)+gather_sems(n,2))
+def ffn(n,zc,part,tok,cot,cotfull,gain,wg,wu,wd):
+    R,F=tok.shape; D=F*zc; FF=wg.shape[1]
+    return call("ffn",2,functools.partial(ffn_kernel,n,zc),(part,tok,cot,cotfull,gain,wg,wu,wd),[ANY]+[VM]*4+[ANY]*3,
+      [S((R,F)),S((R,F)),S((R,D),bf16),S((8,F)),S((R,D),bf16),S((R,FF),bf16),S((R*n,FF),bf16),S((R*n,FF),bf16),S((R*n,D//n),bf16)],
+      [VM]*6+[ANY]*3,
+      [pltpu.VMEM((zc,R,F),bf16),pltpu.VMEM((2*zc,8,R),f32),pltpu.VMEM((R,F),bf16),pltpu.VMEM((R,D),bf16),pltpu.VMEM((D,FF),bf16),pltpu.VMEM((D,FF),bf16),pltpu.VMEM((FF,D),bf16),
+       pltpu.VMEM((R,FF),f32),pltpu.VMEM((R,FF),f32),pltpu.VMEM((R,FF),bf16),pltpu.VMEM((R,FF),bf16),pltpu.VMEM((R,D),bf16)]
+      +pair_sems(zc)*4+pair_sems(n)+pair_sems(zc)*2+gather_sems(n,3)+gather_sems(n,2))
 def tail(n,zc,partdx,partout,res,gres,tok,scale,gain,small,dy,dsm,att):
     R,F=tok.shape; D=F*zc
     full=lambda a: S((a.shape[0]*n,a.shape[1]),bf16)
@@ -707,55 +794,24 @@
     local_ffn_gain = lax.dynamic_slice_in_dim(ffn_gain, feature_start, feature_part)[None]
     local_norm_gain = lax.dynamic_slice_in_dim(norm_gain, feature_start, feature_part)[None]
     tokens_flat, cot_flat = flat(tokens), flat(cotangent)
-    normed_one, scale_one, cot_rows, full_one, cot_cols = front(
-        seq_devices, shard_count, tokens_flat, cot_flat, norm_gain[None], query_weight, key_weight, value_weight, weights_small
+    (
+        normed_one, scale_one, cot_rows, full_one, full_outgate, full_output, cot_cols, normed_one_cols,
+        gate_proj, o_flat, branch, attn_part, taps, *saved,
+    ) = forward(
+        seq_devices, shard_count, copies, head_count, tokens_flat, cot_flat, norm_gain[None], head_gain[None],
+        doc_starts, decay_log, decay_bias, query_weight, key_weight, value_weight, weights_small, outgate_weight,
+        output_weight, key_dim, value_dim,
     )
-    proj = project(normed_one, full_one)
-    proj_qkv = proj[:, : edges[3]].astype(bf16)
-    proj_rates = proj[:, edges[3] : edges[3] + 2 * head_count].reshape(seq_count, local_len, 2, head_count)
-    rates_in = jnp.pad(jnp.transpose(proj_rates, (0, 3, 2, 1)), ((0, 0), (0, 0), (0, 6), (0, 0))).reshape(pairs * 8, local_len)
+    residual, grad_residual, attn_cot, grad_ffn_part, out_part, hidden, dgate_all, dup_all, normed_two_cols = ffn(
+        seq_devices, shard_count, attn_part, tokens_flat, cot_flat, cot_rows, local_ffn_gain, gate_weight, up_weight, down_weight
+    )
     shape4 = (seq_count, local_len, head_count, -1)
-    all_taps = full_one[:, edges[3] + 2 * head_count :][:, :tap_count].reshape(seq_devices, -1, tap_count)
-    count_q = query_conv.shape[0]
-    full_qconv = all_taps[:, :count_q].reshape(-1, tap_count)
-    full_kconv = all_taps[:, count_q : 2 * count_q].reshape(-1, tap_count)
-    full_vconv = all_taps[:, 2 * count_q : tap_rows].reshape(-1, tap_count)
-    taps = jnp.concatenate(
-        [
-            lax.dynamic_slice_in_dim(full_qconv, my_head * key_dim, key_dim),
-            lax.dynamic_slice_in_dim(full_kconv, my_head * key_dim, key_dim),
-            lax.dynamic_slice_in_dim(full_vconv, my_head * value_dim, value_dim),
-        ],
-        axis=0,
-    ).astype(f32).T
-    starts = lax.dynamic_index_in_dim(doc_starts, my_seq, 0, keepdims=False)
-    at_head = head_start + my_head
-    decay_pair = jnp.concatenate(
-        [lax.dynamic_slice_in_dim(decay_log, at_head, 1), lax.dynamic_slice_in_dim(decay_bias, at_head, 1)]
-    )
-    o_flat, *saved = forward(
-        seq_devices, copies, head_count, proj_qkv, rates_in, taps, starts, decay_pair,
-        outgate_weight, output_weight, normed_one, key_dim, value_dim,
-    )
-    saved, (full_outgate, full_output, normed_one_cols) = saved[:12], saved[12:]
-    gate_proj = project(normed_one, full_outgate).reshape(shape4)
+    gate_proj = gate_proj.reshape(shape4)
     o = o_flat.astype(f32).reshape(shape4)
-
     rho = lax.rsqrt(jnp.mean(o * o, axis=3, keepdims=True) + EPSILON)
     gate_sig = jax.nn.sigmoid(gate_proj)
     gate_silu = gate_proj * gate_sig
     z = o * rho
-    branch = (z * head_gain * gate_silu).astype(bf16).reshape(row_count, width_v)
-    attn_part = project(branch, full_output).astype(bf16)
-    residual, scale_two, normed_two, full_gate, full_up, full_down = attn_out(
-        seq_devices, shard_count, attn_part, tokens_flat, local_ffn_gain, gate_weight, up_weight, down_weight
-    )
-    gate_vals = project(normed_two, full_gate)
-    up_vals = project(normed_two, full_up)
-    sigmoid_gate = jax.nn.sigmoid(gate_vals)
-    gate_act = gate_vals * sigmoid_gate
-    hidden = (gate_act * up_vals).astype(bf16)
-    out_part = project(hidden, full_down).astype(bf16)
 
     def back(cols, weight):
         return jnp.einsum("rc,dc->rd", cols, weight, preferred_element_type=f32)
@@ -763,14 +819,6 @@
     def grad(left, right):
         return jnp.einsum("rd,rc->dc", left, right, preferred_element_type=f32)
 
-    grad_hidden = back(cot_rows, full_down)
-    grad_gate_vals = (grad_hidden * up_vals * sigmoid_gate * (1.0 + gate_vals * (1.0 - sigmoid_gate))).astype(bf16)
-    grad_up_vals = (grad_hidden * gate_act).astype(bf16)
-    two_part = (back(grad_gate_vals, full_gate) + back(grad_up_vals, full_up)).astype(bf16)
-    grad_residual, attn_cot, grad_ffn_part, dgate_all, dup_all, normed_two_cols = ffn_back(
-        seq_devices, shard_count, two_part, residual, scale_two, cot_flat, local_ffn_gain,
-        grad_gate_vals, grad_up_vals, normed_two,
-    )
     out_gate, out_up = grad(normed_two_cols, dgate_all), grad(normed_two_cols, dup_all)
     grad_mixed = (
         back(attn_cot, full_output).astype(bf16).astype(f32).reshape(shape4)
@@ -782,7 +830,7 @@
     grad_gate_proj = grad_gate_proj.reshape(row_count, head_count * value_dim)
 
     grad_qkv, drates, dtaps, dhead, hidden_all, branch_all, dgate_proj_all = backward(
-        seq_devices, copies, head_count, grad_o.reshape(row_count, width_v), taps, starts, decay_pair, saved,
+        seq_devices, copies, head_count, grad_o.reshape(row_count, width_v), taps, doc_starts, decay_log, decay_bias, saved,
         hidden, branch, grad_gate_proj,
     )
     drates = jnp.transpose(drates.reshape(seq_count, head_count, 8, local_len)[:, :, :2], (0, 3, 2, 1))
@@ -790,6 +838,7 @@
     one_part = (
         back(grad_qkv, full_one[:, : edges[3]]) + back(grad_small, full_one[:, edges[3] :]) + back(grad_gate_proj, full_outgate)
     ).astype(bf16)
+    at_head = head_start + my_pair % head_count
     primary = jnp.where(seq_pos % copies == 0, 1.0, 0.0)
     total_heads = decay_log.shape[0]
     width_s = max(feature_part, channels)

time: 571 us -> 542 us (0.949)
  matrix products: 74.1 us -> 43.4 us
  Pallas kernels: 452 us -> 460 us
  local copies, waits for them, and re-layouts: 28.4 us -> 22.3 us
    dot_general x6 -> x0, matrix products: 24.4 us -> none  [project(): return jnp.dot(a, b, preferred_element_type=f32)]
    pallas_call x6 -> x4, Pallas kernels: 452 us -> 460 us  [call(): pl.pallas_call(kernel, name=name, out_shape=tuple(outs), in_specs=specs,...]
    dot_general x7 -> x4, matrix products: 22.4 us -> 14.5 us  [back(): return jnp.einsum('rc,dc->rd', cols, weight, preferred_element_type=f32)]
where the time goes in v4:
time: 542 us; the launch traced here: 533 us
  Pallas kernels  460 us (85%)
  matrix products  43.4 us (8%)
  local copies, waits for them, and re-layouts  22.3 us (4%)
    pallas_call x4, Pallas kernels, call(): pl.pallas_call(kernel, name=name, out_shape=tuple(outs), in_specs=specs,...  460 us
    dot_general x9, matrix products, grad(): return jnp.einsum('rd,rc->dc', left, right, preferred_element_type=f32)  29 us
    dot_general x4, matrix products, back(): return jnp.einsum('rc,dc->rd', cols, weight, preferred_element_type=f32)  14.5 us

profile of v4, /device:TPU:0, one launch (start us, length us, event | category | flops | bytes accessed | tf_op | source)
XLA Modules:
  0.0 532.8 jit_solution(5888978196541631306)
XLA Ops:
  0.7 0.8 pad_maximum_fusion
  1.5 1.3 dynamic_slice.15
  2.8 1.3 dynamic_slice.16
  4.1 0.7 broadcast_bitcast_fusion
  4.8 0.1 copy.59
  5.0 0.8 copy.60
  5.8 0.8 copy.61
  6.6 0.7 fusion.17.ws
  7.4 146.0 %mixer.1 = (bf16[256,2048]{1,0:T(8,128)(2,1)}, f32[256,128]{1,0:T(8,128)}, bf16[256,2048]{1,0:T(8,128)(2,1)}, bf16[2048,2176]{1,0:T(8,128)(2,1)}, bf16[2048,1024...) custom-call(bf16[256,512]{1,0:T(8,128)(2,1)} %bitcast.67, ...), custom_call_target="tpu_custom_call" | custom-call | tf_op jit(solution)/shard_map/mixer/pallas_call | solution.py:735
  153.3 1.6 reshape.104
  154.9 0.3 multiply_reduce_fusion.1
  155.3 0.3 mul.116
  155.7 1.2 copy.65
  156.8 0.0 copy-done.1
  156.8 0.5 reshape.106
  157.3 146.1 %ffn.1 = (f32[256,512]{1,0:T(8,128)}, f32[256,512]{1,0:T(8,128)}, bf16[256,2048]{1,0:T(8,128)(2,1)}, f32[8,512]{1,0:T(8,128)}, bf16[256,2048]{1,0:T(8,128)(2,1)}...) custom-call(bf16[256,2048]{1,0:T(8,128)(2,1)} %get-tuple-element.68., ...), custom_call_target="tpu_custom_call" | custom-call | tf_op jit(solution)/shard_map/ffn/pallas_call | solution.py:735
  303.5 0.0 copy-start.15
  303.5 3.5 fusion.10
  306.9 0.7 slice.64
  307.7 1.7 reshape.105
  309.4 0.0 copy-done.15
  309.4 0.0 copy-start.2
  309.4 0.0 copy-start.3
  309.4 0.0 copy-start.4
  309.4 1.0 fusion.14
  310.5 0.3 mul.132
  310.8 0.2 copy.67
  311.0 0.0 copy-done.2
  311.0 0.0 copy-done.3
  311.0 0.2 copy-done.4
  311.2 0.1 copy-done.6
  311.4 1.6 multiply_convert_fusion.1
  313.0 0.1 copy-done.18
  313.1 2.7 fusion.23
  315.8 0.0 slice-start.1
  315.8 5.7 %fusion.27 = f32[256,1408]{1,0:T(8,128)} fusion(bf16[2048,256]{1,0:T(8,128)(2,1)S(1)} %copy-done, bf16[2048,1408]{1,0:T(8,128)(2,1)} %get-tuple-element.110), kind=kOutput, calls=%fused_computation.47 | convolution fusion | flops 1476395008 | bytes 8257536 | tf_op jit(solution)/shard_map/rd,rc->dc/dot_general | solution.py:820
  321.6 0.0 copy-done.7
  321.6 2.9 fusion.28
  324.5 92.0 %rec_bwd.1 = (bf16[256,2048]{1,0:T(8,128)(2,1)}, f32[64,128]{1,0:T(8,128)}, f32[4,512]{1,0:T(4,128)}, f32[2,128]{1,0:T(2,128)}, bf16[2048,1408]{1,0:T(8,128)(2,1...) custom-call(bf16[256,1024]{1,0:T(8,128)(2,1)} %get-tuple-element.114.dall, ...), custom_call_target="tpu_custom_call" | custom-call | tf_op jit(solution)/shard_map/rec_bwd/pallas_call | solution.py:735
  416.5 0.8 convert.4
  417.3 1.3 fusion.21
  418.6 0.7 dynamic_update_slice.6
  419.3 0.8 dynamic_update_slice.7
  420.1 1.3 concatenate.11.small
  421.4 0.1 copy.63
  421.5 0.6 pad.13.dsm
  422.2 5.6 %fusion.29 = f32[1408,256]{1,0:T(8,128)} fusion(bf16[2048,1408]{1,0:T(8,128)(2,1)} %get-tuple-element.112, bf16[2048,256]{1,0:T(8,128)(2,1)S(1)} %copy-done.21), kind=kOutput, calls=%fused_computation.49 | convolution fusion | flops 1476395008 | bytes 8257536 | tf_op jit(solution)/shard_map/rd,rc->dc/dot_general | solution.py:820
  427.8 2.3 fusion.24
  430.0 5.9 %fusion = f32[256,2048]{1,0:T(8,128)S(1)} fusion(bf16[256,2048]{1,0:T(8,128)(2,1)S(1)} %copy-done.9, bf16[2048,2176]{1,0:T(8,128)(2,1)} %get-tuple-element.89), kind=kOutput, calls=%fused_computation | convolution fusion | flops 2147483648 | bytes 11534336 | tf_op jit(solution)/shard_map/rc,dc->rd/dot_general | solution.py:817
  435.9 2.5 fusion.5.partdx
  438.4 76.4 %tail.1 = (f32[256,512]{1,0:T(8,128)}, f32[256,512]{1,0:T(8,128)}, bf16[2048,2048]{1,0:T(8,128)(2,1)}, bf16[2048,128]{1,0:T(8,128)(2,1)}, bf16[2048,256]{1,0:T(8...) custom-call(bf16[256,2048]{1,0:T(8,128)(2,1)} %fusion.5.partdx, bf16[256,2048]{1,0:T(8,128)(2,1)} %get-tuple-element.92.partout, ...), custom_call_target="tpu_custom_call" | custom-call | tf_op jit(solution)/shard_map/tail/pallas_call | solution.py:735
  514.8 3.5 fusion.26
  518.3 0.6 fusion.20
  519.0 0.6 slice.89
  519.5 0.6 slice_bitcast_fusion.2
  520.2 0.7 constant_dynamic-slice_fusion.1
  520.8 0.6 constant_dynamic-slice_fusion
  521.4 0.3 fusion.25
  521.8 0.6 fusion.19
  522.4 3.3 fusion.6
  525.6 3.1 fusion.8
  528.8 2.3 fusion.2
  531.0 0.8 copy.76
  531.8 0.8 copy.77
  (51 shorter events, 0.2 us)
Async XLA Ops:
  153.3 3.5 copy-start.1
  157.3 146.1 %copy-start.20 = (bf16[1024,2048]{1,0:T(8,128)(2,1)S(1)}, bf16[1024,2048]{1,0:T(8,128)(2,1)}, u32[]{:S(2)}) copy-start(bf16[1024,2048]{1,0:T(8,128)(2,1)} %get-tuple-element.71) | copy-start | bytes 12582916
  303.5 5.9 %copy-start.15 = (f32[256]{0:T(256)S(1)}, f32[256]{0:T(256)}, u32[]{:S(2)}) copy-start(f32[256]{0:T(256)} %param.35) | copy-start | bytes 3076
  309.4 1.6 copy-start.2
  309.4 1.6 copy-start.3
  309.4 1.8 copy-start.4
  309.4 2.0 copy-start.6
  310.8 2.3 copy-start.18
  313.0 8.6 %copy-start.7 = (bf16[256,1024]{1,0:T(8,128)(2,1)}, bf16[256,1024]{1,0:T(8,128)(2,1)S(1)}, u32[]{:S(2)}) copy-start(bf16[256,1024]{1,0:T(8,128)(2,1)S(1)} %get-tuple-element.115.dgp) | copy-start | bytes 1572868
  313.0 2.8 copy-start
  313.1 8.4 %slice-start = ((s8[5767168]{0:T(1024)(128)(4,1)}), s8[1572864]{0:T(1024)(128)(4,1)S(1)}, s32[]{:S(2)}) async-start(s8[5767168]{0:T(1024)(128)(4,1)} %bitcast.61), calls=%async_computation | async-start | bytes 3145728
  315.8 5.7 %slice-start.1 = ((s8[5767168]{0:T(1024)(128)(4,1)}), s8[4194304]{0:T(1024)(128)(4,1)S(1)}, s32[]{:S(2)}) async-start(s8[5767168]{0:T(1024)(128)(4,1)} %bitcast.61), calls=%async_computation.1 | async-start | bytes 8388608
  324.5 97.7 %copy-start.21 = (bf16[2048,256]{1,0:T(8,128)(2,1)S(1)}, bf16[2048,256]{1,0:T(8,128)(2,1)}, u32[]{:S(2)}) copy-start(bf16[2048,256]{1,0:T(8,128)(2,1)} %get-tuple-element.113) | copy-start | bytes 3145732
  422.2 5.6 %copy-start.8 = (bf16[2048,256]{1,0:T(8,128)(2,1)S(1)}, bf16[2048,256]{1,0:T(8,128)(2,1)}, u32[]{:S(2)}) copy-start(bf16[2048,256]{1,0:T(8,128)(2,1)} %get-tuple-element.102) | copy-start | bytes 3145732
  422.2 5.6 %copy-start.19 = (bf16[2048,1024]{1,0:T(8,128)(2,1)S(1)}, bf16[2048,1024]{1,0:T(8,128)(2,1)}, u32[]{:S(2)}) copy-start(bf16[2048,1024]{1,0:T(8,128)(2,1)} %get-tuple-element.104) | copy-start | bytes 12582916
  427.8 2.3 copy-start.9
  430.0 5.9 %copy-start.5 = (f32[256,2048]{1,0:T(8,128)S(1)}, f32[256,2048]{1,0:T(8,128)}, u32[]{:S(2)}) copy-start(f32[256,2048]{1,0:T(8,128)} %fusion.23) | copy-start | bytes 6291460
  438.4 76.4 %copy-start.17 = (bf16[2048,1024]{1,0:T(8,128)(2,1)S(1)}, bf16[2048,1024]{1,0:T(8,128)(2,1)}, u32[]{:S(2)}) copy-start(bf16[2048,1024]{1,0:T(8,128)(2,1)} %get-tuple-element.107) | copy-start | bytes 12582916
  514.8 3.6 copy-start.13
  514.8 5.3 %copy-start.14 = (f32[8,8,512]{2,1,0:T(8,128)S(1)}, f32[8,8,512]{2,1,0:T(8,128)}, u32[]{:S(2)}) copy-start(f32[8,8,512]{2,1,0:T(8,128)} %get-tuple-element.106) | copy-start | bytes 393220
  514.8 6.6 %copy-start.12 = (bf16[2048,128]{1,0:T(8,128)(2,1)S(1)}, bf16[2048,128]{1,0:T(8,128)(2,1)}, u32[]{:S(2)}) copy-start(bf16[2048,128]{1,0:T(8,128)(2,1)} %get-tuple-element.105) | copy-start | bytes 1572868
  522.4 6.4 %copy-start.16 = (bf16[2048,2048]{1,0:T(8,128)(2,1)S(1)}, bf16[2048,2048]{1,0:T(8,128)(2,1)}, u32[]{:S(2)}) copy-start(bf16[2048,2048]{1,0:T(8,128)(2,1)} %get-tuple-element.103) | copy-start | bytes 25165828
  528.8 2.3 copy-start.11
  528.8 3.1 copy-start.10

commit v5 on v4

--- a/solution.py
+++ b/solution.py
@@ -94,16 +94,22 @@
         pre=pre+window[8-back:8-back+rows]*ok*taps[3-back:4-back]
     return pre
 
-def forward_kernel(n,zc,copies,heads,DK,DV,tok,cot,gain,hgain,starts2,dlog,dbias,wq,wk,wv,ws,wg,wo,
-                   normed,scale,cotfull,wfull,wgfull,wofull,cotc,n1c,gate_ref,oall,branch,part,taps_ref,u_ref,xr_ref,xc_ref,q_ref,k_ref,v_ref,s_ref,w_ref,t_ref,qt_ref,mh_ref,ml_ref,
-                   tokfull,wbuf,sbuf,pbuf,rbuf,tbuf,upad,un_ref,gc_ref,on_ref,o_ref,zs,zr,cs,cr,ks,kr,es,er,is_,ir,os_,or_,ld,*gs):
+def forward_kernel(n,zc,copies,heads,DK,DV,tok,cot,gain,hgain,starts2,dlog,dbias,wb,wd,qc,kc,vc,wq,wk,wv,wg,wo,wgate,
+                   scale,cotfull,wfull,wgfull,wofull,wgatefull,cotc,n1c,gate_ref,oall,branch,part,taps_ref,u_ref,xr_ref,xc_ref,q_ref,k_ref,v_ref,s_ref,w_ref,t_ref,qt_ref,mh_ref,ml_ref,
+                   tokfull,normed,ws,wbuf,sbuf,pbuf,rbuf,tbuf,upad,un_ref,gc_ref,on_ref,o_ref,zs,zr,cs,cr,ks,kr,es,er,fs,fr,hs,hr,is_,ir,os_,or_,ld,*gs):
     L=u_ref.shape[0]; NC=L//SPAN; local_len=L//n; per=local_len//SPAN
+    put=lambda x,first: dg(x[...],jnp.where(lax.broadcasted_iota(jnp.int32,(x.shape[1],128),0)+first==lax.broadcasted_iota(jnp.int32,(x.shape[1],128),1),1.0,0.0).astype(bf16))
+    ws[...]=(put(wb,0)+put(wd,heads)).astype(bf16)
+    at_row=0
+    for x in (qc,kc,vc):
+        ws[at_row:at_row+x.shape[0]]=(ws[at_row:at_row+x.shape[0]].astype(f32)+put(x,2*heads)).astype(bf16)
+        at_row+=x.shape[0]
     greet(n,zc)
     zt=ShardGather(zc,tok,tokfull,zs,zr); zt.start()
     ws_all=(ws,wq,wk,wv); at=(wq.shape[1]*2+wv.shape[1],0,wq.shape[1],wq.shape[1]*2)
     g1,g2=gs[:3],gs[3:]
     gw=gathers(n,[(w,wfull,0,a) for w,a in zip(ws_all,at)],g1)
-    gb=gathers(n,[(wg,wgfull,0),(wo,wofull,1)],g2)
+    gb=gathers(n,[(wg,wgfull,0),(wo,wofull,1),(wgate,wgatefull,0)],g2)
     each(gw,"start")
     zt.finish()
     zk=ShardGather(zc,cot,cotfull,cs,cr); zk.start()
@@ -121,7 +127,6 @@
     pair=lax.div(lax.axis_index("seq"),copies); my_seq=lax.div(pair,heads); my_head=lax.rem(pair,heads)
     for i,g in enumerate(gw):
         g.late(); g.finish()
-        if i==0: each(gb,"start")
         width=ws_all[i].shape[1]
         buf=sbuf if i==0 else wbuf.at[:,pl.ds(0,width)]
         c=pltpu.make_async_copy(wfull.at[:,pl.ds(at[i],width)],buf,ld.at[0]); c.start(); c.wait()
@@ -155,9 +160,10 @@
     at_head=lax.axis_index("shard")*heads+my_head
     rate=jnp.exp(jnp.full((1,1),dlog[at_head],f32)); bias=dbias[at_head]
     zk.finish()
-    cols=ColumnSplit(n,normed,n1c,es,er); cols.start()
-    ccol=ColumnSplit(n,cotfull,cotc,ks,kr); ccol.start()
     inward.finish()
+    each(gb,"start")
+    cols=SharedColumns(n,zc,normed,n1c,(es,er,fs,fr)); cols.start()
+    ccol=SharedColumns(n,zc,cotfull,cotc,(ks,kr,hs,hr)); ccol.start()
     upad[0:8]=jnp.zeros((8,upad.shape[1]),f32)
     def turn(m,_):
         xc_ref[pl.ds(pl.multiple_of(m*local_len,local_len),local_len),:]=col_form(xr_ref[pl.ds(pl.multiple_of(m*8,8),8),:])
@@ -207,7 +213,7 @@
         for e in range(per): one_span(m*per+e,xr[1:2,e*SPAN:(e+1)*SPAN])
         return 0
     lax.fori_loop(0,n,local,0,unroll=2)
-    each(gb,"middle")
+    each(gb,"middle"); cols.middle(); ccol.middle()
     def chain(n,S):
         s_ref[n]=S
         sh,sl=halves(S); mh=mh_ref[n]; ml=ml_ref[n]
@@ -224,7 +230,7 @@
     outward=FromPairs(n,copies,heads,local_len,[(o_ref,lambda t: (pl.ds(pl.multiple_of(t*local_len,local_len),local_len),slice(None)),
         oall,lambda seq,head: (pl.ds(pl.multiple_of(seq*local_len,local_len),local_len),pl.ds(pl.multiple_of(head*DV,128),DV)))],os_,or_)
     outward.start()
-    each(gb,"late"); cols.finish(); ccol.finish(); gb[0].finish()
+    gb[0].late(); gb[1].late(); gb[0].finish()
     width=wg.shape[1]
     c=pltpu.make_async_copy(wgfull,wbuf.at[:,pl.ds(0,width)],ld.at[0]); c.start(); c.wait()
     def column(j,_):
@@ -253,15 +259,57 @@
         part[:,pl.ds(pl.multiple_of(j*256,256),256)]=jnp.dot(branch[...],w,preferred_element_type=f32).astype(bf16)
         return 0
     lax.fori_loop(0,D//256,column,0)
-
-def backward_kernel(n,copies,heads,dall,u_ref,taps_ref,xc_ref,xr_ref,starts2,dlog,dbias,q_ref,k_ref,v_ref,s_ref,w_ref,t_ref,qt_ref,mh_ref,ml_ref,hid,bra,dgp,
-                    duall,rows_out,dtaps_ref,dh_ref,hidfull,brafull,dgpfull,upad,dpre,ds_ref,dqkv,r_ref,gc_ref,do_ref,du_ref,dx_ref,dxr,is_,ir,os_,or_,*gs):
+    gb[2].late(); cols.finish(); ccol.finish(); gb[2].finish()
+
+def back_kernel(n,zc,copies,heads,total_heads,afull,gate_ref,oall,hgain,tok,scale,gain,res,gres,gffn,taps_ref,u_ref,xc_ref,xr_ref,starts2,dlog,dbias,
+                q_ref,k_ref,v_ref,s_ref,w_ref,t_ref,qt_ref,mh_ref,ml_ref,wofull,wfull,wgfull,outpart,branch,hidfull,dgfull,dufull,n2c,n1c,cotc,
+                output,gtok,smalls,totals,ogate,oup,odown,oout,oog,dyqfull,dsmfull,brafull,dgpfull,attc,
+                upad,dpre,ds_ref,gc_ref,do_ref,du_ref,dx_ref,dxr,bufa,bufb,cola,colb,colc,dob,dgp,dyq,rbuf,dsm,part,upart,box,boxo,sums,
+                is_,ir,os_,or_,as_,ar,bs,br,cs,cr,es,er,fs,fr,hs,hr,zs,zr,ld,*gs):
     L=u_ref.shape[0]; NC=L//SPAN; DV=v_ref.shape[1]; DK=q_ref.shape[1]; local_len=L//n; per=local_len//SPAN
-    greet(n,1)
-    inward=ToPairs(n,copies,heads,local_len,dall,None,do_ref,None,DK,DV,is_,ir); inward.start()
-    gw=gathers(n,[(hid,hidfull,0),(bra,brafull,0),(dgp,dgpfull,0)],gs)
-    pair=lax.div(lax.axis_index("seq"),copies)
-    starts=Row(starts2,lax.div(pair,heads)); at_head=lax.axis_index("shard")*heads+lax.rem(pair,heads)
+    rows_n=tok.shape[0]; F=tok.shape[1]; D=F*zc; VW=wofull.shape[0]; FF=dgfull.shape[1]; wk=heads*DK; wv=heads*DV
+    bufs=(bufa,bufb)
+    loads={}
+    def load_job(key,i,pieces):
+        loads[key]=[]
+        for j,(src,at) in enumerate(pieces):
+            c=pltpu.make_async_copy(src,bufs[i].at[at],ld.at[i,j]); c.start(); loads[key].append(c)
+    def ready(key):
+        for c in loads[key]: c.wait()
+    whole=lambda w: (pl.ds(0,D),pl.ds(0,w))
+    every=lambda w: (pl.ds(0,n*rows_n),pl.ds(0,w))
+    N=n*rows_n
+    load_job("wo",0,[(wofull.at[:,pl.ds(j*VW,VW)],(pl.ds(j*VW,VW),pl.ds(0,VW))) for j in range(D//VW)])
+    load_job("og",1,[(wgfull,whole(wv))])
+    greet(n,zc)
+    so=ShardSplit(zc,outpart,boxo,fs,fr); so.start()
+    ready("wo")
+    dsm[...]=jnp.zeros(dsm.shape,bf16)
+    def heads_back(c,gh):
+        r=pl.ds(pl.multiple_of(c*64,64),64)
+        for h in range(heads):
+            cc=pl.ds(h*DV,DV)
+            dm=dg(afull[r,0:VW],bufa[h*DV:(h+1)*DV,0:VW],1,1)
+            for j in range(1,D//VW):
+                dm=dm+dg(afull[r,j*VW:(j+1)*VW],bufa[j*VW+h*DV:j*VW+(h+1)*DV,0:VW],1,1)
+            dm=dm.astype(bf16).astype(f32)
+            o=oall[r,cc].astype(f32); g=gate_ref[r,cc]
+            rho=lax.rsqrt(jnp.sum(o*o,axis=1,keepdims=True)/DV+EPSILON)
+            z=o*rho; sg=sigmoid(g); sil=g*sg
+            gh=gh+jnp.sum(dm*z*sil,axis=0,keepdims=True)
+            dmg=dm*hgain[...]
+            dz=dmg*sil
+            dob[r,cc]=(rho*(dz-z*(jnp.sum(dz*z,axis=1,keepdims=True)/DV))).astype(bf16)
+            dgp[r,cc]=(dmg*z*sg*(1.0+g*(1.0-sg))).astype(bf16)
+        return gh
+    gh=lax.fori_loop(0,rows_n//64,heads_back,jnp.zeros((1,DV),f32))
+    inward=ToPairs(n,copies,heads,local_len,dob,None,do_ref,None,DK,DV,is_,ir); inward.start()
+    load_job("dgate",0,[(dgfull,every(FF))])
+    c2=pltpu.make_async_copy(n2c,cola,ld.at[0,4]); c2.start()
+    g1,g2=gs[:3],gs[3:]
+    gw=gathers(n,[(dgp,dgpfull,0),(branch,brafull,0)],g1)
+    pair=lax.div(lax.axis_index("seq"),copies); my_head=lax.rem(pair,heads)
+    starts=Row(starts2,lax.div(pair,heads)); at_head=lax.axis_index("shard")*heads+my_head
     rate=jnp.exp(jnp.full((1,1),dlog[at_head],f32)); bias=dbias[at_head]
     taps=taps_ref[...]
     R=128
@@ -273,10 +321,11 @@
     lax.fori_loop(0,L//R,load,0)
     inward.finish()
     each(gw,"start")
+    ca=SharedColumns(n,zc,afull,attc,(es,er,zs,zr)); ca.start()
     dx_ref[...]=jnp.zeros(dx_ref.shape,f32)
     def early(n,_):
         rows=pl.ds(pl.multiple_of(n*SPAN,SPAN),SPAN)
-        r_ref[n]=dg(qt_ref[n][0:SPAN],do_ref[rows,:],0,0)
+        ds_ref[n]=dg(qt_ref[n][0:SPAN],do_ref[rows,:],0,0)
         base=n*SPAN
         G=jnp.sum(-rate*softplus(xc_ref[rows,1:2]+bias),axis=0,keepdims=True)
         alive=jnp.where(count_at(starts,base+SPAN-1)==count_at(starts,base-1),1.0,0.0)
@@ -285,12 +334,13 @@
     lax.fori_loop(0,NC,early,0,unroll=4)
     def chain(m,dS):
         n=NC-1-m
+        r=ds_ref[n]
         ds_ref[n]=dS
         sh,sl=halves(dS); mh=mh_ref[n]; ml=ml_ref[n]
         gc=gc_ref[n][0:1]
-        return jnp.concatenate([gc]*(DV//128),axis=1)*dS+r_ref[n]-(dg(mh,sh,0,0)+(dg(ml,sh,0,0)+dg(mh,sl,0,0)))
+        return jnp.concatenate([gc]*(DV//128),axis=1)*dS+r-(dg(mh,sh,0,0)+(dg(ml,sh,0,0)+dg(mh,sl,0,0)))
     lax.fori_loop(0,NC,chain,jnp.zeros((DK,DV),f32),unroll=2)
-    each(gw,"middle")
+    each(gw,"middle"); ca.middle()
     def one_span(n,xr,sums):
         rows=pl.ds(pl.multiple_of(n*SPAN,SPAN),SPAN)
         q=q_ref[rows,:]; k=k_ref[rows,:]; v=v_ref[rows,:]; dO=do_ref[rows,:]
@@ -314,9 +364,9 @@
         A1=jnp.concatenate([dPD,E],axis=0).astype(bf16)
         r1=dg(A1,k)
         r2=dg(A1,jnp.concatenate([q,k],axis=0),0,0)
-        dqkv[rows,0:DK]=gam*dOS+r1[:SPAN]
-        dqkv[rows,DK:2*DK]=r1[SPAN:]+r2-(beta*gam)*YS+end*Z
-        dqkv[rows,2*DK:]=beta*Y
+        dpre[rows,0:DK]=gam*dOS+r1[:SPAN]
+        dpre[rows,DK:2*DK]=r1[SPAN:]+r2-(beta*gam)*YS+end*Z
+        dpre[rows,2*DK:]=beta*Y
         EK=EA*KK
         kYS=jnp.sum(kf*YS,axis=1,keepdims=True)
         dbeta=jnp.sum(Y*vf,axis=1,keepdims=True)-gam*kYS+jnp.sum(EK,axis=1,keepdims=True)
@@ -347,14 +397,13 @@
         dxr[pl.ds(pl.multiple_of(m*8,8),8),:]=flat_form(dx_ref[pl.ds(pl.multiple_of(m*local_len,local_len),local_len),:])
         return 0
     lax.fori_loop(0,n,turn,0,unroll=2)
-    dh_ref[0:1]=sl; dh_ref[1:2]=sb
     def norms(c,dt):
         base=pl.multiple_of(c*R,R)
         age=doc_age(starts,positions(base,R,128,0))[:,0:1]
         pre=conv_pre(upad,taps,age,base,R)
         sg=sigmoid(pre); act=pre*sg
         rows=pl.ds(base,R)
-        d=dqkv[rows,:]
+        d=dpre[rows,:]
         def unit_back(a,dd,f):
             s=lax.rsqrt(jnp.sum(a*a,axis=1,keepdims=True)+EPSILON)
             dot=jnp.sum(a*dd,axis=1,keepdims=True)
@@ -372,7 +421,11 @@
         return tuple(new)
     zt=jnp.zeros((1,upad.shape[1]),f32)
     dt=lax.fori_loop(0,L//R,norms,(zt,)*4)
-    for j in range(4): dtaps_ref[j:j+1]=dt[j]
+    each(gw,"late")
+    so.finish()
+    y=res[...]
+    for d in range(zc): y=y+boxo[d].astype(f32)
+    output[...]=y
     def back(c,_):
         base=pl.multiple_of(c*R,R)
         window=dpre[pl.ds(base,R+8),:]
@@ -384,39 +437,163 @@
         du_ref[pl.ds(base,R),:]=d.astype(bf16)
         return 0
     lax.fori_loop(0,L//R,back,0)
-    wk=heads*DK
-    at=lambda start,width: (lambda t: (pl.ds(pl.multiple_of(t*local_len,local_len),local_len),pl.ds(start,width)))
+    cut=lambda start,width: (lambda t: (pl.ds(pl.multiple_of(t*local_len,local_len),local_len),pl.ds(start,width)))
     to=lambda start,width: (lambda seq,head: (pl.ds(pl.multiple_of(seq*local_len,local_len),local_len),pl.ds(pl.multiple_of(start+head*width,128),width)))
-    outward=FromPairs(n,copies,heads,local_len,[(du_ref,at(0,DK),duall,to(0,DK)),(du_ref,at(DK,DK),duall,to(wk,DK)),(du_ref,at(2*DK,DV),duall,to(2*wk,DV)),
-        (dxr,lambda t: (pl.ds(pl.multiple_of(t*8,8),8),slice(None)),rows_out,lambda seq,head: (pl.ds(pl.multiple_of((seq*heads+head)*8,8),8),slice(None)))],os_,or_)
+    outward=FromPairs(n,copies,heads,local_len,[(du_ref,cut(0,DK),dyq,to(0,DK)),(du_ref,cut(DK,DK),dyq,to(wk,DK)),(du_ref,cut(2*DK,DV),dyq,to(2*wk,DV)),
+        (dxr,lambda t: (pl.ds(pl.multiple_of(t*8,8),8),slice(None)),rbuf,lambda seq,head: (pl.ds(pl.multiple_of((seq*heads+head)*8,8),8),slice(None)))],os_,or_)
     outward.start()
-    each(gw,"late"); outward.finish(); each(gw,"finish")
+    def tiles(width,step): return [(a,min(a+step,width)) for a in range(0,width,step)]
+    def spread(first,buf,terms):
+        def one(j,_):
+            rr=pl.ds(pl.multiple_of(j*256,256),256)
+            t=0.0
+            for x,a,b in terms: t=t+dg(x[...],buf[rr,a:b],1,1)
+            part[:,rr]=t if first else part[:,rr]+t
+            return 0
+        lax.fori_loop(0,D//256,one,0)
+    ready("og"); spread(True,bufb,[(dgp,0,wv)])
+    load_job("dup",1,[(dufull,every(FF))])
+    ready("dgate"); c2.wait()
+    for a,b in tiles(FF,512): ogate[:,a:b]=dg(cola[...],bufa[0:N,a:b],0,0)
+    load_job("wv",0,[(wfull.at[:,pl.ds(2*wk,wv+128)],whole(wv+128))])
+    outward.finish()
+    for sq in range(rows_n//local_len):
+        fl=[]
+        for e in range(2):
+            for h in range(heads): fl.append(rbuf[(sq*heads+h)*8+e:(sq*heads+h)*8+e+1])
+        fl=jnp.concatenate(fl+[jnp.zeros((-2*heads%8,local_len),f32)]*(1 if 2*heads%8 else 0),axis=0)
+        dsm[sq*local_len:(sq+1)*local_len,0:fl.shape[0]]=col_form(fl).astype(bf16)
+    gd=gathers(n,[(dsm,dsmfull,0),(dyq,dyqfull,0)],g2)
+    each(gd,"start")
+    ready("wv"); spread(False,bufa,[(dyq.at[:,pl.ds(2*wk,wv)],0,wv),(dsm,wv,wv+128)])
+    ready("dup")
+    for a,b in tiles(FF,512): oup[:,a:b]=dg(cola[...],bufb[0:N,a:b],0,0)
+    load_job("wqk",1,[(wfull.at[:,pl.ds(0,2*wk)],whole(2*wk))])
+    load_job("hid",0,[(hidfull,every(FF))])
+    cc_=pltpu.make_async_copy(cotc,colb,ld.at[1,5]); cc_.start()
+    ready("wqk")
+    def last(j,_):
+        rr=pl.ds(pl.multiple_of(j*256,256),256)
+        upart[:,rr]=(part[:,rr]+dg(dyq[:,0:2*wk],bufb[rr,0:2*wk],1,1)).astype(bf16)
+        return 0
+    lax.fori_loop(0,D//256,last,0)
+    split=ShardSplit(zc,upart,box,as_,ar); split.start()
+    each(gd,"middle")
+    for g in gw: g.finish()
+    ca.finish()
+    load_job("bra",1,[(brafull,every(VW))])
+    ready("hid"); cc_.wait()
+    cots=colb[...].reshape(n*rows_n,colb.shape[2])
+    for a,b in tiles(FF,256): odown[a:b,:]=dg(bufa[0:N,a:b],cots,0,0)
+    load_job("dgp",0,[(dgpfull,every(wv))])
+    cc_=pltpu.make_async_copy(attc,colb,ld.at[1,5]); cc_.start()
+    c2=pltpu.make_async_copy(n1c,colc,ld.at[0,4]); c2.start()
+    ready("bra"); cc_.wait()
+    atts=colb[...].reshape(n*rows_n,colb.shape[2])
+    for a,b in tiles(VW,256): oout[a:b,:]=dg(bufb[0:N,a:b],atts,0,0)
+    split.finish()
+    g=box[0].astype(f32)
+    for d in range(1,zc): g=g+box[d].astype(f32)
+    x=tok[...].astype(f32); sc=scale[...][:,0:1]
+    z=lax.axis_index("shard")
+    gained=gain[:,pl.ds(pl.multiple_of(z*F,128),F)]*g
+    sums[z]=row_form(gained*x)
+    tot=ShardAll("shard",zc,sums,bs,br); tot.start()
+    me=lax.axis_index("seq")
+    W=smalls.shape[2]
+    smalls[me]=jnp.zeros(smalls.shape[1:],f32)
+    smalls[me,0:1,0:F]=jnp.sum(g*x*sc,axis=0,keepdims=True)
+    smalls[me,1:2,0:F]=gffn[0:1]
+    smalls[me,2:3,0:DV]=gh
+    lane=lax.broadcasted_iota(jnp.int32,(1,128),1)
+    first=jnp.where(lax.rem(me,copies)==0,1.0,0.0)
+    smalls[me,3:4,0:128]=first*(jnp.where(lane==at_head,sl,0.0)+jnp.where(lane==total_heads+at_head,sb,0.0))
+    for j in range(4): smalls[me,4+j:5+j,0:2*DK+DV]=dt[j]
+    sa=ShardAll("seq",n,smalls,cs,cr); sa.start()
+    tot.finish()
+    t=sums[0]
+    for d in range(1,zc): t=t+sums[d]
+    inner=col_form(t)[:,0:1]/D
+    gtok[...]=gres[...]+sc*(gained-x*(sc*sc*inner))
+    ready("dgp"); c2.wait()
+    n1=colc[...].reshape(n*rows_n,colc.shape[2])
+    for a,b in tiles(wv,512): oog[:,a:b]=dg(n1,bufa[0:N,a:b],0,0)
+    sa.finish()
+    t=smalls[0]
+    for d in range(1,n): t=t+smalls[d]
+    totals[z]=t
+    za=ShardAll("shard",zc,totals,hs,hr); za.start()
+    each(gd,"late"); za.finish(); each(gd,"finish")
 
 SM=pl.BlockSpec(memory_space=pltpu.SMEM); VM=pl.BlockSpec(memory_space=pltpu.VMEM)
 def S(shape,dt=f32): return jax.ShapeDtypeStruct(shape,dt)
-def forward(n,zc,copies,heads,tok,cot,gain,hgain,starts,dlog,dbias,wq,wk,wv,ws,wg,wo,DK,DV):
+def forward(n,zc,copies,heads,tok,cot,gain,hgain,starts,dlog,dbias,wb,wd,qc,kc,vc,wq,wk,wv,wg,wo,wgate,DK,DV):
     R,F=tok.shape; D=F*zc; local_len=R//starts.shape[0]; L=n*local_len; NC=L//SPAN; pairs=n//copies; CH=2*DK+DV; HV=heads*DV
     rows=lambda *w: S((w[0].shape[0]*n,sum(x.shape[1] for x in w)),bf16)
     wide=max(wv.shape[1],wg.shape[1])
-    return call("mixer",5,functools.partial(forward_kernel,n,zc,copies,heads,DK,DV),(tok,cot,gain,hgain,starts,dlog,dbias,wq,wk,wv,ws,wg,wo),[VM,VM,VM,VM,SM,SM,SM]+[ANY]*6,
-      [S((R,D),bf16),S((R,128)),S((R,D),bf16),rows(wq,wk,wv,ws),rows(wg),S((wo.shape[0],wo.shape[1]*n),bf16),S((R*n,D//n),bf16),S((R*n,D//n),bf16),
+    small=S((D//n,128),bf16)
+    return call("mixer",5,functools.partial(forward_kernel,n,zc,copies,heads,DK,DV),(tok,cot,gain,hgain,starts,dlog,dbias,wb,wd,qc,kc,vc,wq,wk,wv,wg,wo,wgate),[VM,VM,VM,VM,SM,SM,SM]+[VM]*5+[ANY]*6,
+      [S((R,128)),S((R,D),bf16),rows(wq,wk,wv,small),rows(wg),S((wo.shape[0],wo.shape[1]*n),bf16),rows(wgate),S((n,R,D//n),bf16),S((n,R,D//n),bf16),
        S((R,HV)),S((R,HV),bf16),S((R,HV),bf16),S((R,D),bf16),S((4,CH)),
        S((L,CH),bf16),S((n*8,local_len)),S((L,8)),S((L,DK),bf16),S((L,DK),bf16),S((L,DV),bf16),S((NC,DK,DV)),S((NC,SPAN,DV)),S((NC,SPAN,SPAN)),
        S((NC,2*SPAN,DK),bf16),S((NC,DK,DK),bf16),S((NC,DK,DK),bf16)],
-      [VM,VM]+[ANY]*6+[VM]*17,
-      [pltpu.VMEM((R,D),bf16),pltpu.VMEM((D,wide),bf16),pltpu.VMEM((D,ws.shape[1]),bf16),pltpu.VMEM((R,heads*CH),bf16),pltpu.VMEM((pairs*8,local_len),f32),pltpu.VMEM((CH,128),bf16),
+      [VM]+[ANY]*7+[VM]*17,
+      [pltpu.VMEM((R,D),bf16),pltpu.VMEM((R,D),bf16),pltpu.VMEM((D//n,128),bf16),pltpu.VMEM((D,wide),bf16),pltpu.VMEM((D,128),bf16),pltpu.VMEM((R,heads*CH),bf16),pltpu.VMEM((pairs*8,local_len),f32),pltpu.VMEM((CH,128),bf16),
        pltpu.VMEM((L+8,CH),f32),pltpu.VMEM((NC,DK,DV),f32),pltpu.VMEM((NC,8,128),f32),pltpu.VMEM((NC,SPAN,DV),f32),pltpu.VMEM((L,DV),bf16)]
-      +pair_sems(zc)*2+pair_sems(n)*2+[pltpu.SemaphoreType.DMA((4,n)),pltpu.SemaphoreType.DMA((4,n)),pltpu.SemaphoreType.DMA((1,pairs)),pltpu.SemaphoreType.DMA((1,pairs)),pltpu.SemaphoreType.DMA((D//wide,))]
-      +gather_sems(n,4)+gather_sems(n,2))
-def backward(n,copies,heads,dall,taps,starts,dlog,dbias,saved,hid,bra,dgp):
+      +pair_sems(zc)*2+pair_sems(n)*2+pair_sems(zc)*2+[pltpu.SemaphoreType.DMA((4,n)),pltpu.SemaphoreType.DMA((4,n)),pltpu.SemaphoreType.DMA((1,pairs)),pltpu.SemaphoreType.DMA((1,pairs)),pltpu.SemaphoreType.DMA((D//wide,))]
+      +gather_sems(n,4)+gather_sems(n,3))
+def back(n,zc,copies,heads,total_heads,afull,gate,oall,hgain,tok,scale,gain,res,gres,gffn,taps,saved,starts,dlog,dbias,wofull,wfull,wgfull,outpart,branch,hidfull,dgfull,dufull,n2c,n1c,cotc):
     u,xr,xc,q,k,v,s,w,t,qt,mh,ml=saved
-    L,CH=u.shape; NC=L//SPAN; DK=q.shape[1]; DV=v.shape[1]; local_len=L//n; pairs=n//copies; R=dall.shape[0]
-    full=lambda a: S((a.shape[0]*n,a.shape[1]),bf16)
-    return call("rec_bwd",6,functools.partial(backward_kernel,n,copies,heads),(dall,u,taps,xc,xr,starts,dlog,dbias,q,k,v,s,w,t,qt,mh,ml,hid,bra,dgp),[ANY]+[VM]*4+[SM]*3+[VM]*9+[ANY]*3,
-      [S((R,heads*CH),bf16),S((pairs*8,local_len)),S((4,CH)),S((2,128)),full(hid),full(bra),full(dgp)],[ANY,ANY,VM,VM,ANY,ANY,ANY],
-      [pltpu.VMEM((L+8,CH),f32),pltpu.VMEM((L+8,CH),f32),pltpu.VMEM((NC,DK,DV),f32),pltpu.VMEM((L,CH),f32),pltpu.VMEM((NC,DK,DV),f32),pltpu.VMEM((NC,8,128),f32),
+    L,CH=u.shape; NC=L//SPAN; DK=q.shape[1]; DV=v.shape[1]; local_len=L//n; pairs=n//copies; R,F=tok.shape; D=F*zc; FF=dgfull.shape[1]; HV=heads*DV; VW=wofull.shape[0]
+    Dc=D//n; W=max(F,CH)
+    bw=max(FF,HV+128,VW,2*heads*DK)
+    ins=(afull,gate,oall,hgain,tok,scale,gain,res,gres,gffn,taps,u,xc,xr,starts,dlog,dbias,q,k,v,s,w,t,qt,mh,ml,wofull,wfull,wgfull,outpart,branch,hidfull,dgfull,dufull,n2c,n1c,cotc)
+    sem=pltpu.SemaphoreType.DMA
+    return call("back",6,functools.partial(back_kernel,n,zc,copies,heads,total_heads),ins,[VM]*14+[SM]*3+[VM]*9+[ANY]*11,
+      [S((R,F)),S((R,F)),S((n,8,W)),S((zc,8,W)),S((Dc,FF)),S((Dc,FF)),S((FF,Dc)),S((VW,Dc)),S((Dc,HV)),S((R*n,heads*CH),bf16),S((R*n,128),bf16),S((R*n,HV),bf16),S((R*n,HV),bf16),S((n,R,Dc),bf16)],
+      [VM]*9+[ANY]*5,
+      [pltpu.VMEM((L+8,CH),f32),pltpu.VMEM((L+8,CH),f32),pltpu.VMEM((NC,DK,DV),f32),pltpu.VMEM((NC,8,128),f32),
        pltpu.VMEM((L,DV),bf16),pltpu.VMEM((L,CH),bf16),pltpu.VMEM((L,8),f32),pltpu.VMEM((n*8,local_len),f32),
-       pltpu.SemaphoreType.DMA((4,n)),pltpu.SemaphoreType.DMA((4,n)),pltpu.SemaphoreType.DMA((4,pairs)),pltpu.SemaphoreType.DMA((4,pairs))]+gather_sems(n,3))
+       pltpu.VMEM((max(D,R*n),bw),bf16),pltpu.VMEM((max(D,R*n),bw),bf16),pltpu.VMEM((R*n,Dc),bf16),pltpu.VMEM((n,R,Dc),bf16),pltpu.VMEM((n,R,Dc),bf16),
+       pltpu.VMEM((R,HV),bf16),pltpu.VMEM((R,HV),bf16),pltpu.VMEM((R,heads*CH),bf16),pltpu.VMEM((pairs*8,local_len),f32),pltpu.VMEM((R,128),bf16),pltpu.VMEM((R,D),f32),pltpu.VMEM((R,D),bf16),
+       pltpu.VMEM((zc,R,F),bf16),pltpu.VMEM((zc,R,F),bf16),pltpu.VMEM((zc,8,R),f32)]
+      +[sem((1,n)),sem((1,n)),sem((4,pairs)),sem((4,pairs))]+pair_sems(zc)*2+pair_sems(n)*2+pair_sems(zc)*3+[sem((2,6))]+gather_sems(n,2)+gather_sems(n,2))
+
+def last_kernel(n,copies,heads,DK,DV,F,H,n1c,dyq,dsm,smalls,totals,oq,ok,ov,ob,od,qc,kc,vc,onorm,offn,ohead,olog,obias):
+    n1=n1c[...].reshape(n1c.shape[0]*n1c.shape[1],n1c.shape[2])
+    wk=heads*DK
+    for ref,start in ((oq,0),(ok,wk),(ov,2*wk)):
+        width=ref.shape[1]
+        for a in range(0,width,512):
+            b=min(a+512,width)
+            ref[:,a:b]=dg(n1,dyq[:,start+a:start+b],0,0)
+    sm=dg(n1,dsm[...],0,0)
+    ob[...]=sm[:,0:heads]; od[...]=sm[:,heads:2*heads]
+    zc=totals.shape[0]
+    for z in range(zc):
+        onorm[0:1,z*F:(z+1)*F]=totals[z,0:1,0:F]
+        offn[0:1,z*F:(z+1)*F]=totals[z,1:2,0:F]
+    t=totals[0]
+    for z in range(1,zc): t=t+totals[z]
+    ohead[...]=t[2:3,0:DV]
+    olog[...]=t[3:4,0:H]; obias[...]=t[3:4,H:2*H]
+    s=lax.axis_index("seq")
+    head=lax.div(s*heads,n)
+    taps=0.0
+    for sq in range(n//copies//heads): taps=taps+smalls[(sq*heads+head)*copies]
+    cols=col_form(taps)
+    cq,cv=qc.shape[0],vc.shape[0]
+    for part in range(n//heads):
+        @pl.when(lax.rem(s,n//heads)==part)
+        def _():
+            qc[...]=cols[part*cq:(part+1)*cq,4:8]
+            kc[...]=cols[DK+part*cq:DK+(part+1)*cq,4:8]
+            vc[...]=cols[2*DK+part*cv:2*DK+(part+1)*cv,4:8]
+def last(n,copies,heads,DK,DV,F,H,n1c,dyq,dsm,smalls,totals,cq,cv):
+    D=F*totals.shape[0]; Dc=n1c.shape[2]
+    return pl.pallas_call(functools.partial(last_kernel,n,copies,heads,DK,DV,F,H),name="last",
+      out_shape=(S((Dc,heads*DK)),S((Dc,heads*DK)),S((Dc,heads*DV)),S((Dc,heads)),S((Dc,heads)),S((cq,4)),S((cq,4)),S((cv,4)),S((1,D)),S((1,D)),S((1,DV)),S((1,H)),S((1,H))),
+      in_specs=[VM]*5,out_specs=(VM,)*13,compiler_params=pltpu.CompilerParams(vmem_limit_bytes=56*2**20))(n1c,dyq,dsm,smalls,totals)
 
 
 MESH=pl.DeviceIdType.MESH
@@ -603,6 +780,29 @@
     i=lax.broadcasted_iota(jnp.int32,(r,r),0); j=lax.broadcasted_iota(jnp.int32,(r,r),1)
     return mmx(cols,jnp.where(i==j,1.0,0.0),0,0)
 
+class SharedColumns:
+    def __init__(self,n,zc,src,dst,sems):
+        self.n=n; self.zc=zc; self.src=src; self.dst=dst; self.send,self.recv,self.zsend,self.zrecv=sems
+        self.s=lax.axis_index("seq"); self.z=lax.axis_index("shard"); self.C=dst.shape[2]; self.q=src.shape[0]//zc
+    def start(self):
+        rows=pl.ds(pl.multiple_of(self.z*self.q,16),self.q)
+        block=lambda t: self.src.at[rows,pl.ds(pl.multiple_of(t*self.C,128),self.C)]
+        self.cs=[]
+        for d in range(self.n):
+            t=lax.rem(self.s+d,self.n)
+            if d==0: c=pltpu.make_async_copy(block(t),self.dst.at[self.s,rows,:],self.recv.at[0])
+            else: c=pltpu.make_async_remote_copy(src_ref=block(t),dst_ref=self.dst.at[self.s,rows,:],send_sem=self.send.at[d],recv_sem=self.recv.at[d],device_id={"seq":t},device_id_type=MESH)
+            c.start(); self.cs.append(c)
+    def middle(self):
+        for c in self.cs: c.wait()
+        strip=self.dst.at[:,pl.ds(pl.multiple_of(self.z*self.q,16),self.q),:]
+        self.cs=[]
+        for d in range(1,self.zc):
+            c=pltpu.make_async_remote_copy(src_ref=strip,dst_ref=strip,send_sem=self.zsend.at[d],recv_sem=self.zrecv.at[d],device_id={"shard":lax.rem(self.z+d,self.zc)},device_id_type=MESH)
+            c.start(); self.cs.append(c)
+    def finish(self):
+        for c in self.cs: c.wait()
+
 def row_form(cols):
     return mmx(jnp.ones((8,cols.shape[1]),f32),cols,1,1)
 
@@ -621,14 +821,16 @@
 def each(ops,name):
     for o in ops: getattr(o,name)()
 
-def ffn_kernel(n,zc,part,tok,cot,cotfull,gain,wg,wu,wd,res,gres,afull,gffn,outpart,hidden,dgfull,dufull,n2c,
-               box,sums,nloc,nfull,gw_,uw_,dw_,gv,uv,dgate,dup,two,as_,ar,bs,br,cs,cr,ds_,dr,es,er,fs,fr,hs,hr,*gs):
+def ffn_kernel(n,zc,part,tok,cot,cotfull,gain_all,wgfull,wu,wd,res,gres,afull,gffn,outpart,hidfull,dgfull,dufull,n2c,
+               box,sums,nloc,nfull,gw_,uw_,dw_,gv,uv,hidden,dgate,dup,two,ld,as_,ar,bs,br,cs,cr,ds_,dr,es,er,fs,fr,hs,hr,*gs):
     greet(n,zc)
     D=part.shape[1]; R=part.shape[0]; FF=gv.shape[1]; z=lax.axis_index("shard")
     split=ShardSplit(zc,part,box,as_,ar); split.start()
     g1,g2=gs[:3],gs[3:]
-    gw=gathers(n,[(wg,gw_,0),(wu,uw_,0),(wd,dw_,1)],g1)
+    gw=gathers(n,[(wu,uw_,0),(wd,dw_,1)],g1)
     each(gw,"start")
+    lg=pltpu.make_async_copy(wgfull,gw_,ld.at[0]); lg.start()
+    gain=gain_all[:,pl.ds(pl.multiple_of(z*tok.shape[1],128),tok.shape[1])]
     split.finish()
     r=tok[...].astype(f32)
     for d in range(zc): r=r+box[d].astype(f32)
@@ -638,15 +840,15 @@
     t=sums[0]
     for d in range(1,zc): t=t+sums[d]
     sc=lax.rsqrt(col_form(t)[:,0:1]/D+EPSILON)
-    nloc[...]=(r*sc*gain[...]).astype(bf16)
+    nloc[...]=(r*sc*gain).astype(bf16)
     zg=ShardGather(zc,nloc,nfull,cs,cr); zg.start()
     each(gw,"middle")
     zg.finish()
     cols=ColumnSplit(n,nfull,n2c,es,er); cols.start()
     tiles=[(a,min(a+512,FF)) for a in range(0,FF,512)]
+    lg.wait()
+    for a,b in tiles: gv[:,a:b]=jnp.dot(nfull[...],gw_[:,a:b],preferred_element_type=f32)
     gw[0].late(); gw[0].finish()
-    for a,b in tiles: gv[:,a:b]=jnp.dot(nfull[...],gw_[:,a:b],preferred_element_type=f32)
-    gw[1].late(); gw[1].finish()
     for a,b in tiles: uv[:,a:b]=jnp.dot(nfull[...],uw_[:,a:b],preferred_element_type=f32)
     def act(c,_):
         rr=pl.ds(pl.multiple_of(c*32,32),32)
@@ -654,14 +856,16 @@
         hidden[rr,:]=(g*sigmoid(g)*uv[rr,:]).astype(bf16)
         return 0
     lax.fori_loop(0,R//32,act,0)
-    gw[2].late(); gw[2].finish()
+    gh=gathers(n,[(hidden,hidfull,0),(dgate,dgfull,0),(dup,dufull,0)],g2)
+    gh[0].start()
+    gw[1].late(); gw[1].finish()
     for a,b in tiles:
         dh=dg(cotfull[...],dw_[a:b,:],1,1)
         g=gv[:,a:b]; sg=sigmoid(g)
         dgate[:,a:b]=(dh*uv[:,a:b]*sg*(1.0+g*(1.0-sg))).astype(bf16)
         dup[:,a:b]=(dh*(g*sg)).astype(bf16)
-    gd=gathers(n,[(dgate,dgfull,0),(dup,dufull,0)],g2)
-    each(gd,"start")
+    gd=gh
+    each(gd[1:],"start")
     def back(j,_):
         rr=pl.ds(pl.multiple_of(j*256,256),256)
         two[:,rr]=(dg(dgate[...],gw_[rr,:],1,1)+dg(dup[...],uw_[rr,:],1,1)).astype(bf16)
@@ -678,7 +882,7 @@
     g=box[0].astype(f32)
     for d in range(1,zc): g=g+box[d].astype(f32)
     r=res[...]
-    gained=gain[...]*g
+    gained=gain*g
     sums[zc+z]=row_form(gained*r)
     tot=ShardAll("shard",zc,sums.at[pl.ds(zc,zc)],ds_,dr); tot.start()
     gffn[...]=jnp.broadcast_to(jnp.sum(g*r*sc,axis=0,keepdims=True),gffn.shape)
@@ -694,62 +898,18 @@
     zg.finish()
     each(gd,"late"); cols.finish(); each(gd,"finish")
 
-def tail_kernel(n,zc,partdx,partout,res,gres,tok,scale,gain,small,dy,dsm,att,output,gtok,dyfull,dsmfull,attc,smalls,totals,box,boxo,sums,as_,ar,bs,br,cs,cr,es,er,fs,fr,hs,hr,*gs):
-    greet(n,zc)
-    D=partdx.shape[1]
-    split=ShardSplit(zc,partdx,box,as_,ar); split.start()
-    gw=gathers(n,[(dy,dyfull,0),(dsm,dsmfull,0)],gs)
-    each(gw,"start")
-    ca=ColumnSplit(n,att,attc,es,er); ca.start()
-    split.finish()
-    so=ShardSplit(zc,partout,boxo,fs,fr); so.start()
-    g=box[0].astype(f32)
-    for d in range(1,zc): g=g+box[d].astype(f32)
-    x=tok[...].astype(f32); sc=scale[...][:,0:1]
-    gained=gain[...]*g
-    sums[lax.axis_index("shard")]=row_form(gained*x)
-    tot=ShardAll("shard",zc,sums,bs,br); tot.start()
-    me=lax.axis_index("seq")
-    smalls[me]=small[...]
-    smalls[me,0:1,0:g.shape[1]]=jnp.sum(g*x*sc,axis=0,keepdims=True)
-    sa=ShardAll("seq",n,smalls,cs,cr); sa.start()
-    tot.finish()
-    t=sums[0]
-    for d in range(1,zc): t=t+sums[d]
-    inner=col_form(t)[:,0:1]/D
-    gtok[...]=gres[...]+sc*(gained-x*(sc*sc*inner))
-    sa.finish()
-    t=smalls[0]
-    for d in range(1,n): t=t+smalls[d]
-    totals[lax.axis_index("shard")]=t
-    za=ShardAll("shard",zc,totals,hs,hr); za.start()
-    each(gw,"middle")
-    so.finish()
-    o=res[...]
-    for d in range(zc): o=o+boxo[d].astype(f32)
-    output[...]=o
-    za.finish()
-    each(gw,"late"); ca.finish(); each(gw,"finish")
-
 def call(name,cid,kernel,args,specs,outs,ospecs,scratch):
     return pl.pallas_call(kernel,name=name,out_shape=tuple(outs),in_specs=specs,out_specs=tuple(ospecs),scratch_shapes=scratch,
-      compiler_params=pltpu.CompilerParams(collective_id=cid,has_side_effects=True,vmem_limit_bytes=56*2**20))(*args)
-
-def ffn(n,zc,part,tok,cot,cotfull,gain,wg,wu,wd):
-    R,F=tok.shape; D=F*zc; FF=wg.shape[1]
-    return call("ffn",2,functools.partial(ffn_kernel,n,zc),(part,tok,cot,cotfull,gain,wg,wu,wd),[ANY]+[VM]*4+[ANY]*3,
-      [S((R,F)),S((R,F)),S((R,D),bf16),S((8,F)),S((R,D),bf16),S((R,FF),bf16),S((R*n,FF),bf16),S((R*n,FF),bf16),S((R*n,D//n),bf16)],
-      [VM]*6+[ANY]*3,
+      compiler_params=pltpu.CompilerParams(collective_id=cid,has_side_effects=True,vmem_limit_bytes=61*2**20))(*args)
+
+def ffn(n,zc,part,tok,cot,cotfull,gain,wgfull,wu,wd):
+    R,F=tok.shape; D=F*zc; FF=wu.shape[1]
+    return call("ffn",2,functools.partial(ffn_kernel,n,zc),(part,tok,cot,cotfull,gain,wgfull,wu,wd),[ANY]+[VM]*4+[ANY]*3,
+      [S((R,F)),S((R,F)),S((R,D),bf16),S((8,F)),S((R,D),bf16),S((R*n,FF),bf16),S((R*n,FF),bf16),S((R*n,FF),bf16),S((R*n,D//n),bf16)],
+      [VM]*5+[ANY]*4,
       [pltpu.VMEM((zc,R,F),bf16),pltpu.VMEM((2*zc,8,R),f32),pltpu.VMEM((R,F),bf16),pltpu.VMEM((R,D),bf16),pltpu.VMEM((D,FF),bf16),pltpu.VMEM((D,FF),bf16),pltpu.VMEM((FF,D),bf16),
-       pltpu.VMEM((R,FF),f32),pltpu.VMEM((R,FF),f32),pltpu.VMEM((R,FF),bf16),pltpu.VMEM((R,FF),bf16),pltpu.VMEM((R,D),bf16)]
-      +pair_sems(zc)*4+pair_sems(n)+pair_sems(zc)*2+gather_sems(n,3)+gather_sems(n,2))
-def tail(n,zc,partdx,partout,res,gres,tok,scale,gain,small,dy,dsm,att):
-    R,F=tok.shape; D=F*zc
-    full=lambda a: S((a.shape[0]*n,a.shape[1]),bf16)
-    return call("tail",4,functools.partial(tail_kernel,n,zc),(partdx,partout,res,gres,tok,scale,gain,small,dy,dsm,att),[ANY,ANY]+[VM]*6+[ANY]*3,
-      [S((R,F)),S((R,F)),full(dy),full(dsm),S((R*n,D//n),bf16),S((n,)+small.shape),S((zc,)+small.shape)],
-      [VM,VM,ANY,ANY,ANY,VM,VM],
-      [pltpu.VMEM((zc,R,F),bf16),pltpu.VMEM((zc,R,F),bf16),pltpu.VMEM((zc,8,R),f32)]+pair_sems(zc)*2+pair_sems(n)*2+pair_sems(zc)*2+gather_sems(n,2))
+       pltpu.VMEM((R,FF),f32),pltpu.VMEM((R,FF),f32),pltpu.VMEM((R,FF),bf16),pltpu.VMEM((R,FF),bf16),pltpu.VMEM((R,FF),bf16),pltpu.VMEM((R,D),bf16),pltpu.SemaphoreType.DMA((1,))]
+      +pair_sems(zc)*4+pair_sems(n)+pair_sems(zc)*2+gather_sems(n,2)+gather_sems(n,3))
 
 
 def per_device(
@@ -760,128 +920,44 @@
     seq_count, local_len, feature_part = tokens.shape
     row_count = seq_count * local_len
     shard_count = lax.axis_size("shard")
-    shard_pos = lax.axis_index("shard")
     seq_devices = lax.axis_size("seq")
-    seq_pos = lax.axis_index("seq")
-    model_dim = feature_part * shard_count
     head_count = beta_weight.shape[1]
     key_dim = query_weight.shape[1] // head_count
     value_dim = value_weight.shape[1] // head_count
-    tap_count = query_conv.shape[1]
-    width_k = head_count * key_dim
-    channels = 2 * key_dim + value_dim
-    feature_start = shard_pos * feature_part
-    head_start = shard_pos * head_count
     pairs = seq_count * head_count
     copies = seq_devices // pairs
-    length = local_len * seq_devices
-    spans = length // SPAN
-    my_pair = seq_pos // copies
-    my_seq = my_pair // head_count
-    my_head = my_pair % head_count
-
-    def project(a, b):
-        return jnp.dot(a, b, preferred_element_type=f32)
-
-    taps_local = jnp.concatenate([query_conv, key_conv, value_conv], axis=0)
-    tap_rows = taps_local.shape[0]
-    width_v = head_count * value_dim
-    padding = -(2 * head_count + tap_count) % 128
-    taps_padded = jnp.pad(taps_local, ((0, query_weight.shape[0] - tap_rows), (0, padding)))
-    weights_small = jnp.concatenate([beta_weight, decay_weight, taps_padded], axis=1)
-    edges = [0, width_k, 2 * width_k, 2 * width_k + width_v]
     flat = lambda x: x.reshape(row_count, x.shape[2])
-    local_ffn_gain = lax.dynamic_slice_in_dim(ffn_gain, feature_start, feature_part)[None]
-    local_norm_gain = lax.dynamic_slice_in_dim(norm_gain, feature_start, feature_part)[None]
     tokens_flat, cot_flat = flat(tokens), flat(cotangent)
+    head_row, norm_row, ffn_row = head_gain[None], norm_gain[None], ffn_gain[None]
     (
-        normed_one, scale_one, cot_rows, full_one, full_outgate, full_output, cot_cols, normed_one_cols,
+        scale_one, cot_rows, full_one, full_outgate, full_output, full_gate, cot_cols, normed_one_cols,
         gate_proj, o_flat, branch, attn_part, taps, *saved,
     ) = forward(
-        seq_devices, shard_count, copies, head_count, tokens_flat, cot_flat, norm_gain[None], head_gain[None],
-        doc_starts, decay_log, decay_bias, query_weight, key_weight, value_weight, weights_small, outgate_weight,
-        output_weight, key_dim, value_dim,
+        seq_devices, shard_count, copies, head_count, tokens_flat, cot_flat, norm_row, head_row, doc_starts, decay_log,
+        decay_bias, beta_weight, decay_weight, query_conv, key_conv, value_conv, query_weight, key_weight, value_weight,
+        outgate_weight, output_weight, gate_weight, key_dim, value_dim,
     )
-    residual, grad_residual, attn_cot, grad_ffn_part, out_part, hidden, dgate_all, dup_all, normed_two_cols = ffn(
-        seq_devices, shard_count, attn_part, tokens_flat, cot_flat, cot_rows, local_ffn_gain, gate_weight, up_weight, down_weight
+    residual, grad_residual, attn_cot, grad_ffn_part, out_part, hidden_all, dgate_all, dup_all, normed_two_cols = ffn(
+        seq_devices, shard_count, attn_part, tokens_flat, cot_flat, cot_rows, ffn_row, full_gate, up_weight, down_weight
     )
-    shape4 = (seq_count, local_len, head_count, -1)
-    gate_proj = gate_proj.reshape(shape4)
-    o = o_flat.astype(f32).reshape(shape4)
-    rho = lax.rsqrt(jnp.mean(o * o, axis=3, keepdims=True) + EPSILON)
-    gate_sig = jax.nn.sigmoid(gate_proj)
-    gate_silu = gate_proj * gate_sig
-    z = o * rho
-
-    def back(cols, weight):
-        return jnp.einsum("rc,dc->rd", cols, weight, preferred_element_type=f32)
-
-    def grad(left, right):
-        return jnp.einsum("rd,rc->dc", left, right, preferred_element_type=f32)
-
-    out_gate, out_up = grad(normed_two_cols, dgate_all), grad(normed_two_cols, dup_all)
-    grad_mixed = (
-        back(attn_cot, full_output).astype(bf16).astype(f32).reshape(shape4)
+    (
+        output, grad_tokens, smalls, totals, out_gate, out_up, out_down, out_output, out_outgate, qkv_all, small_all,
+        unused_branch, unused_gate, unused_cols,
+    ) = back(
+        seq_devices, shard_count, copies, head_count, decay_log.shape[0], attn_cot, gate_proj, o_flat, head_row, tokens_flat,
+        scale_one, norm_row, residual, grad_residual, grad_ffn_part, taps, saved, doc_starts, decay_log, decay_bias,
+        full_output, full_one, full_outgate, out_part, branch, hidden_all, dgate_all, dup_all, normed_two_cols,
+        normed_one_cols, cot_cols,
     )
-    grad_head_gain = jnp.sum(grad_mixed * z * gate_silu, axis=(0, 1, 2))
-    dz = grad_mixed * head_gain * gate_silu
-    grad_o = (rho * (dz - z * jnp.mean(dz * z, axis=3, keepdims=True))).astype(bf16)
-    grad_gate_proj = (grad_mixed * z * head_gain * gate_sig * (1.0 + gate_proj * (1.0 - gate_sig))).astype(bf16)
-    grad_gate_proj = grad_gate_proj.reshape(row_count, head_count * value_dim)
-
-    grad_qkv, drates, dtaps, dhead, hidden_all, branch_all, dgate_proj_all = backward(
-        seq_devices, copies, head_count, grad_o.reshape(row_count, width_v), taps, doc_starts, decay_log, decay_bias, saved,
-        hidden, branch, grad_gate_proj,
+    out_query, out_key, out_value, out_beta, out_decay, out_qconv, out_kconv, out_vconv, out_norm, out_ffn, out_head, out_log, out_bias = last(
+        seq_devices, copies, head_count, key_dim, value_dim, feature_part, decay_log.shape[0], normed_one_cols, qkv_all,
+        small_all, smalls, totals, query_conv.shape[0], value_conv.shape[0],
     )
-    drates = jnp.transpose(drates.reshape(seq_count, head_count, 8, local_len)[:, :, :2], (0, 3, 2, 1))
-    grad_small = jnp.pad(drates.reshape(row_count, 2 * head_count).astype(bf16), ((0, 0), (0, tap_count + padding)))
-    one_part = (
-        back(grad_qkv, full_one[:, : edges[3]]) + back(grad_small, full_one[:, edges[3] :]) + back(grad_gate_proj, full_outgate)
-    ).astype(bf16)
-    at_head = head_start + my_pair % head_count
-    primary = jnp.where(seq_pos % copies == 0, 1.0, 0.0)
-    total_heads = decay_log.shape[0]
-    width_s = max(feature_part, channels)
-    widen = lambda x: jnp.pad(x, ((0, 0), (0, width_s - x.shape[1])))
-    heads_row = lax.dynamic_update_slice(
-        lax.dynamic_update_slice(jnp.zeros((1, width_s), f32), dhead[0:1, :1] * primary, (0, at_head)),
-        dhead[1:2, :1] * primary,
-        (0, total_heads + at_head),
-    )
-    small = jnp.concatenate(
-        [jnp.zeros((1, width_s), f32), widen(grad_ffn_part[:1]), widen(grad_head_gain[None]), heads_row, widen(dtaps)], axis=0
-    )
-    output, grad_tokens, qkv_all, small_all, attn_cols, smalls, totals = tail(
-        seq_devices, shard_count, one_part, out_part, residual, grad_residual, tokens_flat, scale_one,
-        local_norm_gain, small, grad_qkv, grad_small, attn_cot,
-    )
-    outs_one = [grad(normed_one_cols, qkv_all[:, edges[i] : edges[i + 1]]) for i in range(3)]
-    outs_small = grad(normed_one_cols, small_all)
-    outs_one += [
-        grad(normed_one_cols, dgate_proj_all), outs_small[:, :head_count], outs_small[:, head_count : 2 * head_count]
-    ]
-    out_down = grad(hidden_all, cot_cols)
-    out_output = grad(branch_all, attn_cols)
-    tap_sum = jnp.sum(smalls[::copies, 4:].reshape(seq_count, head_count, tap_count, width_s), axis=0)
-
-    def own_rows(taps_part):
-        rows = jnp.swapaxes(taps_part, 1, 2).reshape(-1, tap_count)
-        count = rows.shape[0] // seq_devices
-        return lax.dynamic_slice_in_dim(rows, seq_pos * count, count)
-
-    out_qconv = own_rows(tap_sum[:, :, :key_dim])
-    out_kconv = own_rows(tap_sum[:, :, key_dim : 2 * key_dim])
-    out_vconv = own_rows(tap_sum[:, :, 2 * key_dim : channels])
-    out_norm = totals[:, 0, :feature_part].reshape(-1)
-    out_ffn = totals[:, 1, :feature_part].reshape(-1)
-    totals_all = jnp.sum(totals, axis=0)
-    out_head = totals_all[2, :value_dim]
-    out_log = totals_all[3, :total_heads]
-    out_bias = totals_all[3, total_heads : 2 * total_heads]
     shape3 = (seq_count, local_len, feature_part)
     return (
-        output.reshape(shape3), grad_tokens.reshape(shape3), out_norm, *outs_one, out_qconv, out_kconv, out_vconv,
-        out_log, out_bias, out_head, out_output, out_ffn, out_gate, out_up, out_down,
+        output.reshape(shape3), grad_tokens.reshape(shape3), out_norm[0], out_query, out_key, out_value, out_outgate,
+        out_beta, out_decay, out_qconv, out_kconv, out_vconv, out_log[0], out_bias[0], out_head[0], out_output,
+        out_ffn[0], out_gate, out_up, out_down,
     )
 
 

time: 542 us -> 476 us (0.88); the launches traced: 533 us -> 475 us
  matrix products: 43.4 us -> 0 us
  Pallas kernels: 460 us -> 450 us
    dot_general x13 -> x0, matrix products: 43.4 us -> none  [the longest x9 29 us: grad(): return jnp.einsum('rd,rc->dc', left, right, preferred_element_type=f32)]
    pallas_call x4 -> x3, Pallas kernels: 460 us -> 442 us  [call(): pl.pallas_call(kernel, name=name, out_shape=tuple(outs), in_specs=specs,...]
    unnamed x57 -> x27, local copies, waits for them, and re-layouts: 5.85 us -> 23.7 us
    pallas_call x0 -> x1, Pallas kernels: none -> 8.85 us  [last(): pl.pallas_call(functools.partial(last_kernel, n, copies, heads, DK, DV, F...]
where the time goes in v5:
time: 476 us; the launch traced here: 475 us
  Pallas kernels  450 us (95%)
  local copies, waits for them, and re-layouts  23.7 us (5%)
    pallas_call x3, Pallas kernels, call(): pl.pallas_call(kernel, name=name, out_shape=tuple(outs), in_specs=specs,...  442 us
    unnamed x27, local copies, waits for them, and re-layouts  23.7 us

profile of v5, /device:TPU:0, one launch (start us, length us, event | category | flops | bytes accessed | tf_op | source)
XLA Modules:
  0.0 474.8 jit_solution(1359480842405942804)
XLA Ops:
  0.7 1.4 copy.43.qc
  2.0 1.4 copy.44.kc
  3.4 1.4 copy.45.vc
  4.8 1.4 copy.41.wb
  6.3 1.4 copy.42.wd
  7.7 156.7 %mixer.1 = (f32[256,128]{1,0:T(8,128)}, bf16[256,2048]{1,0:T(8,128)(2,1)}, bf16[2048,2176]{1,0:T(8,128)(2,1)}, bf16[2048,1024]{1,0:T(8,128)(2,1)}, bf16[1024,204...) custom-call(bf16[256,512]{1,0:T(8,128)(2,1)} %bitcast.12, ...), custom_call_target="tpu_custom_call" | custom-call | tf_op jit(solution)/shard_map/mixer/pallas_call | solution.py:902
  164.4 144.7 %ffn.1 = (f32[256,512]{1,0:T(8,128)}, f32[256,512]{1,0:T(8,128)}, bf16[256,2048]{1,0:T(8,128)(2,1)}, f32[8,512]{1,0:T(8,128)}, bf16[256,2048]{1,0:T(8,128)(2,1)}...) custom-call(bf16[256,2048]{1,0:T(8,128)(2,1)} %get-tuple-element.78., ...), custom_call_target="tpu_custom_call" | custom-call | tf_op jit(solution)/shard_map/ffn/pallas_call | solution.py:902
  309.1 140.1 %back.1 = (f32[256,512]{1,0:T(8,128)}, f32[256,512]{1,0:T(8,128)}, f32[8,8,512]{2,1,0:T(8,128)}, f32[4,8,512]{2,1,0:T(8,128)}, f32[256,1408]{1,0:T(8,128)}, /*in...) custom-call(bf16[256,2048]{1,0:T(8,128)(2,1)} %get-tuple-element.81., ...), custom_call_target="tpu_custom_call" | custom-call | tf_op jit(solution)/shard_map/back/pallas_call | solution.py:902
  449.2 0.0 copy-start.4
  449.3 8.8 %last.1 = (f32[256,512]{1,0:T(8,128)}, f32[256,512]{1,0:T(8,128)}, f32[256,1024]{1,0:T(8,128)}, f32[256,4]{1,0:T(8,128)}, f32[256,4]{1,0:T(8,128)}, /*index=5*/f...) custom-call(bf16[8,256,256]{2,1,0:T(8,128)(2,1)} %get-tuple-element., ...), custom_call_target="tpu_custom_call" | custom-call | tf_op jit(solution)/shard_map/last/pallas_call | solution.py:594
  458.1 0.0 copy-start.3
  458.1 0.0 copy-start.2
  458.1 1.6 copy.48
  459.7 1.4 copy.49
  461.1 1.5 copy.50
  462.6 1.6 copy.46
  464.2 1.6 copy.47
  465.7 1.9 copy.58
  467.6 0.0 copy-start.1
  467.6 2.0 copy.59
  469.6 0.0 copy-done.4
  469.6 1.0 copy.60
  470.6 0.0 copy-done.3
  470.6 0.0 copy-start
  470.6 1.0 copy.61
  471.5 0.0 copy-done.2
  471.5 1.1 copy.62
  472.6 0.0 copy-done.1
  472.6 1.1 copy.63
  473.7 0.0 copy-done
  473.7 1.1 copy.64
Async XLA Ops:
  449.2 20.3 %copy-start.4 = (f32[256,1024]{1,0:T(8,128)S(1)}, f32[256,1024]{1,0:T(8,128)}, u32[]{:S(2)}) copy-start(f32[256,1024]{1,0:T(8,128)} %get-tuple-element.182) | copy-start | bytes 3145732
  458.1 12.5 %copy-start.3 = (f32[1024,256]{1,0:T(8,128)S(1)}, f32[1024,256]{1,0:T(8,128)}, u32[]{:S(2)}) copy-start(f32[1024,256]{1,0:T(8,128)} %get-tuple-element.191) | copy-start | bytes 3145732
  458.1 13.4 %copy-start.2 = (f32[256,1408]{1,0:T(8,128)S(1)}, f32[256,1408]{1,0:T(8,128)}, u32[]{:S(2)}) copy-start(f32[256,1408]{1,0:T(8,128)} %get-tuple-element.193) | copy-start | bytes 4325380
  467.6 5.0 %copy-start.1 = (f32[256,1408]{1,0:T(8,128)S(1)}, f32[256,1408]{1,0:T(8,128)}, u32[]{:S(2)}) copy-start(f32[256,1408]{1,0:T(8,128)} %get-tuple-element.194) | copy-start | bytes 4325380
  470.6 3.2 copy-start

commit v6 on v5

--- a/solution.py
+++ b/solution.py
@@ -55,36 +55,40 @@
 
 def inverse(A):
     i,j=square_masks()
-    near=(i//8)==(j//8)
     eye=jnp.where(i==j,1.0,0.0)
-    X=jnp.where(near,-A,0.0); far=jnp.where(near,0.0,A)
-    X2=mm3(X,X); X4=mm3(X2,X2)
-    Di=eye+X; Di=Di+mm3(Di,X2); Di=Di+mm3(Di,X4)
-    Y=-mm3(Di,far)
-    Y2=mm3(Y,Y); Y4=mm3(Y2,Y2)
-    T=Di+mm3(Y4,Di); T=T+mm3(Y2,T); T=T+mm3(Y,T)
-    return T
-
-def span_terms(n,q,k,starts,xc,xr,rate,bias):
+    T=eye-jnp.where((i//2)==(j//2),A,0.0)
+    size=2
+    while size<SPAN:
+        C=jnp.where(((i//(2*size))==(j//(2*size)))&((i//size)!=(j//size)),A,0.0).astype(bf16)
+        Tb=T.astype(bf16)
+        T=T-dg(Tb,dg(C,Tb).astype(bf16))
+        size*=2
+    Tb=T.astype(bf16); Ah,Al=halves(A)
+    rest=eye-Tb.astype(f32)-(dg(Ah,Tb)+dg(Al,Tb))
+    return Tb.astype(f32)+dg(Tb,rest.astype(bf16))
+
+def position_rows(raw,starts,base,rate,bias):
+    r=raw.shape[1]
+    row=lax.broadcasted_iota(jnp.int32,(8,r),0)
+    g=-rate*softplus(raw[1:2]+bias)
+    i=lax.broadcasted_iota(jnp.int32,(r,r),0); j=lax.broadcasted_iota(jnp.int32,(r,r),1)
+    G=mmx(jnp.broadcast_to(g,(8,r)),jnp.where((i<=j)&((i//SPAN)==(j//SPAN)),1.0,0.0))
+    docs=doc_count(starts,positions(base,8,r,1)).astype(f32)
+    out=jnp.where(row==0,sigmoid(raw[0:1]),0.0)
+    for k,x in ((1,g),(2,G),(3,raw[1:2]),(4,docs)): out=jnp.where(row==k,x,out)
+    return out
+
+def span_terms(n,q,k,starts,xc,xr):
     i,j=square_masks()
-    base=n*SPAN
-    docs=doc_count(starts,positions(base,SPAN,128,0))
-    docr=doc_count(starts,positions(base,1,SPAN,1))
-    before=count_at(starts,base-1)
-    lastdoc=count_at(starts,base+SPAN-1)
-    lower=jnp.where(i>=j,1.0,0.0); upper=jnp.where(i<=j,1.0,0.0)
-    beta=sigmoid(xc[:,0:1])
-    g=-rate*softplus(xc[:,1:2]+bias)
-    gr=-rate*softplus(xr+bias)
-    G=mmx(lower,jnp.broadcast_to(g,(SPAN,128)))
-    Gr=mmx(jnp.broadcast_to(gr,(8,SPAN)),upper)[0:1]
-    same=docs[:,:SPAN]==docr
-    incl=(i>=j)&same
-    D=jnp.where(incl,jnp.exp(jnp.where(incl,G[:,:SPAN]-Gr,0.0)),0.0)
+    before=count_at(starts,n*SPAN-1).astype(f32)
+    wide=lambda c: jnp.broadcast_to(c,(SPAN,128))
+    beta=wide(xc[:,0:1]); G=wide(xc[:,2:3]); docs=wide(xc[:,4:5])
+    incl=(i>=j)&(docs[:,:SPAN]==xr[4:5])
+    D=jnp.where(incl,jnp.exp(jnp.where(incl,G[:,:SPAN]-xr[2:3],0.0)),0.0)
     gam=jnp.where(docs==before,jnp.exp(G),0.0)
-    end=jnp.where(docs==lastdoc,jnp.exp(G[SPAN-1:SPAN]-G),0.0)
+    end=jnp.where(docs==docs[SPAN-1:SPAN],jnp.exp(G[SPAN-1:SPAN]-G),0.0)
     KK=dg(k,k,1,1); QK=dg(q,k,1,1)
-    return beta,g,D,gam,end,KK,QK,i,j
+    return beta,D,gam,end,KK,QK,i,j
 
 def conv_pre(upad,taps,age,base,rows):
     window=upad[pl.ds(base,rows+8),:]
@@ -95,15 +99,15 @@
     return pre
 
 def forward_kernel(n,zc,copies,heads,DK,DV,tok,cot,gain,hgain,starts2,dlog,dbias,wb,wd,qc,kc,vc,wq,wk,wv,wg,wo,wgate,
-                   scale,cotfull,wfull,wgfull,wofull,wgatefull,cotc,n1c,gate_ref,oall,branch,part,taps_ref,u_ref,xr_ref,xc_ref,q_ref,k_ref,v_ref,s_ref,w_ref,t_ref,qt_ref,mh_ref,ml_ref,
+                   scale,cotfull,wfull,wgfull,wofull,wgatefull,cotc,n1c,gate_ref,oall,branch,part,taps_ref,u_ref,xr_ref,xc_ref,q_ref,k_ref,v_ref,s_ref,w_ref,t_ref,qt_ref,mh_ref,
                    tokfull,normed,ws,wbuf,sbuf,pbuf,rbuf,tbuf,upad,un_ref,gc_ref,on_ref,o_ref,zs,zr,cs,cr,ks,kr,es,er,fs,fr,hs,hr,is_,ir,os_,or_,ld,*gs):
     L=u_ref.shape[0]; NC=L//SPAN; local_len=L//n; per=local_len//SPAN
-    put=lambda x,first: dg(x[...],jnp.where(lax.broadcasted_iota(jnp.int32,(x.shape[1],128),0)+first==lax.broadcasted_iota(jnp.int32,(x.shape[1],128),1),1.0,0.0).astype(bf16))
+    put=lambda x,first: dg(x[...],jnp.where(lax.broadcasted_iota(jnp.int32,(x.shape[0],128),0)+first==lax.broadcasted_iota(jnp.int32,(x.shape[0],128),1),1.0,0.0).astype(bf16),0,0)
     ws[...]=(put(wb,0)+put(wd,heads)).astype(bf16)
     at_row=0
     for x in (qc,kc,vc):
-        ws[at_row:at_row+x.shape[0]]=(ws[at_row:at_row+x.shape[0]].astype(f32)+put(x,2*heads)).astype(bf16)
-        at_row+=x.shape[0]
+        ws[at_row:at_row+x.shape[1]]=(ws[at_row:at_row+x.shape[1]].astype(f32)+put(x,2*heads)).astype(bf16)
+        at_row+=x.shape[1]
     greet(n,zc)
     zt=ShardGather(zc,tok,tokfull,zs,zr); zt.start()
     ws_all=(ws,wq,wk,wv); at=(wq.shape[1]*2+wv.shape[1],0,wq.shape[1],wq.shape[1]*2)
@@ -111,6 +115,7 @@
     gw=gathers(n,[(w,wfull,0,a) for w,a in zip(ws_all,at)],g1)
     gb=gathers(n,[(wg,wgfull,0),(wo,wofull,1),(wgate,wgatefull,0)],g2)
     each(gw,"start")
+    each(gw,"middle")
     zt.finish()
     zk=ShardGather(zc,cot,cotfull,cs,cr); zk.start()
     rows=tokfull.shape[0]; D=tokfull.shape[1]
@@ -123,7 +128,7 @@
         return 0
     lax.fori_loop(0,rows//32,norm,0)
     rbuf[...]=jnp.zeros(rbuf.shape,f32)
-    each(gw,"middle")
+    inward=ToPairs(n,copies,heads,local_len,pbuf,rbuf,u_ref,xr_ref,DK,DV,is_,ir)
     pair=lax.div(lax.axis_index("seq"),copies); my_seq=lax.div(pair,heads); my_head=lax.rem(pair,heads)
     for i,g in enumerate(gw):
         g.late(); g.finish()
@@ -155,20 +160,23 @@
                 pbuf[:,pl.ds(pl.multiple_of(at[i]+j*tile,128),tile)]=jnp.dot(normed[...],wbuf[:,cc],preferred_element_type=f32).astype(bf16)
                 return 0
             lax.fori_loop(0,width//tile,column,0)
-    inward=ToPairs(n,copies,heads,local_len,pbuf,rbuf,u_ref,xr_ref,DK,DV,is_,ir); inward.start()
+        inward.start((3,0,1,2)[i])
     starts=Row(starts2,my_seq)
     at_head=lax.axis_index("shard")*heads+my_head
     rate=jnp.exp(jnp.full((1,1),dlog[at_head],f32)); bias=dbias[at_head]
     zk.finish()
     inward.finish()
-    each(gb,"start")
     cols=SharedColumns(n,zc,normed,n1c,(es,er,fs,fr)); cols.start()
     ccol=SharedColumns(n,zc,cotfull,cotc,(ks,kr,hs,hr)); ccol.start()
+    each(gb,"start")
     upad[0:8]=jnp.zeros((8,upad.shape[1]),f32)
     def turn(m,_):
-        xc_ref[pl.ds(pl.multiple_of(m*local_len,local_len),local_len),:]=col_form(xr_ref[pl.ds(pl.multiple_of(m*8,8),8),:])
-        return 0
-    lax.fori_loop(0,n,turn,0,unroll=2)
+        r=pl.ds(pl.multiple_of(m*8,8),8)
+        x=position_rows(xr_ref[r,:],starts,m*local_len,rate,bias)
+        xr_ref[r,:]=x
+        xc_ref[pl.ds(pl.multiple_of(m*local_len,local_len),local_len),:]=col_form(x)
+        return 0
+    lax.fori_loop(0,n,turn,0,unroll=4)
     taps=taps_ref[...]
     R=128
     def load(c,_):
@@ -187,38 +195,37 @@
         v_ref[rows,:]=act[:,2*DK:].astype(bf16)
         return 0
     lax.fori_loop(0,L//R,conv,0)
+    cols.middle(); ccol.middle()
     def one_span(n,xr):
         rows=pl.ds(pl.multiple_of(n*SPAN,SPAN),SPAN)
         q=q_ref[rows,:]; k=k_ref[rows,:]; v=v_ref[rows,:]
-        beta,g,D,gam,end,KK,QK,i,j=span_terms(n,q,k,starts,xc_ref[rows,:],xr,rate,bias)
-        A=jnp.where(i>j,beta*D*KK,0.0)
+        beta,D,gam,end,KK,QK,i,j=span_terms(n,q,k,starts,xc_ref[rows,:],xr)
+        A=jnp.where(i>j,beta[:,:SPAN]*D*KK,0.0)
         T=inverse(A)
         kf=k.astype(f32)
-        UW=mm3(T,jnp.concatenate([beta*v.astype(f32),(beta*gam)*kf],axis=1))
-        P=QK*D
-        PW=mm1(P,UW)
-        qt=gam*q.astype(f32)-PW[:,DV:]
-        NM=mm3(end*kf,UW,0,0)
+        UW=mm1(T,jnp.concatenate([jnp.concatenate([beta]*(DV//128),axis=1)*v.astype(f32),(beta*gam)*kf],axis=1))
+        UWb=UW.astype(bf16)
+        PW=dg((QK*D).astype(bf16),UWb)
+        NM=dg((end*kf).astype(bf16),UWb,0,0)
         t_ref[n]=T
         on_ref[n]=PW[:,:DV]
         w_ref[n]=UW[:,:DV]
-        qt_ref[n,0:SPAN]=qt.astype(bf16)
-        qt_ref[n,SPAN:]=UW[:,DV:].astype(bf16)
+        qt_ref[n,0:SPAN]=(gam*q.astype(f32)-PW[:,DV:]).astype(bf16)
+        qt_ref[n,SPAN:]=UWb[:,DV:]
         un_ref[n]=NM[:,:DV]
-        mh,ml=halves(NM[:,DV:])
-        mh_ref[n]=mh; ml_ref[n]=ml
+        mh_ref[n]=NM[:,DV:].astype(bf16)
         gc_ref[n]=jnp.broadcast_to(gam[SPAN-1:SPAN],(8,128))
     def local(m,_):
         xr=xr_ref[pl.ds(pl.multiple_of(m*8,8),8),:]
-        for e in range(per): one_span(m*per+e,xr[1:2,e*SPAN:(e+1)*SPAN])
+        for e in range(per): one_span(m*per+e,xr[:,e*SPAN:(e+1)*SPAN])
         return 0
     lax.fori_loop(0,n,local,0,unroll=2)
-    each(gb,"middle"); cols.middle(); ccol.middle()
+    each(gb,"middle")
     def chain(n,S):
         s_ref[n]=S
-        sh,sl=halves(S); mh=mh_ref[n]; ml=ml_ref[n]
+        sh,sl=halves(S); mh=mh_ref[n]
         gc=gc_ref[n][0:1]
-        return jnp.concatenate([gc]*(DV//128),axis=1)*S+un_ref[n]-(dg(mh,sh)+(dg(ml,sh)+dg(mh,sl)))
+        return jnp.concatenate([gc]*(DV//128),axis=1)*S+un_ref[n]-(dg(mh,sh)+dg(mh,sl))
     lax.fori_loop(0,NC,chain,jnp.zeros((DK,DV),f32),unroll=2)
     def emit(n,_):
         rows=pl.ds(pl.multiple_of(n*SPAN,SPAN),SPAN)
@@ -262,7 +269,7 @@
     gb[2].late(); cols.finish(); ccol.finish(); gb[2].finish()
 
 def back_kernel(n,zc,copies,heads,total_heads,afull,gate_ref,oall,hgain,tok,scale,gain,res,gres,gffn,taps_ref,u_ref,xc_ref,xr_ref,starts2,dlog,dbias,
-                q_ref,k_ref,v_ref,s_ref,w_ref,t_ref,qt_ref,mh_ref,ml_ref,wofull,wfull,wgfull,outpart,branch,hidfull,dgfull,dufull,n2c,n1c,cotc,
+                q_ref,k_ref,v_ref,s_ref,w_ref,t_ref,qt_ref,mh_ref,wofull,wfull,wgfull,outpart,branch,hidfull,dgfull,dufull,n2c,n1c,cotc,
                 output,gtok,smalls,totals,ogate,oup,odown,oout,oog,dyqfull,dsmfull,brafull,dgpfull,attc,
                 upad,dpre,ds_ref,gc_ref,do_ref,du_ref,dx_ref,dxr,bufa,bufb,cola,colb,colc,dob,dgp,dyq,rbuf,dsm,part,upart,box,boxo,sums,
                 is_,ir,os_,or_,as_,ar,bs,br,cs,cr,es,er,fs,fr,hs,hr,zs,zr,ld,*gs):
@@ -303,7 +310,7 @@
             dgp[r,cc]=(dmg*z*sg*(1.0+g*(1.0-sg))).astype(bf16)
         return gh
     gh=lax.fori_loop(0,rows_n//64,heads_back,jnp.zeros((1,DV),f32))
-    inward=ToPairs(n,copies,heads,local_len,dob,None,do_ref,None,DK,DV,is_,ir); inward.start()
+    inward=ToPairs(n,copies,heads,local_len,dob,None,do_ref,None,DK,DV,is_,ir); inward.start(0)
     load_job("dgate",0,[(dgfull,every(FF))])
     c2=pltpu.make_async_copy(n2c,cola,ld.at[0,4]); c2.start()
     g1,g2=gs[:3],gs[3:]
@@ -326,26 +333,25 @@
     def early(n,_):
         rows=pl.ds(pl.multiple_of(n*SPAN,SPAN),SPAN)
         ds_ref[n]=dg(qt_ref[n][0:SPAN],do_ref[rows,:],0,0)
-        base=n*SPAN
-        G=jnp.sum(-rate*softplus(xc_ref[rows,1:2]+bias),axis=0,keepdims=True)
-        alive=jnp.where(count_at(starts,base+SPAN-1)==count_at(starts,base-1),1.0,0.0)
-        gc_ref[n]=jnp.broadcast_to(jnp.exp(G)*alive,(8,128))
+        tail_row=xc_ref[rows,:][SPAN-1:SPAN]
+        gam=jnp.where(tail_row[:,4:5]==count_at(starts,n*SPAN-1).astype(f32),jnp.exp(tail_row[:,2:3]),0.0)
+        gc_ref[n]=jnp.broadcast_to(gam,(8,128))
         return 0
     lax.fori_loop(0,NC,early,0,unroll=4)
     def chain(m,dS):
         n=NC-1-m
         r=ds_ref[n]
         ds_ref[n]=dS
-        sh,sl=halves(dS); mh=mh_ref[n]; ml=ml_ref[n]
+        sh,sl=halves(dS); mh=mh_ref[n]
         gc=gc_ref[n][0:1]
-        return jnp.concatenate([gc]*(DV//128),axis=1)*dS+r-(dg(mh,sh,0,0)+(dg(ml,sh,0,0)+dg(mh,sl,0,0)))
+        return jnp.concatenate([gc]*(DV//128),axis=1)*dS+r-(dg(mh,sh,0,0)+dg(mh,sl,0,0))
     lax.fori_loop(0,NC,chain,jnp.zeros((DK,DV),f32),unroll=2)
     each(gw,"middle"); ca.middle()
-    def one_span(n,xr,sums):
+    def one_span(n,xr):
         rows=pl.ds(pl.multiple_of(n*SPAN,SPAN),SPAN)
         q=q_ref[rows,:]; k=k_ref[rows,:]; v=v_ref[rows,:]; dO=do_ref[rows,:]
-        xc=xc_ref[rows,:]
-        beta,g,D,gam,end,KK,QK,i,j=span_terms(n,q,k,starts,xc,xr,rate,bias)
+        beta,D,gam,end,KK,QK,i,j=span_terms(n,q,k,starts,xc_ref[rows,:],xr)
+        beta2=jnp.concatenate([beta]*(DV//128),axis=1)
         S0=s_ref[n]; dS1=ds_ref[n]
         S0h=S0.astype(bf16); dSh=dS1.astype(bf16)
         kf=k.astype(f32); qf=q.astype(f32); vf=v.astype(f32)
@@ -360,43 +366,45 @@
         Z=dg(W,dSh,1,1)
         dPD=dPA[:SPAN]*D
         EA=jnp.where(i>j,-dPA[SPAN:]*D,0.0)
-        E=beta*EA
+        E=beta[:,:SPAN]*EA
         A1=jnp.concatenate([dPD,E],axis=0).astype(bf16)
         r1=dg(A1,k)
         r2=dg(A1,jnp.concatenate([q,k],axis=0),0,0)
         dpre[rows,0:DK]=gam*dOS+r1[:SPAN]
         dpre[rows,DK:2*DK]=r1[SPAN:]+r2-(beta*gam)*YS+end*Z
-        dpre[rows,2*DK:]=beta*Y
+        dpre[rows,2*DK:]=beta2*Y
         EK=EA*KK
         kYS=jnp.sum(kf*YS,axis=1,keepdims=True)
         dbeta=jnp.sum(Y*vf,axis=1,keepdims=True)-gam*kYS+jnp.sum(EK,axis=1,keepdims=True)
-        Fm=dPD*QK+beta*EK
+        Fm=dPD*QK+beta[:,:SPAN]*EK
         dgam=jnp.sum(qf*dOS,axis=1,keepdims=True)-beta*kYS
         dend=jnp.sum(kf*Z,axis=1,keepdims=True)*end
-        colsum=mmx(Fm,jnp.ones((SPAN,128),f32),0,0)
-        dG=jnp.sum(Fm,axis=1,keepdims=True)-colsum+dgam*gam-dend
+        dG=jnp.sum(Fm,axis=1,keepdims=True)+dgam*gam-dend
         tail=jnp.sum(jnp.sum(S0*dS1,axis=0,keepdims=True),axis=1,keepdims=True)
         last=jnp.sum(dend,axis=0,keepdims=True)+gam[SPAN-1:SPAN]*tail
         row=lax.broadcasted_iota(jnp.int32,(SPAN,128),0)
         dG=dG+jnp.where(row==SPAN-1,last,0.0)
-        upper=jnp.where(i<=j,1.0,0.0)
-        dlog=mmx(upper,dG)
-        dbp=(dbeta*beta*(1.0-beta))
-        ddp=dlog*(-rate)*sigmoid(xc[:,1:2]+bias)
-        dx_ref[rows,0:1]=dbp[:,0:1]
-        dx_ref[rows,1:2]=ddp[:,0:1]
-        sl,sb=sums
-        return (sl+jnp.sum(dlog*g,axis=0,keepdims=True),sb+jnp.sum(ddp,axis=0,keepdims=True))
-    def local(m,sums):
+        dx_ref[rows,0:1]=(dbeta*beta*(1.0-beta))[:,0:1]
+        dx_ref[rows,1:2]=dG[:,0:1]
+        return jnp.sum(Fm,axis=0,keepdims=True)
+    def local(m,_):
         xr=xr_ref[pl.ds(pl.multiple_of(m*8,8),8),:]
-        for e in range(per): sums=one_span(m*per+e,xr[1:2,e*SPAN:(e+1)*SPAN],sums)
-        return sums
-    zero=jnp.zeros((1,128),f32)
-    sl,sb=lax.fori_loop(0,n,local,(zero,zero),unroll=2)
-    def turn(m,_):
-        dxr[pl.ds(pl.multiple_of(m*8,8),8),:]=flat_form(dx_ref[pl.ds(pl.multiple_of(m*local_len,local_len),local_len),:])
-        return 0
-    lax.fori_loop(0,n,turn,0,unroll=2)
+        dxr[pl.ds(pl.multiple_of(m*8,8),8),:]=jnp.broadcast_to(jnp.concatenate([one_span(m*per+e,xr[:,e*SPAN:(e+1)*SPAN]) for e in range(per)],axis=1),(8,local_len))
+        return 0
+    lax.fori_loop(0,n,local,0,unroll=2)
+    i128=lax.broadcasted_iota(jnp.int32,(local_len,local_len),0); j128=lax.broadcasted_iota(jnp.int32,(local_len,local_len),1)
+    later=jnp.where((i128>=j128)&((i128//SPAN)==(j128//SPAN)),1.0,0.0)
+    def turn(m,sums):
+        r=pl.ds(pl.multiple_of(m*8,8),8)
+        f=flat_form(dx_ref[pl.ds(pl.multiple_of(m*local_len,local_len),local_len),:])
+        dlog=mmx(jnp.broadcast_to(f[1:2]-dxr[r,:][0:1],(8,local_len)),later)
+        x=xr_ref[r,:]
+        ddp=dlog*(-rate)*sigmoid(x[3:4]+bias)
+        row=lax.broadcasted_iota(jnp.int32,(8,local_len),0)
+        dxr[r,:]=jnp.where(row==0,f[0:1],jnp.where(row==1,ddp,0.0))
+        return (sums[0]+jnp.sum(dlog[0:1]*x[1:2],axis=1,keepdims=True),sums[1]+jnp.sum(ddp[0:1],axis=1,keepdims=True))
+    zero=jnp.zeros((1,1),f32)
+    sl,sb=lax.fori_loop(0,n,turn,(zero,zero),unroll=4)
     def norms(c,dt):
         base=pl.multiple_of(c*R,R)
         age=doc_age(starts,positions(base,R,128,0))[:,0:1]
@@ -421,7 +429,6 @@
         return tuple(new)
     zt=jnp.zeros((1,upad.shape[1]),f32)
     dt=lax.fori_loop(0,L//R,norms,(zt,)*4)
-    each(gw,"late")
     so.finish()
     y=res[...]
     for d in range(zc): y=y+boxo[d].astype(f32)
@@ -478,6 +485,7 @@
         return 0
     lax.fori_loop(0,D//256,last,0)
     split=ShardSplit(zc,upart,box,as_,ar); split.start()
+    each(gw,"late")
     each(gd,"middle")
     for g in gw: g.finish()
     ca.finish()
@@ -536,20 +544,20 @@
       [S((R,128)),S((R,D),bf16),rows(wq,wk,wv,small),rows(wg),S((wo.shape[0],wo.shape[1]*n),bf16),rows(wgate),S((n,R,D//n),bf16),S((n,R,D//n),bf16),
        S((R,HV)),S((R,HV),bf16),S((R,HV),bf16),S((R,D),bf16),S((4,CH)),
        S((L,CH),bf16),S((n*8,local_len)),S((L,8)),S((L,DK),bf16),S((L,DK),bf16),S((L,DV),bf16),S((NC,DK,DV)),S((NC,SPAN,DV)),S((NC,SPAN,SPAN)),
-       S((NC,2*SPAN,DK),bf16),S((NC,DK,DK),bf16),S((NC,DK,DK),bf16)],
-      [VM]+[ANY]*7+[VM]*17,
+       S((NC,2*SPAN,DK),bf16),S((NC,DK,DK),bf16)],
+      [VM]+[ANY]*7+[VM]*16,
       [pltpu.VMEM((R,D),bf16),pltpu.VMEM((R,D),bf16),pltpu.VMEM((D//n,128),bf16),pltpu.VMEM((D,wide),bf16),pltpu.VMEM((D,128),bf16),pltpu.VMEM((R,heads*CH),bf16),pltpu.VMEM((pairs*8,local_len),f32),pltpu.VMEM((CH,128),bf16),
        pltpu.VMEM((L+8,CH),f32),pltpu.VMEM((NC,DK,DV),f32),pltpu.VMEM((NC,8,128),f32),pltpu.VMEM((NC,SPAN,DV),f32),pltpu.VMEM((L,DV),bf16)]
       +pair_sems(zc)*2+pair_sems(n)*2+pair_sems(zc)*2+[pltpu.SemaphoreType.DMA((4,n)),pltpu.SemaphoreType.DMA((4,n)),pltpu.SemaphoreType.DMA((1,pairs)),pltpu.SemaphoreType.DMA((1,pairs)),pltpu.SemaphoreType.DMA((D//wide,))]
       +gather_sems(n,4)+gather_sems(n,3))
 def back(n,zc,copies,heads,total_heads,afull,gate,oall,hgain,tok,scale,gain,res,gres,gffn,taps,saved,starts,dlog,dbias,wofull,wfull,wgfull,outpart,branch,hidfull,dgfull,dufull,n2c,n1c,cotc):
-    u,xr,xc,q,k,v,s,w,t,qt,mh,ml=saved
+    u,xr,xc,q,k,v,s,w,t,qt,mh=saved
     L,CH=u.shape; NC=L//SPAN; DK=q.shape[1]; DV=v.shape[1]; local_len=L//n; pairs=n//copies; R,F=tok.shape; D=F*zc; FF=dgfull.shape[1]; HV=heads*DV; VW=wofull.shape[0]
     Dc=D//n; W=max(F,CH)
     bw=max(FF,HV+128,VW,2*heads*DK)
-    ins=(afull,gate,oall,hgain,tok,scale,gain,res,gres,gffn,taps,u,xc,xr,starts,dlog,dbias,q,k,v,s,w,t,qt,mh,ml,wofull,wfull,wgfull,outpart,branch,hidfull,dgfull,dufull,n2c,n1c,cotc)
+    ins=(afull,gate,oall,hgain,tok,scale,gain,res,gres,gffn,taps,u,xc,xr,starts,dlog,dbias,q,k,v,s,w,t,qt,mh,wofull,wfull,wgfull,outpart,branch,hidfull,dgfull,dufull,n2c,n1c,cotc)
     sem=pltpu.SemaphoreType.DMA
-    return call("back",6,functools.partial(back_kernel,n,zc,copies,heads,total_heads),ins,[VM]*14+[SM]*3+[VM]*9+[ANY]*11,
+    return call("back",6,functools.partial(back_kernel,n,zc,copies,heads,total_heads),ins,[VM]*14+[SM]*3+[VM]*8+[ANY]*11,
       [S((R,F)),S((R,F)),S((n,8,W)),S((zc,8,W)),S((Dc,FF)),S((Dc,FF)),S((FF,Dc)),S((VW,Dc)),S((Dc,HV)),S((R*n,heads*CH),bf16),S((R*n,128),bf16),S((R*n,HV),bf16),S((R*n,HV),bf16),S((n,R,Dc),bf16)],
       [VM]*9+[ANY]*5,
       [pltpu.VMEM((L+8,CH),f32),pltpu.VMEM((L+8,CH),f32),pltpu.VMEM((NC,DK,DV),f32),pltpu.VMEM((NC,8,128),f32),
@@ -559,16 +567,25 @@
        pltpu.VMEM((zc,R,F),bf16),pltpu.VMEM((zc,R,F),bf16),pltpu.VMEM((zc,8,R),f32)]
       +[sem((1,n)),sem((1,n)),sem((4,pairs)),sem((4,pairs))]+pair_sems(zc)*2+pair_sems(n)*2+pair_sems(zc)*3+[sem((2,6))]+gather_sems(n,2)+gather_sems(n,2))
 
-def last_kernel(n,copies,heads,DK,DV,F,H,n1c,dyq,dsm,smalls,totals,oq,ok,ov,ob,od,qc,kc,vc,onorm,offn,ohead,olog,obias):
+def last_kernel(n,copies,heads,DK,DV,F,H,n1c,dyq,dsm,smalls,totals,*refs):
+    moved=refs[:7]; oq,ok,ov,ob,od,qc,kc,vc,onorm,offn,ohead,olog,obias=refs[7:20]; moved_out=refs[20:27]; buf,sem,msem=refs[27:30]; held=refs[30:]
+    step=buf.shape[1]//4
+    jobs=[pltpu.make_async_copy(dyq.at[:,pl.ds(j*step,step)],buf.at[:,pl.ds(j*step,step)],sem.at[j]) for j in range(4)]
+    for c in jobs: c.start()
+    fetch=[pltpu.make_async_copy(a,b,msem.at[j]) for j,(a,b) in enumerate(zip(moved,held))]
+    for c in fetch: c.start()
     n1=n1c[...].reshape(n1c.shape[0]*n1c.shape[1],n1c.shape[2])
+    sm=dg(dsm[...],n1,0,0)
+    ob[...]=sm[0:heads]; od[...]=sm[heads:2*heads]
     wk=heads*DK
+    got=0
     for ref,start in ((oq,0),(ok,wk),(ov,2*wk)):
-        width=ref.shape[1]
-        for a in range(0,width,512):
-            b=min(a+512,width)
-            ref[:,a:b]=dg(n1,dyq[:,start+a:start+b],0,0)
-    sm=dg(n1,dsm[...],0,0)
-    ob[...]=sm[:,0:heads]; od[...]=sm[:,heads:2*heads]
+        for a in range(0,ref.shape[1],256):
+            b=min(a+256,ref.shape[1])
+            while got*step<start+b: jobs[got].wait(); got+=1
+            ref[:,a:b]=dg(n1,buf[:,start+a:start+b],0,0)
+    moves=[pltpu.make_async_copy(a,b,msem.at[j]) for j,(a,b) in enumerate(zip(held,moved_out))]
+    for f,c in zip(fetch,moves): f.wait(); c.start()
     zc=totals.shape[0]
     for z in range(zc):
         onorm[0:1,z*F:(z+1)*F]=totals[z,0:1,0:F]
@@ -581,19 +598,21 @@
     head=lax.div(s*heads,n)
     taps=0.0
     for sq in range(n//copies//heads): taps=taps+smalls[(sq*heads+head)*copies]
-    cols=col_form(taps)
-    cq,cv=qc.shape[0],vc.shape[0]
+    cq,cv=qc.shape[1],vc.shape[1]
     for part in range(n//heads):
         @pl.when(lax.rem(s,n//heads)==part)
         def _():
-            qc[...]=cols[part*cq:(part+1)*cq,4:8]
-            kc[...]=cols[DK+part*cq:DK+(part+1)*cq,4:8]
-            vc[...]=cols[2*DK+part*cv:2*DK+(part+1)*cv,4:8]
-def last(n,copies,heads,DK,DV,F,H,n1c,dyq,dsm,smalls,totals,cq,cv):
+            qc[...]=taps[4:8,part*cq:(part+1)*cq]
+            kc[...]=taps[4:8,DK+part*cq:DK+(part+1)*cq]
+            vc[...]=taps[4:8,2*DK+part*cv:2*DK+(part+1)*cv]
+    for c in moves: c.wait()
+def last(n,copies,heads,DK,DV,F,H,n1c,dyq,dsm,smalls,totals,cq,cv,moved):
     D=F*totals.shape[0]; Dc=n1c.shape[2]
-    return pl.pallas_call(functools.partial(last_kernel,n,copies,heads,DK,DV,F,H),name="last",
-      out_shape=(S((Dc,heads*DK)),S((Dc,heads*DK)),S((Dc,heads*DV)),S((Dc,heads)),S((Dc,heads)),S((cq,4)),S((cq,4)),S((cv,4)),S((1,D)),S((1,D)),S((1,DV)),S((1,H)),S((1,H))),
-      in_specs=[VM]*5,out_specs=(VM,)*13,compiler_params=pltpu.CompilerParams(vmem_limit_bytes=56*2**20))(n1c,dyq,dsm,smalls,totals)
+    r=pl.pallas_call(functools.partial(last_kernel,n,copies,heads,DK,DV,F,H),name="last",
+      out_shape=(S((Dc,heads*DK)),S((Dc,heads*DK)),S((Dc,heads*DV)),S((heads,Dc)),S((heads,Dc)),S((4,cq)),S((4,cq)),S((4,cv)),S((1,D)),S((1,D)),S((1,DV)),S((1,H)),S((1,H)))+tuple(S(x.shape) for x in moved),
+      in_specs=[VM,ANY,VM,VM,VM]+[ANY]*7,out_specs=(VM,)*13+(ANY,)*7,scratch_shapes=[pltpu.VMEM(dyq.shape,bf16),pltpu.SemaphoreType.DMA((4,)),pltpu.SemaphoreType.DMA((7,))]+[pltpu.VMEM(x.shape,f32) for x in moved],
+      compiler_params=pltpu.CompilerParams(vmem_limit_bytes=56*2**20))(n1c,dyq,dsm,smalls,totals,*moved)
+    return r
 
 
 MESH=pl.DeviceIdType.MESH
@@ -735,6 +754,7 @@
 
 class ToPairs:
     def __init__(self,n,copies,heads,local_len,src,rows_src,dst,rows_dst,DK,DV,send,recv):
+        self.cs=[]
         self.__dict__.update(n=n,copies=copies,heads=heads,ll=local_len,src=src,rows_src=rows_src,dst=dst,rows_dst=rows_dst,DK=DK,DV=DV,send=send,recv=recv)
     def parts(self,t):
         s=lax.axis_index("seq"); ll,DK,DV,heads=self.ll,self.DK,self.DV,self.heads
@@ -748,14 +768,14 @@
             out.append((self.src.at[rows,pl.ds(pl.multiple_of(start+head*width,128),width)],self.dst.at[to,pl.ds(at,width)]))
         out.append((self.rows_src.at[pl.ds(pl.multiple_of(pair*8,8),8),:],self.rows_dst.at[pl.ds(pl.multiple_of(s*8,8),8),:]))
         return out
-    def start(self):
-        s=lax.axis_index("seq"); self.cs=[]
+    def start(self,i):
+        s=lax.axis_index("seq")
         for d in range(self.n):
             t=lax.rem(s+d,self.n)
-            for i,(a,b) in enumerate(self.parts(t)):
-                if d==0: c=pltpu.make_async_copy(a,b,self.recv.at[i,0])
-                else: c=pltpu.make_async_remote_copy(src_ref=a,dst_ref=b,send_sem=self.send.at[i,d],recv_sem=self.recv.at[i,d],device_id={"seq":t},device_id_type=MESH)
-                c.start(); self.cs.append(c)
+            a,b=self.parts(t)[i]
+            if d==0: c=pltpu.make_async_copy(a,b,self.recv.at[i,0])
+            else: c=pltpu.make_async_remote_copy(src_ref=a,dst_ref=b,send_sem=self.send.at[i,d],recv_sem=self.recv.at[i,d],device_id={"seq":t},device_id_type=MESH)
+            c.start(); self.cs.append(c)
     def finish(self):
         for c in self.cs: c.wait()
 
@@ -934,7 +954,7 @@
         gate_proj, o_flat, branch, attn_part, taps, *saved,
     ) = forward(
         seq_devices, shard_count, copies, head_count, tokens_flat, cot_flat, norm_row, head_row, doc_starts, decay_log,
-        decay_bias, beta_weight, decay_weight, query_conv, key_conv, value_conv, query_weight, key_weight, value_weight,
+        decay_bias, beta_weight.T, decay_weight.T, query_conv.T, key_conv.T, value_conv.T, query_weight, key_weight, value_weight,
         outgate_weight, output_weight, gate_weight, key_dim, value_dim,
     )
     residual, grad_residual, attn_cot, grad_ffn_part, out_part, hidden_all, dgate_all, dup_all, normed_two_cols = ffn(
@@ -949,14 +969,18 @@
         full_output, full_one, full_outgate, out_part, branch, hidden_all, dgate_all, dup_all, normed_two_cols,
         normed_one_cols, cot_cols,
     )
-    out_query, out_key, out_value, out_beta, out_decay, out_qconv, out_kconv, out_vconv, out_norm, out_ffn, out_head, out_log, out_bias = last(
+    (
+        out_query, out_key, out_value, out_beta, out_decay, out_qconv, out_kconv, out_vconv, out_norm, out_ffn, out_head,
+        out_log, out_bias, output, grad_tokens, out_gate, out_up, out_down, out_output, out_outgate,
+    ) = last(
         seq_devices, copies, head_count, key_dim, value_dim, feature_part, decay_log.shape[0], normed_one_cols, qkv_all,
         small_all, smalls, totals, query_conv.shape[0], value_conv.shape[0],
+        (output, grad_tokens, out_gate, out_up, out_down, out_output, out_outgate),
     )
     shape3 = (seq_count, local_len, feature_part)
     return (
         output.reshape(shape3), grad_tokens.reshape(shape3), out_norm[0], out_query, out_key, out_value, out_outgate,
-        out_beta, out_decay, out_qconv, out_kconv, out_vconv, out_log[0], out_bias[0], out_head[0], out_output,
+        out_beta.T, out_decay.T, out_qconv.T, out_kconv.T, out_vconv.T, out_log[0], out_bias[0], out_head[0], out_output,
         out_ffn[0], out_gate, out_up, out_down,
     )
 

time: 476 us -> 427 us (0.90)
  Pallas kernels: 450 us -> 426 us
  local copies, waits for them, and re-layouts: 23.7 us -> 0 us
    pallas_call x3, Pallas kernels: 442 us -> 414 us  [call(): pl.pallas_call(kernel, name=name, out_shape=tuple(outs), in_specs=specs,...]
    unnamed x27 -> x0, local copies, waits for them, and re-layouts: 23.7 us -> none
where the time goes in v6:
time: 427 us
  Pallas kernels  426 us (100%)
    pallas_call x3, Pallas kernels, call(): pl.pallas_call(kernel, name=name, out_shape=tuple(outs), in_specs=specs,...  414 us
    pallas_call x1, Pallas kernels, last(): pl.pallas_call(functools.partial(last_kernel, n, copies, heads, DK, DV, F...  12 us

profile of v6, /device:TPU:0, one launch (start us, length us, event | category | flops | bytes accessed | tf_op | source)
XLA Modules:
  0.0 427.0 jit_solution(16120221958744503829)
XLA Ops:
  0.7 142.9 %mixer.1 = (f32[256,128]{1,0:T(8,128)}, bf16[256,2048]{1,0:T(8,128)(2,1)}, bf16[2048,2176]{1,0:T(8,128)(2,1)}, bf16[2048,1024]{1,0:T(8,128)(2,1)}, bf16[1024,204...) custom-call(bf16[256,512]{1,0:T(8,128)(2,1)} %bitcast.22, ...), custom_call_target="tpu_custom_call" | custom-call | tf_op jit(solution)/shard_map/mixer/pallas_call | solution.py:922
  143.6 137.7 %ffn.1 = (f32[256,512]{1,0:T(8,128)}, f32[256,512]{1,0:T(8,128)}, bf16[256,2048]{1,0:T(8,128)(2,1)}, f32[8,512]{1,0:T(8,128)}, bf16[256,2048]{1,0:T(8,128)(2,1)}...) custom-call(bf16[256,2048]{1,0:T(8,128)(2,1)} %get-tuple-element.85., ...), custom_call_target="tpu_custom_call" | custom-call | tf_op jit(solution)/shard_map/ffn/pallas_call | solution.py:922
  281.3 133.5 %back.1 = (f32[256,512]{1,0:T(8,128)}, f32[256,512]{1,0:T(8,128)}, f32[8,8,512]{2,1,0:T(8,128)}, f32[4,8,512]{2,1,0:T(8,128)}, f32[256,1408]{1,0:T(8,128)}, /*in...) custom-call(bf16[256,2048]{1,0:T(8,128)(2,1)} %get-tuple-element.88., ...), custom_call_target="tpu_custom_call" | custom-call | tf_op jit(solution)/shard_map/back/pallas_call | solution.py:922
  414.8 12.0 %last.1 = (f32[256,512]{1,0:T(8,128)}, f32[256,512]{1,0:T(8,128)}, f32[256,1024]{1,0:T(8,128)}, f32[4,256]{1,0:T(4,128)}, f32[4,256]{1,0:T(4,128)}, /*index=5*/f...) custom-call(bf16[8,256,256]{2,1,0:T(8,128)(2,1)} %get-tuple-element., ...), custom_call_target="tpu_custom_call" | custom-call | tf_op jit(solution)/shard_map/last/pallas_call | solution.py:611

commit v7 on v1

v7 whole, which is shorter than its diff:
```python
import functools
from types import SimpleNamespace
import jax, jax.numpy as jnp
from jax import lax
from jax.experimental import pallas as pl
from jax.experimental.pallas import tpu as pltpu
from jax.sharding import PartitionSpec
f32=jnp.float32; bf16=jnp.bfloat16
SPAN=128
EPSILON=1e-6
HI=lax.Precision.HIGHEST

def dg(a,b,ca=1,cb=0):
    return lax.dot_general(a,b,(((ca,),(cb,)),((),())),preferred_element_type=f32)
def halves(x):
    h=x.astype(bf16)
    return h,(x-h.astype(f32)).astype(bf16)
def mm3(a,b,ca=1,cb=0):
    ah,al=halves(a); bh,bl=halves(b)
    return dg(ah,bh,ca,cb)+(dg(al,bh,ca,cb)+dg(ah,bl,ca,cb))
def mm1(a,b,ca=1,cb=0):
    return dg(a.astype(bf16),b.astype(bf16),ca,cb)
def mmx(a,b,ca=1,cb=0):
    return lax.dot_general(a,b,(((ca,),(cb,)),((),())),preferred_element_type=f32,precision=HI)

def square_masks():
    i=lax.broadcasted_iota(jnp.int32,(SPAN,SPAN),0); j=lax.broadcasted_iota(jnp.int32,(SPAN,SPAN),1)
    return i,j
def positions(base,rows,cols,axis):
    return base+lax.broadcasted_iota(jnp.int32,(rows,cols),axis)
class Row:
    def __init__(self,ref,row):
        self.ref=ref; self.row=row; self.shape=ref.shape[1:]
    def __getitem__(self,e):
        return self.ref[self.row,e]

def doc_count(starts,pos):
    n=jnp.zeros(pos.shape,jnp.int32)
    for e in range(starts.shape[0]):
        n=n+jnp.where(starts[e]<=pos,1,0)
    return n
def doc_age(starts,pos):
    s=jnp.zeros(pos.shape,jnp.int32)
    for e in range(starts.shape[0]):
        s=jnp.where(starts[e]<=pos,starts[e],s)
    return pos-s
def count_at(starts,p):
    n=jnp.int32(0)
    for e in range(starts.shape[0]):
        n=n+jnp.where(starts[e]<=p,1,0)
    return n
def sigmoid(x):
    return 1.0/(1.0+jnp.exp(-x))
def softplus(x):
    return jnp.maximum(x,0.0)+jnp.log(1.0+jnp.exp(-jnp.abs(x)))

def inverses(blocks_a,t_ref):
    i,j=square_masks()
    eye=jnp.where(i==j,1.0,0.0)
    blocks=range(t_ref.shape[0])
    for n in blocks: t_ref[n]=eye-jnp.where((i//2)==(j//2),blocks_a(n),0.0)
    size=2
    while size<SPAN:
        part=((i//(2*size))==(j//(2*size)))&((i//size)!=(j//size))
        x=[dg(jnp.where(part,blocks_a(n),0.0).astype(bf16),t_ref[n].astype(bf16)).astype(bf16) for n in blocks]
        for n in blocks: t_ref[n]=t_ref[n]-dg(t_ref[n].astype(bf16),x[n])
        size*=2
    for n in blocks:
        Tb=t_ref[n].astype(bf16); Ah,Al=halves(blocks_a(n))
        rest=eye-Tb.astype(f32)-(dg(Ah,Tb)+dg(Al,Tb))
        t_ref[n]=Tb.astype(f32)+dg(Tb,rest.astype(bf16))

def position_rows(raw,starts,base,rate,bias):
    r=raw.shape[1]
    row=lax.broadcasted_iota(jnp.int32,(8,r),0)
    g=-rate*softplus(raw[1:2]+bias)
    i=lax.broadcasted_iota(jnp.int32,(r,r),0); j=lax.broadcasted_iota(jnp.int32,(r,r),1)
    G=mmx(jnp.broadcast_to(g,(8,r)),jnp.where((i<=j)&((i//SPAN)==(j//SPAN)),1.0,0.0))
    docs=doc_count(starts,positions(base,8,r,1)).astype(f32)
    out=jnp.where(row==0,sigmoid(raw[0:1]),0.0)
    for k,x in ((1,g),(2,G),(3,raw[1:2]),(4,docs)): out=jnp.where(row==k,x,out)
    return out

def span_terms(n,q,k,starts,xc,xr):
    i,j=square_masks()
    before=count_at(starts,n*SPAN-1).astype(f32)
    wide=lambda c: jnp.broadcast_to(c,(SPAN,128))
    beta=wide(xc[:,0:1]); G=wide(xc[:,2:3]); docs=wide(xc[:,4:5])
    incl=(i>=j)&(docs[:,:SPAN]==xr[4:5])
    D=jnp.where(incl,jnp.exp(jnp.where(incl,G[:,:SPAN]-xr[2:3],0.0)),0.0)
    gam=jnp.where(docs==before,jnp.exp(G),0.0)
    end=jnp.where(docs==docs[SPAN-1:SPAN],jnp.exp(G[SPAN-1:SPAN]-G),0.0)
    KK=dg(k,k,1,1); QK=dg(q,k,1,1)
    return beta,D,gam,end,KK,QK,i,j


SM=pl.BlockSpec(memory_space=pltpu.SMEM); VM=pl.BlockSpec(memory_space=pltpu.VMEM)
def S(shape,dt=f32): return jax.ShapeDtypeStruct(shape,dt)


MESH=pl.DeviceIdType.MESH
ANY=pl.BlockSpec(memory_space=pl.ANY)

def flip(s,bit):
    return s+bit-2*bit*lax.rem(lax.div(s,bit),2)

def flips(s,mask):
    bit=1
    while bit<=mask:
        if mask&bit: s=flip(s,bit)
        bit*=2
    return s

def greet(n,zc):
    s=lax.axis_index("seq"); z=lax.axis_index("shard")
    bar=pltpu.get_barrier_semaphore()
    for d in range(1,n):
        pl.semaphore_signal(bar,inc=1,device_id={"seq":lax.rem(s+d,n)},device_id_type=MESH)
    for d in range(1,zc):
        pl.semaphore_signal(bar,inc=1,device_id={"shard":lax.rem(z+d,zc)},device_id_type=MESH)
    pl.semaphore_wait(bar,n-1+zc-1)

def links(n):
    return 8 if n==8 else n

class SeqGather:
    def __init__(self,n,src,dst,axis,sems,c0=0):
        self.n=n; self.src=src; self.dst=dst; self.axis=axis; self.send,self.recv,self.loc=sems
        self.R,self.C=src.shape
        self.r0=0; self.nr=self.R; self.c0=c0
        self.s=lax.axis_index("seq")
        self.open=[]
    def slot(self,t,a,b):
        if self.axis==0:
            return self.dst.at[pl.ds(pl.multiple_of(t*self.R+self.r0+a,16),b-a),pl.ds(self.c0,self.C)]
        return self.dst.at[pl.ds(self.r0+a,b-a),pl.ds(pl.multiple_of(t*self.C,128),self.C)]
    def copy(self,src,t,a,b,k,to):
        c=pltpu.make_async_remote_copy(src_ref=src,dst_ref=self.slot(t,a,b),send_sem=self.send.at[k],recv_sem=self.recv.at[k],device_id={"seq":to},device_id_type=MESH)
        c.start()
        return c
    def pass_on(self,t,a,b,k,to):
        return self.copy(self.slot(t,a,b),t,a,b,k,to)
    def start(self):
        s=self.s; nr=self.nr
        mine=self.src.at[pl.ds(self.r0,nr),:]
        self.own=pltpu.make_async_copy(mine,self.slot(s,0,nr),self.loc)
        self.own.start()
        masks=(2,4) if self.n==8 else range(2,self.n,2)
        self.direct=[self.copy(mine,s,0,nr,i+1,flips(s,m)) for i,m in enumerate(masks)]
        self.open.append(self.copy(mine,s,0,nr,0,flip(s,1)))
    def middle(self):
        s=self.s; nr=self.nr; h=nr//2
        if self.n!=8: return
        x,y=flip(s,2),flip(s,4)
        self.direct[0].wait_recv()
        fa=self.pass_on(x,0,h,3,y)
        self.open.append(self.pass_on(x,0,nr,5,flip(s,1)))
        self.direct[1].wait_recv()
        fb=self.pass_on(y,h,nr,4,x)
        self.open.append(self.pass_on(y,0,nr,6,flip(s,1)))
        self.diag=(fa,fb)
    def late(self):
        s=self.s; nr=self.nr
        if self.n==8:
            for f in self.diag: f.wait_recv()
            self.open.append(self.pass_on(flips(s,6),0,nr,7,flip(s,1)))
            for f in self.diag: f.wait_send()
        else:
            for i,m in enumerate(range(2,self.n,2)):
                self.direct[i].wait_recv()
                self.open.append(self.pass_on(flips(s,m),0,nr,self.n//2+i,flip(s,1)))
        for f in self.direct: f.wait_send()
    def finish(self):
        for f in self.open: f.wait()
        self.own.wait()

class ShardGather:
    def __init__(self,zc,src,dst,send,recv):
        self.zc=zc; self.src=src; self.dst=dst; self.send=send; self.recv=recv
        self.z=lax.axis_index("shard"); self.C=src.shape[1]
    def slot(self):
        return self.dst.at[:,pl.ds(pl.multiple_of(self.z*self.C,128),self.C)]
    def start(self):
        self.own=pltpu.make_async_copy(self.src,self.slot(),self.recv.at[0]); self.own.start()
        self.cs=[]
        for d in range(1,self.zc):
            c=pltpu.make_async_remote_copy(src_ref=self.src,dst_ref=self.slot(),send_sem=self.send.at[d],recv_sem=self.recv.at[d],device_id={"shard":lax.rem(self.z+d,self.zc)},device_id_type=MESH)
            c.start(); self.cs.append(c)
    def finish(self):
        for c in self.cs: c.wait()
        self.own.wait()

class ShardSplit:
    def __init__(self,zc,src,box,send,recv):
        self.zc=zc; self.src=src; self.box=box; self.send=send; self.recv=recv
        self.z=lax.axis_index("shard"); self.C=box.shape[2]
    def start(self):
        C=self.C
        self.own=pltpu.make_async_copy(self.src.at[:,pl.ds(pl.multiple_of(self.z*C,128),C)],self.box.at[0],self.recv.at[0]); self.own.start()
        self.cs=[]
        for d in range(1,self.zc):
            to=lax.rem(self.z+d,self.zc)
            c=pltpu.make_async_remote_copy(src_ref=self.src.at[:,pl.ds(pl.multiple_of(to*C,128),C)],dst_ref=self.box.at[d],send_sem=self.send.at[d],recv_sem=self.recv.at[d],device_id={"shard":to},device_id_type=MESH)
            c.start(); self.cs.append(c)
    def finish(self):
        for c in self.cs: c.wait()
        self.own.wait()

class ShardAll:
    def __init__(self,axis,n,box,send,recv):
        self.axis=axis; self.n=n; self.box=box; self.send=send; self.recv=recv; self.me=lax.axis_index(axis)
    def start(self):
        self.cs=[]
        for d in range(1,self.n):
            c=pltpu.make_async_remote_copy(src_ref=self.box.at[self.me],dst_ref=self.box.at[self.me],send_sem=self.send.at[d],recv_sem=self.recv.at[d],device_id={self.axis:lax.rem(self.me+d,self.n)},device_id_type=MESH)
            c.start(); self.cs.append(c)
    def finish(self):
        for c in self.cs: c.wait()

class ColumnSplit:
    def __init__(self,n,src,dst,send,recv):
        self.n=n; self.src=src; self.dst=dst; self.send=send; self.recv=recv
        self.s=lax.axis_index("seq"); self.C=dst.shape[1]; self.R=src.shape[0]
    def start(self):
        n,s,C,R=self.n,self.s,self.C,self.R
        to_rows=self.dst.at[pl.ds(pl.multiple_of(s*R,16),R),:]
        block=lambda t: self.src.at[:,pl.ds(pl.multiple_of(t*C,128),C)]
        self.own=pltpu.make_async_copy(block(s),to_rows,self.recv.at[0]); self.own.start()
        self.cs=[]
        for d in range(1,n):
            t=lax.rem(s+d,n)
            c=pltpu.make_async_remote_copy(src_ref=block(t),dst_ref=to_rows,send_sem=self.send.at[d],recv_sem=self.recv.at[d],device_id={"seq":t},device_id_type=MESH)
            c.start(); self.cs.append(c)
    def finish(self):
        for c in self.cs: c.wait()
        self.own.wait()

class ToPairs:
    def __init__(self,n,copies,heads,local_len,src,rows_src,dst,rows_dst,DK,DV,send,recv,off=0):
        self.cs=[]
        self.__dict__.update(n=n,copies=copies,heads=heads,ll=local_len,src=src,rows_src=rows_src,dst=dst,rows_dst=rows_dst,DK=DK,DV=DV,send=send,recv=recv,off=off)
    def parts(self,t):
        s=lax.axis_index("seq"); ll,DK,DV,heads=self.ll,self.DK,self.DV,self.heads
        pair=lax.div(t,self.copies); seq=lax.div(pair,heads); head=lax.rem(pair,heads)
        rows=pl.ds(pl.multiple_of(seq*ll,ll),ll); to=pl.ds(pl.multiple_of(s*ll+self.off,16),ll)
        if self.rows_src is None:
            return [(self.src.at[rows,pl.ds(pl.multiple_of(head*DV,128),DV)],self.dst.at[to,:])]
        wk=heads*DK
        out=[]
        for start,width,at in ((0,DK,0),(wk,DK,DK),(2*wk,DV,2*DK)):
            out.append((self.src.at[rows,pl.ds(pl.multiple_of(start+head*width,128),width)],self.dst.at[to,pl.ds(at,width)]))
        out.append((self.rows_src.at[pl.ds(pl.multiple_of(pair*8,8),8),:],self.rows_dst.at[pl.ds(pl.multiple_of(s*8,8),8),:]))
        return out
    def start(self,i):
        s=lax.axis_index("seq")
        for d in range(self.n):
            t=lax.rem(s+d,self.n)
            a,b=self.parts(t)[i]
            if d==0: c=pltpu.make_async_copy(a,b,self.recv.at[i,0])
            else: c=pltpu.make_async_remote_copy(src_ref=a,dst_ref=b,send_sem=self.send.at[i,d],recv_sem=self.recv.at[i,d],device_id={"seq":t},device_id_type=MESH)
            c.start(); self.cs.append(c)
    def finish(self):
        for c in self.cs: c.wait()

class FromPairs:
    def __init__(self,n,copies,heads,local_len,items,send,recv):
        self.__dict__.update(n=n,copies=copies,heads=heads,items=items,send=send,recv=recv)
    def start(self):
        s=lax.axis_index("seq"); pairs=self.n//self.copies; p=lax.div(s,self.copies); r=lax.rem(s,self.copies)
        seq=lax.div(p,self.heads); head=lax.rem(p,self.heads); self.cs=[]
        for d in range(pairs):
            t=lax.rem(p+d,pairs)*self.copies+r
            for i,(src,at,dst,to) in enumerate(self.items):
                a=src.at[at(t)]; b=dst.at[to(seq,head)]
                if d==0: c=pltpu.make_async_copy(a,b,self.recv.at[i,0])
                else: c=pltpu.make_async_remote_copy(src_ref=a,dst_ref=b,send_sem=self.send.at[i,d],recv_sem=self.recv.at[i,d],device_id={"seq":t},device_id_type=MESH)
                c.start(); self.cs.append(c)
    def finish(self):
        for c in self.cs: c.wait()

def flat_form(cols):
    r=cols.shape[0]
    i=lax.broadcasted_iota(jnp.int32,(r,r),0); j=lax.broadcasted_iota(jnp.int32,(r,r),1)
    return mmx(cols,jnp.where(i==j,1.0,0.0),0,0)

class SharedColumns:
    def __init__(self,n,zc,src,dst,sems):
        self.n=n; self.zc=zc; self.src=src; self.dst=dst; self.send,self.recv,self.zsend,self.zrecv=sems
        self.s=lax.axis_index("seq"); self.z=lax.axis_index("shard"); self.C=dst.shape[2]; self.q=src.shape[0]//zc
    def start(self):
        rows=pl.ds(pl.multiple_of(self.z*self.q,16),self.q)
        block=lambda t: self.src.at[rows,pl.ds(pl.multiple_of(t*self.C,128),self.C)]
        self.cs=[]
        for d in range(self.n):
            t=lax.rem(self.s+d,self.n)
            if d==0: c=pltpu.make_async_copy(block(t),self.dst.at[self.s,rows,:],self.recv.at[0])
            else: c=pltpu.make_async_remote_copy(src_ref=block(t),dst_ref=self.dst.at[self.s,rows,:],send_sem=self.send.at[d],recv_sem=self.recv.at[d],device_id={"seq":t},device_id_type=MESH)
            c.start(); self.cs.append(c)
    def middle(self):
        for c in self.cs: c.wait()
        strip=self.dst.at[:,pl.ds(pl.multiple_of(self.z*self.q,16),self.q),:]
        self.cs=[]
        for d in range(1,self.zc):
            c=pltpu.make_async_remote_copy(src_ref=strip,dst_ref=strip,send_sem=self.zsend.at[d],recv_sem=self.zrecv.at[d],device_id={"shard":lax.rem(self.z+d,self.zc)},device_id_type=MESH)
            c.start(); self.cs.append(c)
    def finish(self):
        for c in self.cs: c.wait()

def row_form(cols):
    return mmx(jnp.ones((8,cols.shape[1]),f32),cols,1,1)

def col_form(rows):
    r=rows.shape[1]
    i=lax.broadcasted_iota(jnp.int32,(r,r),0); j=lax.broadcasted_iota(jnp.int32,(r,r),1)
    return mmx(jnp.where(i==j,1.0,0.0),rows,1,1)

def gathers(n,pairs,sems):
    send,recv,loc=sems
    return [SeqGather(n,src,dst,axis,(send.at[i],recv.at[i],loc.at[i]),*c0) for i,(src,dst,axis,*c0) in enumerate(pairs)]
def gather_sems(n,k):
    return [pltpu.SemaphoreType.DMA((k,links(n))),pltpu.SemaphoreType.DMA((k,links(n))),pltpu.SemaphoreType.DMA((k,))]
def pair_sems(k):
    return [pltpu.SemaphoreType.DMA((k,)),pltpu.SemaphoreType.DMA((k,))]
def each(ops,name):
    for o in ops: getattr(o,name)()


def conv_pre(u,taps,age,base,rows):
    window=u[pl.ds(base,rows+16),:].astype(f32)
    pre=window[16:]*taps[3:4]
    for back in range(1,4):
        ok=jnp.where(age>=back,1.0,0.0)
        pre=pre+window[16-back:16-back+rows]*ok*taps[3-back:4-back]
    return pre,window

def tiles(width,step): return [(a,min(a+step,width)) for a in range(0,width,step)]

def layer_kernel(cfg,names,*refs):
    n,zc,copies,heads,DK,DV,H=cfg
    r_=SimpleNamespace(**dict(zip(names,refs)))
    tok,cot=r_.tok,r_.cot
    RN,F=tok.shape; D=F*zc; seqs=r_.starts.shape[0]; ll=RN//seqs; L=n*ll; NC=L//SPAN; per=ll//SPAN
    wk=heads*DK; wv=heads*DV; CH=2*DK+DV; FF=r_.wup.shape[1]; N=n*RN; VW=wv
    s=lax.axis_index("seq"); z=lax.axis_index("shard")
    pair=lax.div(s,copies); my_head=lax.rem(pair,heads); at_head=z*heads+my_head
    starts=Row(r_.starts,lax.div(pair,heads))
    count=[0,0,0]
    def zsems():
        count[0]+=1; return r_.zsend.at[count[0]-1],r_.zrecv.at[count[0]-1]
    def qsems():
        count[1]+=1; return r_.qsend.at[count[1]-1],r_.qrecv.at[count[1]-1]
    def gather(src,dst,axis,c0=0):
        count[2]+=1; i=count[2]-1
        return SeqGather(n,src,dst,axis,(r_.gsend.at[i],r_.grecv.at[i],r_.gloc.at[i]),c0)
    def span(m): return pl.ds(pl.multiple_of(m*SPAN,SPAN),SPAN)
    def loop(count_,body,unroll=1): lax.fori_loop(0,count_,lambda i,c: (body(i),c)[1],0,unroll=unroll)
    normed,scale=r_.normed,r_.scale
    pbuf=r_.tokfull.at[:,pl.ds(0,heads*CH)]
    gw_=r_.bufa.at[pl.ds(0,D),pl.ds(0,FF)]; uw_=r_.bufb.at[pl.ds(0,D),pl.ds(0,FF)]; dw_=r_.dw
    wbuf=r_.bufb
    gv=r_.gv; uv=r_.uv
    cotfull,oall,branch,pbf,u_ref,taps_ref=r_.cotfull,r_.oall,r_.branch,r_.pbf,r_.u,r_.taps
    xr_ref,xc_ref,q_ref,k_ref,v_ref,s_ref,w_ref,t_ref,qt_ref,mh_ref,gc_ref=r_.xr,r_.xc,r_.q,r_.k,r_.v,r_.s,r_.w,r_.t,r_.qt,r_.mh,r_.gc
    gate_ref,rbuf,dpre,du_ref,dx_ref,do_ref,dxr,ds_ref=r_.gate,r_.rbuf,r_.dpre,r_.du,r_.dx,r_.do,r_.dxr,r_.ds
    heads_v=pl.ds(0,DV); rest_v=pl.ds(DV,DV)

    put=lambda x,first: dg(x[...],jnp.where(lax.broadcasted_iota(jnp.int32,(x.shape[0],128),0)+first==lax.broadcasted_iota(jnp.int32,(x.shape[0],128),1),1.0,0.0).astype(bf16),0,0)
    ws=r_.ws
    ws[...]=(put(r_.wb,0)+put(r_.wd,heads)).astype(bf16)
    at_row=0
    for x in (r_.qc,r_.kc,r_.vc):
        ws[at_row:at_row+x.shape[1]]=(ws[at_row:at_row+x.shape[1]].astype(f32)+put(x,2*heads)).astype(bf16)
        at_row+=x.shape[1]
    greet(n,zc)
    zt=ShardGather(zc,tok,r_.tokfull,*zsems()); zt.start()
    ws_all=(ws,r_.wq,r_.wk,r_.wv); at=(wk*2+wv,0,wk,wk*2)
    gw=[gather(w,r_.wfull,0,a) for w,a in zip(ws_all,at)]
    each(gw,"start")
    u_ref[0:16]=jnp.zeros((16,CH),bf16)
    rbuf[...]=jnp.zeros(rbuf.shape,f32)
    dx_ref[...]=jnp.zeros(dx_ref.shape,f32)
    rate=jnp.exp(jnp.full((1,1),r_.dlog[at_head],f32)); bias=r_.dbias[at_head]
    each(gw,"middle")
    zt.finish()
    zk=ShardGather(zc,cot,cotfull,*zsems()); zk.start()
    def norm(c):
        r=pl.ds(pl.multiple_of(c*32,32),32)
        x=r_.tokfull[r,:].astype(f32)
        sc=lax.rsqrt(jnp.sum(x*x,axis=1,keepdims=True)/D+EPSILON)
        normed[r,:]=(x*sc*r_.gain[...]).astype(bf16)
        scale[r,:]=jnp.broadcast_to(sc,(32,128))
    loop(RN//32,norm)
    inward=ToPairs(n,copies,heads,ll,pbuf,rbuf,u_ref,xr_ref,DK,DV,r_.isend,r_.irecv,16)
    for i,g in enumerate(gw):
        g.late(); g.finish()
        width=ws_all[i].shape[1]
        buf=r_.sbuf if i==0 else wbuf.at[pl.ds(0,D),pl.ds(0,width)]
        c=pltpu.make_async_copy(r_.wfull.at[:,pl.ds(at[i],width)],buf,r_.ld.at[0,0]); c.start(); c.wait()
        if i==0:
            small=jnp.dot(normed[...],r_.sbuf[...],preferred_element_type=f32)
            for sq in range(seqs):
                fl=flat_form(small[sq*ll:(sq+1)*ll,0:8*((2*heads+7)//8)])
                for h in range(heads):
                    base=(sq*heads+h)*8
                    rbuf[base:base+1]=fl[h:h+1]
                    rbuf[base+1:base+2]=fl[heads+h:heads+h+1]
            cq=wk//n; cv=wv//n; step=D//n
            for kind,(width_c,total,skip) in enumerate(((cq,DK,0),(cq,DK,cq),(cv,DV,2*cq))):
                for j in range(total//width_c):
                    dev=my_head*(total//width_c)+j
                    to=(0,DK,2*DK)[kind]+j*width_c
                    r_.tbuf[to:to+width_c]=r_.sbuf[pl.ds(pl.multiple_of(dev*step+skip,16),width_c),:]
            ident=jnp.where(lax.broadcasted_iota(jnp.int32,(CH,CH),0)==lax.broadcasted_iota(jnp.int32,(CH,CH),1),1.0,0.0).astype(bf16)
            tt=dg(r_.tbuf[...],ident,0,0)
            taps_ref[...]=tt[2*heads:2*heads+4]
        else:
            def column(j,i=i):
                pbuf[:,pl.ds(pl.multiple_of(at[i]+j*256,128),256)]=jnp.dot(normed[...],wbuf[0:D,pl.ds(pl.multiple_of(j*256,256),256)],preferred_element_type=f32).astype(bf16)
            loop(width//256,column)
        inward.start((3,0,1,2)[i])
    n1=SharedColumns(n,zc,normed,r_.n1c,(*qsems(),*zsems())); n1.start()
    zk.finish()
    cc=SharedColumns(n,zc,cotfull,r_.cotc,(*qsems(),*zsems())); cc.start()
    inward.finish()
    gb=[gather(r_.wg,r_.wgfull,0),gather(r_.wo,r_.wofull,1),gather(r_.wgate,gw_,0)]
    each(gb,"start")

    def turn(m):
        r=pl.ds(pl.multiple_of(m*8,8),8)
        x=position_rows(xr_ref[r,:],starts,m*ll,rate,bias)
        xr_ref[r,:]=x
        xc_ref[pl.ds(pl.multiple_of(m*ll,ll),ll),:]=col_form(x)
    loop(n,turn,4)
    taps=taps_ref[...]
    R=128
    def conv(c):
        base=pl.multiple_of(c*R,R)
        age=doc_age(starts,positions(base,R,128,0))[:,0:1]
        pre,unused=conv_pre(u_ref,taps,age,base,R)
        act=pre*sigmoid(pre)
        rows=pl.ds(base,R)
        aq=act[:,:DK]; ak=act[:,DK:2*DK]
        q_ref[rows,:]=(aq*lax.rsqrt(jnp.sum(aq*aq,axis=1,keepdims=True)+EPSILON)*DK**-0.5).astype(bf16)
        k_ref[rows,:]=(ak*lax.rsqrt(jnp.sum(ak*ak,axis=1,keepdims=True)+EPSILON)).astype(bf16)
        v_ref[rows,:]=act[:,2*DK:].astype(bf16)
    loop(L//R,conv)
    n1.middle(); cc.middle()
    kcol,pcol,ecol=pl.ds(0,DK),pl.ds(DK,SPAN),pl.ds(DK+SPAN,DK)
    def local(m):
        xr=xr_ref[pl.ds(pl.multiple_of(m*8,8),8),:]
        for e in range(per):
            b=m*per+e; rows=span(b)
            q=q_ref[rows,:]; k=k_ref[rows,:]; v=v_ref[rows,:]
            beta,Dm,gam,end,KK,QK,i,j=span_terms(b,q,k,starts,xc_ref[rows,:],xr[:,e*SPAN:(e+1)*SPAN])
            dx_ref[rows,0:SPAN]=jnp.where(i>j,beta[:,:SPAN]*Dm*KK,0.0)
            kf=k.astype(f32)
            dpre[rows,rest_v]=jnp.concatenate([beta]*(DV//128),axis=1)*v.astype(f32)
            du_ref[rows,kcol]=((beta*gam)*kf).astype(bf16)
            du_ref[rows,pcol]=(QK*Dm).astype(bf16)
            qt_ref[b,0:SPAN]=(gam*q.astype(f32)).astype(bf16)
            du_ref[rows,ecol]=(end*kf).astype(bf16)
            gc_ref[b]=jnp.broadcast_to(gam[SPAN-1:SPAN],(8,128))
    loop(n,local,4)
    inverses(lambda b: dx_ref[b*SPAN:(b+1)*SPAN,0:SPAN],t_ref)
    def solve(b):
        rows=span(b)
        T=t_ref[b].astype(bf16)
        U=dg(T,dpre[rows,rest_v].astype(bf16)); Wk=dg(T,du_ref[rows,kcol])
        Ub=U.astype(bf16); Wb=Wk.astype(bf16); Pm=du_ref[rows,pcol]; ek=du_ref[rows,ecol]
        dpre[rows,heads_v]=dg(Pm,Ub)
        w_ref[b]=U
        qt_ref[b,0:SPAN]=(qt_ref[b,0:SPAN].astype(f32)-dg(Pm,Wb)).astype(bf16)
        qt_ref[b,SPAN:]=Wb
        ds_ref[b]=dg(ek,Ub,0,0)
        mh_ref[b]=dg(ek,Wb,0,0).astype(bf16)
    loop(NC,solve,4)
    def chain(b,St):
        s_ref[b]=St
        sh,sl=halves(St); mh=mh_ref[b]
        return jnp.concatenate([gc_ref[b][0:1]]*(DV//128),axis=1)*St+ds_ref[b]-(dg(mh,sh)+dg(mh,sl))
    lax.fori_loop(0,NC,chain,jnp.zeros((DK,DV),f32),unroll=2)
    def emit(b):
        rows=span(b)
        x=dg(qt_ref[b],s_ref[b].astype(bf16))
        do_ref[rows,:]=(dpre[rows,heads_v]+x[:SPAN]).astype(bf16)
        w_ref[b]=w_ref[b]-x[SPAN:]
    loop(NC,emit,4)
    seq_rows=lambda t: pl.ds(pl.multiple_of(t*ll,ll),ll)
    outward=FromPairs(n,copies,heads,ll,[(do_ref,lambda t: (seq_rows(t),slice(None)),oall,lambda seq,head: (seq_rows(seq),pl.ds(pl.multiple_of(head*DV,128),DV)))],r_.osend,r_.orecv)
    outward.start()

    gb[0].middle(); gb[0].late(); gb[0].finish()
    c=pltpu.make_async_copy(r_.wgfull,wbuf.at[pl.ds(0,D),pl.ds(0,wv)],r_.ld.at[0,0]); c.start(); c.wait()
    def column(j):
        k_=pl.ds(pl.multiple_of(j*256,256),256)
        gate_ref[:,k_]=jnp.dot(normed[...],wbuf[0:D,k_],preferred_element_type=f32)
    loop(wv//256,column)
    gb[1].middle(); gb[1].late(); gb[1].finish()
    blocks=D//VW
    def load_wo(buf,sems):
        cs=[pltpu.make_async_copy(r_.wofull.at[:,pl.ds(j*VW,VW)],buf.at[pl.ds(j*VW,VW),pl.ds(0,VW)],sems.at[j]) for j in range(blocks)]
        for c in cs: c.start()
        return cs
    for c in load_wo(wbuf,r_.ld.at[0]): c.wait()
    outward.finish()
    def mix(c):
        r=pl.ds(pl.multiple_of(c*32,32),32)
        for h in range(heads):
            hc=pl.ds(h*DV,DV)
            o=oall[r,hc].astype(f32); g=gate_ref[r,hc]
            rho=lax.rsqrt(jnp.sum(o*o,axis=1,keepdims=True)/DV+EPSILON)
            branch[r,hc]=(o*rho*r_.hgain[...]*(g*sigmoid(g))).astype(bf16)
    loop(RN//32,mix)
    inner_tiles=VW//256
    def column(j):
        blk=lax.div(j,inner_tiles); at_=lax.rem(j,inner_tiles)
        w=wbuf[pl.ds(pl.multiple_of(blk*VW,16),VW),pl.ds(pl.multiple_of(at_*256,256),256)]
        pbf[:,pl.ds(pl.multiple_of(j*256,256),256)]=jnp.dot(branch[...],w,preferred_element_type=f32).astype(bf16)
    loop(D//256,column)
    split=ShardSplit(zc,pbf,r_.box,*zsems()); split.start()
    for d in range(1,n): pl.semaphore_signal(r_.free,inc=1,device_id={"seq":lax.rem(s+d,n)},device_id_type=MESH)
    pl.semaphore_wait(r_.free,n-1)
    gu=[gather(r_.wup,uw_,0),gather(r_.wdown,dw_,1)]
    each(gu,"start")
    gb[2].middle()

    F_at=pl.ds(pl.multiple_of(z*F,128),F)
    fgain=r_.fgain[:,F_at]
    sums=r_.sums
    def shard_sum(k,rows8,meanwhile=None):
        sums[k*zc+z]=rows8
        tot=ShardAll("shard",zc,sums.at[pl.ds(k*zc,zc)],*zsems()); tot.start()
        if meanwhile: meanwhile()
        tot.finish()
        t=sums[k*zc]
        for d in range(1,zc): t=t+sums[k*zc+d]
        return col_form(t)[:,0:1]/D
    def boxed(box):
        g=box[0].astype(f32)
        for d in range(1,zc): g=g+box[d].astype(f32)
        return g
    res,gres,nloc,nfull,afull=r_.res,r_.gres,r_.nloc,r_.nfull,r_.normed
    split.finish()
    x=tok[...].astype(f32)+boxed(r_.box)
    res[...]=x
    sc=lax.rsqrt(shard_sum(0,row_form(x*x))+EPSILON)
    nloc[...]=(res[...]*sc*fgain).astype(bf16)
    zg=ShardGather(zc,nloc,nfull,*zsems()); zg.start()
    gb[2].late(); each(gu,"middle"); gb[2].finish()
    zg.finish()
    n2=ColumnSplit(n,nfull,r_.n2c,*qsems()); n2.start()
    for a,b in tiles(FF,512): gv[:,a:b]=jnp.dot(nfull[...],gw_[:,a:b],preferred_element_type=f32)
    gu[0].late(); gu[0].finish()
    for a,b in tiles(FF,512): uv[:,a:b]=jnp.dot(nfull[...],uw_[:,a:b],preferred_element_type=f32)
    hidden,dgate,dup=r_.hidden,r_.dgate,r_.dup
    def act(c):
        rr=pl.ds(pl.multiple_of(c*32,32),32)
        g=gv[rr,:]
        hidden[rr,:]=(g*sigmoid(g)*uv[rr,:]).astype(bf16)
    loop(RN//32,act)
    gh=[gather(hidden,r_.hidfull,0),gather(dgate,r_.dgfull,0),gather(dup,r_.dufull,0)]
    gu[1].late(); gu[1].finish()
    for a,b in tiles(FF,512):
        dh=dg(cotfull[...],dw_[a:b,:],1,1)
        g=gv[:,a:b]; sg=sigmoid(g)
        dgate[:,a:b]=(dh*uv[:,a:b]*sg*(1.0+g*(1.0-sg))).astype(bf16)
        dup[:,a:b]=(dh*(g*sg)).astype(bf16)
    each(gh[1:]+gh[:1],"start")
    def back_two(j):
        rr=pl.ds(pl.multiple_of(j*256,256),256)
        pbf[:,rr]=(dg(dgate[...],gw_[rr,:],1,1)+dg(dup[...],uw_[rr,:],1,1)).astype(bf16)
    loop(D//256,back_two)
    split=ShardSplit(zc,pbf,r_.box,*zsems()); split.start()
    ld=r_.ld
    bufs=(r_.bufa,r_.bufb)
    loads={}
    def load_job(key,i,pieces):
        loads[key]=[]
        for j,(src,to) in enumerate(pieces):
            c=pltpu.make_async_copy(src,bufs[i].at[to],ld.at[i,j]); c.start(); loads[key].append(c)
    def ready(key):
        for c in loads[key]: c.wait()
    whole=lambda w: (pl.ds(0,D),pl.ds(0,w))
    every=lambda w: (pl.ds(0,N),pl.ds(0,w))
    loads["wo"]=load_wo(r_.bufa,ld.at[0])
    load_job("og",1,[(r_.wgfull,whole(wv))])
    def outp(j):
        c_=pl.ds(pl.multiple_of(j*256,256),256)
        r_.outpart[:,c_]=jnp.dot(hidden[...],dw_[:,c_],preferred_element_type=f32).astype(bf16)
    loop(D//256,outp)
    split.finish()
    g=boxed(r_.box)
    gained=fgain*g
    gffn=[None]
    def meanwhile(): gffn[0]=jnp.sum(g*res[...]*sc,axis=0,keepdims=True)
    inner=shard_sum(1,row_form(gained*res[...]),meanwhile)
    gr=cot[...].astype(f32)+sc*(gained-res[...]*(sc*sc*inner))
    gres[...]=gr
    nloc[...]=gr.astype(bf16)
    zg=ShardGather(zc,nloc,afull,*zsems()); zg.start()
    each(gh[1:]+gh[:1],"middle")
    zg.finish()
    so=ShardSplit(zc,r_.outpart,r_.boxo,*zsems()); so.start()

    ready("wo")
    r_.dsm[...]=jnp.zeros(r_.dsm.shape,bf16)
    dob,dgp,bufa,bufb=r_.dob,r_.dgp,r_.bufa,r_.bufb
    def heads_back(c,gh_):
        r=pl.ds(pl.multiple_of(c*64,64),64)
        for h in range(heads):
            hc=pl.ds(h*DV,DV)
            dm=dg(afull[r,0:VW],bufa[h*DV:(h+1)*DV,0:VW],1,1)
            for j in range(1,blocks):
                dm=dm+dg(afull[r,j*VW:(j+1)*VW],bufa[j*VW+h*DV:j*VW+(h+1)*DV,0:VW],1,1)
            dm=dm.astype(bf16).astype(f32)
            o=oall[r,hc].astype(f32); g=gate_ref[r,hc]
            rho=lax.rsqrt(jnp.sum(o*o,axis=1,keepdims=True)/DV+EPSILON)
            zz=o*rho; sg=sigmoid(g); sil=g*sg
            gh_=gh_+jnp.sum(dm*zz*sil,axis=0,keepdims=True)
            dmg=dm*r_.hgain[...]
            dz=dmg*sil
            dob[r,hc]=(rho*(dz-zz*(jnp.sum(dz*zz,axis=1,keepdims=True)/DV))).astype(bf16)
            dgp[r,hc]=(dmg*zz*sg*(1.0+g*(1.0-sg))).astype(bf16)
        return gh_
    grad_head=lax.fori_loop(0,RN//64,heads_back,jnp.zeros((1,DV),f32))
    inward=ToPairs(n,copies,heads,ll,dob,None,do_ref,None,DK,DV,r_.i2send,r_.i2recv); inward.start(0)
    each(gh[1:]+gh[:1],"late")
    n2.finish()
    gk=[gather(dgp,r_.dgpfull,0),gather(branch,r_.brafull,0)]
    inward.finish()
    ca=SharedColumns(n,zc,afull,r_.attc,(*qsems(),*zsems())); ca.start()
    each(gk,"start")

    dpre[L:L+8]=jnp.zeros((8,CH),f32)
    def early(b):
        ds_ref[b]=dg(qt_ref[b][0:SPAN],do_ref[span(b),:],0,0)
    loop(NC,early,4)
    def chain_back(m,dS):
        b=NC-1-m
        x=ds_ref[b]
        ds_ref[b]=dS
        sh,sl=halves(dS); mh=mh_ref[b]
        return jnp.concatenate([gc_ref[b][0:1]]*(DV//128),axis=1)*dS+x-(dg(mh,sh,0,0)+dg(mh,sl,0,0))
    lax.fori_loop(0,NC,chain_back,jnp.zeros((DK,DV),f32),unroll=2)
    def one_span(b,xr):
        rows=span(b)
        q=q_ref[rows,:]; k=k_ref[rows,:]; v=v_ref[rows,:]; dO=do_ref[rows,:]
        beta,Dm,gam,end,KK,QK,i,j=span_terms(b,q,k,starts,xc_ref[rows,:],xr)
        beta2=jnp.concatenate([beta]*(DV//128),axis=1)
        S0=s_ref[b]; dS1=ds_ref[b]
        S0h=S0.astype(bf16); dSh=dS1.astype(bf16)
        kf=k.astype(f32); qf=q.astype(f32); vf=v.astype(f32)
        W=w_ref[b].astype(bf16); T=t_ref[b].astype(bf16)
        Pm=(QK*Dm).astype(bf16)
        dW=dg(Pm,dO,0,0)+jnp.concatenate([end]*(DV//128),axis=1)*dg(k,dSh)
        Y=dg(T,dW.astype(bf16),0,0)
        dOY=jnp.concatenate([dO,Y.astype(bf16)],axis=0)
        dPA=dg(dOY,W,1,1)
        GS=dg(dOY,S0h,1,1)
        dOS=GS[:SPAN]; YS=GS[SPAN:]
        Z=dg(W,dSh,1,1)
        dPD=dPA[:SPAN]*Dm
        EA=jnp.where(i>j,-dPA[SPAN:]*Dm,0.0)
        A1=jnp.concatenate([dPD,beta[:,:SPAN]*EA],axis=0).astype(bf16)
        r1=dg(A1,k)
        r2=dg(A1,jnp.concatenate([q,k],axis=0),0,0)
        dpre[rows,0:DK]=gam*dOS+r1[:SPAN]
        dpre[rows,DK:2*DK]=r1[SPAN:]+r2-(beta*gam)*YS+end*Z
        dpre[rows,2*DK:]=beta2*Y
        EK=EA*KK
        kYS=jnp.sum(kf*YS,axis=1,keepdims=True)
        dbeta=jnp.sum(Y*vf,axis=1,keepdims=True)-gam*kYS+jnp.sum(EK,axis=1,keepdims=True)
        Fm=dPD*QK+beta[:,:SPAN]*EK
        dgam=jnp.sum(qf*dOS,axis=1,keepdims=True)-beta*kYS
        dend=jnp.sum(kf*Z,axis=1,keepdims=True)*end
        dG=jnp.sum(Fm,axis=1,keepdims=True)+dgam*gam-dend
        tail=jnp.sum(jnp.sum(S0*dS1,axis=0,keepdims=True),axis=1,keepdims=True)
        last=jnp.sum(dend,axis=0,keepdims=True)+gam[SPAN-1:SPAN]*tail
        row=lax.broadcasted_iota(jnp.int32,(SPAN,128),0)
        dG=dG+jnp.where(row==SPAN-1,last,0.0)
        dx_ref[rows,0:1]=(dbeta*beta*(1.0-beta))[:,0:1]
        dx_ref[rows,1:2]=dG[:,0:1]
        return jnp.sum(Fm,axis=0,keepdims=True)
    def local_back(m):
        r=pl.ds(pl.multiple_of(m*8,8),8)
        xr=xr_ref[r,:]
        dxr[r,:]=jnp.broadcast_to(jnp.concatenate([one_span(m*per+e,xr[:,e*SPAN:(e+1)*SPAN]) for e in range(per)],axis=1),(8,ll))
    loop(n,local_back,2)
    ca.middle()
    il=lax.broadcasted_iota(jnp.int32,(ll,ll),0); jl=lax.broadcasted_iota(jnp.int32,(ll,ll),1)
    later=jnp.where((il>=jl)&((il//SPAN)==(jl//SPAN)),1.0,0.0)
    def turn_back(m,carry):
        r=pl.ds(pl.multiple_of(m*8,8),8)
        f=flat_form(dx_ref[pl.ds(pl.multiple_of(m*ll,ll),ll),0:8])
        dlog=mmx(jnp.broadcast_to(f[1:2]-dxr[r,:][0:1],(8,ll)),later)
        x=xr_ref[r,:]
        ddp=dlog*(-rate)*sigmoid(x[3:4]+bias)
        row=lax.broadcasted_iota(jnp.int32,(8,ll),0)
        dxr[r,:]=jnp.where(row==0,f[0:1],jnp.where(row==1,ddp,0.0))
        return (carry[0]+jnp.sum(dlog[0:1]*x[1:2],axis=1,keepdims=True),carry[1]+jnp.sum(ddp[0:1],axis=1,keepdims=True))
    zero=jnp.zeros((1,1),f32)
    sl,sb=lax.fori_loop(0,n,turn_back,(zero,zero),unroll=4)
    def norms(c,dt):
        base=pl.multiple_of(c*R,R)
        age=doc_age(starts,positions(base,R,128,0))[:,0:1]
        pre,window=conv_pre(u_ref,taps,age,base,R)
        sg=sigmoid(pre); a_=pre*sg
        rows=pl.ds(base,R)
        d=dpre[rows,:]
        def unit_back(a,dd,f):
            sc_=lax.rsqrt(jnp.sum(a*a,axis=1,keepdims=True)+EPSILON)
            dot=jnp.sum(a*dd,axis=1,keepdims=True)
            return f*(sc_*dd-a*(sc_*sc_*sc_*dot))
        dact=jnp.concatenate([unit_back(a_[:,:DK],d[:,:DK],DK**-0.5),unit_back(a_[:,DK:2*DK],d[:,DK:2*DK],1.0),d[:,2*DK:]],axis=1)
        dp=dact*sg*(1.0+pre*(1.0-sg))
        dpre[rows,:]=dp
        new=[]
        for j in range(4):
            back=3-j
            x=window[16-back:16-back+R]
            if back: x=x*jnp.where(age>=back,1.0,0.0)
            new.append(dt[j]+jnp.sum(x*dp,axis=0,keepdims=True))
        return tuple(new)
    dt=lax.fori_loop(0,L//R,norms,(jnp.zeros((1,CH),f32),)*4)
    def back(c):
        base=pl.multiple_of(c*R,R)
        window=dpre[pl.ds(base,R+8),:]
        age=doc_age(starts,positions(base,R+8,128,0))[:,0:1]
        d=window[:R]*taps[3:4]
        for sh in range(1,4):
            d=d+window[sh:sh+R]*jnp.where(age[sh:sh+R]>=sh,1.0,0.0)*taps[3-sh:4-sh]
        du_ref[pl.ds(base,R),:]=d.astype(bf16)
    loop(L//R,back)
    dyq,dsm=pbuf,r_.dsm
    cut=lambda start,width: (lambda t: (seq_rows(t),pl.ds(start,width)))
    to=lambda start,width: (lambda seq,head: (seq_rows(seq),pl.ds(pl.multiple_of(start+head*width,128),width)))
    outward=FromPairs(n,copies,heads,ll,[(du_ref,cut(0,DK),dyq,to(0,DK)),(du_ref,cut(DK,DK),dyq,to(wk,DK)),(du_ref,cut(2*DK,DV),dyq,to(2*wk,DV)),
        (dxr,lambda t: (pl.ds(pl.multiple_of(t*8,8),8),slice(None)),rbuf,lambda seq,head: (pl.ds(pl.multiple_of((seq*heads+head)*8,8),8),slice(None)))],r_.o2send,r_.o2recv)
    outward.start()

    part=r_.acc
    def spread(first,buf,terms):
        def one(j):
            rr=pl.ds(pl.multiple_of(j*256,256),256)
            t=0.0
            for x,a,b in terms: t=t+dg(x[...],buf[rr,a:b],1,1)
            part[:,rr]=t if first else part[:,rr]+t
        loop(D//256,one)
    staged={}
    def stage(k,ref,shape):
        if k in staged: staged[k].wait()
        return r_.sta.at[pl.ds(0,shape[0]),pl.ds(0,shape[1])] if k==0 else r_.stb.at[pl.ds(0,shape[0]),pl.ds(0,shape[1])]
    def send(k,view,ref):
        staged[k]=pltpu.make_async_copy(view,ref,r_.stsem.at[k]); staged[k].start()
    ready("og"); spread(True,bufb,[(dgp,0,wv)])
    each(gh,"finish")
    load_job("dgate",0,[(r_.dgfull,every(FF))])
    c2=pltpu.make_async_copy(r_.n2c,r_.cola,ld.at[0,4]); c2.start()
    load_job("wqk",1,[(r_.wfull.at[:,pl.ds(0,2*wk)],whole(2*wk))])
    so.finish()
    r_.output[...]=res[...]+boxed(r_.boxo)
    ready("dgate"); c2.wait()
    v_=stage(0,r_.ogate,(D//n,FF))
    for a,b in tiles(FF,512): v_[:,a:b]=dg(r_.cola[...],bufa[0:N,a:b],0,0)
    send(0,v_,r_.ogate)
    load_job("wv",0,[(r_.wfull.at[:,pl.ds(2*wk,wv+128)],whole(wv+128))])
    outward.finish()
    for sq in range(seqs):
        fl=[]
        for e in range(2):
            for h in range(heads): fl.append(rbuf[(sq*heads+h)*8+e:(sq*heads+h)*8+e+1])
        fl=jnp.concatenate(fl+[jnp.zeros((-2*heads%8,ll),f32)]*(1 if 2*heads%8 else 0),axis=0)
        dsm[sq*ll:(sq+1)*ll,0:fl.shape[0]]=col_form(fl).astype(bf16)
    gd=[gather(dsm,r_.dsmfull,0),gather(dyq,r_.dyqfull,0)]
    each(gd,"start")
    ready("wqk"); spread(False,bufb,[(dyq.at[:,pl.ds(0,2*wk)],0,2*wk)])
    load_job("dup",1,[(r_.dufull,every(FF))])
    ready("wv")
    def final(j):
        rr=pl.ds(pl.multiple_of(j*256,256),256)
        pbf[:,rr]=(part[:,rr]+dg(dyq[:,2*wk:],bufa[rr,0:wv],1,1)+dg(dsm[...],bufa[rr,wv:wv+128],1,1)).astype(bf16)
    loop(D//256,final)
    split=ShardSplit(zc,pbf,r_.box,*zsems()); split.start()
    load_job("hid",0,[(r_.hidfull,every(FF))])
    each(gk,"middle"); each(gk,"late")
    ready("dup")
    v_=stage(0,r_.oup,(D//n,FF))
    for a,b in tiles(FF,512): v_[:,a:b]=dg(r_.cola[...],bufb[0:N,a:b],0,0)
    send(0,v_,r_.oup)
    n1.finish(); cc.finish(); ca.finish()
    for g in gk: g.finish()
    cb=pltpu.make_async_copy(r_.cotc,r_.colb,ld.at[1,5]); cb.start()
    load_job("bra",1,[(r_.brafull,every(VW))])
    ready("hid"); cb.wait()
    cots=r_.colb[...].reshape(N,D//n)
    v_=stage(1,r_.odown,(FF,D//n))
    for a,b in tiles(FF,256): v_[a:b,:]=dg(bufa[0:N,a:b],cots,0,0)
    send(1,v_,r_.odown)
    load_job("dgp",0,[(r_.dgpfull,every(wv))])
    split.finish()
    g=boxed(r_.box)
    sc=scale[...][:,0:1]
    gained=r_.gain[:,F_at]*g
    smalls,totals=r_.smalls,r_.totals
    smalls[s]=jnp.zeros(smalls.shape[1:],f32)
    smalls[s,0:1,0:F]=jnp.sum(g*tok[...].astype(f32)*sc,axis=0,keepdims=True)
    smalls[s,1:2,0:F]=gffn[0]
    smalls[s,2:3,0:DV]=grad_head
    lane=lax.broadcasted_iota(jnp.int32,(1,128),1)
    first=jnp.where(lax.rem(s,copies)==0,1.0,0.0)
    smalls[s,3:4,0:128]=first*(jnp.where(lane==at_head,sl,0.0)+jnp.where(lane==H+at_head,sb,0.0))
    for j in range(4): smalls[s,4+j:5+j,0:CH]=dt[j]
    sa=ShardAll("seq",n,smalls,*qsems()); sa.start()
    inner=shard_sum(2,row_form(gained*tok[...].astype(f32)))
    r_.gtok[...]=gres[...]+sc*(gained-tok[...].astype(f32)*(sc*sc*inner))
    each(gd,"middle")
    sa.finish()
    t=smalls[0]
    for d in range(1,n): t=t+smalls[d]
    totals[z]=t
    za=ShardAll("shard",zc,totals,*zsems()); za.start()
    cb=pltpu.make_async_copy(r_.attc,r_.colb,ld.at[1,5]); cb.start()
    ready("bra"); cb.wait()
    atts=r_.colb[...].reshape(N,D//n)
    v_=stage(1,r_.oout,(VW,D//n))
    for a,b in tiles(VW,256): v_[a:b,:]=dg(bufb[0:N,a:b],atts,0,0)
    send(1,v_,r_.oout)
    cb=pltpu.make_async_copy(r_.n1c,r_.colb,ld.at[1,5]); cb.start()
    ready("dgp"); cb.wait()
    n1s=r_.colb[...].reshape(N,D//n)
    v_=stage(0,r_.oog,(D//n,wv))
    for a,b in tiles(wv,512): v_[:,a:b]=dg(n1s,bufa[0:N,a:b],0,0)
    send(0,v_,r_.oog)
    each(gd,"late"); za.finish(); each(gd,"finish")
    staged[0].wait(); staged[1].wait()

def layer(n,zc,copies,heads,DK,DV,H,ins):
    names=("tok","cot","gain","hgain","fgain","starts","dlog","dbias","wb","wd","qc","kc","vc","wq","wk","wv","wg","wo","wgate","wup","wdown")
    RN,F=ins[0].shape; D=F*zc; seqs=ins[5].shape[0]; ll=RN//seqs; L=n*ll; NC=L//SPAN; pairs=n//copies
    wk=heads*DK; wv=heads*DV; CH=2*DK+DV; FF=ins[19].shape[1]; N=n*RN; Dc=D//n; W=max(F,CH)
    bw=max(FF,wv+128,2*wk); big=max(D,N)
    specs=[VM]*5+[SM]*3+[VM]*10+[ANY]*3
    outs=[("output",S((RN,F)),VM),("gtok",S((RN,F)),VM),("smalls",S((n,8,W)),VM),("totals",S((zc,8,W)),VM)]
    for name,shape in (("ogate",(Dc,FF)),("oup",(Dc,FF)),("odown",(FF,Dc)),("oout",(wv,Dc)),("oog",(Dc,wv))): outs.append((name,S(shape),ANY))
    for name,shape in (("dyqfull",(N,heads*CH)),("dsmfull",(N,128)),("n1c",(n,RN,Dc)),("cotc",(n,RN,Dc)),("attc",(n,RN,Dc)),("n2c",(N,Dc)),("wfull",(D,heads*CH+128)),("wgfull",(D,wv)),("wofull",(wv,D)),
        ("hidfull",(N,FF)),("dgfull",(N,FF)),("dufull",(N,FF)),("dgpfull",(N,wv)),("brafull",(N,wv))): outs.append((name,S(shape,bf16),ANY))
    V=pltpu.VMEM; sem=pltpu.SemaphoreType.DMA
    scratch=[("scale",V((RN,128),f32)),("ws",V((Dc,128),bf16)),("sbuf",V((D,128),bf16)),("tbuf",V((CH,128),bf16)),("tokfull",V((RN,D),bf16)),("normed",V((RN,D),bf16)),("cotfull",V((RN,D),bf16)),
        ("nfull",V((RN,D),bf16)),("pbf",V((RN,D),bf16)),("outpart",V((RN,D),bf16)),("acc",V((RN,D),f32)),("uv",V((RN,FF),f32)),("gv",V((RN,FF),f32)),("rbuf",V((pairs*8,ll),f32)),("taps",V((4,CH),f32)),
        ("bufa",V((big,bw),bf16)),("bufb",V((big,bw),bf16)),("dw",V((FF,D),bf16)),("u",V((L+16,CH),bf16)),("xr",V((n*8,ll),f32)),("xc",V((L,8),f32)),("q",V((L,DK),bf16)),("k",V((L,DK),bf16)),("v",V((L,DV),bf16)),
        ("s",V((NC,DK,DV),f32)),("w",V((NC,SPAN,DV),f32)),("t",V((NC,SPAN,SPAN),f32)),("qt",V((NC,2*SPAN,DK),bf16)),("mh",V((NC,DK,DK),bf16)),("gc",V((NC,8,128),f32)),("ds",V((NC,DK,DV),f32)),
        ("dpre",V((L+8,CH),f32)),("du",V((L,CH),bf16)),("dx",V((L,SPAN),f32)),("do",V((L,DV),bf16)),("dxr",V((n*8,ll),f32)),("gate",V((RN,wv),f32)),("oall",V((RN,wv),bf16)),("branch",V((RN,wv),bf16)),
        ("dob",V((RN,wv),bf16)),("dgp",V((RN,wv),bf16)),("dsm",V((RN,128),bf16)),("res",V((RN,F),f32)),("gres",V((RN,F),f32)),("nloc",V((RN,F),bf16)),("box",V((zc,RN,F),bf16)),("boxo",V((zc,RN,F),bf16)),
        ("hidden",V((RN,FF),bf16)),("dgate",V((RN,FF),bf16)),("dup",V((RN,FF),bf16)),("sums",V((3*zc,8,RN),f32)),("cola",V((N,Dc),bf16)),("colb",V((n,RN,Dc),bf16)),("sta",V((Dc,max(FF,wv)),f32)),("stb",V((max(FF,wv),Dc),f32)),
        ("zsend",sem((16,zc))),("zrecv",sem((16,zc))),("qsend",sem((6,n))),("qrecv",sem((6,n))),("gsend",sem((16,links(n)))),("grecv",sem((16,links(n)))),("gloc",sem((16,))),("isend",sem((4,n))),("irecv",sem((4,n))),("i2send",sem((1,n))),("i2recv",sem((1,n))),
        ("osend",sem((1,pairs))),("orecv",sem((1,pairs))),("o2send",sem((4,pairs))),("o2recv",sem((4,pairs))),("ld",sem((2,6))),("stsem",sem((2,))),("free",pltpu.SemaphoreType.REGULAR)]
    all_names=names+tuple(o[0] for o in outs)+tuple(x[0] for x in scratch)
    r=pl.pallas_call(functools.partial(layer_kernel,(n,zc,copies,heads,DK,DV,H),all_names),name="layer",out_shape=tuple(o[1] for o in outs),in_specs=specs,out_specs=tuple(o[2] for o in outs),
        scratch_shapes=[x[1] for x in scratch],compiler_params=pltpu.CompilerParams(collective_id=1,has_side_effects=True,vmem_limit_bytes=63*2**20))(*ins)
    return SimpleNamespace(**{o[0]:x for o,x in zip(outs,r)})


def last_kernel(n,copies,heads,DK,DV,F,H,n1c,dyq,dsm,smalls,totals,*refs):
    moved=refs[:7]; oq,ok,ov,ob,od,qc,kc,vc,onorm,offn,ohead,olog,obias=refs[7:20]; moved_out=refs[20:27]; buf,sem,msem=refs[27:30]; held=refs[30:]
    step=buf.shape[1]//4
    jobs=[pltpu.make_async_copy(dyq.at[:,pl.ds(j*step,step)],buf.at[:,pl.ds(j*step,step)],sem.at[j]) for j in range(4)]
    for c in jobs: c.start()
    fetch=[pltpu.make_async_copy(a,b,msem.at[j]) for j,(a,b) in enumerate(zip(moved,held))]
    for c in fetch: c.start()
    n1=n1c[...].reshape(n1c.shape[0]*n1c.shape[1],n1c.shape[2])
    sm=dg(dsm[...],n1,0,0)
    ob[...]=sm[0:heads]; od[...]=sm[heads:2*heads]
    wk=heads*DK
    got=0
    for ref,start in ((oq,0),(ok,wk),(ov,2*wk)):
        for a in range(0,ref.shape[1],256):
            b=min(a+256,ref.shape[1])
            while got*step<start+b: jobs[got].wait(); got+=1
            ref[:,a:b]=dg(n1,buf[:,start+a:start+b],0,0)
    moves=[pltpu.make_async_copy(a,b,msem.at[j]) for j,(a,b) in enumerate(zip(held,moved_out))]
    for f,c in zip(fetch,moves): f.wait(); c.start()
    zc=totals.shape[0]
    for z in range(zc):
        onorm[0:1,z*F:(z+1)*F]=totals[z,0:1,0:F]
        offn[0:1,z*F:(z+1)*F]=totals[z,1:2,0:F]
    t=totals[0]
    for z in range(1,zc): t=t+totals[z]
    ohead[...]=t[2:3,0:DV]
    olog[...]=t[3:4,0:H]; obias[...]=t[3:4,H:2*H]
    s=lax.axis_index("seq")
    head=lax.div(s*heads,n)
    taps=0.0
    for sq in range(n//copies//heads): taps=taps+smalls[(sq*heads+head)*copies]
    cq,cv=qc.shape[1],vc.shape[1]
    for part in range(n//heads):
        @pl.when(lax.rem(s,n//heads)==part)
        def _():
            qc[...]=taps[4:8,part*cq:(part+1)*cq]
            kc[...]=taps[4:8,DK+part*cq:DK+(part+1)*cq]
            vc[...]=taps[4:8,2*DK+part*cv:2*DK+(part+1)*cv]
    for c in moves: c.wait()
def last(n,copies,heads,DK,DV,F,H,n1c,dyq,dsm,smalls,totals,cq,cv,moved):
    D=F*totals.shape[0]; Dc=n1c.shape[2]
    r=pl.pallas_call(functools.partial(last_kernel,n,copies,heads,DK,DV,F,H),name="last",
      out_shape=(S((Dc,heads*DK)),S((Dc,heads*DK)),S((Dc,heads*DV)),S((heads,Dc)),S((heads,Dc)),S((4,cq)),S((4,cq)),S((4,cv)),S((1,D)),S((1,D)),S((1,DV)),S((1,H)),S((1,H)))+tuple(S(x.shape) for x in moved),
      in_specs=[VM,ANY,VM,VM,VM]+[ANY]*7,out_specs=(VM,)*13+(ANY,)*7,scratch_shapes=[pltpu.VMEM(dyq.shape,bf16),pltpu.SemaphoreType.DMA((4,)),pltpu.SemaphoreType.DMA((7,))]+[pltpu.VMEM(x.shape,f32) for x in moved],
      compiler_params=pltpu.CompilerParams(vmem_limit_bytes=56*2**20))(n1c,dyq,dsm,smalls,totals,*moved)
    return r


def per_device(
    tokens, doc_starts, norm_gain, query_weight, key_weight, value_weight, outgate_weight,
    beta_weight, decay_weight, query_conv, key_conv, value_conv, decay_log, decay_bias, head_gain,
    output_weight, ffn_gain, gate_weight, up_weight, down_weight, cotangent,
):
    seq_count, local_len, feature_part = tokens.shape
    row_count = seq_count * local_len
    shard_count = lax.axis_size("shard")
    seq_devices = lax.axis_size("seq")
    head_count = beta_weight.shape[1]
    key_dim = query_weight.shape[1] // head_count
    value_dim = value_weight.shape[1] // head_count
    pairs = seq_count * head_count
    copies = seq_devices // pairs
    flat = lambda x: x.reshape(row_count, x.shape[2])
    tokens_flat, cot_flat = flat(tokens), flat(cotangent)
    head_row, norm_row, ffn_row = head_gain[None], norm_gain[None], ffn_gain[None]
    ran = layer(
        seq_devices, shard_count, copies, head_count, key_dim, value_dim, decay_log.shape[0],
        (
            tokens_flat, cot_flat, norm_row, head_row, ffn_row, doc_starts, decay_log, decay_bias, beta_weight.T,
            decay_weight.T, query_conv.T, key_conv.T, value_conv.T, query_weight, key_weight, value_weight, outgate_weight,
            output_weight, gate_weight, up_weight, down_weight,
        ),
    )
    (
        out_query, out_key, out_value, out_beta, out_decay, out_qconv, out_kconv, out_vconv, out_norm, out_ffn, out_head,
        out_log, out_bias, output, grad_tokens, out_gate, out_up, out_down, out_output, out_outgate,
    ) = last(
        seq_devices, copies, head_count, key_dim, value_dim, feature_part, decay_log.shape[0], ran.n1c, ran.dyqfull,
        ran.dsmfull, ran.smalls, ran.totals, query_conv.shape[0], value_conv.shape[0],
        (ran.output, ran.gtok, ran.ogate, ran.oup, ran.odown, ran.oout, ran.oog),
    )
    shape3 = (seq_count, local_len, feature_part)
    return (
        output.reshape(shape3), grad_tokens.reshape(shape3), out_norm[0], out_query, out_key, out_value, out_outgate,
        out_beta.T, out_decay.T, out_qconv.T, out_kconv.T, out_vconv.T, out_log[0], out_bias[0], out_head[0], out_output,
        out_ffn[0], out_gate, out_up, out_down,
    )


def solution(mesh):
    P = PartitionSpec
    rows, cols = P("seq", "shard"), P("shard", "seq")
    both, acts = P(("shard", "seq"), None), P(None, "seq", "shard")
    return jax.shard_map(
        per_device,
        mesh=mesh,
        in_specs=(acts, P(), P()) + (rows,) * 6 + (both,) * 3 + (P(), P(), P(), cols, P(), rows, rows, cols, acts),
        out_specs=(acts, acts, P()) + (rows,) * 6 + (both,) * 3 + (P(), P(), P(), cols, P(), rows, rows, cols),
        check_vma=False,
    )
```

time: 1230 us -> 407 us (0.33)
  waiting for transfers between devices: 787 us -> 0 us
  Pallas kernels: 75.6 us -> 406 us
  blocking collectives: 157 us -> 0 us
  matrix products: 92.2 us -> 0 us
  other arithmetic: 37.9 us -> 0 us
  local copies, waits for them, and re-layouts: 37 us -> 0 us
  starting transfers between devices: 16.3 us -> 0 us
  between operations: 15.2 us -> 0.85 us
    reduce_scatter x12 -> x0, waiting for transfers between devices: 482 us -> none  [the longest x8 401 us: scattered(): lax.psum_scatter(grad.astype(bf16), 'seq', scatter_dimension=axis, tiled=...]
    pallas_call x2, Pallas kernels: 75.6 us -> 406 us  [the longest x1 394 us: layer(): pl.pallas_call(functools.partial(layer_kernel, (n, zc, copies, heads, DK,...]
    all_gather x12 -> x0, waiting for transfers between devices: 290 us -> none  [the longest x4 90.8 us: whole_rows(): return lax.all_gather(part_rows, 'shard', axis=2, tiled=True)]
    dot_general x30 -> x0, matrix products: 92.2 us -> none  [the longest x10 35.1 us: project(): return jnp.dot(a, b, preferred_element_type=f32)]
    psum x4 -> x0, blocking collectives: 68.4 us -> none  [the longest x1 40 us: per_device(): lax.psum((place_into(model_dim, grad_norm_part, feature_start), place_int...]
    all_gather x6 -> x0, blocking collectives: 68.1 us -> none  [the longest x5 59.8 us: per_device(): lax.all_gather(w, 'seq', axis=0, tiled=True)]
    convert_element_type x14 -> x0, other arithmetic: 24.9 us -> none  [the longest x10 18.1 us: scattered(): lax.psum_scatter(grad.astype(bf16), 'seq', scatter_dimension=axis, tiled=...]
    all_to_all x2 -> x0, blocking collectives: 20.3 us -> none  [the longest x1 13.3 us: to_pairs(): y = lax.all_to_all(y, 'seq', 0, 0)]
  transfers between devices with their start and end apart: 30 -> 0, of which waited for: 24 -> 0; matrix products, arithmetic and copies ran while one was open for 10% -> 0% of each run, Pallas kernels for 3% -> 0%
where the time goes in v7:
time: 407 us
  Pallas kernels  406 us (100%)
    pallas_call x1, Pallas kernels, layer(): pl.pallas_call(functools.partial(layer_kernel, (n, zc, copies, heads, DK,...  394 us
    pallas_call x1, Pallas kernels, last(): pl.pallas_call(functools.partial(last_kernel, n, copies, heads, DK, DV, F...  12 us

profile of v7, /device:TPU:0, one launch (start us, length us, event | category | flops | bytes accessed | tf_op | source)
XLA Modules:
  0.0 406.5 jit_solution(3067207478387512093)
XLA Ops:
  0.7 393.6 %layer.1 = (f32[256,512]{1,0:T(8,128)}, f32[256,512]{1,0:T(8,128)}, f32[8,8,512]{2,1,0:T(8,128)}, f32[4,8,512]{2,1,0:T(8,128)}, f32[256,1408]{1,0:T(8,128)}, /*i...) custom-call(bf16[256,512]{1,0:T(8,128)(2,1)} %bitcast.22, ...), custom_call_target="tpu_custom_call" | custom-call | tf_op jit(solution)/shard_map/layer/pallas_call | solution.py:858
  394.3 12.0 %last.1 = (f32[256,512]{1,0:T(8,128)}, f32[256,512]{1,0:T(8,128)}, f32[256,1024]{1,0:T(8,128)}, f32[4,256]{1,0:T(4,128)}, f32[4,256]{1,0:T(4,128)}, /*index=5*/f...) custom-call(bf16[8,256,256]{2,1,0:T(8,128)(2,1)} %get-tuple-element., ...), custom_call_target="tpu_custom_call" | custom-call | tf_op jit(solution)/shard_map/last/pallas_call | solution.py:904

commit v8 on v7

--- a/solution.py
+++ b/solution.py
@@ -364,6 +364,8 @@
     gate_ref,rbuf,dpre,du_ref,dx_ref,do_ref,dxr,ds_ref=r_.gate,r_.rbuf,r_.dpre,r_.du,r_.dx,r_.do,r_.dxr,r_.ds
     heads_v=pl.ds(0,DV); rest_v=pl.ds(DV,DV)
 
+    greet(n,zc)
+    zt=ShardGather(zc,tok,r_.tokfull,*zsems()); zt.start()
     put=lambda x,first: dg(x[...],jnp.where(lax.broadcasted_iota(jnp.int32,(x.shape[0],128),0)+first==lax.broadcasted_iota(jnp.int32,(x.shape[0],128),1),1.0,0.0).astype(bf16),0,0)
     ws=r_.ws
     ws[...]=(put(r_.wb,0)+put(r_.wd,heads)).astype(bf16)
@@ -371,8 +373,6 @@
     for x in (r_.qc,r_.kc,r_.vc):
         ws[at_row:at_row+x.shape[1]]=(ws[at_row:at_row+x.shape[1]].astype(f32)+put(x,2*heads)).astype(bf16)
         at_row+=x.shape[1]
-    greet(n,zc)
-    zt=ShardGather(zc,tok,r_.tokfull,*zsems()); zt.start()
     ws_all=(ws,r_.wq,r_.wk,r_.wv); at=(wk*2+wv,0,wk,wk*2)
     gw=[gather(w,r_.wfull,0,a) for w,a in zip(ws_all,at)]
     each(gw,"start")
@@ -381,6 +381,9 @@
     dx_ref[...]=jnp.zeros(dx_ref.shape,f32)
     rate=jnp.exp(jnp.full((1,1),r_.dlog[at_head],f32)); bias=r_.dbias[at_head]
     each(gw,"middle")
+    gb=[gather(r_.wg,r_.wgfull,0),gather(r_.wo,r_.wofull,1),gather(r_.wgate,gw_,0)]
+    gu=[gather(r_.wup,uw_,0),gather(r_.wdown,dw_,1)]
+    gb[0].start()
     zt.finish()
     zk=ShardGather(zc,cot,cotfull,*zsems()); zk.start()
     def norm(c):
@@ -390,6 +393,7 @@
         normed[r,:]=(x*sc*r_.gain[...]).astype(bf16)
         scale[r,:]=jnp.broadcast_to(sc,(32,128))
     loop(RN//32,norm)
+    n1=SharedColumns(n,zc,normed,r_.n1c,(*qsems(),*zsems())); n1.start()
     inward=ToPairs(n,copies,heads,ll,pbuf,rbuf,u_ref,xr_ref,DK,DV,r_.isend,r_.irecv,16)
     for i,g in enumerate(gw):
         g.late(); g.finish()
@@ -418,12 +422,14 @@
                 pbuf[:,pl.ds(pl.multiple_of(at[i]+j*256,128),256)]=jnp.dot(normed[...],wbuf[0:D,pl.ds(pl.multiple_of(j*256,256),256)],preferred_element_type=f32).astype(bf16)
             loop(width//256,column)
         inward.start((3,0,1,2)[i])
-    n1=SharedColumns(n,zc,normed,r_.n1c,(*qsems(),*zsems())); n1.start()
+    gb[1].start()
     zk.finish()
     cc=SharedColumns(n,zc,cotfull,r_.cotc,(*qsems(),*zsems())); cc.start()
+    n1.middle()
+    gb[0].middle()
     inward.finish()
-    gb=[gather(r_.wg,r_.wgfull,0),gather(r_.wo,r_.wofull,1),gather(r_.wgate,gw_,0)]
-    each(gb,"start")
+    gb[2].start()
+    cc.middle()
 
     def turn(m):
         r=pl.ds(pl.multiple_of(m*8,8),8)
@@ -444,7 +450,8 @@
         k_ref[rows,:]=(ak*lax.rsqrt(jnp.sum(ak*ak,axis=1,keepdims=True)+EPSILON)).astype(bf16)
         v_ref[rows,:]=act[:,2*DK:].astype(bf16)
     loop(L//R,conv)
-    n1.middle(); cc.middle()
+    gb[1].middle()
+    gu[1].start()
     kcol,pcol,ecol=pl.ds(0,DK),pl.ds(DK,SPAN),pl.ds(DK+SPAN,DK)
     def local(m):
         xr=xr_ref[pl.ds(pl.multiple_of(m*8,8),8),:]
@@ -464,20 +471,20 @@
     inverses(lambda b: dx_ref[b*SPAN:(b+1)*SPAN,0:SPAN],t_ref)
     def solve(b):
         rows=span(b)
-        T=t_ref[b].astype(bf16)
-        U=dg(T,dpre[rows,rest_v].astype(bf16)); Wk=dg(T,du_ref[rows,kcol])
-        Ub=U.astype(bf16); Wb=Wk.astype(bf16); Pm=du_ref[rows,pcol]; ek=du_ref[rows,ecol]
+        Th,Tl=halves(t_ref[b]); Vh,Vl=halves(dpre[rows,rest_v]); bk=du_ref[rows,kcol]
+        U=dg(Th,Vh)+(dg(Tl,Vh)+dg(Th,Vl)); Wk=dg(Th,bk)+dg(Tl,bk)
+        Ub,Ul=halves(U); Wb,Wl=halves(Wk); Pm=du_ref[rows,pcol]; ek=du_ref[rows,ecol]
         dpre[rows,heads_v]=dg(Pm,Ub)
         w_ref[b]=U
         qt_ref[b,0:SPAN]=(qt_ref[b,0:SPAN].astype(f32)-dg(Pm,Wb)).astype(bf16)
         qt_ref[b,SPAN:]=Wb
-        ds_ref[b]=dg(ek,Ub,0,0)
-        mh_ref[b]=dg(ek,Wb,0,0).astype(bf16)
+        ds_ref[b]=dg(ek,Ub,0,0)+dg(ek,Ul,0,0)
+        mh_ref[b,0],mh_ref[b,1]=halves(dg(ek,Wb,0,0)+dg(ek,Wl,0,0))
     loop(NC,solve,4)
     def chain(b,St):
         s_ref[b]=St
-        sh,sl=halves(St); mh=mh_ref[b]
-        return jnp.concatenate([gc_ref[b][0:1]]*(DV//128),axis=1)*St+ds_ref[b]-(dg(mh,sh)+dg(mh,sl))
+        sh,sl=halves(St); mh=mh_ref[b,0]
+        return jnp.concatenate([gc_ref[b][0:1]]*(DV//128),axis=1)*St+ds_ref[b]-(dg(mh,sh)+(dg(mh,sl)+dg(mh_ref[b,1],sh)))
     lax.fori_loop(0,NC,chain,jnp.zeros((DK,DV),f32),unroll=2)
     def emit(b):
         rows=span(b)
@@ -489,13 +496,13 @@
     outward=FromPairs(n,copies,heads,ll,[(do_ref,lambda t: (seq_rows(t),slice(None)),oall,lambda seq,head: (seq_rows(seq),pl.ds(pl.multiple_of(head*DV,128),DV)))],r_.osend,r_.orecv)
     outward.start()
 
-    gb[0].middle(); gb[0].late(); gb[0].finish()
+    gb[0].late(); gb[0].finish()
     c=pltpu.make_async_copy(r_.wgfull,wbuf.at[pl.ds(0,D),pl.ds(0,wv)],r_.ld.at[0,0]); c.start(); c.wait()
     def column(j):
         k_=pl.ds(pl.multiple_of(j*256,256),256)
         gate_ref[:,k_]=jnp.dot(normed[...],wbuf[0:D,k_],preferred_element_type=f32)
     loop(wv//256,column)
-    gb[1].middle(); gb[1].late(); gb[1].finish()
+    gb[1].late(); gb[1].finish(); gb[2].middle()
     blocks=D//VW
     def load_wo(buf,sems):
         cs=[pltpu.make_async_copy(r_.wofull.at[:,pl.ds(j*VW,VW)],buf.at[pl.ds(j*VW,VW),pl.ds(0,VW)],sems.at[j]) for j in range(blocks)]
@@ -520,9 +527,8 @@
     split=ShardSplit(zc,pbf,r_.box,*zsems()); split.start()
     for d in range(1,n): pl.semaphore_signal(r_.free,inc=1,device_id={"seq":lax.rem(s+d,n)},device_id_type=MESH)
     pl.semaphore_wait(r_.free,n-1)
-    gu=[gather(r_.wup,uw_,0),gather(r_.wdown,dw_,1)]
-    each(gu,"start")
-    gb[2].middle()
+    gu[0].start()
+    gu[1].middle()
 
     F_at=pl.ds(pl.multiple_of(z*F,128),F)
     fgain=r_.fgain[:,F_at]
@@ -546,9 +552,10 @@
     sc=lax.rsqrt(shard_sum(0,row_form(x*x))+EPSILON)
     nloc[...]=(res[...]*sc*fgain).astype(bf16)
     zg=ShardGather(zc,nloc,nfull,*zsems()); zg.start()
-    gb[2].late(); each(gu,"middle"); gb[2].finish()
+    gb[2].late(); gb[2].finish(); gu[0].middle(); gu[1].late()
+    gk=[gather(r_.dgp,r_.dgpfull,0),gather(branch,r_.brafull,0)]
+    gk[1].start()
     zg.finish()
-    n2=ColumnSplit(n,nfull,r_.n2c,*qsems()); n2.start()
     for a,b in tiles(FF,512): gv[:,a:b]=jnp.dot(nfull[...],gw_[:,a:b],preferred_element_type=f32)
     gu[0].late(); gu[0].finish()
     for a,b in tiles(FF,512): uv[:,a:b]=jnp.dot(nfull[...],uw_[:,a:b],preferred_element_type=f32)
@@ -559,13 +566,13 @@
         hidden[rr,:]=(g*sigmoid(g)*uv[rr,:]).astype(bf16)
     loop(RN//32,act)
     gh=[gather(hidden,r_.hidfull,0),gather(dgate,r_.dgfull,0),gather(dup,r_.dufull,0)]
-    gu[1].late(); gu[1].finish()
+    gu[1].finish()
     for a,b in tiles(FF,512):
         dh=dg(cotfull[...],dw_[a:b,:],1,1)
         g=gv[:,a:b]; sg=sigmoid(g)
         dgate[:,a:b]=(dh*uv[:,a:b]*sg*(1.0+g*(1.0-sg))).astype(bf16)
         dup[:,a:b]=(dh*(g*sg)).astype(bf16)
-    each(gh[1:]+gh[:1],"start")
+    each(gh[1:],"start")
     def back_two(j):
         rr=pl.ds(pl.multiple_of(j*256,256),256)
         pbf[:,rr]=(dg(dgate[...],gw_[rr,:],1,1)+dg(dup[...],uw_[rr,:],1,1)).astype(bf16)
@@ -589,6 +596,8 @@
         r_.outpart[:,c_]=jnp.dot(hidden[...],dw_[:,c_],preferred_element_type=f32).astype(bf16)
     loop(D//256,outp)
     split.finish()
+    gk[1].middle(); gh[1].middle()
+    gh[0].start()
     g=boxed(r_.box)
     gained=fgain*g
     gffn=[None]
@@ -598,8 +607,9 @@
     gres[...]=gr
     nloc[...]=gr.astype(bf16)
     zg=ShardGather(zc,nloc,afull,*zsems()); zg.start()
-    each(gh[1:]+gh[:1],"middle")
+    gh[2].middle()
     zg.finish()
+    n2=SharedColumns(n,zc,nfull,r_.n2c,(*qsems(),*zsems())); n2.start()
     so=ShardSplit(zc,r_.outpart,r_.boxo,*zsems()); so.start()
 
     ready("wo")
@@ -624,12 +634,11 @@
         return gh_
     grad_head=lax.fori_loop(0,RN//64,heads_back,jnp.zeros((1,DV),f32))
     inward=ToPairs(n,copies,heads,ll,dob,None,do_ref,None,DK,DV,r_.i2send,r_.i2recv); inward.start(0)
-    each(gh[1:]+gh[:1],"late")
-    n2.finish()
-    gk=[gather(dgp,r_.dgpfull,0),gather(branch,r_.brafull,0)]
+    each(gh[1:],"late"); gh[0].middle()
+    gk[1].late()
     inward.finish()
     ca=SharedColumns(n,zc,afull,r_.attc,(*qsems(),*zsems())); ca.start()
-    each(gk,"start")
+    gk[0].start()
 
     dpre[L:L+8]=jnp.zeros((8,CH),f32)
     def early(b):
@@ -639,8 +648,8 @@
         b=NC-1-m
         x=ds_ref[b]
         ds_ref[b]=dS
-        sh,sl=halves(dS); mh=mh_ref[b]
-        return jnp.concatenate([gc_ref[b][0:1]]*(DV//128),axis=1)*dS+x-(dg(mh,sh,0,0)+dg(mh,sl,0,0))
+        sh,sl=halves(dS); mh=mh_ref[b,0]
+        return jnp.concatenate([gc_ref[b][0:1]]*(DV//128),axis=1)*dS+x-(dg(mh,sh,0,0)+(dg(mh,sl,0,0)+dg(mh_ref[b,1],sh,0,0)))
     lax.fori_loop(0,NC,chain_back,jnp.zeros((DK,DV),f32),unroll=2)
     def one_span(b,xr):
         rows=span(b)
@@ -648,15 +657,15 @@
         beta,Dm,gam,end,KK,QK,i,j=span_terms(b,q,k,starts,xc_ref[rows,:],xr)
         beta2=jnp.concatenate([beta]*(DV//128),axis=1)
         S0=s_ref[b]; dS1=ds_ref[b]
-        S0h=S0.astype(bf16); dSh=dS1.astype(bf16)
+        S0h,S0l=halves(S0); dSh,dSl=halves(dS1)
         kf=k.astype(f32); qf=q.astype(f32); vf=v.astype(f32)
-        W=w_ref[b].astype(bf16); T=t_ref[b].astype(bf16)
-        Pm=(QK*Dm).astype(bf16)
-        dW=dg(Pm,dO,0,0)+jnp.concatenate([end]*(DV//128),axis=1)*dg(k,dSh)
-        Y=dg(T,dW.astype(bf16),0,0)
+        W,Wl=halves(w_ref[b])
+        Ph,Pl=halves(QK*Dm)
+        dW=dg(Ph,dO,0,0)+dg(Pl,dO,0,0)+jnp.concatenate([end]*(DV//128),axis=1)*(dg(k,dSh)+dg(k,dSl))
+        Y=mm3(t_ref[b],dW,0,0)
         dOY=jnp.concatenate([dO,Y.astype(bf16)],axis=0)
-        dPA=dg(dOY,W,1,1)
-        GS=dg(dOY,S0h,1,1)
+        dPA=dg(dOY,W,1,1)+dg(dOY,Wl,1,1)
+        GS=dg(dOY,S0h,1,1)+dg(dOY,S0l,1,1)
         dOS=GS[:SPAN]; YS=GS[SPAN:]
         Z=dg(W,dSh,1,1)
         dPD=dPA[:SPAN]*Dm
@@ -686,7 +695,7 @@
         xr=xr_ref[r,:]
         dxr[r,:]=jnp.broadcast_to(jnp.concatenate([one_span(m*per+e,xr[:,e*SPAN:(e+1)*SPAN]) for e in range(per)],axis=1),(8,ll))
     loop(n,local_back,2)
-    ca.middle()
+    n2.middle(); ca.middle()
     il=lax.broadcasted_iota(jnp.int32,(ll,ll),0); jl=lax.broadcasted_iota(jnp.int32,(ll,ll),1)
     later=jnp.where((il>=jl)&((il//SPAN)==(jl//SPAN)),1.0,0.0)
     def turn_back(m,carry):
@@ -731,6 +740,7 @@
             d=d+window[sh:sh+R]*jnp.where(age[sh:sh+R]>=sh,1.0,0.0)*taps[3-sh:4-sh]
         du_ref[pl.ds(base,R),:]=d.astype(bf16)
     loop(L//R,back)
+    gk[0].middle()
     dyq,dsm=pbuf,r_.dsm
     cut=lambda start,width: (lambda t: (seq_rows(t),pl.ds(start,width)))
     to=lambda start,width: (lambda seq,head: (seq_rows(seq),pl.ds(pl.multiple_of(start+head*width,128),width)))
@@ -753,6 +763,7 @@
     def send(k,view,ref):
         staged[k]=pltpu.make_async_copy(view,ref,r_.stsem.at[k]); staged[k].start()
     ready("og"); spread(True,bufb,[(dgp,0,wv)])
+    gh[0].late(); n2.finish()
     each(gh,"finish")
     load_job("dgate",0,[(r_.dgfull,every(FF))])
     c2=pltpu.make_async_copy(r_.n2c,r_.cola,ld.at[0,4]); c2.start()
@@ -760,8 +771,9 @@
     so.finish()
     r_.output[...]=res[...]+boxed(r_.boxo)
     ready("dgate"); c2.wait()
+    n2s=r_.cola[...].reshape(N,D//n)
     v_=stage(0,r_.ogate,(D//n,FF))
-    for a,b in tiles(FF,512): v_[:,a:b]=dg(r_.cola[...],bufa[0:N,a:b],0,0)
+    for a,b in tiles(FF,512): v_[:,a:b]=dg(n2s,bufa[0:N,a:b],0,0)
     send(0,v_,r_.ogate)
     load_job("wv",0,[(r_.wfull.at[:,pl.ds(2*wk,wv+128)],whole(wv+128))])
     outward.finish()
@@ -782,15 +794,14 @@
     loop(D//256,final)
     split=ShardSplit(zc,pbf,r_.box,*zsems()); split.start()
     load_job("hid",0,[(r_.hidfull,every(FF))])
-    each(gk,"middle"); each(gk,"late")
+    gk[0].late()
     ready("dup")
     v_=stage(0,r_.oup,(D//n,FF))
-    for a,b in tiles(FF,512): v_[:,a:b]=dg(r_.cola[...],bufb[0:N,a:b],0,0)
+    for a,b in tiles(FF,512): v_[:,a:b]=dg(n2s,bufb[0:N,a:b],0,0)
     send(0,v_,r_.oup)
-    n1.finish(); cc.finish(); ca.finish()
-    for g in gk: g.finish()
+    n1.finish(); cc.finish(); ca.finish(); gk[0].finish()
+    each(gd,"middle")
     cb=pltpu.make_async_copy(r_.cotc,r_.colb,ld.at[1,5]); cb.start()
-    load_job("bra",1,[(r_.brafull,every(VW))])
     ready("hid"); cb.wait()
     cots=r_.colb[...].reshape(N,D//n)
     v_=stage(1,r_.odown,(FF,D//n))
@@ -813,13 +824,14 @@
     sa=ShardAll("seq",n,smalls,*qsems()); sa.start()
     inner=shard_sum(2,row_form(gained*tok[...].astype(f32)))
     r_.gtok[...]=gres[...]+sc*(gained-tok[...].astype(f32)*(sc*sc*inner))
-    each(gd,"middle")
     sa.finish()
     t=smalls[0]
     for d in range(1,n): t=t+smalls[d]
     totals[z]=t
     za=ShardAll("shard",zc,totals,*zsems()); za.start()
     cb=pltpu.make_async_copy(r_.attc,r_.colb,ld.at[1,5]); cb.start()
+    gk[1].finish()
+    load_job("bra",1,[(r_.brafull,every(VW))])
     ready("bra"); cb.wait()
     atts=r_.colb[...].reshape(N,D//n)
     v_=stage(1,r_.oout,(VW,D//n))
@@ -842,16 +854,16 @@
     specs=[VM]*5+[SM]*3+[VM]*10+[ANY]*3
     outs=[("output",S((RN,F)),VM),("gtok",S((RN,F)),VM),("smalls",S((n,8,W)),VM),("totals",S((zc,8,W)),VM)]
     for name,shape in (("ogate",(Dc,FF)),("oup",(Dc,FF)),("odown",(FF,Dc)),("oout",(wv,Dc)),("oog",(Dc,wv))): outs.append((name,S(shape),ANY))
-    for name,shape in (("dyqfull",(N,heads*CH)),("dsmfull",(N,128)),("n1c",(n,RN,Dc)),("cotc",(n,RN,Dc)),("attc",(n,RN,Dc)),("n2c",(N,Dc)),("wfull",(D,heads*CH+128)),("wgfull",(D,wv)),("wofull",(wv,D)),
+    for name,shape in (("dyqfull",(N,heads*CH)),("dsmfull",(N,128)),("n1c",(n,RN,Dc)),("cotc",(n,RN,Dc)),("attc",(n,RN,Dc)),("n2c",(n,RN,Dc)),("wfull",(D,heads*CH+128)),("wgfull",(D,wv)),("wofull",(wv,D)),
         ("hidfull",(N,FF)),("dgfull",(N,FF)),("dufull",(N,FF)),("dgpfull",(N,wv)),("brafull",(N,wv))): outs.append((name,S(shape,bf16),ANY))
     V=pltpu.VMEM; sem=pltpu.SemaphoreType.DMA
     scratch=[("scale",V((RN,128),f32)),("ws",V((Dc,128),bf16)),("sbuf",V((D,128),bf16)),("tbuf",V((CH,128),bf16)),("tokfull",V((RN,D),bf16)),("normed",V((RN,D),bf16)),("cotfull",V((RN,D),bf16)),
         ("nfull",V((RN,D),bf16)),("pbf",V((RN,D),bf16)),("outpart",V((RN,D),bf16)),("acc",V((RN,D),f32)),("uv",V((RN,FF),f32)),("gv",V((RN,FF),f32)),("rbuf",V((pairs*8,ll),f32)),("taps",V((4,CH),f32)),
         ("bufa",V((big,bw),bf16)),("bufb",V((big,bw),bf16)),("dw",V((FF,D),bf16)),("u",V((L+16,CH),bf16)),("xr",V((n*8,ll),f32)),("xc",V((L,8),f32)),("q",V((L,DK),bf16)),("k",V((L,DK),bf16)),("v",V((L,DV),bf16)),
-        ("s",V((NC,DK,DV),f32)),("w",V((NC,SPAN,DV),f32)),("t",V((NC,SPAN,SPAN),f32)),("qt",V((NC,2*SPAN,DK),bf16)),("mh",V((NC,DK,DK),bf16)),("gc",V((NC,8,128),f32)),("ds",V((NC,DK,DV),f32)),
+        ("s",V((NC,DK,DV),f32)),("w",V((NC,SPAN,DV),f32)),("t",V((NC,SPAN,SPAN),f32)),("qt",V((NC,2*SPAN,DK),bf16)),("mh",V((NC,2,DK,DK),bf16)),("gc",V((NC,8,128),f32)),("ds",V((NC,DK,DV),f32)),
         ("dpre",V((L+8,CH),f32)),("du",V((L,CH),bf16)),("dx",V((L,SPAN),f32)),("do",V((L,DV),bf16)),("dxr",V((n*8,ll),f32)),("gate",V((RN,wv),f32)),("oall",V((RN,wv),bf16)),("branch",V((RN,wv),bf16)),
         ("dob",V((RN,wv),bf16)),("dgp",V((RN,wv),bf16)),("dsm",V((RN,128),bf16)),("res",V((RN,F),f32)),("gres",V((RN,F),f32)),("nloc",V((RN,F),bf16)),("box",V((zc,RN,F),bf16)),("boxo",V((zc,RN,F),bf16)),
-        ("hidden",V((RN,FF),bf16)),("dgate",V((RN,FF),bf16)),("dup",V((RN,FF),bf16)),("sums",V((3*zc,8,RN),f32)),("cola",V((N,Dc),bf16)),("colb",V((n,RN,Dc),bf16)),("sta",V((Dc,max(FF,wv)),f32)),("stb",V((max(FF,wv),Dc),f32)),
+        ("hidden",V((RN,FF),bf16)),("dgate",V((RN,FF),bf16)),("dup",V((RN,FF),bf16)),("sums",V((3*zc,8,RN),f32)),("cola",V((n,RN,Dc),bf16)),("colb",V((n,RN,Dc),bf16)),("sta",V((Dc,max(FF,wv)),f32)),("stb",V((max(FF,wv),Dc),f32)),
         ("zsend",sem((16,zc))),("zrecv",sem((16,zc))),("qsend",sem((6,n))),("qrecv",sem((6,n))),("gsend",sem((16,links(n)))),("grecv",sem((16,links(n)))),("gloc",sem((16,))),("isend",sem((4,n))),("irecv",sem((4,n))),("i2send",sem((1,n))),("i2recv",sem((1,n))),
         ("osend",sem((1,pairs))),("orecv",sem((1,pairs))),("o2send",sem((4,pairs))),("o2recv",sem((4,pairs))),("ld",sem((2,6))),("stsem",sem((2,))),("free",pltpu.SemaphoreType.REGULAR)]
     all_names=names+tuple(o[0] for o in outs)+tuple(x[0] for x in scratch)
@@ -863,10 +875,12 @@
 def last_kernel(n,copies,heads,DK,DV,F,H,n1c,dyq,dsm,smalls,totals,*refs):
     moved=refs[:7]; oq,ok,ov,ob,od,qc,kc,vc,onorm,offn,ohead,olog,obias=refs[7:20]; moved_out=refs[20:27]; buf,sem,msem=refs[27:30]; held=refs[30:]
     step=buf.shape[1]//4
+    fetch=[pltpu.make_async_copy(a,b,msem.at[j]) for j,(a,b) in enumerate(zip(moved,held))]
+    for c in fetch: c.start()
     jobs=[pltpu.make_async_copy(dyq.at[:,pl.ds(j*step,step)],buf.at[:,pl.ds(j*step,step)],sem.at[j]) for j in range(4)]
     for c in jobs: c.start()
-    fetch=[pltpu.make_async_copy(a,b,msem.at[j]) for j,(a,b) in enumerate(zip(moved,held))]
-    for c in fetch: c.start()
+    moves=[pltpu.make_async_copy(a,b,msem.at[j]) for j,(a,b) in enumerate(zip(held,moved_out))]
+    for f,c in zip(fetch,moves): f.wait(); c.start()
     n1=n1c[...].reshape(n1c.shape[0]*n1c.shape[1],n1c.shape[2])
     sm=dg(dsm[...],n1,0,0)
     ob[...]=sm[0:heads]; od[...]=sm[heads:2*heads]
@@ -877,8 +891,6 @@
             b=min(a+256,ref.shape[1])
             while got*step<start+b: jobs[got].wait(); got+=1
             ref[:,a:b]=dg(n1,buf[:,start+a:start+b],0,0)
-    moves=[pltpu.make_async_copy(a,b,msem.at[j]) for j,(a,b) in enumerate(zip(held,moved_out))]
-    for f,c in zip(fetch,moves): f.wait(); c.start()
     zc=totals.shape[0]
     for z in range(zc):
         onorm[0:1,z*F:(z+1)*F]=totals[z,0:1,0:F]

time: 407 us -> 396 us (0.973)
  Pallas kernels: 406 us -> 393 us
    pallas_call x1, Pallas kernels: 394 us -> 379 us  [layer(): pl.pallas_call(functools.partial(layer_kernel, (n, zc, copies, heads, DK,...]
where the time goes in v8:
time: 396 us; the launch traced here: 394 us
  Pallas kernels  393 us (99%)
    pallas_call x1, Pallas kernels, layer(): pl.pallas_call(functools.partial(layer_kernel, (n, zc, copies, heads, DK,...  379 us
    pallas_call x1, Pallas kernels, last(): pl.pallas_call(functools.partial(last_kernel, n, copies, heads, DK, DV, F...  13.6 us

profile of v8, /device:TPU:0, one launch (start us, length us, event | category | flops | bytes accessed | tf_op | source)
XLA Modules:
  0.0 393.5 jit_solution(10796948230181680103)
XLA Ops:
  0.7 379.1 %layer.1 = (f32[256,512]{1,0:T(8,128)}, f32[256,512]{1,0:T(8,128)}, f32[8,8,512]{2,1,0:T(8,128)}, f32[4,8,512]{2,1,0:T(8,128)}, f32[256,1408]{1,0:T(8,128)}, /*i...) custom-call(bf16[256,512]{1,0:T(8,128)(2,1)} %bitcast.22, ...), custom_call_target="tpu_custom_call" | custom-call | tf_op jit(solution)/shard_map/layer/pallas_call | solution.py:870
  379.8 13.6 %last.1 = (f32[256,512]{1,0:T(8,128)}, f32[256,512]{1,0:T(8,128)}, f32[256,1024]{1,0:T(8,128)}, f32[4,256]{1,0:T(4,128)}, f32[4,256]{1,0:T(4,128)}, /*index=5*/f...) custom-call(bf16[8,256,256]{2,1,0:T(8,128)(2,1)} %get-tuple-element., ...), custom_call_target="tpu_custom_call" | custom-call | tf_op jit(solution)/shard_map/last/pallas_call | solution.py:916

commit v9 on v8

--- a/solution.py
+++ b/solution.py
@@ -244,7 +244,7 @@
         pair=lax.div(t,self.copies); seq=lax.div(pair,heads); head=lax.rem(pair,heads)
         rows=pl.ds(pl.multiple_of(seq*ll,ll),ll); to=pl.ds(pl.multiple_of(s*ll+self.off,16),ll)
         if self.rows_src is None:
-            return [(self.src.at[rows,pl.ds(pl.multiple_of(head*DV,128),DV)],self.dst.at[to,:])]
+            return [(a.at[rows,pl.ds(pl.multiple_of(head*DV,128),DV)],b.at[to,:]) for a,b in zip(self.src,self.dst)]
         wk=heads*DK
         out=[]
         for start,width,at in ((0,DK,0),(wk,DK,DK),(2*wk,DV,2*DK)):
@@ -629,11 +629,11 @@
             gh_=gh_+jnp.sum(dm*zz*sil,axis=0,keepdims=True)
             dmg=dm*r_.hgain[...]
             dz=dmg*sil
-            dob[r,hc]=(rho*(dz-zz*(jnp.sum(dz*zz,axis=1,keepdims=True)/DV))).astype(bf16)
+            dob[r,hc],r_.dobl[r,hc]=halves(rho*(dz-zz*(jnp.sum(dz*zz,axis=1,keepdims=True)/DV)))
             dgp[r,hc]=(dmg*zz*sg*(1.0+g*(1.0-sg))).astype(bf16)
         return gh_
     grad_head=lax.fori_loop(0,RN//64,heads_back,jnp.zeros((1,DV),f32))
-    inward=ToPairs(n,copies,heads,ll,dob,None,do_ref,None,DK,DV,r_.i2send,r_.i2recv); inward.start(0)
+    inward=ToPairs(n,copies,heads,ll,(dob,r_.dobl),None,(do_ref,r_.dol),None,DK,DV,r_.i2send,r_.i2recv); inward.start(0); inward.start(1)
     each(gh[1:],"late"); gh[0].middle()
     gk[1].late()
     inward.finish()
@@ -642,7 +642,7 @@
 
     dpre[L:L+8]=jnp.zeros((8,CH),f32)
     def early(b):
-        ds_ref[b]=dg(qt_ref[b][0:SPAN],do_ref[span(b),:],0,0)
+        ds_ref[b]=dg(qt_ref[b][0:SPAN],do_ref[span(b),:],0,0)+dg(qt_ref[b][0:SPAN],r_.dol[span(b),:],0,0)
     loop(NC,early,4)
     def chain_back(m,dS):
         b=NC-1-m
@@ -653,7 +653,7 @@
     lax.fori_loop(0,NC,chain_back,jnp.zeros((DK,DV),f32),unroll=2)
     def one_span(b,xr):
         rows=span(b)
-        q=q_ref[rows,:]; k=k_ref[rows,:]; v=v_ref[rows,:]; dO=do_ref[rows,:]
+        q=q_ref[rows,:]; k=k_ref[rows,:]; v=v_ref[rows,:]; dO=do_ref[rows,:]; dOl=r_.dol[rows,:]
         beta,Dm,gam,end,KK,QK,i,j=span_terms(b,q,k,starts,xc_ref[rows,:],xr)
         beta2=jnp.concatenate([beta]*(DV//128),axis=1)
         S0=s_ref[b]; dS1=ds_ref[b]
@@ -661,13 +661,14 @@
         kf=k.astype(f32); qf=q.astype(f32); vf=v.astype(f32)
         W,Wl=halves(w_ref[b])
         Ph,Pl=halves(QK*Dm)
-        dW=dg(Ph,dO,0,0)+dg(Pl,dO,0,0)+jnp.concatenate([end]*(DV//128),axis=1)*(dg(k,dSh)+dg(k,dSl))
+        dW=dg(Ph,dO,0,0)+(dg(Pl,dO,0,0)+dg(Ph,dOl,0,0))+jnp.concatenate([end]*(DV//128),axis=1)*(dg(k,dSh)+dg(k,dSl))
         Y=mm3(t_ref[b],dW,0,0)
-        dOY=jnp.concatenate([dO,Y.astype(bf16)],axis=0)
-        dPA=dg(dOY,W,1,1)+dg(dOY,Wl,1,1)
-        GS=dg(dOY,S0h,1,1)+dg(dOY,S0l,1,1)
+        Yh,Yl=halves(Y)
+        dOY=jnp.concatenate([dO,Yh],axis=0); dOYl=jnp.concatenate([dOl,Yl],axis=0)
+        dPA=dg(dOY,W,1,1)+(dg(dOY,Wl,1,1)+dg(dOYl,W,1,1))
+        GS=dg(dOY,S0h,1,1)+(dg(dOY,S0l,1,1)+dg(dOYl,S0h,1,1))
         dOS=GS[:SPAN]; YS=GS[SPAN:]
-        Z=dg(W,dSh,1,1)
+        Z=dg(W,dSh,1,1)+(dg(Wl,dSh,1,1)+dg(W,dSl,1,1))
         dPD=dPA[:SPAN]*Dm
         EA=jnp.where(i>j,-dPA[SPAN:]*Dm,0.0)
         A1=jnp.concatenate([dPD,beta[:,:SPAN]*EA],axis=0).astype(bf16)
@@ -862,9 +863,9 @@
         ("bufa",V((big,bw),bf16)),("bufb",V((big,bw),bf16)),("dw",V((FF,D),bf16)),("u",V((L+16,CH),bf16)),("xr",V((n*8,ll),f32)),("xc",V((L,8),f32)),("q",V((L,DK),bf16)),("k",V((L,DK),bf16)),("v",V((L,DV),bf16)),
         ("s",V((NC,DK,DV),f32)),("w",V((NC,SPAN,DV),f32)),("t",V((NC,SPAN,SPAN),f32)),("qt",V((NC,2*SPAN,DK),bf16)),("mh",V((NC,2,DK,DK),bf16)),("gc",V((NC,8,128),f32)),("ds",V((NC,DK,DV),f32)),
         ("dpre",V((L+8,CH),f32)),("du",V((L,CH),bf16)),("dx",V((L,SPAN),f32)),("do",V((L,DV),bf16)),("dxr",V((n*8,ll),f32)),("gate",V((RN,wv),f32)),("oall",V((RN,wv),bf16)),("branch",V((RN,wv),bf16)),
-        ("dob",V((RN,wv),bf16)),("dgp",V((RN,wv),bf16)),("dsm",V((RN,128),bf16)),("res",V((RN,F),f32)),("gres",V((RN,F),f32)),("nloc",V((RN,F),bf16)),("box",V((zc,RN,F),bf16)),("boxo",V((zc,RN,F),bf16)),
+        ("dob",V((RN,wv),bf16)),("dobl",V((RN,wv),bf16)),("dol",V((L,DV),bf16)),("dgp",V((RN,wv),bf16)),("dsm",V((RN,128),bf16)),("res",V((RN,F),f32)),("gres",V((RN,F),f32)),("nloc",V((RN,F),bf16)),("box",V((zc,RN,F),bf16)),("boxo",V((zc,RN,F),bf16)),
         ("hidden",V((RN,FF),bf16)),("dgate",V((RN,FF),bf16)),("dup",V((RN,FF),bf16)),("sums",V((3*zc,8,RN),f32)),("cola",V((n,RN,Dc),bf16)),("colb",V((n,RN,Dc),bf16)),("sta",V((Dc,max(FF,wv)),f32)),("stb",V((max(FF,wv),Dc),f32)),
-        ("zsend",sem((16,zc))),("zrecv",sem((16,zc))),("qsend",sem((6,n))),("qrecv",sem((6,n))),("gsend",sem((16,links(n)))),("grecv",sem((16,links(n)))),("gloc",sem((16,))),("isend",sem((4,n))),("irecv",sem((4,n))),("i2send",sem((1,n))),("i2recv",sem((1,n))),
+        ("zsend",sem((16,zc))),("zrecv",sem((16,zc))),("qsend",sem((6,n))),("qrecv",sem((6,n))),("gsend",sem((16,links(n)))),("grecv",sem((16,links(n)))),("gloc",sem((16,))),("isend",sem((4,n))),("irecv",sem((4,n))),("i2send",sem((2,n))),("i2recv",sem((2,n))),
         ("osend",sem((1,pairs))),("orecv",sem((1,pairs))),("o2send",sem((4,pairs))),("o2recv",sem((4,pairs))),("ld",sem((2,6))),("stsem",sem((2,))),("free",pltpu.SemaphoreType.REGULAR)]
     all_names=names+tuple(o[0] for o in outs)+tuple(x[0] for x in scratch)
     r=pl.pallas_call(functools.partial(layer_kernel,(n,zc,copies,heads,DK,DV,H),all_names),name="layer",out_shape=tuple(o[1] for o in outs),in_specs=specs,out_specs=tuple(o[2] for o in outs),

time: 396 us -> 403 us (1.018)
  Pallas kernels: 393 us -> 400 us
    pallas_call x1, Pallas kernels: 379 us -> 386 us  [layer(): pl.pallas_call(functools.partial(layer_kernel, (n, zc, copies, heads, DK,...]
where the time goes in v9:
time: 403 us; the launch traced here: 400 us
  Pallas kernels  400 us (99%)
    pallas_call x1, Pallas kernels, layer(): pl.pallas_call(functools.partial(layer_kernel, (n, zc, copies, heads, DK,...  386 us
    pallas_call x1, Pallas kernels, last(): pl.pallas_call(functools.partial(last_kernel, n, copies, heads, DK, DV, F...  13.6 us

profile of v9, /device:TPU:0, one launch (start us, length us, event | category | flops | bytes accessed | tf_op | source)
XLA Modules:
  0.0 400.5 jit_solution(14007562143030968900)
XLA Ops:
  0.7 386.0 %layer.1 = (f32[256,512]{1,0:T(8,128)}, f32[256,512]{1,0:T(8,128)}, f32[8,8,512]{2,1,0:T(8,128)}, f32[4,8,512]{2,1,0:T(8,128)}, f32[256,1408]{1,0:T(8,128)}, /*i...) custom-call(bf16[256,512]{1,0:T(8,128)(2,1)} %bitcast.22, ...), custom_call_target="tpu_custom_call" | custom-call | tf_op jit(solution)/shard_map/layer/pallas_call | solution.py:871
  386.7 13.6 %last.1 = (f32[256,512]{1,0:T(8,128)}, f32[256,512]{1,0:T(8,128)}, f32[256,1024]{1,0:T(8,128)}, f32[4,256]{1,0:T(4,128)}, f32[4,256]{1,0:T(4,128)}, /*index=5*/f...) custom-call(bf16[8,256,256]{2,1,0:T(8,128)(2,1)} %get-tuple-element., ...), custom_call_target="tpu_custom_call" | custom-call | tf_op jit(solution)/shard_map/last/pallas_call | solution.py:917

commit v10 on v9

--- a/solution.py
+++ b/solution.py
@@ -800,8 +800,7 @@
     v_=stage(0,r_.oup,(D//n,FF))
     for a,b in tiles(FF,512): v_[:,a:b]=dg(n2s,bufb[0:N,a:b],0,0)
     send(0,v_,r_.oup)
-    n1.finish(); cc.finish(); ca.finish(); gk[0].finish()
-    each(gd,"middle")
+    n1.finish(); cc.finish(); gk[0].finish()
     cb=pltpu.make_async_copy(r_.cotc,r_.colb,ld.at[1,5]); cb.start()
     ready("hid"); cb.wait()
     cots=r_.colb[...].reshape(N,D//n)
@@ -809,6 +808,14 @@
     for a,b in tiles(FF,256): v_[a:b,:]=dg(bufa[0:N,a:b],cots,0,0)
     send(1,v_,r_.odown)
     load_job("dgp",0,[(r_.dgpfull,every(wv))])
+    cb=pltpu.make_async_copy(r_.n1c,r_.colb,ld.at[1,5]); cb.start()
+    ready("dgp"); cb.wait()
+    n1s=r_.colb[...].reshape(N,D//n)
+    v_=stage(0,r_.oog,(D//n,wv))
+    for a,b in tiles(wv,512): v_[:,a:b]=dg(n1s,bufa[0:N,a:b],0,0)
+    send(0,v_,r_.oog)
+    each(gd,"middle")
+    ca.finish()
     split.finish()
     g=boxed(r_.box)
     sc=scale[...][:,0:1]
@@ -838,12 +845,6 @@
     v_=stage(1,r_.oout,(VW,D//n))
     for a,b in tiles(VW,256): v_[a:b,:]=dg(bufb[0:N,a:b],atts,0,0)
     send(1,v_,r_.oout)
-    cb=pltpu.make_async_copy(r_.n1c,r_.colb,ld.at[1,5]); cb.start()
-    ready("dgp"); cb.wait()
-    n1s=r_.colb[...].reshape(N,D//n)
-    v_=stage(0,r_.oog,(D//n,wv))
-    for a,b in tiles(wv,512): v_[:,a:b]=dg(n1s,bufa[0:N,a:b],0,0)
-    send(0,v_,r_.oog)
     each(gd,"late"); za.finish(); each(gd,"finish")
     staged[0].wait(); staged[1].wait()
 
@@ -876,12 +877,10 @@
 def last_kernel(n,copies,heads,DK,DV,F,H,n1c,dyq,dsm,smalls,totals,*refs):
     moved=refs[:7]; oq,ok,ov,ob,od,qc,kc,vc,onorm,offn,ohead,olog,obias=refs[7:20]; moved_out=refs[20:27]; buf,sem,msem=refs[27:30]; held=refs[30:]
     step=buf.shape[1]//4
+    jobs=[pltpu.make_async_copy(dyq.at[:,pl.ds(j*step,step)],buf.at[:,pl.ds(j*step,step)],sem.at[j]) for j in range(4)]
+    for c in jobs: c.start()
     fetch=[pltpu.make_async_copy(a,b,msem.at[j]) for j,(a,b) in enumerate(zip(moved,held))]
     for c in fetch: c.start()
-    jobs=[pltpu.make_async_copy(dyq.at[:,pl.ds(j*step,step)],buf.at[:,pl.ds(j*step,step)],sem.at[j]) for j in range(4)]
-    for c in jobs: c.start()
-    moves=[pltpu.make_async_copy(a,b,msem.at[j]) for j,(a,b) in enumerate(zip(held,moved_out))]
-    for f,c in zip(fetch,moves): f.wait(); c.start()
     n1=n1c[...].reshape(n1c.shape[0]*n1c.shape[1],n1c.shape[2])
     sm=dg(dsm[...],n1,0,0)
     ob[...]=sm[0:heads]; od[...]=sm[heads:2*heads]
@@ -892,6 +891,8 @@
             b=min(a+256,ref.shape[1])
             while got*step<start+b: jobs[got].wait(); got+=1
             ref[:,a:b]=dg(n1,buf[:,start+a:start+b],0,0)
+    moves=[pltpu.make_async_copy(a,b,msem.at[j]) for j,(a,b) in enumerate(zip(held,moved_out))]
+    for f,c in zip(fetch,moves): f.wait(); c.start()
     zc=totals.shape[0]
     for z in range(zc):
         onorm[0:1,z*F:(z+1)*F]=totals[z,0:1,0:F]

time: 403 us -> 400 us (level)
  no operation moved by 1% of the time
where the time goes in v10:
time: 400 us; the launch traced here: 399 us
  Pallas kernels  398 us (100%)
    pallas_call x1, Pallas kernels, layer(): pl.pallas_call(functools.partial(layer_kernel, (n, zc, copies, heads, DK,...  386 us
    pallas_call x1, Pallas kernels, last(): pl.pallas_call(functools.partial(last_kernel, n, copies, heads, DK, DV, F...  12 us

profile of v10, /device:TPU:0, one launch (start us, length us, event | category | flops | bytes accessed | tf_op | source)
XLA Modules:
  0.0 398.9 jit_solution(7146407019783492679)
XLA Ops:
  0.7 386.0 %layer.1 = (f32[256,512]{1,0:T(8,128)}, f32[256,512]{1,0:T(8,128)}, f32[8,8,512]{2,1,0:T(8,128)}, f32[4,8,512]{2,1,0:T(8,128)}, f32[256,1408]{1,0:T(8,128)}, /*i...) custom-call(bf16[256,512]{1,0:T(8,128)(2,1)} %bitcast.22, ...), custom_call_target="tpu_custom_call" | custom-call | tf_op jit(solution)/shard_map/layer/pallas_call | solution.py:872
  386.7 12.0 %last.1 = (f32[256,512]{1,0:T(8,128)}, f32[256,512]{1,0:T(8,128)}, f32[256,1024]{1,0:T(8,128)}, f32[4,256]{1,0:T(4,128)}, f32[4,256]{1,0:T(4,128)}, /*index=5*/f...) custom-call(bf16[8,256,256]{2,1,0:T(8,128)(2,1)} %get-tuple-element., ...), custom_call_target="tpu_custom_call" | custom-call | tf_op jit(solution)/shard_map/last/pallas_call | solution.py:918
